TPU v7x, 32 devices: a whole 2x2x4 slice. The times are simulated.
32 devices in a mesh: shard: 2 (over x), ctx: 4 (over z), tp: 4 (over y, core).
Axes of the slice: x: 2, y: 2, z: 4, core: 2. Of those that a mesh axis runs over, the one named last changes fastest.
Arguments:
- hidden_in: bfloat16 [4096, 2048], P(('shard', 'ctx'), 'tp'), may hold values from -6 to 6
- out_grad: bfloat16 [4096, 2048], P(('shard', 'ctx'), 'tp'), may hold values from -6 to 6
- seq_lengths: int32 [2, 3], P('shard'), may hold values from 1 to 1792, 2048 in all within a row
- deal_order: int32 [2, 16], P('shard'), may hold values from 0 to 15, as said below
- in_weight: bfloat16 [2048, 3, 2048], P('shard', None, 'tp'), may hold values from -0.125 to 0.125
- conv_weight: bfloat16 [3, 2048], P(None, 'tp'), may hold values from -3.5 to 3.5
- out_weight: bfloat16 [2048, 2048], P('shard', 'tp'), may hold values from -0.125 to 0.125
- norm1_gain: bfloat16 [2048], P('tp'), may hold values from 0.099609375 to 1.8984375
- norm2_gain: bfloat16 [2048], P('tp'), may hold values from 0.099609375 to 1.8984375
- gate_weight: bfloat16 [2048, 8192], P('shard', 'tp'), may hold values from -0.125 to 0.125
- up_weight: bfloat16 [2048, 8192], P('shard', 'tp'), may hold values from -0.125 to 0.125
- down_weight: bfloat16 [2048, 8192], P('shard', 'tp'), may hold values from -0.125 to 0.125
Outputs:
- block_out: bfloat16 [4096, 2048], P(('shard', 'ctx'), 'tp')
- input_grad: bfloat16 [4096, 2048], P(('shard', 'ctx'), 'tp')
- in_weight_grad: float32 [2048, 3, 2048], P('shard', None, 'tp')
- conv_weight_grad: float32 [3, 2048], P(None, 'tp')
- out_weight_grad: float32 [2048, 2048], P('shard', 'tp')
- norm1_gain_grad: float32 [2048], P('tp')
- norm2_gain_grad: float32 [2048], P('tp')
- gate_weight_grad: float32 [2048, 8192], P('shard', 'tp')
- up_weight_grad: float32 [2048, 8192], P('shard', 'tp')
- down_weight_grad: float32 [2048, 8192], P('shard', 'tp')
Inputs may be any that keep to these rules, and one draw needn't show every extreme that they name: `seq_lengths`: each row sums to 2048; one entry of each row equals exactly 1792. `deal_order`: each row is a permutation; the 4 slots of each device hold exactly 1 block of every device's packed range.
All inputs are finite; a program needn't handle non-finite values.
Results may differ from a plain program's by a relative error of at most 0.012.
Values may be sent and summed in bfloat16 or wider, within the bound.
A program may use at most 320 MiB of HBM per device.

v0:
```python
import jax
import jax.numpy as jnp
from jax import lax
from jax.sharding import PartitionSpec as P

EPS = 1e-05


def shifted(value, axis, steps):
    count = lax.axis_size(axis)
    leading, last = (max(0, -steps), min(count, count - steps))
    return lax.ppermute(value, axis, [(source, source + steps) for source in range(leading, last)])


def contract_rows(left, right):
    return lax.dot_general(
        left, right, (((0,), (0,)), ((), ())), preferred_element_type=jnp.float32
    )


def contract_cols(left, right):
    return lax.dot_general(
        left, right, (((1,), (1,)), ((), ())), preferred_element_type=jnp.float32
    )


def norm_back(grad_out, normed, scale_row, gain):
    scaled = grad_out * gain
    return scale_row * (scaled - normed * jnp.mean(scaled * normed, axis=1, keepdims=True))


def on_device(
    hidden_in,
    out_grad,
    seq_lengths,
    deal_order,
    in_weight,
    conv_weight,
    out_weight,
    norm1_gain,
    norm2_gain,
    gate_weight,
    up_weight,
    down_weight,
):
    ctx_size = lax.axis_size("ctx")
    ctx_rank = lax.axis_index("ctx")
    tp_rank = lax.axis_index("tp")
    row_count, col_count = hidden_in.shape
    per_dev = deal_order.shape[1] // ctx_size
    per_peer = per_dev // ctx_size
    block_rows = row_count // per_dev
    dealing = deal_order[0].reshape(ctx_size, per_dev)
    own_blocks = lax.dynamic_index_in_dim(dealing, ctx_rank, 0, keepdims=False)
    send_order = jnp.argsort(own_blocks // per_dev, stable=True)
    wanted = jnp.where(dealing // per_dev == ctx_rank, 0, 1)
    chosen = jnp.argsort(wanted, axis=1, stable=True)[:, :per_peer]
    targets = (jnp.take_along_axis(dealing, chosen, 1) % per_dev).reshape(-1)
    placing = jnp.argsort(targets)
    returning = jnp.argsort(send_order)

    def reorder(values, index):
        blocks = values.reshape(per_dev, block_rows, values.shape[1])
        return blocks[index].reshape(row_count, values.shape[1])

    got_x, got_grad = (
        lax.all_to_all(
            reorder(hidden_in, send_order), "ctx", split_axis=0, concat_axis=0, tiled=True
        ),
        lax.all_to_all(
            reorder(out_grad, send_order), "ctx", split_axis=0, concat_axis=0, tiled=True
        ),
    )
    x_packed = reorder(got_x, placing)
    grad_packed = reorder(got_grad, placing)
    gains = jnp.stack([norm1_gain, norm2_gain])
    x_full, cotangent, gains_full = (
        lax.all_gather(x_packed, "tp", axis=1, tiled=True),
        lax.all_gather(grad_packed, "tp", axis=1, tiled=True),
        lax.all_gather(gains, "tp", axis=1, tiled=True),
    )
    gain_one = gains_full[0].astype(jnp.float32)
    gain_two = gains_full[1].astype(jnp.float32)
    in_w, out_w, gate_w, up_w, down_w = (
        lax.all_gather(in_weight, "shard", axis=0, tiled=True),
        lax.all_gather(out_weight, "shard", axis=0, tiled=True),
        lax.all_gather(gate_weight, "shard", axis=0, tiled=True),
        lax.all_gather(up_weight, "shard", axis=0, tiled=True),
        lax.all_gather(down_weight, "shard", axis=0, tiled=True),
    )
    lengths = seq_lengths[0]
    starts = jnp.cumsum(lengths) - lengths
    where_t = ctx_rank * row_count - 2 + jnp.arange(row_count + 4, dtype=jnp.int32)
    seq_begin = jnp.max(jnp.where(starts[None, :] <= where_t[:, None], starts[None, :], 0), axis=1)
    position = where_t - seq_begin
    first_own = (position[2 : row_count + 2] >= 1).astype(jnp.float32)[:, None]
    second_own = (position[2 : row_count + 2] >= 2).astype(jnp.float32)[:, None]
    first_next = (position[3 : row_count + 3] >= 1).astype(jnp.float32)[:, None]
    second_next = (position[4 : row_count + 4] >= 2).astype(jnp.float32)[:, None]
    x_float = x_full.astype(jnp.float32)
    scale_one = lax.rsqrt(jnp.mean(x_float * x_float, axis=1, keepdims=True) + EPS)
    normed_one = x_float * scale_one
    h_one = (normed_one * gain_one).astype(jnp.bfloat16)
    projected = jnp.einsum("td,dpe->tpe", h_one, in_w, preferred_element_type=jnp.float32)
    b_part = projected[:, 0]
    c_part = projected[:, 1]
    v_part = projected[:, 2]
    mixed = (b_part * v_part).astype(jnp.bfloat16)
    rim = shifted(mixed[-2:], "ctx", 1)
    extended = jnp.concatenate([rim, mixed], axis=0).astype(jnp.float32)
    conv_taps = conv_weight.astype(jnp.float32)
    prev_one = extended[1 : row_count + 1] * first_own
    prev_two = extended[0:row_count] * second_own
    mixed_float = extended[2:]
    conv_out = conv_taps[0] * mixed_float + conv_taps[1] * prev_one + conv_taps[2] * prev_two
    gated = (c_part * conv_out).astype(jnp.bfloat16)
    mixer_out = lax.psum(contract_cols(gated, out_w), "tp")
    resid = x_float + mixer_out
    scale_two = lax.rsqrt(jnp.mean(resid * resid, axis=1, keepdims=True) + EPS)
    normed_two = resid * scale_two
    h_two = (normed_two * gain_two).astype(jnp.bfloat16)
    gate_pre = jnp.dot(h_two, gate_w, preferred_element_type=jnp.float32)
    up_pre = jnp.dot(h_two, up_w, preferred_element_type=jnp.float32)
    sigmoid_gate = jax.nn.sigmoid(gate_pre)
    silu_gate = gate_pre * sigmoid_gate
    activated = (silu_gate * up_pre).astype(jnp.bfloat16)
    ffn_out = lax.psum_scatter(
        contract_cols(activated, down_w), "tp", scatter_dimension=1, tiled=True
    )
    resid_own = lax.dynamic_slice_in_dim(resid, tp_rank * col_count, col_count, 1)
    block_out = (resid_own + ffn_out).astype(jnp.bfloat16)
    d_act = jnp.dot(cotangent, down_w, preferred_element_type=jnp.float32)
    down_grad = contract_rows(cotangent, activated)
    d_gate = (d_act * up_pre * sigmoid_gate * (1.0 + gate_pre * (1.0 - sigmoid_gate))).astype(
        jnp.bfloat16
    )
    d_up = (d_act * silu_gate).astype(jnp.bfloat16)
    gate_grad = contract_rows(h_two, d_gate)
    up_grad = contract_rows(h_two, d_up)
    dh_two = lax.psum(contract_cols(d_gate, gate_w) + contract_cols(d_up, up_w), "tp")
    gain_two_grad = jnp.sum(dh_two * normed_two, axis=0)
    d_resid = cotangent.astype(jnp.float32) + norm_back(dh_two, normed_two, scale_two, gain_two)
    d_resid_low = d_resid.astype(jnp.bfloat16)
    d_gated = jnp.dot(d_resid_low, out_w, preferred_element_type=jnp.float32)
    out_grad_w = contract_rows(d_resid_low, gated)
    d_conv = (d_gated * c_part).astype(jnp.bfloat16)
    d_c_part = d_gated * conv_out
    rim_back = shifted(d_conv[:2], "ctx", -1)
    d_conv_float = d_conv.astype(jnp.float32)
    back_ext = jnp.concatenate([d_conv, rim_back], axis=0).astype(jnp.float32)
    d_mixed = (
        conv_taps[0] * d_conv_float
        + conv_taps[1] * back_ext[1 : row_count + 1] * first_next
        + conv_taps[2] * back_ext[2:] * second_next
    )
    taps_grad = jnp.stack(
        [
            jnp.sum(d_conv_float * mixed_float, axis=0),
            jnp.sum(d_conv_float * prev_one, axis=0),
            jnp.sum(d_conv_float * prev_two, axis=0),
        ]
    )
    d_proj = jnp.stack([d_mixed * v_part, d_c_part, d_mixed * b_part], axis=1).astype(jnp.bfloat16)
    in_grad = jnp.einsum("td,tpe->dpe", h_one, d_proj, preferred_element_type=jnp.float32)
    dh_one = lax.psum(
        jnp.einsum("tpe,dpe->td", d_proj, in_w, preferred_element_type=jnp.float32), "tp"
    )
    gain_one_grad = jnp.sum(dh_one * normed_one, axis=0)
    d_input = d_resid + norm_back(dh_one, normed_one, scale_one, gain_one)
    d_input_own = lax.dynamic_slice_in_dim(d_input, tp_rank * col_count, col_count, 1).astype(
        jnp.bfloat16
    )
    back_out, back_input = (
        lax.all_to_all(reorder(block_out, targets), "ctx", split_axis=0, concat_axis=0, tiled=True),
        lax.all_to_all(
            reorder(d_input_own, targets), "ctx", split_axis=0, concat_axis=0, tiled=True
        ),
    )
    block_dealt = reorder(back_out, returning)
    input_dealt = reorder(back_input, returning)
    small_grads = jnp.concatenate(
        [
            taps_grad,
            lax.dynamic_slice_in_dim(gain_one_grad, tp_rank * col_count, col_count, 0)[None],
            lax.dynamic_slice_in_dim(gain_two_grad, tp_rank * col_count, col_count, 0)[None],
        ],
        axis=0,
    )
    copies = lax.axis_size("shard") * ctx_size
    pieces = (
        lax.psum_scatter(in_grad, ("shard", "ctx"), scatter_dimension=0, tiled=True),
        lax.psum_scatter(out_grad_w, ("shard", "ctx"), scatter_dimension=0, tiled=True),
        lax.psum_scatter(gate_grad, ("shard", "ctx"), scatter_dimension=0, tiled=True),
        lax.psum_scatter(up_grad, ("shard", "ctx"), scatter_dimension=0, tiled=True),
        lax.psum_scatter(down_grad, ("shard", "ctx"), scatter_dimension=0, tiled=True),
        lax.psum_scatter(
            jnp.tile(small_grads, (copies, 1)), ("shard", "ctx"), scatter_dimension=0, tiled=True
        ),
    )
    small_sum = pieces[5]
    in_total, out_total, gate_total, up_total, down_total = (
        lax.all_gather(pieces[0], "ctx", axis=0, tiled=True),
        lax.all_gather(pieces[1], "ctx", axis=0, tiled=True),
        lax.all_gather(pieces[2], "ctx", axis=0, tiled=True),
        lax.all_gather(pieces[3], "ctx", axis=0, tiled=True),
        lax.all_gather(pieces[4], "ctx", axis=0, tiled=True),
    )
    return (
        block_dealt,
        input_dealt,
        in_total,
        small_sum[0:3],
        out_total,
        small_sum[3],
        small_sum[4],
        gate_total,
        up_total,
        down_total,
    )


def solution(mesh):
    placed = (
        P(("shard", "ctx"), "tp"),
        P(("shard", "ctx"), "tp"),
        P("shard", None),
        P("shard", None),
        P("shard", None, "tp"),
        P(None, "tp"),
        P("shard", "tp"),
        P("tp"),
        P("tp"),
        P("shard", "tp"),
        P("shard", "tp"),
        P("shard", "tp"),
    )
    return jax.shard_map(
        on_device,
        mesh=mesh,
        in_specs=placed,
        out_specs=(
            P(("shard", "ctx"), "tp"),
            P(("shard", "ctx"), "tp"),
            P("shard", None, "tp"),
            P(None, "tp"),
            P("shard", "tp"),
            P("tp"),
            P("tp"),
            P("shard", "tp"),
            P("shard", "tp"),
            P("shard", "tp"),
        ),
        check_vma=False,
    )
```

profile of v0, /device:TPU:0, one launch (start us, length us, event | category | flops | bytes accessed | tf_op | source)
XLA Modules:
  0.0 2751.7 jit_solution(8536980168878349302)
XLA Ops:
  9.9 1.4 gather_fusion
  11.3 6.3 all-to-all-start
  20.3 11.8 all-to-all-done
  35.1 5.2 all_gather.40
  40.7 14.7 all-gather.13.cloned.1.call-done
  55.4 2.1 fusion
  57.5 79.9 %all-gather.15.cloned.1.call-done = bf16[2048,3,512]{2,0,1:T(8,128)(2,1)} async-done(((bf16[1024,3,512]{2,0,1:T(8,128)(2,1)}), bf16[2048,3,512]{2,0,1:T(8,128)(2,1)}) %all-gather.15.cloned.1.call-update) | async-done | bytes 6291472 | tf_op jit(solution)/shard_map/all_gather | solution.py:85
  137.3 6.5 fusion.5
  144.0 3.4 collective-permute-start
  149.4 22.6 all-gather.17.cloned.1.call-done
  172.0 4.9 fusion.37
  178.2 1.4 gather_fusion.4
  179.6 19.1 all_to_all.24
  201.3 61.3 %all-reduce.6.cloned.1.call-done = f32[512,2048]{1,0:T(8,128)} async-done(((f32[512,2048]{1,0:T(8,128)}), f32[512,2048]{1,0:T(8,128)}) %all-reduce.6.cloned.1.call-update) | async-done | bytes 4194320 | tf_op jit(solution)/shard_map/psum | solution.py:117
  262.6 3.5 multiply_reduce_fusion.4
  266.1 2.0 copy-done.2
  268.1 1.7 multiply_convert_fusion.3
  269.9 98.4 %all-gather.19.cloned.1.call-done = bf16[2048,2048]{1,0:T(8,128)(2,1)} async-done(((bf16[1024,2048]{1,0:T(8,128)(2,1)}), bf16[2048,2048]{1,0:T(8,128)(2,1)}) %all-gather.19.cloned.1.call-update) | async-done | bytes 8388624 | tf_op jit(solution)/shard_map/all_gather | solution.py:87
  368.3 10.7 fusion.38
  378.9 94.8 %all-gather.21.cloned.1.call-done = bf16[2048,2048]{1,0:T(8,128)(2,1)} async-done(((bf16[1024,2048]{1,0:T(8,128)(2,1)}), bf16[2048,2048]{1,0:T(8,128)(2,1)}) %all-gather.21.cloned.1.call-update) | async-done | bytes 8388624 | tf_op jit(solution)/shard_map/all_gather | solution.py:88
  473.8 10.5 fusion.39
  484.3 14.3 all-gather.25.cloned.1.call-done
  498.6 105.6 %all-gather.23.cloned.1.call-done = bf16[2048,2048]{1,0:T(8,128)(2,1)} async-done(((bf16[1024,2048]{1,0:T(8,128)(2,1)}), bf16[2048,2048]{1,0:T(8,128)(2,1)}) %all-gather.23.cloned.1.call-update) | async-done | bytes 8388624 | tf_op jit(solution)/shard_map/all_gather | solution.py:89
  604.3 13.6 multiply_convert_fusion
  617.9 8.7 fusion.41
  626.6 6.1 convolution_add_fusion
  632.8 85.6 %all-reduce.8.cloned.1.call-done = f32[512,2048]{1,0:T(8,128)} async-done(((f32[512,2048]{1,0:T(8,128)}), f32[512,2048]{1,0:T(8,128)}) %all-reduce.8.cloned.1.call-update) | async-done | bytes 4194320 | tf_op jit(solution)/shard_map/psum | solution.py:140
  718.4 4.6 multiply_reduce_fusion
  724.4 2.8 multiply_add_fusion
  731.2 1.4 collective-permute-start.1
  732.6 4.2 collective-permute-done.1
  738.4 5.0 convolution_bitcast_fusion
  743.5 5.7 fusion.16
  749.3 1.5 copy-done.5
  750.9 7.8 fusion.3
  758.7 12.6 fusion.42
  771.4 12.5 fusion.43
  784.2 13.3 fusion.44
  797.6 10.7 fusion.40
  808.4 19.9 all-reduce.10.cloned.1.call-done
  828.3 6.7 multiply_reduce_fusion.1
  835.8 84.6 %reduce-scatter.11.cloned.1.call-done = f32[256,512]{1,0:T(8,128)} async-done(((f32[2048,512]{1,0:T(8,128)}), f32[256,512]{1,0:T(8,128)}) %reduce-scatter.11.cloned.1.call-update) | async-done | bytes 524304 | tf_op jit(solution)/shard_map/reduce_scatter | solution.py:192
  920.5 211.0 %reduce-scatter.9.cloned.1.call-done = f32[256,3,512]{2,0,1:T(8,128)} async-done(((f32[2048,3,512]{2,0,1:T(8,128)}), f32[256,3,512]{2,0,1:T(8,128)}) %reduce-scatter.9.cloned.1.call-update) | async-done | bytes 1572880 | tf_op jit(solution)/shard_map/reduce_scatter | solution.py:191
  1131.5 284.8 %reduce-scatter.13.cloned.1.call-done = f32[256,2048]{1,0:T(8,128)} async-done(((f32[2048,2048]{1,0:T(8,128)}), f32[256,2048]{1,0:T(8,128)}) %reduce-scatter.13.cloned.1.call-update) | async-done | bytes 2097168 | tf_op jit(solution)/shard_map/reduce_scatter | solution.py:193
  1416.4 285.1 %reduce-scatter.15.cloned.1.call-done = f32[256,2048]{1,0:T(8,128)} async-done(((f32[2048,2048]{1,0:T(8,128)}), f32[256,2048]{1,0:T(8,128)}) %reduce-scatter.15.cloned.1.call-update) | async-done | bytes 2097168 | tf_op jit(solution)/shard_map/reduce_scatter | solution.py:194
  1701.6 284.7 %reduce-scatter.17.cloned.1.call-done = f32[256,2048]{1,0:T(8,128)} async-done(((f32[2048,2048]{1,0:T(8,128)}), f32[256,2048]{1,0:T(8,128)}) %reduce-scatter.17.cloned.1.call-update) | async-done | bytes 2097168 | tf_op jit(solution)/shard_map/reduce_scatter | solution.py:195
  1986.4 2.2 fusion.12
  1990.0 3.5 all-to-all-start.3
  1993.5 39.5 %reduce-scatter.7.cloned.1.call-done = f32[512,512]{1,0:T(8,128)} async-done(((f32[512,2048]{1,0:T(8,128)}), f32[512,512]{1,0:T(8,128)}) %reduce-scatter.7.cloned.1.call-update) | async-done | bytes 1048592 | tf_op jit(solution)/shard_map/reduce_scatter | solution.py:127
  2033.0 1.7 add_convert_fusion
  2034.7 1.4 gather_fusion.2
  2036.0 4.6 all-to-all-start.1
  2042.7 65.0 %all-reduce.12.cloned.1.call-done = f32[40,512]{1,0:T(8,128)} async-done(((f32[40,512]{1,0:T(8,128)}), f32[40,512]{1,0:T(8,128)}) %all-reduce.12.cloned.1.call-update) | async-done | bytes 81936
  2107.7 1.4 constant_dynamic-slice_fusion.3
  2113.2 41.6 %all-gather.29.cloned.1.call-done = f32[1024,512]{1,0:T(8,128)} async-done(((f32[256,512]{1,0:T(8,128)}), f32[1024,512]{1,0:T(8,128)}) %all-gather.29.cloned.1.call-update) | async-done | bytes 2097168 | tf_op jit(solution)/shard_map/all_gather | solution.py:203
  2154.8 115.7 %all-gather.27.cloned.1.call-done = f32[1024,3,512]{2,0,1:T(8,128)} async-done(((f32[256,3,512]{2,0,1:T(8,128)}), f32[1024,3,512]{2,0,1:T(8,128)}) %all-gather.27.cloned.1.call-update) | async-done | bytes 6291472 | tf_op jit(solution)/shard_map/all_gather | solution.py:202
  2270.5 149.3 %all-gather.31.cloned.1.call-done = f32[1024,2048]{1,0:T(8,128)} async-done(((f32[256,2048]{1,0:T(8,128)}), f32[1024,2048]{1,0:T(8,128)}) %all-gather.31.cloned.1.call-update) | async-done | bytes 8388624 | tf_op jit(solution)/shard_map/all_gather | solution.py:204
  2419.8 149.5 %all-gather.33.cloned.1.call-done = f32[1024,2048]{1,0:T(8,128)} async-done(((f32[256,2048]{1,0:T(8,128)}), f32[1024,2048]{1,0:T(8,128)}) %all-gather.33.cloned.1.call-update) | async-done | bytes 8388624 | tf_op jit(solution)/shard_map/all_gather | solution.py:205
  2569.2 149.5 %all-gather.35.cloned.1.call-done = f32[1024,2048]{1,0:T(8,128)} async-done(((f32[256,2048]{1,0:T(8,128)}), f32[1024,2048]{1,0:T(8,128)}) %all-gather.35.cloned.1.call-update) | async-done | bytes 8388624 | tf_op jit(solution)/shard_map/all_gather | solution.py:206
  2718.7 6.9 copy.49
  2727.3 4.3 copy.51
  2731.5 1.5 slice-done.1
  2733.1 3.4 copy.52
  2736.5 7.9 copy.53
  (172 shorter events, 32.0 us)
Async XLA Ops:
  7.2 2.7 copy-start
  9.9 7.8 copy-start.23
  9.9 25.1 copy-start.18
  9.9 25.2 copy-start.19
  9.9 30.4 %copy-start.21 = (s32[1,3]{1,0:T(1,128)S(1)}, s32[1,3]{1,0:T(1,128)}, u32[]{:S(2)}) copy-start(s32[1,3]{1,0:T(1,128)} %param.14) | copy-start | bytes 40
  11.3 20.8 all-to-all-start
  17.6 37.7 %all-gather.13.cloned.1.call-start = ((), (), s32[]{:S(2)}) async-start(), calls=%async_computation.10 | async-start | bytes 2621440 | tf_op jit(solution)/shard_map/all_gather | solution.py:78
  33.5 103.8 %all-gather.15.cloned.1.call-start = ((), (), s32[]{:S(2)}) async-start(), calls=%async_computation.11 | async-start | bytes 9437184 | tf_op jit(solution)/shard_map/all_gather | solution.py:85
  34.3 137.8 %all-gather.17.cloned.1.call-start = ((), (), s32[]{:S(2)}) async-start(), calls=%async_computation.12 | async-start | bytes 3145728 | tf_op jit(solution)/shard_map/all_gather | solution.py:86
  35.0 227.6 %all-reduce.6.cloned.1.call-start = ((), (), s32[]{:S(2)}) async-start(), calls=%async_computation.13 | async-start | bytes 8388608 | tf_op jit(solution)/shard_map/psum | solution.py:117
  137.3 10.1 copy-start.16
  143.9 5.0 copy-start.7
  144.0 4.7 collective-permute-start
  176.9 1.2 copy-start.12
  177.0 191.3 %all-gather.19.cloned.1.call-start = ((), (), s32[]{:S(2)}) async-start(), calls=%async_computation.14 | async-start | bytes 12582912 | tf_op jit(solution)/shard_map/all_gather | solution.py:87
  177.5 296.2 %all-gather.21.cloned.1.call-start = ((), (), s32[]{:S(2)}) async-start(), calls=%async_computation.15 | async-start | bytes 12582912 | tf_op jit(solution)/shard_map/all_gather | solution.py:88
  178.1 320.5 %all-gather.25.cloned.1.call-start = ((), (), s32[]{:S(2)}) async-start(), calls=%async_computation.18 | async-start | bytes 2621440 | tf_op jit(solution)/shard_map/all_gather | solution.py:79
  200.0 404.2 %all-gather.23.cloned.1.call-start = ((), (), s32[]{:S(2)}) async-start(), calls=%async_computation.16 | async-start | bytes 12582912 | tf_op jit(solution)/shard_map/all_gather | solution.py:89
  200.8 517.6 %all-reduce.8.cloned.1.call-start = ((), (), s32[]{:S(2)}) async-start(), calls=%async_computation.19 | async-start | bytes 8388608 | tf_op jit(solution)/shard_map/psum | solution.py:140
  266.1 2.0 copy-start.2
  617.9 8.7 copy-start.26
  617.9 8.7 copy-start.25
  617.9 8.7 copy-start.20
  632.8 195.5 %all-reduce.10.cloned.1.call-start = ((), (), s32[]{:S(2)}) async-start(), calls=%async_computation.20 | async-start | bytes 8388608 | tf_op jit(solution)/shard_map/psum | solution.py:165
  718.4 4.6 copy-start.3
  718.4 5.9 copy-start.6
  724.3 2.8 copy-start.11
  727.2 2.1 copy-start.4
  727.2 3.4 copy-start.8
  727.2 11.2 slice-start.2
  730.6 7.8 slice-start.3
  731.2 5.6 collective-permute-start.1
  737.5 0.8 copy-start.13
  737.5 1.0 copy-start.15
  743.5 177.0 %reduce-scatter.11.cloned.1.call-start = ((), (), s32[]{:S(2)}) async-start(), calls=%async_computation.23 | async-start | bytes 4718592 | tf_op jit(solution)/shard_map/reduce_scatter | solution.py:192
  749.2 1.6 copy-start.5
  749.2 1.7 copy-start.14
  749.2 382.3 %reduce-scatter.9.cloned.1.call-start = ((), (), s32[]{:S(2)}) async-start(), calls=%async_computation.21 | async-start | bytes 14155776 | tf_op jit(solution)/shard_map/reduce_scatter | solution.py:191
  758.7 657.7 %reduce-scatter.13.cloned.1.call-start = ((), (), s32[]{:S(2)}) async-start(), calls=%async_computation.25 | async-start | bytes 18874368 | tf_op jit(solution)/shard_map/reduce_scatter | solution.py:193
  771.3 930.2 %reduce-scatter.15.cloned.1.call-start = ((), (), s32[]{:S(2)}) async-start(), calls=%async_computation.27 | async-start | bytes 18874368 | tf_op jit(solution)/shard_map/reduce_scatter | solution.py:194
  783.9 1202.4 %reduce-scatter.17.cloned.1.call-start = ((), (), s32[]{:S(2)}) async-start(), calls=%async_computation.29 | async-start | bytes 18874368 | tf_op jit(solution)/shard_map/reduce_scatter | solution.py:195
  797.6 1235.4 %reduce-scatter.7.cloned.1.call-start = ((), (), s32[]{:S(2)}) async-start(), calls=%async_computation.17 | async-start | bytes 5242880 | tf_op jit(solution)/shard_map/reduce_scatter | solution.py:127
  808.3 1299.4 %all-reduce.12.cloned.1.call-start = ((), (), s32[]{:S(2)}) async-start(), calls=%async_computation.31 | async-start | bytes 163840
  835.8 1319.1 %all-gather.29.cloned.1.call-start = ((), (), s32[]{:S(2)}) async-start(), calls=%async_computation.24 | async-start | bytes 2621440 | tf_op jit(solution)/shard_map/all_gather | solution.py:203
  920.4 1065.9 %copy-start.17 = (s32[4]{0:T(128)S(1)}, s32[4]{0:T(128)}, u32[]{:S(2)}) copy-start(s32[4]{0:T(128)} %get-tuple-element.27) | copy-start | bytes 52
  920.5 1350.0 %all-gather.27.cloned.1.call-start = ((), (), s32[]{:S(2)}) async-start(), calls=%async_computation.22 | async-start | bytes 7864320 | tf_op jit(solution)/shard_map/all_gather | solution.py:202
  1131.5 1288.3 %all-gather.31.cloned.1.call-start = ((), (), s32[]{:S(2)}) async-start(), calls=%async_computation.26 | async-start | bytes 10485760 | tf_op jit(solution)/shard_map/all_gather | solution.py:204
  1416.4 1152.8 %all-gather.33.cloned.1.call-start = ((), (), s32[]{:S(2)}) async-start(), calls=%async_computation.28 | async-start | bytes 10485760 | tf_op jit(solution)/shard_map/all_gather | solution.py:205
  1701.6 1017.1 %all-gather.35.cloned.1.call-start = ((), (), s32[]{:S(2)}) async-start(), calls=%async_computation.30 | async-start | bytes 10485760 | tf_op jit(solution)/shard_map/all_gather | solution.py:206
  1988.6 52.1 %copy-start.24 = (s32[4]{0:T(128)S(1)}, s32[4]{0:T(128)}, u32[]{:S(2)}) copy-start(s32[4]{0:T(128)} %copy-done.23) | copy-start | bytes 52
  1988.6 52.8 %copy-start.22 = (u32[32]{0:T(128)S(1)}, u32[32]{0:T(128)}, u32[]{:S(2)}) copy-start(u32[32]{0:T(128)} %constant.107) | copy-start | bytes 388
  1990.0 46.1 %all-to-all-start.3 = ((bf16[4,128,512]{2,1,0:T(8,128)(2,1)}), bf16[4,128,512]{2,1,0:T(8,128)(2,1)S(1)}, u32[]{:S(2)}, u32[]{:S(2)}) async-start(bf16[4,128,512]{2,1,0:T(8,128)(2,1)} %gather_fusion.6), calls=%async_computation.4 | async-start | bytes 1048576 | tf_op jit(solution)/shard_map/all_to_all | solution.py:175
  2036.0 75.7 %all-to-all-start.1 = ((bf16[4,128,512]{2,1,0:T(8,128)(2,1)}), bf16[4,128,512]{2,1,0:T(8,128)(2,1)S(1)}, u32[]{:S(2)}, u32[]{:S(2)}) async-start(bf16[4,128,512]{2,1,0:T(8,128)(2,1)} %gather_fusion.2), calls=%async_computation.2 | async-start | bytes 1048576 | tf_op jit(solution)/shard_map/all_to_all | solution.py:174
  2718.7 6.9 copy-start.10
  2718.7 8.6 copy-start.9
  2725.6 5.9 slice-start
  2727.3 5.8 slice-start.1
  2736.5 7.9 copy-start.1
Sparse Core Ops, SparseCore 0:
  33.6 21.6 all-gather.12
  56.9 80.3 all-gather.14
  138.9 33.1 all-gather.16
  177.1 85.5 all-reduce.5
  264.1 104.1 all-gather.18
  369.7 103.9 all-gather.20
  476.0 22.5 all-gather.24
  500.2 103.9 all-gather.22
  632.9 85.4 all-reduce.7
  743.6 84.6 all-reduce.9
  832.4 88.0 reduce-scatter.10
  923.9 207.5 reduce-scatter.8
  1135.2 281.0 reduce-scatter.12
  1420.5 281.0 reduce-scatter.14
  1705.2 281.0 reduce-scatter.16
  1989.4 43.5 reduce-scatter.6
  2036.8 70.8 all-reduce.11
  2109.1 45.6 all-gather.28
  2156.4 114.0 all-gather.26
  2271.9 147.8 all-gather.30
  2421.3 147.8 all-gather.32
  2570.8 147.8 all-gather.34
where the time goes:
time: 2760 us; the launch traced here: 2750 us
  waiting for transfers between devices  2480 us (90%)
  matrix products  130 us (5%)
  local copies, waits for them, and re-layouts  50.4 us (2%)
  other arithmetic  32.5 us (1%)
    reduce_scatter x1, waiting for transfers between devices, on_device(): lax.psum_scatter(up_grad, ('shard', 'ctx'), scatter_dimension=0, tiled=True)  285 us
    reduce_scatter x1, waiting for transfers between devices, on_device(): lax.psum_scatter(gate_grad, ('shard', 'ctx'), scatter_dimension=0, tiled=...  285 us
    reduce_scatter x1, waiting for transfers between devices, on_device(): lax.psum_scatter(down_grad, ('shard', 'ctx'), scatter_dimension=0, tiled=...  285 us
    reduce_scatter x1, waiting for transfers between devices, on_device(): lax.psum_scatter(in_grad, ('shard', 'ctx'), scatter_dimension=0, tiled=True)  211 us
    all_gather x1, waiting for transfers between devices, on_device(): lax.all_gather(pieces[3], 'ctx', axis=0, tiled=True)  149 us
    all_gather x1, waiting for transfers between devices, on_device(): lax.all_gather(pieces[4], 'ctx', axis=0, tiled=True)  149 us
    all_gather x1, waiting for transfers between devices, on_device(): lax.all_gather(pieces[2], 'ctx', axis=0, tiled=True)  149 us
    all_gather x1, waiting for transfers between devices, on_device(): lax.all_gather(pieces[0], 'ctx', axis=0, tiled=True)  116 us
  transfers between devices with their start and end apart: 27, of which 25 were waited for; matrix products, arithmetic and copies ran while one was open for 5% of the time, Pallas kernels for 0%

commit v1 on v0

v1 whole, which is shorter than its diff:
```python
import jax
import jax.numpy as jnp
from jax import lax
from jax.sharding import PartitionSpec as P

EPS = 1e-05
LOW = jnp.bfloat16
WIDE = jnp.float32
CHUNKS = 4


def shifted(value, axis, steps):
    count = lax.axis_size(axis)
    leading, last = (max(0, -steps), min(count, count - steps))
    return lax.ppermute(value, axis, [(source, source + steps) for source in range(leading, last)])


def swapped(value, axis, step):
    count = lax.axis_size(axis)
    return lax.ppermute(value, axis, [(source, source ^ step) for source in range(count)])


def matmul(left, right):
    return jnp.dot(left, right, preferred_element_type=WIDE)


def contract_rows(left, right):
    return lax.dot_general(left, right, (((0,), (0,)), ((), ())), preferred_element_type=WIDE)


def contract_cols(left, right):
    return lax.dot_general(left, right, (((1,), (1,)), ((), ())), preferred_element_type=WIDE)


def norm_back(grad_out, normed, scale_row, gain):
    scaled = grad_out * gain
    return scale_row * (scaled - normed * jnp.mean(scaled * normed, axis=1, keepdims=True))


def butterfly_sum(value, axis):
    step = 1
    while step < lax.axis_size(axis):
        value = value + swapped(value, axis, step)
        step *= 2
    return value


def sum_line(piece, rank):
    from_end = lax.ppermute(piece, "ctx", [(0, 1), (3, 2)])
    half = (piece.astype(WIDE) + from_end.astype(WIDE)).astype(LOW)
    from_middle = lax.ppermute(half, "ctx", [(1, 2), (2, 1)])
    total = (half.astype(WIDE) + from_middle.astype(WIDE)).astype(LOW)
    handed = lax.ppermute(total, "ctx", [(1, 0), (2, 3)])
    inner = jnp.logical_or(rank == 1, rank == 2)
    return jnp.where(inner, total, handed).astype(WIDE)


class Features:
    def __init__(self):
        rank = lax.axis_index("tp")
        self.rank = rank
        self.inner = rank % 2
        self.outer = rank // 2

    def gather(self, own):
        other = swapped(own, "tp", 2)
        first = self.outer == 0
        pair = jnp.stack([jnp.where(first, own, other), jnp.where(first, other, own)])
        more = swapped(pair, "tp", 1)
        even = self.inner == 0
        left, right = jnp.where(even, pair, more), jnp.where(even, more, pair)
        return jnp.concatenate([left[0], right[0], left[1], right[1]], axis=1)

    def total(self, first_half, second_half):
        even = self.inner == 0
        kept = jnp.where(even, first_half, second_half)
        sent = jnp.where(even, second_half, first_half).astype(LOW)
        pair = (kept.astype(WIDE) + swapped(sent, "tp", 1).astype(WIDE)).astype(LOW)
        both = (pair.astype(WIDE) + swapped(pair, "tp", 2).astype(WIDE)).astype(LOW)
        other = swapped(both, "tp", 1)
        return jnp.where(even, both, other), jnp.where(even, other, both)

    def scatter(self, full):
        rows, width = full.shape
        blocks = full.reshape(rows, 2, 2, width // 4)
        even = self.inner == 0
        kept = jnp.where(even, blocks[:, :, 0], blocks[:, :, 1])
        sent = jnp.where(even, blocks[:, :, 1], blocks[:, :, 0]).astype(LOW)
        pair = kept.astype(WIDE) + swapped(sent, "tp", 1).astype(WIDE)
        first = self.outer == 0
        mine = jnp.where(first, pair[:, 0], pair[:, 1])
        away = jnp.where(first, pair[:, 1], pair[:, 0]).astype(LOW)
        return mine + swapped(away, "tp", 2).astype(WIDE)

    def own(self, full, axis):
        width = full.shape[axis] // lax.axis_size("tp")
        return lax.dynamic_slice_in_dim(full, self.rank * width, width, axis)


class Shards:
    def __init__(self, tp):
        self.count = lax.axis_size("shard")
        self.rank = lax.axis_index("shard")
        self.ctx_rank = lax.axis_index("ctx")
        self.tp = tp
        self.paired = self.count == 2

    def weight(self, rows, direct):
        if not self.paired:
            return (lax.all_gather(rows, "shard", axis=0, tiled=True),)
        parts = []
        if direct < rows.shape[0]:
            share = (rows.shape[0] - direct) // lax.axis_size("ctx")
            part = lax.dynamic_slice_in_dim(rows, direct + self.ctx_rank * share, share, 0)
            parts.append(lax.all_gather(swapped(part, "shard", 1), "ctx", axis=0, tiled=True))
        if direct > 0:
            parts.insert(0, swapped(rows[:direct], "shard", 1))
        other = parts[0] if len(parts) == 1 else jnp.concatenate(parts, axis=0)
        return (rows, other)

    def split(self, full):
        if not self.paired:
            return (full,)
        width = full.shape[1] // 2
        return (
            lax.dynamic_slice_in_dim(full, self.rank * width, width, 1),
            lax.dynamic_slice_in_dim(full, (1 - self.rank) * width, width, 1),
        )

    def join(self, parts):
        if not self.paired:
            return parts[0]
        first = self.rank == 0
        return jnp.concatenate(
            [jnp.where(first, parts[0], parts[1]), jnp.where(first, parts[1], parts[0])], axis=1
        )

    def halves(self, parts):
        if self.paired:
            return parts
        return jnp.split(parts[0], 2, axis=1)

    def joined(self, halves):
        if self.paired:
            return self.join(halves)
        return jnp.concatenate(halves, axis=1)

    def columns(self, full):
        if not self.paired:
            return lax.all_to_all(full, "shard", split_axis=1, concat_axis=0, tiled=True)
        own, other = self.split(full)
        width = own.shape[1] // 2
        part = lax.dynamic_slice_in_dim(other, self.tp.inner * width, width, 1)
        got = swapped(part, "shard", 1)
        rest = swapped(got, "tp", 1)
        even = self.tp.inner == 0
        peer = jnp.concatenate([jnp.where(even, got, rest), jnp.where(even, rest, got)], axis=1)
        return jnp.concatenate([own, peer], axis=0)

    def tokens(self, own):
        if not self.paired:
            return lax.all_gather(own, "shard", axis=0, tiled=True)
        return jnp.concatenate([own, swapped(own, "shard", 1)], axis=0)

    def own_total(self, product):
        if not self.paired:
            return lax.psum_scatter(product, "shard", scatter_dimension=0, tiled=True)
        rows = product.shape[0] // 2
        return product[:rows] + swapped(product[rows:].astype(LOW), "shard", 1).astype(WIDE)

    def own_tokens(self, product):
        if not self.paired:
            return lax.all_to_all(product.astype(LOW), "shard", split_axis=0, concat_axis=1, tiled=True)
        rows = product.shape[0] // 2
        return self.join([product[:rows].astype(LOW), swapped(product[rows:].astype(LOW), "shard", 1)])


def on_device(
    hidden_in,
    out_grad,
    seq_lengths,
    deal_order,
    in_weight,
    conv_weight,
    out_weight,
    norm1_gain,
    norm2_gain,
    gate_weight,
    up_weight,
    down_weight,
):
    ctx_size = lax.axis_size("ctx")
    ctx_rank = lax.axis_index("ctx")
    tp = Features()
    shards = Shards(tp)
    row_count, col_count = hidden_in.shape
    hidden_count = gate_weight.shape[1]
    weight_rows = in_weight.shape[0]
    per_dev = deal_order.shape[1] // ctx_size
    per_peer = per_dev // ctx_size
    block_rows = row_count // per_dev
    dealing = deal_order[0].reshape(ctx_size, per_dev)
    own_blocks = lax.dynamic_index_in_dim(dealing, ctx_rank, 0, keepdims=False)
    send_order = jnp.argsort(own_blocks // per_dev, stable=True)
    wanted = jnp.where(dealing // per_dev == ctx_rank, 0, 1)
    chosen = jnp.argsort(wanted, axis=1, stable=True)[:, :per_peer]
    targets = (jnp.take_along_axis(dealing, chosen, 1) % per_dev).reshape(-1)
    placing = jnp.argsort(targets)
    returning = jnp.argsort(send_order)

    def reorder(values, index):
        blocks = values.reshape(per_dev, block_rows, values.shape[1])
        return blocks[index].reshape(row_count, values.shape[1])

    def to_packed(values):
        got = lax.all_to_all(
            reorder(values, send_order), "ctx", split_axis=0, concat_axis=0, tiled=True
        )
        return reorder(got, placing)

    def to_dealt(values):
        got = lax.all_to_all(
            reorder(values, targets), "ctx", split_axis=0, concat_axis=0, tiled=True
        )
        return reorder(got, returning)

    in_flat = in_weight.reshape(weight_rows, -1)
    in_w = shards.weight(in_flat, weight_rows // 4)
    x_packed = to_packed(hidden_in)
    gains = tp.gather(jnp.stack([norm1_gain, norm2_gain])).astype(WIDE)
    gain_one, gain_two = gains[0], gains[1]
    x_full = tp.gather(x_packed)
    out_w = shards.weight(out_weight, weight_rows)
    cot_full = tp.gather(to_packed(out_grad))

    width = hidden_count // CHUNKS

    def chunk(weight, index):
        return weight[:, index * width : (index + 1) * width]

    directs = [0, 0, weight_rows, weight_rows]
    gate_w, up_w = [], []
    for index in range(CHUNKS):
        gate_w.append(shards.weight(chunk(gate_weight, index), directs[index]))
        up_w.append(shards.weight(chunk(up_weight, index), directs[index]))

    lengths = seq_lengths[0]
    starts = jnp.cumsum(lengths) - lengths
    where_t = ctx_rank * row_count - 2 + jnp.arange(row_count + 4, dtype=jnp.int32)
    seq_begin = jnp.max(jnp.where(starts[None, :] <= where_t[:, None], starts[None, :], 0), axis=1)
    position = where_t - seq_begin
    first_own = (position[2 : row_count + 2] >= 1).astype(WIDE)[:, None]
    second_own = (position[2 : row_count + 2] >= 2).astype(WIDE)[:, None]
    first_next = (position[3 : row_count + 3] >= 1).astype(WIDE)[:, None]
    second_next = (position[4 : row_count + 4] >= 2).astype(WIDE)[:, None]

    x_float = x_full.astype(WIDE)
    scale_one = lax.rsqrt(jnp.mean(x_float * x_float, axis=1, keepdims=True) + EPS)
    normed_one = x_float * scale_one
    h_one = (normed_one * gain_one).astype(LOW)
    projected = sum(matmul(part, w) for part, w in zip(shards.split(h_one), in_w))
    b_part = projected[:, :col_count]
    c_part = projected[:, col_count : 2 * col_count]
    v_part = projected[:, 2 * col_count :]
    mixed = (b_part * v_part).astype(LOW)
    rim = shifted(mixed[-2:], "ctx", 1)
    extended = jnp.concatenate([rim, mixed], axis=0).astype(WIDE)
    conv_taps = conv_weight.astype(WIDE)
    prev_one = extended[1 : row_count + 1] * first_own
    prev_two = extended[0:row_count] * second_own
    mixed_float = extended[2:]
    conv_out = conv_taps[0] * mixed_float + conv_taps[1] * prev_one + conv_taps[2] * prev_two
    gated = (c_part * conv_out).astype(LOW)
    mixer_parts = [contract_cols(gated, w) for w in out_w]
    mixer_out = shards.joined(tp.total(*shards.halves(mixer_parts)))
    resid = x_float + mixer_out.astype(WIDE)
    scale_two = lax.rsqrt(jnp.mean(resid * resid, axis=1, keepdims=True) + EPS)
    normed_two = resid * scale_two
    h_two = (normed_two * gain_two).astype(LOW)
    h_two_parts = shards.split(h_two)

    cot_cols = shards.columns(cot_full)
    h_two_cols = shards.columns(h_two)
    h_one_cols = shards.columns(h_one)

    down_parts, gate_parts, up_parts = [], [], []
    ffn = None
    dh_parts = [None] * len(h_two_parts)
    for index in range(CHUNKS):
        down_w = chunk(down_weight, index)
        gate_pre = sum(matmul(part, w) for part, w in zip(h_two_parts, gate_w[index]))
        up_pre = sum(matmul(part, w) for part, w in zip(h_two_parts, up_w[index]))
        d_act = shards.own_total(matmul(cot_cols, down_w))
        sigmoid_gate = jax.nn.sigmoid(gate_pre)
        silu_gate = gate_pre * sigmoid_gate
        activated = (silu_gate * up_pre).astype(LOW)
        d_gate = (d_act * up_pre * sigmoid_gate * (1.0 + gate_pre * (1.0 - sigmoid_gate))).astype(LOW)
        d_up = (d_act * silu_gate).astype(LOW)
        act_all = shards.tokens(activated)
        d_gate_all = shards.tokens(d_gate)
        d_up_all = shards.tokens(d_up)
        down_parts.append(sum_line(contract_rows(cot_cols, act_all).astype(LOW), ctx_rank))
        gate_parts.append(sum_line(contract_rows(h_two_cols, d_gate_all).astype(LOW), ctx_rank))
        up_parts.append(sum_line(contract_rows(h_two_cols, d_up_all).astype(LOW), ctx_rank))
        term = contract_cols(act_all, down_w)
        ffn = term if ffn is None else ffn + term
        for place in range(len(dh_parts)):
            term = contract_cols(d_gate, gate_w[index][place]) + contract_cols(d_up, up_w[index][place])
            dh_parts[place] = term if dh_parts[place] is None else dh_parts[place] + term
    down_total = jnp.concatenate(down_parts, axis=1)
    gate_total = jnp.concatenate(gate_parts, axis=1)
    up_total = jnp.concatenate(up_parts, axis=1)

    ffn_own = tp.scatter(shards.own_tokens(ffn))
    block_out = (tp.own(resid, 1) + ffn_own).astype(LOW)
    block_dealt = to_dealt(block_out)

    dh_two = shards.joined(tp.total(*shards.halves(dh_parts))).astype(WIDE)
    gain_two_grad = tp.own(jnp.sum(dh_two * normed_two, axis=0), 0)
    d_resid = cot_full.astype(WIDE) + norm_back(dh_two, normed_two, scale_two, gain_two)
    d_resid_low = d_resid.astype(LOW)
    d_gated = sum(matmul(part, w) for part, w in zip(shards.split(d_resid_low), out_w))
    out_part = contract_rows(shards.columns(d_resid_low), shards.tokens(gated)).astype(LOW)
    out_total = sum_line(out_part, ctx_rank)
    d_conv = (d_gated * c_part).astype(LOW)
    d_c_part = d_gated * conv_out
    rim_back = shifted(d_conv[:2], "ctx", -1)
    d_conv_float = d_conv.astype(WIDE)
    back_ext = jnp.concatenate([d_conv, rim_back], axis=0).astype(WIDE)
    d_mixed = (
        conv_taps[0] * d_conv_float
        + conv_taps[1] * back_ext[1 : row_count + 1] * first_next
        + conv_taps[2] * back_ext[2:] * second_next
    )
    taps_grad = jnp.stack(
        [
            jnp.sum(d_conv_float * mixed_float, axis=0),
            jnp.sum(d_conv_float * prev_one, axis=0),
            jnp.sum(d_conv_float * prev_two, axis=0),
        ]
    )
    d_proj = [
        (d_mixed * v_part).astype(LOW),
        d_c_part.astype(LOW),
        (d_mixed * b_part).astype(LOW),
    ]
    in_parts = [
        sum_line(contract_rows(h_one_cols, shards.tokens(part)).astype(LOW), ctx_rank)
        for part in d_proj
    ]
    in_total = jnp.stack(in_parts, axis=1)
    d_proj_flat = jnp.concatenate(d_proj, axis=1)
    dh_one_parts = [contract_cols(d_proj_flat, w) for w in in_w]
    dh_one = shards.joined(tp.total(*shards.halves(dh_one_parts))).astype(WIDE)
    gain_one_grad = tp.own(jnp.sum(dh_one * normed_one, axis=0), 0)
    d_input = d_resid + norm_back(dh_one, normed_one, scale_one, gain_one)
    input_dealt = to_dealt(tp.own(d_input, 1).astype(LOW))

    small = jnp.concatenate([taps_grad, gain_one_grad[None], gain_two_grad[None]], axis=0)
    small_sum = butterfly_sum(butterfly_sum(small, "shard"), "ctx")
    return (
        block_dealt,
        input_dealt,
        in_total,
        small_sum[0:3],
        out_total,
        small_sum[3],
        small_sum[4],
        gate_total,
        up_total,
        down_total,
    )


def solution(mesh):
    placed = (
        P(("shard", "ctx"), "tp"),
        P(("shard", "ctx"), "tp"),
        P("shard", None),
        P("shard", None),
        P("shard", None, "tp"),
        P(None, "tp"),
        P("shard", "tp"),
        P("tp"),
        P("tp"),
        P("shard", "tp"),
        P("shard", "tp"),
        P("shard", "tp"),
    )
    return jax.shard_map(
        on_device,
        mesh=mesh,
        in_specs=placed,
        out_specs=(
            P(("shard", "ctx"), "tp"),
            P(("shard", "ctx"), "tp"),
            P("shard", None, "tp"),
            P(None, "tp"),
            P("shard", "tp"),
            P("tp"),
            P("tp"),
            P("shard", "tp"),
            P("shard", "tp"),
            P("shard", "tp"),
        ),
        check_vma=False,
    )
```

time: 2760 us -> 1360 us (0.49)
  waiting for transfers between devices: 2480 us -> 780 us
  starting transfers between devices: 20.8 us -> 232 us
  other arithmetic: 32.5 us -> 123 us
    reduce_scatter x6 -> x0, waiting for transfers between devices: 1190 us -> none  [the longest x1 285 us: on_device(): lax.psum_scatter(up_grad, ('shard', 'ctx'), scatter_dimension=0, tiled=True)]
    all_gather x12 -> x5, waiting for transfers between devices: 1040 us -> 0.01 us  [weight(): lax.all_gather(swapped(part, 'shard', 1), 'ctx', axis=0, tiled=True)]
    ppermute x0 -> x108, waiting for transfers between devices: none -> 613 us  [the longest x60 260 us: swapped(): lax.ppermute(value, axis, [(source, source ^ step) for source in range(co...]
    ppermute x0 -> x108, starting transfers between devices: none -> 169 us  [the longest x60 73.9 us: swapped(): lax.ppermute(value, axis, [(source, source ^ step) for source in range(co...]
    psum x3 -> x0, waiting for transfers between devices: 167 us -> none  [the longest x1 85.6 us: on_device(): lax.psum(contract_cols(d_gate, gate_w) + contract_cols(d_up, up_w), 'tp')]
    ppermute x2, waiting for transfers between devices: 5.44 us -> 141 us  [shifted(): lax.ppermute(value, axis, [(source, source + steps) for source in range(l...]
    unnamed x23 -> x5, waiting for transfers between devices: 68.4 us -> 0.67 us
    convert_element_type x8 -> x56, other arithmetic: 6.63 us -> 73.6 us  [the longest x16 25.6 us: sum_line(): total = (half.astype(WIDE) + from_middle.astype(WIDE)).astype(LOW)]
  transfers between devices with their start and end apart: 27 -> 119, of which waited for: 25 -> 48; matrix products, arithmetic and copies ran while one was open for 5% -> 22% of each run, Pallas kernels for 0% -> 0%
where the time goes in v1:
time: 1360 us; the launch traced here: 1350 us
  waiting for transfers between devices  780 us (57%)
  starting transfers between devices  232 us (17%)
  matrix products  135 us (10%)
  other arithmetic  123 us (9%)
  local copies, waits for them, and re-layouts  61 us (4%)
  between operations  16.9 us (1%)
    ppermute x60, waiting for transfers between devices, swapped(): lax.ppermute(value, axis, [(source, source ^ step) for source in range(co...  260 us
    ppermute x16, waiting for transfers between devices, sum_line(): from_end = lax.ppermute(piece, 'ctx', [(0, 1), (3, 2)])  208 us
    ppermute x16, waiting for transfers between devices, sum_line(): handed = lax.ppermute(total, 'ctx', [(1, 0), (2, 3)])  145 us
    ppermute x2, waiting for transfers between devices, shifted(): lax.ppermute(value, axis, [(source, source + steps) for source in range(l...  141 us
    ppermute x60, starting transfers between devices, swapped(): lax.ppermute(value, axis, [(source, source ^ step) for source in range(co...  73.9 us
    ppermute x16, starting transfers between devices, sum_line(): from_end = lax.ppermute(piece, 'ctx', [(0, 1), (3, 2)])  56.6 us
    dot_general x24, matrix products, matmul(): return jnp.dot(left, right, preferred_element_type=WIDE)  52.5 us
    all_to_all x2, starting transfers between devices, to_dealt(): lax.all_to_all(reorder(values, targets), 'ctx', split_axis=0, concat_axis...  50.2 us
  transfers between devices with their start and end apart: 119, of which 48 were waited for; matrix products, arithmetic and copies ran while one was open for 22% of the time, Pallas kernels for 0%

profile of v1, /device:TPU:0, one launch (start us, length us, event | category | flops | bytes accessed | tf_op | source)
XLA Modules:
  0.0 1347.6 jit_solution(555465770381333236)
XLA Ops:
  7.2 4.7 copy.94
  16.8 13.3 collective-permute-done.5
  36.3 4.7 all-to-all-start
  45.2 4.0 fusion.178
  54.9 37.1 %collective-permute-done.11 = bf16[256,512]{1,0:T(8,128)(2,1)S(1)} collective-permute-done((bf16[256,512]{1,0:T(8,128)(2,1)S(1)}, bf16[256,512]{1,0:T(8,128)(2,1)S(1)}, u32[]{:S(2)}, u32[]{:S(2)}) %collective-permute-start.11) | collective-permute-done | bytes 262176 | tf_op jit(solution)/shard_map/ppermute | solution.py:20
  96.5 5.0 all-to-all-start.2
  103.6 20.6 %all-to-all-done.2 = bf16[4,128,512]{2,1,0:T(8,128)(2,1)S(1)} async-done(((bf16[4,128,512]{2,1,0:T(8,128)(2,1)}), bf16[4,128,512]{2,1,0:T(8,128)(2,1)S(1)}, u32[]{:S(2)}, u32[]{:S(2)}) %all-to-all-start.2) | async-done | bytes 524320 | tf_op jit(solution)/shard_map/all_to_all | solution.py:216
  129.1 5.0 collective-permute-done.26
  143.9 5.0 convolution_add_fusion
  156.0 4.6 select_convert_fusion.2
  170.7 7.8 collective-permute-done.28
  179.1 5.0 collective-permute-done.15
  186.3 9.1 collective-permute-done.41
  201.1 20.4 %collective-permute-done.9 = bf16[512,1024]{1,0:T(8,128)(2,1)S(1)} collective-permute-done((bf16[512,1024]{1,0:T(8,128)(2,1)S(1)}, bf16[512,1024]{1,0:T(8,128)(2,1)S(1)}, u32[]{:S(2)}, u32[]{:S(2)}) %collective-permute-start.9) | collective-permute-done | bytes 1048608 | tf_op jit(solution)/shard_map/ppermute | solution.py:20
  251.7 22.2 %collective-permute-done.32 = bf16[512,512]{1,0:T(8,128)(2,1)S(1)} collective-permute-done((bf16[512,512]{1,0:T(8,128)(2,1)S(1)}, bf16[512,512]{1,0:T(8,128)(2,1)S(1)}, u32[]{:S(2)}, u32[]{:S(2)}) %collective-permute-start.32) | collective-permute-done | bytes 524320 | tf_op jit(solution)/shard_map/ppermute | solution.py:20
  295.0 12.7 collective-permute-done.33
  352.5 11.2 collective-permute-done.16
  375.6 10.6 collective-permute-done.64
  412.4 8.3 collective-permute-done.66
  423.7 8.3 collective-permute-done.94
  435.3 7.9 collective-permute-done.90
  443.1 5.1 collective-permute-start.107
  450.6 3.8 collective-permute-done.86
  454.4 5.1 collective-permute-start.104
  461.8 3.8 collective-permute-done.82
  465.6 5.2 collective-permute-start.101
  473.1 14.6 %collective-permute-done.23 = bf16[512,1024]{1,0:T(8,128)(2,1)S(1)} collective-permute-done((bf16[512,1024]{1,0:T(8,128)(2,1)S(1)}, bf16[512,1024]{1,0:T(8,128)(2,1)S(1)}, u32[]{:S(2)}, u32[]{:S(2)}) %collective-permute-start.23) | collective-permute-done | bytes 1048608 | tf_op jit(solution)/shard_map/ppermute | solution.py:20
  487.7 5.2 collective-permute-start.98
  507.8 8.3 collective-permute-done.101
  516.2 4.4 collective-permute-start.75
  522.5 16.2 %collective-permute-done.98 = bf16[1024,512]{1,0:T(8,128)(2,1)} collective-permute-done((bf16[1024,512]{1,0:T(8,128)(2,1)}, bf16[1024,512]{1,0:T(8,128)(2,1)}, u32[]{:S(2)}, u32[]{:S(2)}) %collective-permute-start.98) | collective-permute-done | bytes 1048608 | tf_op jit(solution)/shard_map/ppermute | solution.py:49
  538.7 4.4 collective-permute-start.71
  546.9 14.1 %collective-permute-done.79 = bf16[1024,512]{1,0:T(8,128)(2,1)S(1)} collective-permute-done((bf16[1024,512]{1,0:T(8,128)(2,1)S(1)}, bf16[1024,512]{1,0:T(8,128)(2,1)S(1)}, u32[]{:S(2)}, u32[]{:S(2)}) %collective-permute-start.79) | collective-permute-done | bytes 1048608 | tf_op jit(solution)/shard_map/ppermute | solution.py:49
  561.0 4.4 collective-permute-start.95
  565.8 17.7 %collective-permute-done.75 = bf16[1024,512]{1,0:T(8,128)(2,1)S(1)} collective-permute-done((bf16[1024,512]{1,0:T(8,128)(2,1)S(1)}, bf16[1024,512]{1,0:T(8,128)(2,1)S(1)}, u32[]{:S(2)}, u32[]{:S(2)}) %collective-permute-start.75) | collective-permute-done | bytes 1048608 | tf_op jit(solution)/shard_map/ppermute | solution.py:49
  583.5 4.4 collective-permute-start.91
  589.2 16.8 %collective-permute-done.71 = bf16[1024,512]{1,0:T(8,128)(2,1)S(1)} collective-permute-done((bf16[1024,512]{1,0:T(8,128)(2,1)S(1)}, bf16[1024,512]{1,0:T(8,128)(2,1)S(1)}, u32[]{:S(2)}, u32[]{:S(2)}) %collective-permute-start.71) | collective-permute-done | bytes 1048608 | tf_op jit(solution)/shard_map/ppermute | solution.py:49
  606.0 4.4 collective-permute-start.87
  611.7 16.7 %collective-permute-done.67 = bf16[1024,512]{1,0:T(8,128)(2,1)S(1)} collective-permute-done((bf16[1024,512]{1,0:T(8,128)(2,1)S(1)}, bf16[1024,512]{1,0:T(8,128)(2,1)S(1)}, u32[]{:S(2)}, u32[]{:S(2)}) %collective-permute-start.67) | collective-permute-done | bytes 1048608 | tf_op jit(solution)/shard_map/ppermute | solution.py:49
  628.4 4.4 collective-permute-start.83
  634.2 16.7 %collective-permute-done.95 = bf16[1024,512]{1,0:T(8,128)(2,1)S(1)} collective-permute-done((bf16[1024,512]{1,0:T(8,128)(2,1)S(1)}, bf16[1024,512]{1,0:T(8,128)(2,1)S(1)}, u32[]{:S(2)}, u32[]{:S(2)}) %collective-permute-start.95) | collective-permute-done | bytes 1048608 | tf_op jit(solution)/shard_map/ppermute | solution.py:49
  652.3 21.1 %collective-permute-done.91 = bf16[1024,512]{1,0:T(8,128)(2,1)S(1)} collective-permute-done((bf16[1024,512]{1,0:T(8,128)(2,1)S(1)}, bf16[1024,512]{1,0:T(8,128)(2,1)S(1)}, u32[]{:S(2)}, u32[]{:S(2)}) %collective-permute-start.91) | collective-permute-done | bytes 1048608 | tf_op jit(solution)/shard_map/ppermute | solution.py:49
  675.4 20.5 %collective-permute-done.87 = bf16[1024,512]{1,0:T(8,128)(2,1)S(1)} collective-permute-done((bf16[1024,512]{1,0:T(8,128)(2,1)S(1)}, bf16[1024,512]{1,0:T(8,128)(2,1)S(1)}, u32[]{:S(2)}, u32[]{:S(2)}) %collective-permute-start.87) | collective-permute-done | bytes 1048608 | tf_op jit(solution)/shard_map/ppermute | solution.py:49
  697.9 18.8 %collective-permute-done.83 = bf16[1024,512]{1,0:T(8,128)(2,1)S(1)} collective-permute-done((bf16[1024,512]{1,0:T(8,128)(2,1)S(1)}, bf16[1024,512]{1,0:T(8,128)(2,1)S(1)}, u32[]{:S(2)}, u32[]{:S(2)}) %collective-permute-start.83) | collective-permute-done | bytes 1048608 | tf_op jit(solution)/shard_map/ppermute | solution.py:49
  750.7 46.2 %all-to-all-start.1 = ((bf16[4,128,512]{2,1,0:T(8,128)(2,1)}), bf16[4,128,512]{2,1,0:T(8,128)(2,1)}, u32[]{:S(2)}, u32[]{:S(2)}) async-start(bf16[4,128,512]{2,1,0:T(8,128)(2,1)} %gather_fusion.2), calls=%async_computation.1 | async-start | bytes 1048576 | tf_op jit(solution)/shard_map/all_to_all | solution.py:222
  821.4 140.0 %collective-permute-done.37 = bf16[2,512]{1,0:T(2,128)(2,1)S(1)} collective-permute-done((bf16[2,512]{1,0:T(2,128)(2,1)S(1)}, bf16[2,512]{1,0:T(2,128)(2,1)S(1)}, u32[]{:S(2)}, u32[]{:S(2)}) %collective-permute-start.37) | collective-permute-done | bytes 2080 | tf_op jit(solution)/shard_map/ppermute | solution.py:15
  974.2 15.3 %collective-permute-done.100 = bf16[1024,512]{1,0:T(8,128)(2,1)S(1)} collective-permute-done((bf16[1024,512]{1,0:T(8,128)(2,1)S(1)}, bf16[1024,512]{1,0:T(8,128)(2,1)S(1)}, u32[]{:S(2)}, u32[]{:S(2)}) %collective-permute-start.100) | collective-permute-done | bytes 1048608 | tf_op jit(solution)/shard_map/ppermute | solution.py:53
  990.2 4.0 maximum_convert_fusion.2
  1014.8 19.7 %collective-permute-done.77 = bf16[1024,512]{1,0:T(8,128)(2,1)} collective-permute-done((bf16[1024,512]{1,0:T(8,128)(2,1)}, bf16[1024,512]{1,0:T(8,128)(2,1)}, u32[]{:S(2)}, u32[]{:S(2)}) %collective-permute-start.77) | collective-permute-done | bytes 1048608 | tf_op jit(solution)/shard_map/ppermute | solution.py:53
  1037.1 19.8 %collective-permute-done.73 = bf16[1024,512]{1,0:T(8,128)(2,1)} collective-permute-done((bf16[1024,512]{1,0:T(8,128)(2,1)}, bf16[1024,512]{1,0:T(8,128)(2,1)}, u32[]{:S(2)}, u32[]{:S(2)}) %collective-permute-start.73) | collective-permute-done | bytes 1048608 | tf_op jit(solution)/shard_map/ppermute | solution.py:53
  1058.9 20.5 %collective-permute-done.69 = bf16[1024,512]{1,0:T(8,128)(2,1)} collective-permute-done((bf16[1024,512]{1,0:T(8,128)(2,1)}, bf16[1024,512]{1,0:T(8,128)(2,1)}, u32[]{:S(2)}, u32[]{:S(2)}) %collective-permute-start.69) | collective-permute-done | bytes 1048608 | tf_op jit(solution)/shard_map/ppermute | solution.py:53
  1083.5 18.3 %collective-permute-done.97 = bf16[1024,512]{1,0:T(8,128)(2,1)S(1)} collective-permute-done((bf16[1024,512]{1,0:T(8,128)(2,1)}, bf16[1024,512]{1,0:T(8,128)(2,1)S(1)}, u32[]{:S(2)}, u32[]{:S(2)}) %collective-permute-start.97) | collective-permute-done | bytes 1048608 | tf_op jit(solution)/shard_map/ppermute | solution.py:53
  1101.9 22.3 %collective-permute-done.93 = bf16[1024,512]{1,0:T(8,128)(2,1)S(1)} collective-permute-done((bf16[1024,512]{1,0:T(8,128)(2,1)S(1)}, bf16[1024,512]{1,0:T(8,128)(2,1)S(1)}, u32[]{:S(2)}, u32[]{:S(2)}) %collective-permute-start.93) | collective-permute-done | bytes 1048608 | tf_op jit(solution)/shard_map/ppermute | solution.py:53
  1130.2 16.6 %collective-permute-done.89 = bf16[1024,512]{1,0:T(8,128)(2,1)S(1)} collective-permute-done((bf16[1024,512]{1,0:T(8,128)(2,1)S(1)}, bf16[1024,512]{1,0:T(8,128)(2,1)S(1)}, u32[]{:S(2)}, u32[]{:S(2)}) %collective-permute-start.89) | collective-permute-done | bytes 1048608 | tf_op jit(solution)/shard_map/ppermute | solution.py:53
  1148.4 4.0 maximum_convert_fusion
  1152.4 12.5 collective-permute-done.85
  1168.0 3.9 maximum_convert_fusion.1
  1174.0 20.4 %collective-permute-done.44 = bf16[1024,512]{1,0:T(8,128)(2,1)S(1)} collective-permute-done((bf16[1024,512]{1,0:T(8,128)(2,1)S(1)}, bf16[1024,512]{1,0:T(8,128)(2,1)S(1)}, u32[]{:S(2)}, u32[]{:S(2)}) %collective-permute-start.44) | collective-permute-done | bytes 1048608 | tf_op jit(solution)/shard_map/ppermute | solution.py:49
  1196.0 20.5 %collective-permute-done.61 = bf16[1024,512]{1,0:T(8,128)(2,1)S(1)} collective-permute-done((bf16[1024,512]{1,0:T(8,128)(2,1)S(1)}, bf16[1024,512]{1,0:T(8,128)(2,1)S(1)}, u32[]{:S(2)}, u32[]{:S(2)}) %collective-permute-start.61) | collective-permute-done | bytes 1048608 | tf_op jit(solution)/shard_map/ppermute | solution.py:49
  1226.5 4.0 fusion.6
  1234.4 30.9 %collective-permute-start.56 = (f32[5,512]{1,0:T(8,128)S(1)}, f32[5,512]{1,0:T(8,128)S(1)}, u32[]{:S(2)}, u32[]{:S(2)}) collective-permute-start(f32[5,512]{1,0:T(8,128)S(1)} %add.469), channel_id=1, source_target_pairs={{0,4},{4,0},{8,12},{12,8},{1,5},{5,1},{9,13},{13,9},{2,6},{6,2},{1... | collective-permute-start | bytes 30728 | tf_op jit(solution)/shard_map/ppermute | solution.py:20
  1265.3 50.0 %collective-permute-done.56 = f32[5,512]{1,0:T(8,128)S(1)} collective-permute-done((f32[5,512]{1,0:T(8,128)S(1)}, f32[5,512]{1,0:T(8,128)S(1)}, u32[]{:S(2)}, u32[]{:S(2)}) %collective-permute-start.56) | collective-permute-done | bytes 10272 | tf_op jit(solution)/shard_map/ppermute | solution.py:20
  1319.0 4.0 all-to-all-start.3
  1331.5 4.8 all-to-all-done.3
  (689 shorter events, 389.1 us)
Async XLA Ops:
  7.2 136.7 %all-gather.6.cloned.1.call-start = ((), (), s32[]{:S(2)}) async-start(), calls=%async_computation.4 | async-start | bytes 2949120 | tf_op jit(solution)/shard_map/all_gather | solution.py:115
  31.1 65.4 %collective-permute-start.2 = (bf16[2,512]{1,0:T(2,128)(2,1)S(1)}, bf16[2,512]{1,0:T(2,128)(2,1)S(1)}, u32[]{:S(2)}, u32[]{:S(2)}) collective-permute-start(bf16[2,512]{1,0:T(2,128)(2,1)S(1)} %pad_maximum_fusion.26), channel_id=1, source_target_pairs={{0,2},{1,3},{2,0},{3,1},{4,6},{5,7},{6,4},{7,5},{8,10},{9,11},{10,... | collective-permute-start | bytes 6152 | tf_op jit(solution)/shard_map/ppermute | solution.py:20
  36.3 60.1 %all-to-all-start = ((bf16[4,128,512]{2,1,0:T(8,128)(2,1)}), bf16[4,128,512]{2,1,0:T(8,128)(2,1)S(1)}, u32[]{:S(2)}, u32[]{:S(2)}) async-start(bf16[4,128,512]{2,1,0:T(8,128)(2,1)} %gather_fusion), calls=%async_computation | async-start | bytes 1048576 | tf_op jit(solution)/shard_map/all_to_all | solution.py:216
  41.1 237.1 %all-gather.8.cloned.1.call-start = ((), (), s32[]{:S(2)}) async-start(), calls=%async_computation.5 | async-start | bytes 1310720 | tf_op jit(solution)/shard_map/all_gather | solution.py:115
  43.2 83.6 %collective-permute-start.4 = (bf16[256,1536]{0,1:T(8,128)(2,1)}, bf16[256,1536]{0,1:T(8,128)(2,1)}, u32[]{:S(2)}, u32[]{:S(2)}) collective-permute-start(bf16[256,1536]{0,1:T(8,128)(2,1)} %bitcast.22), channel_id=1, source_target_pairs={{0,16},{16,0},{1,17},{17,1},{2,18},{18,2},{3,19},{19,3},{4,20},{20... | collective-permute-start | bytes 2359304 | tf_op jit(solution)/shard_map/ppermute | solution.py:20
  44.7 111.3 %collective-permute-start.7 = (bf16[1024,512]{1,0:T(8,128)(2,1)}, bf16[1024,512]{1,0:T(8,128)(2,1)}, u32[]{:S(2)}, u32[]{:S(2)}) collective-permute-start(bf16[1024,512]{1,0:T(8,128)(2,1)} %param.18), channel_id=1, source_target_pairs={{0,16},{16,0},{1,17},{17,1},{2,18},{18,2},{3,19},{19,3},{4,20},{20... | collective-permute-start | bytes 3145736 | tf_op jit(solution)/shard_map/ppermute | solution.py:20
  52.7 49.0 %collective-permute-start.12 = (bf16[256,512]{1,0:T(8,128)(2,1)S(1)}, bf16[256,512]{1,0:T(8,128)(2,1)}, u32[]{:S(2)}, u32[]{:S(2)}) collective-permute-start(bf16[256,512]{1,0:T(8,128)(2,1)S(1)} %constant_dynamic-slice_fusion.8), channel_id=1, source_target_pairs={{0,16},{16,0},{1,17},{17,1},{2,18},{18,2},{3,19},{19,3},{4,20},{20... | collective-permute-start | bytes 786440 | tf_op jit(solution)/shard_map/ppermute | solution.py:20
  101.5 180.0 %all-gather.10.cloned.1.call-start = ((), (), s32[]{:S(2)}) async-start(), calls=%async_computation.6 | async-start | bytes 1310720 | tf_op jit(solution)/shard_map/all_gather | solution.py:115
  102.2 214.8 %all-gather.12.cloned.1.call-start = ((), (), s32[]{:S(2)}) async-start(), calls=%async_computation.7 | async-start | bytes 1310720 | tf_op jit(solution)/shard_map/all_gather | solution.py:115
  126.3 119.4 %collective-permute-start.17 = (bf16[1024,512]{1,0:T(8,128)(2,1)}, bf16[1024,512]{1,0:T(8,128)(2,1)}, u32[]{:S(2)}, u32[]{:S(2)}) collective-permute-start(bf16[1024,512]{1,0:T(8,128)(2,1)} %get-tuple-element.38), channel_id=1, source_target_pairs={{0,16},{16,0},{1,17},{17,1},{2,18},{18,2},{3,19},{19,3},{4,20},{20... | collective-permute-start | bytes 3145736 | tf_op jit(solution)/shard_map/ppermute | solution.py:20
  126.8 193.5 %all-gather.14.cloned.1.call-start = ((), (), s32[]{:S(2)}) async-start(), calls=%async_computation.8 | async-start | bytes 1310720 | tf_op jit(solution)/shard_map/all_gather | solution.py:115
  184.1 64.9 %collective-permute-start.18 = (bf16[1024,512]{1,0:T(8,128)(2,1)}, bf16[1024,512]{1,0:T(8,128)(2,1)}, u32[]{:S(2)}, u32[]{:S(2)}) collective-permute-start(bf16[1024,512]{1,0:T(8,128)(2,1)} %get-tuple-element.42), channel_id=1, source_target_pairs={{0,16},{16,0},{1,17},{17,1},{2,18},{18,2},{3,19},{19,3},{4,20},{20... | collective-permute-start | bytes 3145736 | tf_op jit(solution)/shard_map/ppermute | solution.py:20
  195.3 93.6 %collective-permute-start.20 = (bf16[1024,512]{1,0:T(8,128)(2,1)}, bf16[1024,512]{1,0:T(8,128)(2,1)}, u32[]{:S(2)}, u32[]{:S(2)}) collective-permute-start(bf16[1024,512]{1,0:T(8,128)(2,1)} %get-tuple-element.35), channel_id=1, source_target_pairs={{0,16},{16,0},{1,17},{17,1},{2,18},{18,2},{3,19},{19,3},{4,20},{20... | collective-permute-start | bytes 3145736 | tf_op jit(solution)/shard_map/ppermute | solution.py:20
  229.0 63.2 %collective-permute-start.21 = (bf16[1024,512]{1,0:T(8,128)(2,1)}, bf16[1024,512]{1,0:T(8,128)(2,1)}, u32[]{:S(2)}, u32[]{:S(2)}) collective-permute-start(bf16[1024,512]{1,0:T(8,128)(2,1)} %get-tuple-element.39), channel_id=1, source_target_pairs={{0,16},{16,0},{1,17},{17,1},{2,18},{18,2},{3,19},{19,3},{4,20},{20... | collective-permute-start | bytes 3145736 | tf_op jit(solution)/shard_map/ppermute | solution.py:20
  249.0 76.2 %collective-permute-start.31 = (bf16[512,512]{1,0:T(8,128)(2,1)}, bf16[512,512]{1,0:T(8,128)(2,1)}, u32[]{:S(2)}, u32[]{:S(2)}) collective-permute-start(bf16[512,512]{1,0:T(8,128)(2,1)} %slice.474), channel_id=1, source_target_pairs={{0,16},{16,0},{1,17},{17,1},{2,18},{18,2},{3,19},{19,3},{4,20},{20... | collective-permute-start | bytes 1572872 | tf_op jit(solution)/shard_map/ppermute | solution.py:20
  285.2 841.0 %collective-permute-start.60 = (bf16[512,512]{1,0:T(8,128)(2,1)}, bf16[512,512]{1,0:T(8,128)(2,1)}, u32[]{:S(2)}, u32[]{:S(2)}) collective-permute-start(bf16[512,512]{1,0:T(8,128)(2,1)} %get-tuple-element.30), channel_id=1, source_target_pairs={{0,16},{16,0},{1,17},{17,1},{2,18},{18,2},{3,19},{19,3},{4,20},{20... | collective-permute-start | bytes 1572872 | tf_op jit(solution)/shard_map/ppermute | solution.py:20
  288.9 59.6 %collective-permute-start.19 = (bf16[512,512]{1,0:T(8,128)(2,1)}, bf16[512,512]{1,0:T(8,128)(2,1)}, u32[]{:S(2)}, u32[]{:S(2)}) collective-permute-start(bf16[512,512]{1,0:T(8,128)(2,1)} %get-tuple-element.55), channel_id=1, source_target_pairs={{0,16},{16,0},{1,17},{17,1},{2,18},{18,2},{3,19},{19,3},{4,20},{20... | collective-permute-start | bytes 1572872 | tf_op jit(solution)/shard_map/ppermute | solution.py:20
  292.2 79.4 %collective-permute-start.13 = (bf16[512,512]{1,0:T(8,128)(2,1)}, bf16[512,512]{1,0:T(8,128)(2,1)}, u32[]{:S(2)}, u32[]{:S(2)}) collective-permute-start(bf16[512,512]{1,0:T(8,128)(2,1)} %get-tuple-element.57), channel_id=1, source_target_pairs={{0,16},{16,0},{1,17},{17,1},{2,18},{18,2},{3,19},{19,3},{4,20},{20... | collective-permute-start | bytes 1572872 | tf_op jit(solution)/shard_map/ppermute | solution.py:20
  310.6 87.9 %collective-permute-start.78 = (bf16[512,512]{1,0:T(8,128)(2,1)}, bf16[512,512]{1,0:T(8,128)(2,1)}, u32[]{:S(2)}, u32[]{:S(2)}) collective-permute-start(bf16[512,512]{1,0:T(8,128)(2,1)} %get-tuple-element.43), channel_id=1, source_target_pairs={{0,16},{16,0},{1,17},{17,1},{2,18},{18,2},{3,19},{19,3},{4,20},{20... | collective-permute-start | bytes 1572872 | tf_op jit(solution)/shard_map/ppermute | solution.py:20
  409.4 44.9 %collective-permute-start.86 = (bf16[512,512]{1,0:T(8,128)(2,1)S(1)}, bf16[512,512]{1,0:T(8,128)(2,1)S(1)}, u32[]{:S(2)}, u32[]{:S(2)}) collective-permute-start(bf16[512,512]{1,0:T(8,128)(2,1)S(1)} %get-tuple-element.47), channel_id=1, source_target_pairs={{0,16},{16,0},{1,17},{17,1},{2,18},{18,2},{3,19},{19,3},{4,20},{20... | collective-permute-start | bytes 1572872 | tf_op jit(solution)/shard_map/ppermute | solution.py:20
  420.7 44.9 %collective-permute-start.82 = (bf16[512,512]{1,0:T(8,128)(2,1)S(1)}, bf16[512,512]{1,0:T(8,128)(2,1)S(1)}, u32[]{:S(2)}, u32[]{:S(2)}) collective-permute-start(bf16[512,512]{1,0:T(8,128)(2,1)S(1)} %copy-done.26), channel_id=1, source_target_pairs={{0,16},{16,0},{1,17},{17,1},{2,18},{18,2},{3,19},{19,3},{4,20},{20... | collective-permute-start | bytes 1572872 | tf_op jit(solution)/shard_map/ppermute | solution.py:20
  431.9 55.8 %collective-permute-start.23 = (bf16[512,1024]{1,0:T(8,128)(2,1)S(1)}, bf16[512,1024]{1,0:T(8,128)(2,1)S(1)}, u32[]{:S(2)}, u32[]{:S(2)}) collective-permute-start(bf16[512,1024]{1,0:T(8,128)(2,1)S(1)} %slice.302), channel_id=1, source_target_pairs={{0,16},{16,0},{1,17},{17,1},{2,18},{18,2},{3,19},{19,3},{4,20},{20... | collective-permute-start | bytes 3145736 | tf_op jit(solution)/shard_map/ppermute | solution.py:20
  443.1 58.3 %collective-permute-start.107 = (bf16[1024,512]{1,0:T(8,128)(2,1)}, bf16[1024,512]{1,0:T(8,128)(2,1)}, u32[]{:S(2)}, u32[]{:S(2)}) collective-permute-start(bf16[1024,512]{1,0:T(8,128)(2,1)} %convolution_convert_fusion), channel_id=1, source_target_pairs={{0,4},{12,8},{1,5},{13,9},{2,6},{14,10},{3,7},{15,11},{16,20},{28,... | collective-permute-start | bytes 3145736 | tf_op jit(solution)/shard_map/ppermute | solution.py:49
  454.4 50.1 %collective-permute-start.104 = (bf16[1024,512]{1,0:T(8,128)(2,1)}, bf16[1024,512]{1,0:T(8,128)(2,1)}, u32[]{:S(2)}, u32[]{:S(2)}) collective-permute-start(bf16[1024,512]{1,0:T(8,128)(2,1)} %convolution_convert_fusion.1), channel_id=1, source_target_pairs={{0,4},{12,8},{1,5},{13,9},{2,6},{14,10},{3,7},{15,11},{16,20},{28,... | collective-permute-start | bytes 3145736 | tf_op jit(solution)/shard_map/ppermute | solution.py:49
  465.6 50.6 %collective-permute-start.101 = (bf16[1024,512]{1,0:T(8,128)(2,1)}, bf16[1024,512]{1,0:T(8,128)(2,1)}, u32[]{:S(2)}, u32[]{:S(2)}) collective-permute-start(bf16[1024,512]{1,0:T(8,128)(2,1)} %convolution_convert_fusion.2), channel_id=1, source_target_pairs={{0,4},{12,8},{1,5},{13,9},{2,6},{14,10},{3,7},{15,11},{16,20},{28,... | collective-permute-start | bytes 3145736 | tf_op jit(solution)/shard_map/ppermute | solution.py:49
  487.7 50.9 %collective-permute-start.98 = (bf16[1024,512]{1,0:T(8,128)(2,1)}, bf16[1024,512]{1,0:T(8,128)(2,1)}, u32[]{:S(2)}, u32[]{:S(2)}) collective-permute-start(bf16[1024,512]{1,0:T(8,128)(2,1)} %convolution_convert_fusion.3), channel_id=1, source_target_pairs={{0,4},{12,8},{1,5},{13,9},{2,6},{14,10},{3,7},{15,11},{16,20},{28,... | collective-permute-start | bytes 3145736 | tf_op jit(solution)/shard_map/ppermute | solution.py:49
  502.1 42.9 %collective-permute-start.35 = (bf16[512,1024]{1,0:T(8,128)(2,1)S(1)}, bf16[512,1024]{1,0:T(8,128)(2,1)S(1)}, u32[]{:S(2)}, u32[]{:S(2)}) collective-permute-start(bf16[512,1024]{1,0:T(8,128)(2,1)S(1)} %copy-done.46), channel_id=1, source_target_pairs={{0,2},{1,3},{2,0},{3,1},{4,6},{5,7},{6,4},{7,5},{8,10},{9,11},{10,... | collective-permute-start | bytes 3145736 | tf_op jit(solution)/shard_map/ppermute | solution.py:20
  504.5 56.5 %collective-permute-start.79 = (bf16[1024,512]{1,0:T(8,128)(2,1)S(1)}, bf16[1024,512]{1,0:T(8,128)(2,1)S(1)}, u32[]{:S(2)}, u32[]{:S(2)}) collective-permute-start(bf16[1024,512]{1,0:T(8,128)(2,1)S(1)} %copy-done.72), channel_id=1, source_target_pairs={{0,4},{12,8},{1,5},{13,9},{2,6},{14,10},{3,7},{15,11},{16,20},{28,... | collective-permute-start | bytes 3145736 | tf_op jit(solution)/shard_map/ppermute | solution.py:49
  516.2 67.3 %collective-permute-start.75 = (bf16[1024,512]{1,0:T(8,128)(2,1)S(1)}, bf16[1024,512]{1,0:T(8,128)(2,1)S(1)}, u32[]{:S(2)}, u32[]{:S(2)}) collective-permute-start(bf16[1024,512]{1,0:T(8,128)(2,1)S(1)} %copy-done.73), channel_id=1, source_target_pairs={{0,4},{12,8},{1,5},{13,9},{2,6},{14,10},{3,7},{15,11},{16,20},{28,... | collective-permute-start | bytes 3145736 | tf_op jit(solution)/shard_map/ppermute | solution.py:49
  538.7 67.3 %collective-permute-start.71 = (bf16[1024,512]{1,0:T(8,128)(2,1)S(1)}, bf16[1024,512]{1,0:T(8,128)(2,1)S(1)}, u32[]{:S(2)}, u32[]{:S(2)}) collective-permute-start(bf16[1024,512]{1,0:T(8,128)(2,1)S(1)} %copy-done.74), channel_id=1, source_target_pairs={{0,4},{12,8},{1,5},{13,9},{2,6},{14,10},{3,7},{15,11},{16,20},{28,... | collective-permute-start | bytes 3145736 | tf_op jit(solution)/shard_map/ppermute | solution.py:49
  545.0 83.5 %collective-permute-start.67 = (bf16[1024,512]{1,0:T(8,128)(2,1)S(1)}, bf16[1024,512]{1,0:T(8,128)(2,1)S(1)}, u32[]{:S(2)}, u32[]{:S(2)}) collective-permute-start(bf16[1024,512]{1,0:T(8,128)(2,1)S(1)} %copy-done.75), channel_id=1, source_target_pairs={{0,4},{12,8},{1,5},{13,9},{2,6},{14,10},{3,7},{15,11},{16,20},{28,... | collective-permute-start | bytes 3145736 | tf_op jit(solution)/shard_map/ppermute | solution.py:49
  561.0 89.9 %collective-permute-start.95 = (bf16[1024,512]{1,0:T(8,128)(2,1)S(1)}, bf16[1024,512]{1,0:T(8,128)(2,1)S(1)}, u32[]{:S(2)}, u32[]{:S(2)}) collective-permute-start(bf16[1024,512]{1,0:T(8,128)(2,1)S(1)} %copy-done.76), channel_id=1, source_target_pairs={{0,4},{12,8},{1,5},{13,9},{2,6},{14,10},{3,7},{15,11},{16,20},{28,... | collective-permute-start | bytes 3145736 | tf_op jit(solution)/shard_map/ppermute | solution.py:49
  583.5 89.9 %collective-permute-start.91 = (bf16[1024,512]{1,0:T(8,128)(2,1)S(1)}, bf16[1024,512]{1,0:T(8,128)(2,1)S(1)}, u32[]{:S(2)}, u32[]{:S(2)}) collective-permute-start(bf16[1024,512]{1,0:T(8,128)(2,1)S(1)} %copy-done.77), channel_id=1, source_target_pairs={{0,4},{12,8},{1,5},{13,9},{2,6},{14,10},{3,7},{15,11},{16,20},{28,... | collective-permute-start | bytes 3145736 | tf_op jit(solution)/shard_map/ppermute | solution.py:49
  606.0 89.9 %collective-permute-start.87 = (bf16[1024,512]{1,0:T(8,128)(2,1)S(1)}, bf16[1024,512]{1,0:T(8,128)(2,1)S(1)}, u32[]{:S(2)}, u32[]{:S(2)}) collective-permute-start(bf16[1024,512]{1,0:T(8,128)(2,1)S(1)} %copy-done.78), channel_id=1, source_target_pairs={{0,4},{12,8},{1,5},{13,9},{2,6},{14,10},{3,7},{15,11},{16,20},{28,... | collective-permute-start | bytes 3145736 | tf_op jit(solution)/shard_map/ppermute | solution.py:49
  628.4 88.2 %collective-permute-start.83 = (bf16[1024,512]{1,0:T(8,128)(2,1)S(1)}, bf16[1024,512]{1,0:T(8,128)(2,1)S(1)}, u32[]{:S(2)}, u32[]{:S(2)}) collective-permute-start(bf16[1024,512]{1,0:T(8,128)(2,1)S(1)} %copy-done.79), channel_id=1, source_target_pairs={{0,4},{12,8},{1,5},{13,9},{2,6},{14,10},{3,7},{15,11},{16,20},{28,... | collective-permute-start | bytes 3145736 | tf_op jit(solution)/shard_map/ppermute | solution.py:49
  650.9 67.9 %collective-permute-start.24 = (bf16[512,2,512]{2,0,1:T(8,128)(2,1)S(1)}, bf16[512,2,512]{2,0,1:T(8,128)(2,1)S(1)}, u32[]{:S(2)}, u32[]{:S(2)}) collective-permute-start(bf16[512,2,512]{2,0,1:T(8,128)(2,1)S(1)} %select_bitcast_fusion.3), channel_id=1, source_target_pairs={{0,1},{1,0},{2,3},{3,2},{4,5},{5,4},{6,7},{7,6},{8,9},{9,8},{10,11... | collective-permute-start | bytes 3145736 | tf_op jit(solution)/shard_map/ppermute | solution.py:20
  673.4 46.9 %collective-permute-start.108 = (bf16[1024,512]{1,0:T(8,128)(2,1)S(1)}, bf16[1024,512]{1,0:T(8,128)(2,1)S(1)}, u32[]{:S(2)}, u32[]{:S(2)}) collective-permute-start(bf16[1024,512]{1,0:T(8,128)(2,1)S(1)} %add_convert_fusion.2), channel_id=1, source_target_pairs={{4,8},{8,4},{5,9},{9,5},{6,10},{10,6},{7,11},{11,7},{20,24},{24,20... | collective-permute-start | bytes 3145736 | tf_op jit(solution)/shard_map/ppermute | solution.py:51
  721.8 75.2 %collective-permute-start.80 = (bf16[1024,512]{1,0:T(8,128)(2,1)S(1)}, bf16[1024,512]{1,0:T(8,128)(2,1)}, u32[]{:S(2)}, u32[]{:S(2)}) collective-permute-start(bf16[1024,512]{1,0:T(8,128)(2,1)S(1)} %add_convert_fusion.18), channel_id=1, source_target_pairs={{4,8},{8,4},{5,9},{9,5},{6,10},{10,6},{7,11},{11,7},{20,24},{24,20... | collective-permute-start | bytes 3145736 | tf_op jit(solution)/shard_map/ppermute | solution.py:51
  724.7 75.6 %collective-permute-start.76 = (bf16[1024,512]{1,0:T(8,128)(2,1)}, bf16[1024,512]{1,0:T(8,128)(2,1)}, u32[]{:S(2)}, u32[]{:S(2)}) collective-permute-start(bf16[1024,512]{1,0:T(8,128)(2,1)} %add_convert_fusion.20), channel_id=1, source_target_pairs={{4,8},{8,4},{5,9},{9,5},{6,10},{10,6},{7,11},{11,7},{20,24},{24,20... | collective-permute-start | bytes 3145736 | tf_op jit(solution)/shard_map/ppermute | solution.py:51
  727.6 76.3 %collective-permute-start.72 = (bf16[1024,512]{1,0:T(8,128)(2,1)}, bf16[1024,512]{1,0:T(8,128)(2,1)}, u32[]{:S(2)}, u32[]{:S(2)}) collective-permute-start(bf16[1024,512]{1,0:T(8,128)(2,1)} %add_convert_fusion.22), channel_id=1, source_target_pairs={{4,8},{8,4},{5,9},{9,5},{6,10},{10,6},{7,11},{11,7},{20,24},{24,20... | collective-permute-start | bytes 3145736 | tf_op jit(solution)/shard_map/ppermute | solution.py:51
  745.2 62.4 %collective-permute-start.68 = (bf16[1024,512]{1,0:T(8,128)(2,1)}, bf16[1024,512]{1,0:T(8,128)(2,1)}, u32[]{:S(2)}, u32[]{:S(2)}) collective-permute-start(bf16[1024,512]{1,0:T(8,128)(2,1)} %add_convert_fusion.24), channel_id=1, source_target_pairs={{4,8},{8,4},{5,9},{9,5},{6,10},{10,6},{7,11},{11,7},{20,24},{24,20... | collective-permute-start | bytes 3145736 | tf_op jit(solution)/shard_map/ppermute | solution.py:51
  750.7 258.7 %all-to-all-start.1 = ((bf16[4,128,512]{2,1,0:T(8,128)(2,1)}), bf16[4,128,512]{2,1,0:T(8,128)(2,1)}, u32[]{:S(2)}, u32[]{:S(2)}) async-start(bf16[4,128,512]{2,1,0:T(8,128)(2,1)} %gather_fusion.2), calls=%async_computation.1 | async-start | bytes 1048576 | tf_op jit(solution)/shard_map/all_to_all | solution.py:222
  811.3 159.3 %collective-permute-start.109 = (bf16[1024,512]{1,0:T(8,128)(2,1)S(1)}, bf16[1024,512]{1,0:T(8,128)(2,1)S(1)}, u32[]{:S(2)}, u32[]{:S(2)}) collective-permute-start(bf16[1024,512]{1,0:T(8,128)(2,1)S(1)} %copy-done.50), channel_id=1, source_target_pairs={{4,0},{8,12},{5,1},{9,13},{6,2},{10,14},{7,3},{11,15},{20,16},{24,... | collective-permute-start | bytes 3145736 | tf_op jit(solution)/shard_map/ppermute | solution.py:53
  814.1 157.2 %collective-permute-start.106 = (bf16[1024,512]{1,0:T(8,128)(2,1)S(1)}, bf16[1024,512]{1,0:T(8,128)(2,1)S(1)}, u32[]{:S(2)}, u32[]{:S(2)}) collective-permute-start(bf16[1024,512]{1,0:T(8,128)(2,1)S(1)} %copy-done.51), channel_id=1, source_target_pairs={{4,0},{8,12},{5,1},{9,13},{6,2},{10,14},{7,3},{11,15},{20,16},{24,... | collective-permute-start | bytes 3145736 | tf_op jit(solution)/shard_map/ppermute | solution.py:53
  816.8 155.9 %collective-permute-start.103 = (bf16[1024,512]{1,0:T(8,128)(2,1)S(1)}, bf16[1024,512]{1,0:T(8,128)(2,1)S(1)}, u32[]{:S(2)}, u32[]{:S(2)}) collective-permute-start(bf16[1024,512]{1,0:T(8,128)(2,1)S(1)} %copy-done.52), channel_id=1, source_target_pairs={{4,0},{8,12},{5,1},{9,13},{6,2},{10,14},{7,3},{11,15},{20,16},{24,... | collective-permute-start | bytes 3145736 | tf_op jit(solution)/shard_map/ppermute | solution.py:53
  819.6 141.9 %collective-permute-start.37 = (bf16[2,512]{1,0:T(2,128)(2,1)S(1)}, bf16[2,512]{1,0:T(2,128)(2,1)S(1)}, u32[]{:S(2)}, u32[]{:S(2)}) collective-permute-start(bf16[2,512]{1,0:T(2,128)(2,1)S(1)} %slice.319), channel_id=1, source_target_pairs={{4,0},{8,4},{12,8},{5,1},{9,5},{13,9},{6,2},{10,6},{14,10},{7,3},{... | collective-permute-start | bytes 6152 | tf_op jit(solution)/shard_map/ppermute | solution.py:15
  972.7 61.7 %collective-permute-start.77 = (bf16[1024,512]{1,0:T(8,128)(2,1)}, bf16[1024,512]{1,0:T(8,128)(2,1)}, u32[]{:S(2)}, u32[]{:S(2)}) collective-permute-start(bf16[1024,512]{1,0:T(8,128)(2,1)} %add_convert_fusion.19), channel_id=1, source_target_pairs={{4,0},{8,12},{5,1},{9,13},{6,2},{10,14},{7,3},{11,15},{20,16},{24,... | collective-permute-start | bytes 3145736 | tf_op jit(solution)/shard_map/ppermute | solution.py:53
  1000.2 56.7 %collective-permute-start.73 = (bf16[1024,512]{1,0:T(8,128)(2,1)}, bf16[1024,512]{1,0:T(8,128)(2,1)}, u32[]{:S(2)}, u32[]{:S(2)}) collective-permute-start(bf16[1024,512]{1,0:T(8,128)(2,1)} %add_convert_fusion.21), channel_id=1, source_target_pairs={{4,0},{8,12},{5,1},{9,13},{6,2},{10,14},{7,3},{11,15},{20,16},{24,... | collective-permute-start | bytes 3145736 | tf_op jit(solution)/shard_map/ppermute | solution.py:53
  1005.8 73.6 %collective-permute-start.69 = (bf16[1024,512]{1,0:T(8,128)(2,1)}, bf16[1024,512]{1,0:T(8,128)(2,1)}, u32[]{:S(2)}, u32[]{:S(2)}) collective-permute-start(bf16[1024,512]{1,0:T(8,128)(2,1)} %add_convert_fusion.23), channel_id=1, source_target_pairs={{4,0},{8,12},{5,1},{9,13},{6,2},{10,14},{7,3},{11,15},{20,16},{24,... | collective-permute-start | bytes 3145736 | tf_op jit(solution)/shard_map/ppermute | solution.py:53
  1012.0 89.8 %collective-permute-start.97 = (bf16[1024,512]{1,0:T(8,128)(2,1)}, bf16[1024,512]{1,0:T(8,128)(2,1)S(1)}, u32[]{:S(2)}, u32[]{:S(2)}) collective-permute-start(bf16[1024,512]{1,0:T(8,128)(2,1)} %add_convert_fusion.9), channel_id=1, source_target_pairs={{4,0},{8,12},{5,1},{9,13},{6,2},{10,14},{7,3},{11,15},{20,16},{24,... | collective-permute-start | bytes 3145736 | tf_op jit(solution)/shard_map/ppermute | solution.py:53
  1034.5 89.8 %collective-permute-start.93 = (bf16[1024,512]{1,0:T(8,128)(2,1)S(1)}, bf16[1024,512]{1,0:T(8,128)(2,1)S(1)}, u32[]{:S(2)}, u32[]{:S(2)}) collective-permute-start(bf16[1024,512]{1,0:T(8,128)(2,1)S(1)} %copy-done.55), channel_id=1, source_target_pairs={{4,0},{8,12},{5,1},{9,13},{6,2},{10,14},{7,3},{11,15},{20,16},{24,... | collective-permute-start | bytes 3145736 | tf_op jit(solution)/shard_map/ppermute | solution.py:53
  1079.4 67.3 %collective-permute-start.89 = (bf16[1024,512]{1,0:T(8,128)(2,1)S(1)}, bf16[1024,512]{1,0:T(8,128)(2,1)S(1)}, u32[]{:S(2)}, u32[]{:S(2)}) collective-permute-start(bf16[1024,512]{1,0:T(8,128)(2,1)S(1)} %copy-done.49), channel_id=1, source_target_pairs={{4,0},{8,12},{5,1},{9,13},{6,2},{10,14},{7,3},{11,15},{20,16},{24,... | collective-permute-start | bytes 3145736 | tf_op jit(solution)/shard_map/ppermute | solution.py:53
  1082.1 82.7 %collective-permute-start.85 = (bf16[1024,512]{1,0:T(8,128)(2,1)S(1)}, bf16[1024,512]{1,0:T(8,128)(2,1)S(1)}, u32[]{:S(2)}, u32[]{:S(2)}) collective-permute-start(bf16[1024,512]{1,0:T(8,128)(2,1)S(1)} %add_convert_fusion.15), channel_id=1, source_target_pairs={{4,0},{8,12},{5,1},{9,13},{6,2},{10,14},{7,3},{11,15},{20,16},{24,... | collective-permute-start | bytes 3145736 | tf_op jit(solution)/shard_map/ppermute | solution.py:53
  1124.4 47.5 %collective-permute-start.48 = (bf16[1024,512]{1,0:T(8,128)(2,1)S(1)}, bf16[1024,512]{1,0:T(8,128)(2,1)S(1)}, u32[]{:S(2)}, u32[]{:S(2)}) collective-permute-start(bf16[1024,512]{1,0:T(8,128)(2,1)S(1)} %copy-done.69), channel_id=1, source_target_pairs={{0,4},{12,8},{1,5},{13,9},{2,6},{14,10},{3,7},{15,11},{16,20},{28,... | collective-permute-start | bytes 3145736 | tf_op jit(solution)/shard_map/ppermute | solution.py:49
  1126.2 46.8 %collective-permute-start.52 = (bf16[1024,512]{1,0:T(8,128)(2,1)S(1)}, bf16[1024,512]{1,0:T(8,128)(2,1)S(1)}, u32[]{:S(2)}, u32[]{:S(2)}) collective-permute-start(bf16[1024,512]{1,0:T(8,128)(2,1)S(1)} %copy-done.70), channel_id=1, source_target_pairs={{0,4},{12,8},{1,5},{13,9},{2,6},{14,10},{3,7},{15,11},{16,20},{28,... | collective-permute-start | bytes 3145736 | tf_op jit(solution)/shard_map/ppermute | solution.py:49
  1146.7 47.7 %collective-permute-start.44 = (bf16[1024,512]{1,0:T(8,128)(2,1)S(1)}, bf16[1024,512]{1,0:T(8,128)(2,1)S(1)}, u32[]{:S(2)}, u32[]{:S(2)}) collective-permute-start(bf16[1024,512]{1,0:T(8,128)(2,1)S(1)} %copy-done.71), channel_id=1, source_target_pairs={{0,4},{12,8},{1,5},{13,9},{2,6},{14,10},{3,7},{15,11},{16,20},{28,... | collective-permute-start | bytes 3145736 | tf_op jit(solution)/shard_map/ppermute | solution.py:49
  1164.8 51.7 %collective-permute-start.61 = (bf16[1024,512]{1,0:T(8,128)(2,1)S(1)}, bf16[1024,512]{1,0:T(8,128)(2,1)S(1)}, u32[]{:S(2)}, u32[]{:S(2)}) collective-permute-start(bf16[1024,512]{1,0:T(8,128)(2,1)S(1)} %fusion.15), channel_id=1, source_target_pairs={{0,4},{12,8},{1,5},{13,9},{2,6},{14,10},{3,7},{15,11},{16,20},{28,... | collective-permute-start | bytes 3145736 | tf_op jit(solution)/shard_map/ppermute | solution.py:49
  1172.2 46.2 %collective-permute-start.49 = (bf16[1024,512]{1,0:T(8,128)(2,1)S(1)}, bf16[1024,512]{1,0:T(8,128)(2,1)S(1)}, u32[]{:S(2)}, u32[]{:S(2)}) collective-permute-start(bf16[1024,512]{1,0:T(8,128)(2,1)S(1)} %add_convert_fusion.30), channel_id=1, source_target_pairs={{4,8},{8,4},{5,9},{9,5},{6,10},{10,6},{7,11},{11,7},{20,24},{24,20... | collective-permute-start | bytes 3145736 | tf_op jit(solution)/shard_map/ppermute | solution.py:51
  1173.3 47.7 %collective-permute-start.53 = (bf16[1024,512]{1,0:T(8,128)(2,1)S(1)}, bf16[1024,512]{1,0:T(8,128)(2,1)S(1)}, u32[]{:S(2)}, u32[]{:S(2)}) collective-permute-start(bf16[1024,512]{1,0:T(8,128)(2,1)S(1)} %add_convert_fusion.28), channel_id=1, source_target_pairs={{4,8},{8,4},{5,9},{9,5},{6,10},{10,6},{7,11},{11,7},{20,24},{24,20... | collective-permute-start | bytes 3145736 | tf_op jit(solution)/shard_map/ppermute | solution.py:51
  1219.7 104.5 %collective-permute-start.50 = (bf16[1024,512]{1,0:T(8,128)(2,1)}, bf16[1024,512]{1,0:T(8,128)(2,1)}, u32[]{:S(2)}, u32[]{:S(2)}) collective-permute-start(bf16[1024,512]{1,0:T(8,128)(2,1)} %add_convert_fusion.29), channel_id=1, source_target_pairs={{4,0},{8,12},{5,1},{9,13},{6,2},{10,14},{7,3},{11,15},{20,16},{24,... | collective-permute-start | bytes 3145736 | tf_op jit(solution)/shard_map/ppermute | solution.py:53
  1222.2 103.3 %collective-permute-start.54 = (bf16[1024,512]{1,0:T(8,128)(2,1)}, bf16[1024,512]{1,0:T(8,128)(2,1)}, u32[]{:S(2)}, u32[]{:S(2)}) collective-permute-start(bf16[1024,512]{1,0:T(8,128)(2,1)} %add_convert_fusion.27), channel_id=1, source_target_pairs={{4,0},{8,12},{5,1},{9,13},{6,2},{10,14},{7,3},{11,15},{20,16},{24,... | collective-permute-start | bytes 3145736 | tf_op jit(solution)/shard_map/ppermute | solution.py:53
  1224.8 102.1 %collective-permute-start.46 = (bf16[1024,512]{1,0:T(8,128)(2,1)}, bf16[1024,512]{1,0:T(8,128)(2,1)}, u32[]{:S(2)}, u32[]{:S(2)}) collective-permute-start(bf16[1024,512]{1,0:T(8,128)(2,1)} %add_convert_fusion.31), channel_id=1, source_target_pairs={{4,0},{8,12},{5,1},{9,13},{6,2},{10,14},{7,3},{11,15},{20,16},{24,... | collective-permute-start | bytes 3145736 | tf_op jit(solution)/shard_map/ppermute | solution.py:53
  1232.8 105.1 %collective-permute-start.63 = (bf16[1024,512]{1,0:T(8,128)(2,1)S(1)}, bf16[1024,512]{1,0:T(8,128)(2,1)}, u32[]{:S(2)}, u32[]{:S(2)}) collective-permute-start(bf16[1024,512]{1,0:T(8,128)(2,1)S(1)} %add_convert_fusion.25), channel_id=1, source_target_pairs={{4,0},{8,12},{5,1},{9,13},{6,2},{10,14},{7,3},{11,15},{20,16},{24,... | collective-permute-start | bytes 3145736 | tf_op jit(solution)/shard_map/ppermute | solution.py:53
  1234.4 80.8 %collective-permute-start.56 = (f32[5,512]{1,0:T(8,128)S(1)}, f32[5,512]{1,0:T(8,128)S(1)}, u32[]{:S(2)}, u32[]{:S(2)}) collective-permute-start(f32[5,512]{1,0:T(8,128)S(1)} %add.469), channel_id=1, source_target_pairs={{0,4},{4,0},{8,12},{12,8},{1,5},{5,1},{9,13},{13,9},{2,6},{6,2},{1... | collective-permute-start | bytes 30728 | tf_op jit(solution)/shard_map/ppermute | solution.py:20
  (184 other events, 3943.1 us)
Sparse Core Ops, SparseCore 0:
  31.1 61.7 all-gather.5
  94.5 33.0 all-gather.7
  129.2 26.5 all-gather.9
  157.3 27.4 all-gather.11
  186.2 27.9 all-gather.13

commit v2 on v1

--- a/solution.py
+++ b/solution.py
@@ -1,6 +1,10 @@
+import functools
+
 import jax
 import jax.numpy as jnp
 from jax import lax
+from jax.experimental import pallas as pl
+from jax.experimental.pallas import tpu as pltpu
 from jax.sharding import PartitionSpec as P
 
 EPS = 1e-05
@@ -53,6 +57,208 @@
     handed = lax.ppermute(total, "ctx", [(1, 0), (2, 3)])
     inner = jnp.logical_or(rank == 1, rank == 2)
     return jnp.where(inner, total, handed).astype(WIDE)
+
+
+PIECE = 256
+AHEAD = 4
+SLOTS = 4
+MESH = pl.DeviceIdType.MESH
+
+
+def line_kernel(
+    pieces, left_of, left_ref, right_ref, out_ref, peer, outer_part, middle_part, held,
+    peer_send, peer_recv, in_send, outer_recv, middle_recv, out_send, out_recv, own_done,
+):
+    shard = lax.axis_index("shard")
+    ctx = lax.axis_index("ctx")
+    tokens = right_ref.shape[0]
+    rows = left_ref.shape[1]
+    middle = jnp.logical_or(ctx == 1, ctx == 2)
+    end = jnp.logical_not(middle)
+    low_side = ctx < 2
+    inward = jnp.where(low_side, ctx + 1, ctx - 1)
+    outward = jnp.where(ctx == 1, 0, 3)
+
+    barrier = pltpu.get_barrier_semaphore()
+    pl.semaphore_signal(barrier, inc=1, device_id={"shard": 1 - shard}, device_id_type=MESH)
+    pl.semaphore_signal(barrier, inc=1, device_id={"ctx": inward}, device_id_type=MESH)
+
+    @pl.when(middle)
+    def _():
+        pl.semaphore_signal(barrier, inc=1, device_id={"ctx": outward}, device_id_type=MESH)
+        pl.semaphore_wait(barrier, 3)
+
+    @pl.when(end)
+    def _():
+        pl.semaphore_wait(barrier, 2)
+
+    def columns(index):
+        return pl.ds(pl.multiple_of(index * PIECE, PIECE), PIECE)
+
+    def peer_copy(index):
+        return pltpu.make_async_remote_copy(
+            src_ref=right_ref.at[:, columns(index)],
+            dst_ref=peer.at[index],
+            send_sem=peer_send.at[index],
+            recv_sem=peer_recv.at[index],
+            device_id={"shard": 1 - shard},
+            device_id_type=MESH,
+        )
+
+    def end_copy(index):
+        return pltpu.make_async_remote_copy(
+            src_ref=held.at[index % SLOTS],
+            dst_ref=outer_part.at[index],
+            send_sem=in_send.at[index],
+            recv_sem=outer_recv.at[index],
+            device_id={"ctx": inward},
+            device_id_type=MESH,
+        )
+
+    def middle_copy(index):
+        return pltpu.make_async_remote_copy(
+            src_ref=held.at[index % SLOTS],
+            dst_ref=middle_part.at[index],
+            send_sem=in_send.at[index],
+            recv_sem=middle_recv.at[index],
+            device_id={"ctx": inward},
+            device_id_type=MESH,
+        )
+
+    def out_copy(index):
+        return pltpu.make_async_remote_copy(
+            src_ref=outer_part.at[index],
+            dst_ref=out_ref.at[:, columns(index)],
+            send_sem=out_send.at[index],
+            recv_sem=out_recv.at[index],
+            device_id={"ctx": outward},
+            device_id_type=MESH,
+        )
+
+    def own_copy(index):
+        return pltpu.make_async_copy(
+            outer_part.at[index], out_ref.at[:, columns(index)], own_done.at[index]
+        )
+
+    tile = min(256, rows)
+
+    def product(index, start):
+        lines = pl.ds(pl.multiple_of(start * tile, tile), tile)
+        left = left_of(index)
+        own = jnp.dot(
+            left_ref[left, lines, :tokens],
+            right_ref[:, columns(index)],
+            preferred_element_type=WIDE,
+        )
+        other = jnp.dot(
+            left_ref[left, lines, tokens:], peer[index], preferred_element_type=WIDE
+        )
+        return lines, own + other
+
+    def finish(index):
+        middle_copy(index).wait_recv()
+
+        @pl.loop(0, rows // tile)
+        def _(start):
+            lines = pl.ds(pl.multiple_of(start * tile, tile), tile)
+            total = held[index % SLOTS, lines].astype(WIDE) + middle_part[index, lines].astype(WIDE)
+            outer_part[index, lines] = total.astype(LOW)
+
+        out_copy(index).start()
+        own_copy(index).start()
+
+    for index in range(min(AHEAD, pieces)):
+        peer_copy(index).start()
+
+    @pl.loop(0, pieces)
+    def _(index):
+        @pl.when(index + AHEAD < pieces)
+        def _():
+            peer_copy(index + AHEAD).start()
+
+        @pl.when(index >= SLOTS)
+        def _():
+            end_copy(index - SLOTS).wait_send()
+
+        peer_copy(index).wait_recv()
+
+        @pl.when(end)
+        def _():
+            @pl.loop(0, rows // tile)
+            def _(start):
+                lines, value = product(index, start)
+                held[index % SLOTS, lines] = value.astype(LOW)
+
+            end_copy(index).start()
+
+        @pl.when(middle)
+        def _():
+            end_copy(index).wait_recv()
+
+            @pl.loop(0, rows // tile)
+            def _(start):
+                lines, value = product(index, start)
+                value = value + outer_part[index, lines].astype(WIDE)
+                held[index % SLOTS, lines] = value.astype(LOW)
+
+            middle_copy(index).start()
+
+            @pl.when(index >= 1)
+            def _():
+                finish(index - 1)
+
+    @pl.when(middle)
+    def _():
+        finish(pieces - 1)
+
+    @pl.loop(0, pieces)
+    def _(index):
+        peer_copy(index).wait_send()
+
+        @pl.when(index >= pieces - SLOTS)
+        def _():
+            end_copy(index).wait_send()
+
+        @pl.when(middle)
+        def _():
+            out_copy(index).wait_send()
+            own_copy(index).wait()
+
+        @pl.when(end)
+        def _():
+            out_copy(index).wait_recv()
+
+
+def line_grads(lefts, rights, identity):
+    left = jnp.stack([value.T for value in lefts])
+    right = jnp.concatenate(rights, axis=1)
+    tokens, width = right.shape
+    rows = left.shape[1]
+    pieces = width // PIECE
+    first = rights[0].shape[1] // PIECE
+
+    def left_of(index):
+        return jnp.where(index < first, 0, 1)
+
+    flops = 4 * tokens * rows * width
+    dma = pltpu.SemaphoreType.DMA
+    return pl.pallas_call(
+        functools.partial(line_kernel, pieces, left_of),
+        out_shape=jax.ShapeDtypeStruct((rows, width), LOW),
+        in_specs=[pl.BlockSpec(memory_space=pltpu.VMEM)] * 2,
+        out_specs=pl.BlockSpec(memory_space=pl.ANY),
+        scratch_shapes=[
+            pltpu.VMEM((pieces, tokens, PIECE), LOW),
+            pltpu.VMEM((pieces, rows, PIECE), LOW),
+            pltpu.VMEM((pieces, rows, PIECE), LOW),
+            pltpu.VMEM((SLOTS, rows, PIECE), LOW),
+        ]
+        + [dma((pieces,)) for _ in range(8)],
+        compiler_params=pltpu.CompilerParams(
+            collective_id=identity, has_side_effects=True, vmem_limit_bytes=56 * 1024 * 1024
+        ),
+        cost_estimate=pl.CostEstimate(flops=flops * 8, bytes_accessed=rows * width * 64, transcendentals=0),
+    )(left, right)
 
 
 class Features:
@@ -91,6 +297,21 @@
         mine = jnp.where(first, pair[:, 0], pair[:, 1])
         away = jnp.where(first, pair[:, 1], pair[:, 0]).astype(LOW)
         return mine + swapped(away, "tp", 2).astype(WIDE)
+
+    def total_direct(self, full):
+        low = full.astype(LOW)
+        total = full
+        for step in (1, 2, 3):
+            total = total + swapped(low, "tp", step).astype(WIDE)
+        return total
+
+    def scatter_direct(self, full):
+        width = full.shape[1] // 4
+        total = lax.dynamic_slice_in_dim(full, self.rank * width, width, 1)
+        for step in (1, 2, 3):
+            block = lax.dynamic_slice_in_dim(full, (self.rank ^ step) * width, width, 1).astype(LOW)
+            total = total + swapped(block, "tp", step).astype(WIDE)
+        return total
 
     def own(self, full, axis):
         width = full.shape[axis] // lax.axis_size("tp")
@@ -224,6 +445,20 @@
         )
         return reorder(got, returning)
 
+    def weight_grads(lefts, rights, identity):
+        flat = [value for group in rights for value in group]
+        if shards.paired:
+            summed = line_grads([group[0] for group in lefts], flat, identity)
+            ends = [0]
+            for value in flat:
+                ends.append(ends[-1] + value.shape[1])
+            return [summed[:, a:b].astype(WIDE) for a, b in zip(ends, ends[1:])]
+        flat_lefts = [value for group in lefts for value in group]
+        return [
+            sum_line(contract_rows(left, shards.tokens(right)).astype(LOW), ctx_rank)
+            for left, right in zip(flat_lefts, flat)
+        ]
+
     in_flat = in_weight.reshape(weight_rows, -1)
     in_w = shards.weight(in_flat, weight_rows // 4)
     x_packed = to_packed(hidden_in)
@@ -283,45 +518,38 @@
     h_two_cols = shards.columns(h_two)
     h_one_cols = shards.columns(h_one)
 
-    down_parts, gate_parts, up_parts = [], [], []
-    ffn = None
+    acts, d_gates, d_ups = [], [], []
     dh_parts = [None] * len(h_two_parts)
     for index in range(CHUNKS):
-        down_w = chunk(down_weight, index)
+        down_rows = chunk(down_weight, index)
         gate_pre = sum(matmul(part, w) for part, w in zip(h_two_parts, gate_w[index]))
         up_pre = sum(matmul(part, w) for part, w in zip(h_two_parts, up_w[index]))
-        d_act = shards.own_total(matmul(cot_cols, down_w))
+        d_act = shards.own_total(matmul(cot_cols, down_rows))
         sigmoid_gate = jax.nn.sigmoid(gate_pre)
         silu_gate = gate_pre * sigmoid_gate
-        activated = (silu_gate * up_pre).astype(LOW)
-        d_gate = (d_act * up_pre * sigmoid_gate * (1.0 + gate_pre * (1.0 - sigmoid_gate))).astype(LOW)
-        d_up = (d_act * silu_gate).astype(LOW)
-        act_all = shards.tokens(activated)
-        d_gate_all = shards.tokens(d_gate)
-        d_up_all = shards.tokens(d_up)
-        down_parts.append(sum_line(contract_rows(cot_cols, act_all).astype(LOW), ctx_rank))
-        gate_parts.append(sum_line(contract_rows(h_two_cols, d_gate_all).astype(LOW), ctx_rank))
-        up_parts.append(sum_line(contract_rows(h_two_cols, d_up_all).astype(LOW), ctx_rank))
-        term = contract_cols(act_all, down_w)
-        ffn = term if ffn is None else ffn + term
+        acts.append((silu_gate * up_pre).astype(LOW))
+        d_gates.append(
+            (d_act * up_pre * sigmoid_gate * (1.0 + gate_pre * (1.0 - sigmoid_gate))).astype(LOW)
+        )
+        d_ups.append((d_act * silu_gate).astype(LOW))
         for place in range(len(dh_parts)):
-            term = contract_cols(d_gate, gate_w[index][place]) + contract_cols(d_up, up_w[index][place])
+            term = contract_cols(d_gates[-1], gate_w[index][place])
+            term = term + contract_cols(d_ups[-1], up_w[index][place])
             dh_parts[place] = term if dh_parts[place] is None else dh_parts[place] + term
-    down_total = jnp.concatenate(down_parts, axis=1)
-    gate_total = jnp.concatenate(gate_parts, axis=1)
-    up_total = jnp.concatenate(up_parts, axis=1)
-
-    ffn_own = tp.scatter(shards.own_tokens(ffn))
+    dh_two = tp.total_direct(shards.join(dh_parts))
+    down_w = shards.weight(down_weight, weight_rows)
+    ffn_rights = [jnp.concatenate(parts, axis=1) for parts in (acts, d_gates, d_ups)]
+    down_total, gate_total, up_total = weight_grads(
+        [[cot_cols], [h_two_cols, h_two_cols]], [ffn_rights[:1], ffn_rights[1:]], 0
+    )
+    activated = ffn_rights[0]
+    ffn_own = tp.scatter_direct(shards.join([contract_cols(activated, w) for w in down_w]))
     block_out = (tp.own(resid, 1) + ffn_own).astype(LOW)
-    block_dealt = to_dealt(block_out)
-
-    dh_two = shards.joined(tp.total(*shards.halves(dh_parts))).astype(WIDE)
+
     gain_two_grad = tp.own(jnp.sum(dh_two * normed_two, axis=0), 0)
     d_resid = cot_full.astype(WIDE) + norm_back(dh_two, normed_two, scale_two, gain_two)
     d_resid_low = d_resid.astype(LOW)
     d_gated = sum(matmul(part, w) for part, w in zip(shards.split(d_resid_low), out_w))
-    out_part = contract_rows(shards.columns(d_resid_low), shards.tokens(gated)).astype(LOW)
-    out_total = sum_line(out_part, ctx_rank)
     d_conv = (d_gated * c_part).astype(LOW)
     d_c_part = d_gated * conv_out
     rim_back = shifted(d_conv[:2], "ctx", -1)
@@ -344,17 +572,16 @@
         d_c_part.astype(LOW),
         (d_mixed * b_part).astype(LOW),
     ]
-    in_parts = [
-        sum_line(contract_rows(h_one_cols, shards.tokens(part)).astype(LOW), ctx_rank)
-        for part in d_proj
-    ]
-    in_total = jnp.stack(in_parts, axis=1)
     d_proj_flat = jnp.concatenate(d_proj, axis=1)
-    dh_one_parts = [contract_cols(d_proj_flat, w) for w in in_w]
-    dh_one = shards.joined(tp.total(*shards.halves(dh_one_parts))).astype(WIDE)
+    dh_one = tp.total_direct(shards.join([contract_cols(d_proj_flat, w) for w in in_w]))
+    out_total, in_flat_total = weight_grads(
+        [[shards.columns(d_resid_low)], [h_one_cols]], [[gated], [d_proj_flat]], 1
+    )
+    in_total = in_flat_total.reshape(in_weight.shape)
     gain_one_grad = tp.own(jnp.sum(dh_one * normed_one, axis=0), 0)
     d_input = d_resid + norm_back(dh_one, normed_one, scale_one, gain_one)
-    input_dealt = to_dealt(tp.own(d_input, 1).astype(LOW))
+    dealt = to_dealt(jnp.concatenate([block_out, tp.own(d_input, 1).astype(LOW)], axis=1))
+    block_dealt, input_dealt = dealt[:, :col_count], dealt[:, col_count:]
 
     small = jnp.concatenate([taps_grad, gain_one_grad[None], gain_two_grad[None]], axis=0)
     small_sum = butterfly_sum(butterfly_sum(small, "shard"), "ctx")

time: 1360 us -> 1120 us (0.82)
  waiting for transfers between devices: 780 us -> 312 us
  Pallas kernels: 0 us -> 450 us
  starting transfers between devices: 232 us -> 51 us
  matrix products: 135 us -> 91.6 us
    pallas_call x0 -> x2, Pallas kernels: none -> 450 us  [line_grads(): pl.pallas_call(functools.partial(line_kernel, pieces, left_of), out_shape...]
    ppermute x48 -> x0, waiting for transfers between devices: 353 us -> none  [the longest x16 208 us: sum_line(): from_end = lax.ppermute(piece, 'ctx', [(0, 1), (3, 2)])]
    ppermute x2, waiting for transfers between devices: 141 us -> 3.67 us  [shifted(): lax.ppermute(value, axis, [(source, source + steps) for source in range(l...]
    ppermute x48 -> x0, starting transfers between devices: 95 us -> none  [the longest x16 56.6 us: sum_line(): from_end = lax.ppermute(piece, 'ctx', [(0, 1), (3, 2)])]
    all_to_all x2 -> x1, starting transfers between devices: 50.2 us -> 3.51 us  [to_dealt(): lax.all_to_all(reorder(values, targets), 'ctx', split_axis=0, concat_axis...]
    dot_general x16 -> x0, matrix products: 40.7 us -> none  [contract_rows(): lax.dot_general(left, right, (((0,), (0,)), ((), ())), preferred_element_...]
    ppermute x60 -> x45, starting transfers between devices: 73.9 us -> 34.3 us  [swapped(): lax.ppermute(value, axis, [(source, source ^ step) for source in range(co...]
    convert_element_type x40 -> x6, other arithmetic: 60.7 us -> 22.3 us  [the longest x2 14.7 us: weight_grads(): return [summed[:, a:b].astype(WIDE) for a, b in zip(ends, ends[1:])]]
  transfers between devices with their start and end apart: 119 -> 55, of which waited for: 48 -> 18; matrix products, arithmetic and copies ran while one was open for 22% -> 19% of each run, Pallas kernels for 0% -> 41%
where the time goes in v2:
time: 1120 us; the launch traced here: 1110 us
  Pallas kernels  450 us (40%)
  waiting for transfers between devices  312 us (28%)
  other arithmetic  118 us (11%)
  matrix products  91.6 us (8%)
  local copies, waits for them, and re-layouts  68.3 us (6%)
  starting transfers between devices  51 us (5%)
  between operations  16 us (1%)
    pallas_call x2, Pallas kernels, line_grads(): pl.pallas_call(functools.partial(line_kernel, pieces, left_of), out_shape...  450 us
    ppermute x45, waiting for transfers between devices, swapped(): lax.ppermute(value, axis, [(source, source ^ step) for source in range(co...  288 us
    dot_general x24, matrix products, matmul(): return jnp.dot(left, right, preferred_element_type=WIDE)  52.2 us
    dot_general x22, matrix products, contract_cols(): lax.dot_general(left, right, (((1,), (1,)), ((), ())), preferred_element_...  39.4 us
    ppermute x45, starting transfers between devices, swapped(): lax.ppermute(value, axis, [(source, source ^ step) for source in range(co...  34.3 us
    unnamed x226, local copies, waits for them, and re-layouts  28.5 us
  transfers between devices with their start and end apart: 55, of which 18 were waited for; matrix products, arithmetic and copies ran while one was open for 19% of the time, Pallas kernels for 41%

profile of v2, /device:TPU:0, one launch (start us, length us, event | category | flops | bytes accessed | tf_op | source)
XLA Modules:
  0.0 1106.2 jit_solution(18442368641796552794)
XLA Ops:
  7.2 4.7 copy.209
  13.8 3.0 collective-permute-start.5
  16.8 13.3 %collective-permute-done.5 = bf16[192,1536]{1,0:T(8,128)(2,1)S(1)} collective-permute-done((bf16[192,1536]{1,0:T(8,128)(2,1)S(1)}, bf16[192,1536]{1,0:T(8,128)(2,1)S(1)}, u32[]{:S(2)}, u32[]{:S(2)}) %collective-permute-start.5) | collective-permute-done | bytes 589856 | tf_op jit(solution)/shard_map/ppermute | solution.py:24
  36.3 4.7 all-to-all-start
  41.1 2.1 slice.283
  45.2 4.0 fusion.112
  54.8 37.1 %collective-permute-done.11 = bf16[256,512]{1,0:T(8,128)(2,1)S(1)} collective-permute-done((bf16[256,512]{1,0:T(8,128)(2,1)S(1)}, bf16[256,512]{1,0:T(8,128)(2,1)S(1)}, u32[]{:S(2)}, u32[]{:S(2)}) %collective-permute-start.11) | collective-permute-done | bytes 262176 | tf_op jit(solution)/shard_map/ppermute | solution.py:24
  96.5 5.0 all-to-all-start.1
  103.9 20.3 %all-to-all-done.1 = bf16[4,128,512]{2,1,0:T(8,128)(2,1)S(1)} async-done(((bf16[4,128,512]{2,1,0:T(8,128)(2,1)}), bf16[4,128,512]{2,1,0:T(8,128)(2,1)S(1)}, u32[]{:S(2)}, u32[]{:S(2)}) %all-to-all-start.1) | async-done | bytes 524320 | tf_op jit(solution)/shard_map/all_to_all | solution.py:437
  126.6 2.3 copy.212
  128.9 5.4 collective-permute-done.23
  137.2 3.0 multiply_convert_fusion.1
  141.6 3.5 fusion.118
  146.2 5.2 convolution_add_fusion
  156.2 2.1 fusion.119
  158.4 4.4 select_convert_fusion
  169.6 2.0 constant_dynamic-slice_fusion.1
  173.6 6.6 collective-permute-done.25
  180.8 5.0 collective-permute-done.14
  187.9 31.6 %collective-permute-done.40 = bf16[512,512]{0,1:T(8,128)(2,1)} collective-permute-done((bf16[512,512]{0,1:T(8,128)(2,1)}, bf16[512,512]{0,1:T(8,128)(2,1)}, u32[]{:S(2)}, u32[]{:S(2)}) %collective-permute-start.40) | collective-permute-done | bytes 524320 | tf_op jit(solution)/shard_map/ppermute | solution.py:24
  225.3 20.4 %collective-permute-done.9 = bf16[512,1024]{0,1:T(8,128)(2,1)S(1)} collective-permute-done((bf16[512,1024]{0,1:T(8,128)(2,1)S(1)}, bf16[512,1024]{0,1:T(8,128)(2,1)S(1)}, u32[]{:S(2)}, u32[]{:S(2)}) %collective-permute-start.9) | collective-permute-done | bytes 1048608 | tf_op jit(solution)/shard_map/ppermute | solution.py:24
  262.7 17.7 %convert_add_fusion = (f32[512,2048]{0,1:T(8,128)}, bf16[512,2048]{0,1:T(8,128)(2,1)S(1)}) fusion(bf16[512,1024]{0,1:T(8,128)(2,1)S(1)} %get-tuple-element.127, bf16[512,1024]{0,1:T(8,128)(2,1)S(1)} %get-tuple-element.126, bf16[512,512]{0,1:T(8,128)(2,1)S(1)} %get-tuple-element.149, bf16[512,512]{0,1:T(8,128)(2,1)S(1)} %get-tuple-element.179, ...), kind=kLoop, calls=%fused_computation.15 | loop fusion | flops 16777216 | bytes 10496000 | tf_op jit(solution)/shard_map/add | solution.py:511
  289.4 3.2 convolution_add_fusion.8
  292.6 3.3 convolution_add_fusion.6
  295.9 3.9 constant_dynamic-update-slice_fusion.11
  299.8 3.6 constant_dynamic-update-slice_fusion.10
  309.5 2.0 convolution_add_fusion.4
  312.1 2.9 constant_dynamic-update-slice_fusion.9
  315.0 39.4 %collective-permute-done.17 = bf16[1024,512]{1,0:T(8,128)(2,1)} collective-permute-done((bf16[1024,512]{1,0:T(8,128)(2,1)}, bf16[1024,512]{1,0:T(8,128)(2,1)}, u32[]{:S(2)}, u32[]{:S(2)}) %collective-permute-start.17) | collective-permute-done | bytes 1048608 | tf_op jit(solution)/shard_map/ppermute | solution.py:24
  355.0 2.0 convolution_add_fusion.2
  356.9 19.9 %collective-permute-done.18 = bf16[1024,512]{1,0:T(8,128)(2,1)} collective-permute-done((bf16[1024,512]{1,0:T(8,128)(2,1)}, bf16[1024,512]{1,0:T(8,128)(2,1)}, u32[]{:S(2)}, u32[]{:S(2)}) %collective-permute-start.18) | collective-permute-done | bytes 1048608 | tf_op jit(solution)/shard_map/ppermute | solution.py:24
  377.5 3.0 constant_dynamic-update-slice_fusion.8
  380.5 7.5 collective-permute-done.27
  389.3 9.9 collective-permute-done.28
  401.4 9.0 collective-permute-done.29
  411.7 9.5 collective-permute-done.30
  432.4 2.4 fusion.42
  434.8 4.9 broadcast_select_fusion.6
  439.7 2.8 fusion.18
  444.9 2.0 fusion.124
  446.9 2.0 fusion.125
  455.7 2.0 fusion.126
  457.7 4.0 add_add_fusion
  461.7 3.2 broadcast_select_fusion.5
  468.9 3.2 fusion.16
  473.8 2.4 pad_maximum_fusion.3.left_ref
  476.3 314.0 %shard_map.196 = bf16[1024,6144]{1,0:T(8,128)(2,1)} custom-call(bf16[2,1024,1024]{2,1,0:T(8,128)(2,1)} %pad_maximum_fusion.3.left_ref, bf16[512,6144]{1,0:T(8,128)(2,1)} %get-tuple-element.65.right_ref), custom_call_target="tpu_custom_call" | custom-call | flops 103079215104 | bytes 402653184 | tf_op jit(solution)/shard_map/pallas_call | solution.py:245
  790.4 7.7 multiply_reduce_fusion
  798.2 12.7 %fusion.111 = (bf16[512,2048]{0,1:T(8,128)(2,1)S(1)}, f32[512,2048]{0,1:T(8,128)}) fusion(f32[512]{0:T(512)S(1)} %broadcast_multiply_fusion.2, bf16[512,1024]{0,1:T(8,128)(2,1)S(1)} %copy-done.13, bf16[512,1024]{0,1:T(8,128)(2,1)S(1)} %copy-done.11, bf16[512,512]{0,1:T(8,128)(2,1)S(1)} %copy-done.5, bf16[512,512]{0,1:T(8,128)(2,1)S(1)} %copy-done.7, ...), kind=kLoop, calls=%fused_computation.326 | loop fusion | flops 29360128 | bytes 16789504 | tf_op jit(solution)/shard_map/convert_element_type | solution.py:551
  810.9 2.1 fusion.127
  813.7 2.4 fusion.8
  818.8 2.8 collective-permute-done.34
  830.9 11.8 %slice_convert_fusion = (f32[1024,2048]{1,0:T(8,128)}, f32[1024,2048]{1,0:T(8,128)}, f32[1024,2048]{1,0:T(8,128)}) fusion(bf16[1024,6144]{1,0:T(8,128)(2,1)} %shard_map.196), kind=kLoop, calls=%fused_computation.23 | loop fusion | flops 6291456 | bytes 37748736 | tf_op jit(solution)/shard_map/convert_element_type | solution.py:455
  846.0 2.4 pad_maximum_fusion.2.left_ref
  848.4 28.6 %collective-permute-done.37 = bf16[512,2048]{0,1:T(8,128)(2,1)S(1)} collective-permute-done((bf16[512,2048]{0,1:T(8,128)(2,1)}, bf16[512,2048]{0,1:T(8,128)(2,1)S(1)}, u32[]{:S(2)}, u32[]{:S(2)}) %collective-permute-start.37) | collective-permute-done | bytes 2097184 | tf_op jit(solution)/shard_map/ppermute | solution.py:24
  877.0 44.4 %collective-permute-done.36 = bf16[512,2048]{0,1:T(8,128)(2,1)S(1)} collective-permute-done((bf16[512,2048]{0,1:T(8,128)(2,1)}, bf16[512,2048]{0,1:T(8,128)(2,1)S(1)}, u32[]{:S(2)}, u32[]{:S(2)}) %collective-permute-start.36) | collective-permute-done | bytes 2097184 | tf_op jit(solution)/shard_map/ppermute | solution.py:24
  921.4 6.8 multiply_reduce_fusion.1
  932.2 3.5 all-to-all-start.2
  936.7 136.0 %shard_map.195 = bf16[1024,2048]{1,0:T(8,128)(2,1)} custom-call(bf16[2,1024,1024]{2,1,0:T(8,128)(2,1)} %pad_maximum_fusion.2.left_ref, bf16[512,2048]{1,0:T(8,128)(2,1)} %pad_maximum_fusion.8.right_ref), custom_call_target="tpu_custom_call" | custom-call | flops 34359738368 | bytes 134217728 | tf_op jit(solution)/shard_map/pallas_call | solution.py:245
  1072.8 5.5 slice_convert_fusion.3
  1078.3 2.0 collective-permute-start.44
  1080.3 2.8 slice_convert_fusion.8
  1083.1 6.6 copy.267
  1089.7 6.6 copy.268
  (465 shorter events, 140.0 us)
Async XLA Ops:
  7.2 139.0 %all-gather.6.cloned.1.call-start = ((), (), s32[]{:S(2)}) async-start(), calls=%async_computation.3 | async-start | bytes 2949120 | tf_op jit(solution)/shard_map/all_gather | solution.py:336
  13.8 16.3 %collective-permute-start.5 = (bf16[192,1536]{1,0:T(8,128)(2,1)S(1)}, bf16[192,1536]{1,0:T(8,128)(2,1)S(1)}, u32[]{:S(2)}, u32[]{:S(2)}) collective-permute-start(bf16[192,1536]{1,0:T(8,128)(2,1)S(1)} %copy.211), channel_id=1, source_target_pairs={{0,16},{16,0},{1,17},{17,1},{2,18},{18,2},{3,19},{19,3},{4,20},{20... | collective-permute-start | bytes 1769480 | tf_op jit(solution)/shard_map/ppermute | solution.py:24
  31.1 65.4 %collective-permute-start.2 = (bf16[2,512]{1,0:T(2,128)(2,1)S(1)}, bf16[2,512]{1,0:T(2,128)(2,1)S(1)}, u32[]{:S(2)}, u32[]{:S(2)}) collective-permute-start(bf16[2,512]{1,0:T(2,128)(2,1)S(1)} %pad_maximum_fusion.20), channel_id=1, source_target_pairs={{0,2},{1,3},{2,0},{3,1},{4,6},{5,7},{6,4},{7,5},{8,10},{9,11},{10,... | collective-permute-start | bytes 6152 | tf_op jit(solution)/shard_map/ppermute | solution.py:24
  36.3 60.1 %all-to-all-start = ((bf16[4,128,512]{2,1,0:T(8,128)(2,1)}), bf16[4,128,512]{2,1,0:T(8,128)(2,1)S(1)}, u32[]{:S(2)}, u32[]{:S(2)}) async-start(bf16[4,128,512]{2,1,0:T(8,128)(2,1)} %gather_fusion), calls=%async_computation | async-start | bytes 1048576 | tf_op jit(solution)/shard_map/all_to_all | solution.py:437
  41.1 248.3 %all-gather.8.cloned.1.call-start = ((), (), s32[]{:S(2)}) async-start(), calls=%async_computation.4 | async-start | bytes 1310720 | tf_op jit(solution)/shard_map/all_gather | solution.py:336
  43.2 83.4 %collective-permute-start.4 = (bf16[256,1536]{0,1:T(8,128)(2,1)}, bf16[256,1536]{0,1:T(8,128)(2,1)}, u32[]{:S(2)}, u32[]{:S(2)}) collective-permute-start(bf16[256,1536]{0,1:T(8,128)(2,1)} %bitcast.22), channel_id=1, source_target_pairs={{0,16},{16,0},{1,17},{17,1},{2,18},{18,2},{3,19},{19,3},{4,20},{20... | collective-permute-start | bytes 2359304 | tf_op jit(solution)/shard_map/ppermute | solution.py:24
  44.7 113.6 %collective-permute-start.7 = (bf16[1024,512]{1,0:T(8,128)(2,1)}, bf16[1024,512]{1,0:T(8,128)(2,1)}, u32[]{:S(2)}, u32[]{:S(2)}) collective-permute-start(bf16[1024,512]{1,0:T(8,128)(2,1)} %param.18), channel_id=1, source_target_pairs={{0,16},{16,0},{1,17},{17,1},{2,18},{18,2},{3,19},{19,3},{4,20},{20... | collective-permute-start | bytes 3145736 | tf_op jit(solution)/shard_map/ppermute | solution.py:24
  49.3 42.7 %collective-permute-start.11 = (bf16[256,512]{1,0:T(8,128)(2,1)S(1)}, bf16[256,512]{1,0:T(8,128)(2,1)S(1)}, u32[]{:S(2)}, u32[]{:S(2)}) collective-permute-start(bf16[256,512]{1,0:T(8,128)(2,1)S(1)} %constant_dynamic-slice_fusion.9), channel_id=1, source_target_pairs={{0,16},{16,0},{1,17},{17,1},{2,18},{18,2},{3,19},{19,3},{4,20},{20... | collective-permute-start | bytes 786440 | tf_op jit(solution)/shard_map/ppermute | solution.py:24
  52.6 73.9 %collective-permute-start.12 = (bf16[256,512]{1,0:T(8,128)(2,1)S(1)}, bf16[256,512]{1,0:T(8,128)(2,1)}, u32[]{:S(2)}, u32[]{:S(2)}) collective-permute-start(bf16[256,512]{1,0:T(8,128)(2,1)S(1)} %constant_dynamic-slice_fusion.8), channel_id=1, source_target_pairs={{0,16},{16,0},{1,17},{17,1},{2,18},{18,2},{3,19},{19,3},{4,20},{20... | collective-permute-start | bytes 786440 | tf_op jit(solution)/shard_map/ppermute | solution.py:24
  92.0 9.7 collective-permute-start.13
  96.5 27.7 %all-to-all-start.1 = ((bf16[4,128,512]{2,1,0:T(8,128)(2,1)}), bf16[4,128,512]{2,1,0:T(8,128)(2,1)S(1)}, u32[]{:S(2)}, u32[]{:S(2)}) async-start(bf16[4,128,512]{2,1,0:T(8,128)(2,1)} %gather_fusion.2), calls=%async_computation.1 | async-start | bytes 1048576 | tf_op jit(solution)/shard_map/all_to_all | solution.py:437
  101.5 191.1 %all-gather.12.cloned.1.call-start = ((), (), s32[]{:S(2)}) async-start(), calls=%async_computation.6 | async-start | bytes 1310720 | tf_op jit(solution)/shard_map/all_gather | solution.py:336
  101.5 2.3 collective-permute-start.3
  102.3 193.5 %all-gather.10.cloned.1.call-start = ((), (), s32[]{:S(2)}) async-start(), calls=%async_computation.5 | async-start | bytes 1310720 | tf_op jit(solution)/shard_map/all_gather | solution.py:336
  103.2 22.1 %collective-permute-start = (bf16[512,512]{0,1:T(8,128)(2,1)S(1)}, bf16[512,512]{0,1:T(8,128)(2,1)S(1)}, u32[]{:S(2)}, u32[]{:S(2)}) collective-permute-start(bf16[512,512]{0,1:T(8,128)(2,1)S(1)} %copy.311), channel_id=1, source_target_pairs={{0,2},{1,3},{2,0},{3,1},{4,6},{5,7},{6,4},{7,5},{8,10},{9,11},{10,... | collective-permute-start | bytes 1572872 | tf_op jit(solution)/shard_map/ppermute | solution.py:24
  124.9 9.4 collective-permute-start.23
  126.5 9.2 collective-permute-start.1
  126.5 136.1 %copy-start.80 = (f32[1,2048]{1,0:T(1,128)}, f32[1,2048]{1,0:T(1,128)S(1)}, u32[]{:S(2)}) copy-start(f32[1,2048]{1,0:T(1,128)S(1)} %get-tuple-element.154) | copy-start | bytes 24580
  126.6 173.3 %all-gather.14.cloned.1.call-start = ((), (), s32[]{:S(2)}) async-start(), calls=%async_computation.7 | async-start | bytes 1310720 | tf_op jit(solution)/shard_map/all_gather | solution.py:336
  135.5 9.6 collective-permute-start.24
  151.6 2.9 collective-permute-start.6
  162.8 57.4 %collective-permute-start.8 = (bf16[512,1024]{0,1:T(8,128)(2,1)}, bf16[512,1024]{0,1:T(8,128)(2,1)S(1)}, u32[]{:S(2)}, u32[]{:S(2)}) collective-permute-start(bf16[512,1024]{0,1:T(8,128)(2,1)} %get-tuple-element.171), channel_id=1, source_target_pairs={{0,1},{1,0},{2,3},{3,2},{4,5},{5,4},{6,7},{7,6},{8,9},{9,8},{10,11... | collective-permute-start | bytes 3145736 | tf_op jit(solution)/shard_map/ppermute | solution.py:24
  165.2 15.0 %collective-permute-start.25 = (bf16[512,512]{0,1:T(8,128)(2,1)}, bf16[512,512]{0,1:T(8,128)(2,1)}, u32[]{:S(2)}, u32[]{:S(2)}) collective-permute-start(bf16[512,512]{0,1:T(8,128)(2,1)} %constant_dynamic-slice_fusion.4), channel_id=1, source_target_pairs={{0,16},{16,0},{1,17},{17,1},{2,18},{18,2},{3,19},{19,3},{4,20},{20... | collective-permute-start | bytes 1572872 | tf_op jit(solution)/shard_map/ppermute | solution.py:24
  166.8 19.1 %collective-permute-start.14 = (bf16[256,512]{1,0:T(8,128)(2,1)S(1)}, bf16[256,512]{1,0:T(8,128)(2,1)}, u32[]{:S(2)}, u32[]{:S(2)}) collective-permute-start(bf16[256,512]{1,0:T(8,128)(2,1)S(1)} %constant_dynamic-slice_fusion.6), channel_id=1, source_target_pairs={{0,16},{16,0},{1,17},{17,1},{2,18},{18,2},{3,19},{19,3},{4,20},{20... | collective-permute-start | bytes 786440 | tf_op jit(solution)/shard_map/ppermute | solution.py:24
  168.2 139.7 %collective-permute-start.15 = (bf16[1024,512]{1,0:T(8,128)(2,1)}, bf16[1024,512]{1,0:T(8,128)(2,1)}, u32[]{:S(2)}, u32[]{:S(2)}) collective-permute-start(bf16[1024,512]{1,0:T(8,128)(2,1)} %get-tuple-element.117), channel_id=1, source_target_pairs={{0,16},{16,0},{1,17},{17,1},{2,18},{18,2},{3,19},{19,3},{4,20},{20... | collective-permute-start | bytes 3145736 | tf_op jit(solution)/shard_map/ppermute | solution.py:24
  171.6 48.0 %collective-permute-start.40 = (bf16[512,512]{0,1:T(8,128)(2,1)}, bf16[512,512]{0,1:T(8,128)(2,1)}, u32[]{:S(2)}, u32[]{:S(2)}) collective-permute-start(bf16[512,512]{0,1:T(8,128)(2,1)} %constant_dynamic-slice_fusion.1), channel_id=1, source_target_pairs={{0,16},{16,0},{1,17},{17,1},{2,18},{18,2},{3,19},{19,3},{4,20},{20... | collective-permute-start | bytes 1572872 | tf_op jit(solution)/shard_map/ppermute | solution.py:24
  180.2 40.6 %collective-permute-start.26 = (bf16[512,512]{0,1:T(8,128)(2,1)}, bf16[512,512]{0,1:T(8,128)(2,1)}, u32[]{:S(2)}, u32[]{:S(2)}) collective-permute-start(bf16[512,512]{0,1:T(8,128)(2,1)} %collective-permute-done.25), channel_id=1, source_target_pairs={{0,1},{1,0},{2,3},{3,2},{4,5},{5,4},{6,7},{7,6},{8,9},{9,8},{10,11... | collective-permute-start | bytes 1572872 | tf_op jit(solution)/shard_map/ppermute | solution.py:24
  185.8 125.6 %collective-permute-start.16 = (bf16[1024,512]{1,0:T(8,128)(2,1)}, bf16[1024,512]{1,0:T(8,128)(2,1)}, u32[]{:S(2)}, u32[]{:S(2)}) collective-permute-start(bf16[1024,512]{1,0:T(8,128)(2,1)} %get-tuple-element.121), channel_id=1, source_target_pairs={{0,16},{16,0},{1,17},{17,1},{2,18},{18,2},{3,19},{19,3},{4,20},{20... | collective-permute-start | bytes 3145736 | tf_op jit(solution)/shard_map/ppermute | solution.py:24
  219.5 215.2 %collective-permute-start.19 = (bf16[1024,2048]{1,0:T(8,128)(2,1)}, bf16[1024,2048]{1,0:T(8,128)(2,1)}, u32[]{:S(2)}, u32[]{:S(2)}) collective-permute-start(bf16[1024,2048]{1,0:T(8,128)(2,1)} %param.23), channel_id=1, source_target_pairs={{0,16},{16,0},{1,17},{17,1},{2,18},{18,2},{3,19},{19,3},{4,20},{20... | collective-permute-start | bytes 12582920 | tf_op jit(solution)/shard_map/ppermute | solution.py:24
  220.2 36.6 %collective-permute-start.41 = (bf16[512,512]{0,1:T(8,128)(2,1)}, bf16[512,512]{0,1:T(8,128)(2,1)S(1)}, u32[]{:S(2)}, u32[]{:S(2)}) collective-permute-start(bf16[512,512]{0,1:T(8,128)(2,1)} %collective-permute-done.40), channel_id=1, source_target_pairs={{0,1},{1,0},{2,3},{3,2},{4,5},{5,4},{6,7},{7,6},{8,9},{9,8},{10,11... | collective-permute-start | bytes 1572872 | tf_op jit(solution)/shard_map/ppermute | solution.py:24
  220.9 24.8 %collective-permute-start.9 = (bf16[512,1024]{0,1:T(8,128)(2,1)S(1)}, bf16[512,1024]{0,1:T(8,128)(2,1)S(1)}, u32[]{:S(2)}, u32[]{:S(2)}) collective-permute-start(bf16[512,1024]{0,1:T(8,128)(2,1)S(1)} %add_convert_fusion.1), channel_id=1, source_target_pairs={{0,2},{1,3},{2,0},{3,1},{4,6},{5,7},{6,4},{7,5},{8,10},{9,11},{10,... | collective-permute-start | bytes 3145736 | tf_op jit(solution)/shard_map/ppermute | solution.py:24
  246.0 15.0 %collective-permute-start.10 = (bf16[512,1024]{0,1:T(8,128)(2,1)S(1)}, bf16[512,1024]{0,1:T(8,128)(2,1)S(1)}, u32[]{:S(2)}, u32[]{:S(2)}) collective-permute-start(bf16[512,1024]{0,1:T(8,128)(2,1)S(1)} %add_convert_fusion), channel_id=1, source_target_pairs={{0,1},{1,0},{2,3},{3,2},{4,5},{5,4},{6,7},{7,6},{8,9},{9,8},{10,11... | collective-permute-start | bytes 3145736 | tf_op jit(solution)/shard_map/ppermute | solution.py:24
  256.7 97.6 %collective-permute-start.17 = (bf16[1024,512]{1,0:T(8,128)(2,1)}, bf16[1024,512]{1,0:T(8,128)(2,1)}, u32[]{:S(2)}, u32[]{:S(2)}) collective-permute-start(bf16[1024,512]{1,0:T(8,128)(2,1)} %get-tuple-element.114), channel_id=1, source_target_pairs={{0,16},{16,0},{1,17},{17,1},{2,18},{18,2},{3,19},{19,3},{4,20},{20... | collective-permute-start | bytes 3145736 | tf_op jit(solution)/shard_map/ppermute | solution.py:24
  260.9 115.9 %collective-permute-start.18 = (bf16[1024,512]{1,0:T(8,128)(2,1)}, bf16[1024,512]{1,0:T(8,128)(2,1)}, u32[]{:S(2)}, u32[]{:S(2)}) collective-permute-start(bf16[1024,512]{1,0:T(8,128)(2,1)} %get-tuple-element.118), channel_id=1, source_target_pairs={{0,16},{16,0},{1,17},{17,1},{2,18},{18,2},{3,19},{19,3},{4,20},{20... | collective-permute-start | bytes 3145736 | tf_op jit(solution)/shard_map/ppermute | solution.py:24
  308.0 80.0 %collective-permute-start.27 = (bf16[512,512]{1,0:T(8,128)(2,1)}, bf16[512,512]{1,0:T(8,128)(2,1)S(1)}, u32[]{:S(2)}, u32[]{:S(2)}) collective-permute-start(bf16[512,512]{1,0:T(8,128)(2,1)} %slice.450), channel_id=1, source_target_pairs={{0,16},{16,0},{1,17},{17,1},{2,18},{18,2},{3,19},{19,3},{4,20},{20... | collective-permute-start | bytes 1572872 | tf_op jit(solution)/shard_map/ppermute | solution.py:24
  311.4 87.8 %collective-permute-start.28 = (bf16[512,512]{1,0:T(8,128)(2,1)}, bf16[512,512]{1,0:T(8,128)(2,1)S(1)}, u32[]{:S(2)}, u32[]{:S(2)}) collective-permute-start(bf16[512,512]{1,0:T(8,128)(2,1)} %slice.449), channel_id=1, source_target_pairs={{0,16},{16,0},{1,17},{17,1},{2,18},{18,2},{3,19},{19,3},{4,20},{20... | collective-permute-start | bytes 1572872 | tf_op jit(solution)/shard_map/ppermute | solution.py:24
  354.4 56.1 %collective-permute-start.29 = (bf16[512,512]{1,0:T(8,128)(2,1)}, bf16[512,512]{1,0:T(8,128)(2,1)S(1)}, u32[]{:S(2)}, u32[]{:S(2)}) collective-permute-start(bf16[512,512]{1,0:T(8,128)(2,1)} %slice.448), channel_id=1, source_target_pairs={{0,16},{16,0},{1,17},{17,1},{2,18},{18,2},{3,19},{19,3},{4,20},{20... | collective-permute-start | bytes 1572872 | tf_op jit(solution)/shard_map/ppermute | solution.py:24
  376.8 44.4 %collective-permute-start.30 = (bf16[512,512]{1,0:T(8,128)(2,1)S(1)}, bf16[512,512]{1,0:T(8,128)(2,1)S(1)}, u32[]{:S(2)}, u32[]{:S(2)}) collective-permute-start(bf16[512,512]{1,0:T(8,128)(2,1)S(1)} %copy-done.76), channel_id=1, source_target_pairs={{0,16},{16,0},{1,17},{17,1},{2,18},{18,2},{3,19},{19,3},{4,20},{20... | collective-permute-start | bytes 1572872 | tf_op jit(solution)/shard_map/ppermute | solution.py:24
  442.4 24.5 %collective-permute-start.22 = (bf16[512,512]{0,1:T(8,128)(2,1)}, bf16[512,512]{0,1:T(8,128)(2,1)}, u32[]{:S(2)}, u32[]{:S(2)}) collective-permute-start(bf16[512,512]{0,1:T(8,128)(2,1)} %get-tuple-element.107), channel_id=1, source_target_pairs={{0,3},{1,2},{2,1},{3,0},{4,7},{5,6},{6,5},{7,4},{8,11},{9,10},{10,... | collective-permute-start | bytes 1572872 | tf_op jit(solution)/shard_map/ppermute | solution.py:24
  442.5 26.2 %collective-permute-start.21 = (bf16[512,512]{0,1:T(8,128)(2,1)}, bf16[512,512]{0,1:T(8,128)(2,1)}, u32[]{:S(2)}, u32[]{:S(2)}) collective-permute-start(bf16[512,512]{0,1:T(8,128)(2,1)} %get-tuple-element.106), channel_id=1, source_target_pairs={{0,2},{1,3},{2,0},{3,1},{4,6},{5,7},{6,4},{7,5},{8,10},{9,11},{10,... | collective-permute-start | bytes 1572872 | tf_op jit(solution)/shard_map/ppermute | solution.py:24
  443.8 25.1 %collective-permute-start.20 = (bf16[512,512]{0,1:T(8,128)(2,1)S(1)}, bf16[512,512]{0,1:T(8,128)(2,1)}, u32[]{:S(2)}, u32[]{:S(2)}) collective-permute-start(bf16[512,512]{0,1:T(8,128)(2,1)S(1)} %get-tuple-element.105), channel_id=1, source_target_pairs={{0,1},{1,0},{2,3},{3,2},{4,5},{5,4},{6,7},{7,6},{8,9},{9,8},{10,11... | collective-permute-start | bytes 1572872 | tf_op jit(solution)/shard_map/ppermute | solution.py:24
  444.3 20.5 %collective-permute-start.45 = (bf16[512,512]{0,1:T(8,128)(2,1)}, bf16[512,512]{0,1:T(8,128)(2,1)}, u32[]{:S(2)}, u32[]{:S(2)}) collective-permute-start(bf16[512,512]{0,1:T(8,128)(2,1)} %constant_dynamic-slice_fusion), channel_id=1, source_target_pairs={{0,16},{16,0},{1,17},{17,1},{2,18},{18,2},{3,19},{19,3},{4,20},{20... | collective-permute-start | bytes 1572872 | tf_op jit(solution)/shard_map/ppermute | solution.py:24
  464.9 7.2 collective-permute-start.46
  467.0 323.3 %collective-permute-start.33 = (bf16[512,2048]{0,1:T(8,128)(2,1)}, bf16[512,2048]{0,1:T(8,128)(2,1)}, u32[]{:S(2)}, u32[]{:S(2)}) collective-permute-start(bf16[512,2048]{0,1:T(8,128)(2,1)} %fusion.2), channel_id=1, source_target_pairs={{0,3},{1,2},{2,1},{3,0},{4,7},{5,6},{6,5},{7,4},{8,11},{9,10},{10,... | collective-permute-start | bytes 6291464 | tf_op jit(solution)/shard_map/ppermute | solution.py:24
  467.0 323.3 %collective-permute-start.32 = (bf16[512,2048]{0,1:T(8,128)(2,1)}, bf16[512,2048]{0,1:T(8,128)(2,1)}, u32[]{:S(2)}, u32[]{:S(2)}) collective-permute-start(bf16[512,2048]{0,1:T(8,128)(2,1)} %fusion.2), channel_id=1, source_target_pairs={{0,2},{1,3},{2,0},{3,1},{4,6},{5,7},{6,4},{7,5},{8,10},{9,11},{10,... | collective-permute-start | bytes 6291464 | tf_op jit(solution)/shard_map/ppermute | solution.py:24
  468.7 321.6 %collective-permute-start.31 = (bf16[512,2048]{0,1:T(8,128)(2,1)}, bf16[512,2048]{0,1:T(8,128)(2,1)}, u32[]{:S(2)}, u32[]{:S(2)}) collective-permute-start(bf16[512,2048]{0,1:T(8,128)(2,1)} %fusion.2), channel_id=1, source_target_pairs={{0,1},{1,0},{2,3},{3,2},{4,5},{5,4},{6,7},{7,6},{8,9},{9,8},{10,11... | collective-permute-start | bytes 6291464 | tf_op jit(solution)/shard_map/ppermute | solution.py:24
  476.2 314.1 %copy-start.3 = (bf16[512,512]{0,1:T(8,128)(2,1)S(1)}, bf16[512,512]{0,1:T(8,128)(2,1)}, u32[]{:S(2)}) copy-start(bf16[512,512]{0,1:T(8,128)(2,1)} %copy-done.2) | copy-start | bytes 1572868
  476.2 314.1 %copy-start.5 = (bf16[512,512]{0,1:T(8,128)(2,1)S(1)}, bf16[512,512]{0,1:T(8,128)(2,1)}, u32[]{:S(2)}) copy-start(bf16[512,512]{0,1:T(8,128)(2,1)} %copy-done.4) | copy-start | bytes 1572868
  476.2 314.1 %copy-start.7 = (bf16[512,512]{0,1:T(8,128)(2,1)S(1)}, bf16[512,512]{0,1:T(8,128)(2,1)}, u32[]{:S(2)}) copy-start(bf16[512,512]{0,1:T(8,128)(2,1)} %copy-done.6) | copy-start | bytes 1572868
  476.2 314.1 %copy-start.9 = (bf16[512,512]{0,1:T(8,128)(2,1)S(1)}, bf16[512,512]{0,1:T(8,128)(2,1)}, u32[]{:S(2)}) copy-start(bf16[512,512]{0,1:T(8,128)(2,1)} %copy-done.8) | copy-start | bytes 1572868
  476.2 314.1 %copy-start.11 = (bf16[512,1024]{0,1:T(8,128)(2,1)S(1)}, bf16[512,1024]{0,1:T(8,128)(2,1)}, u32[]{:S(2)}) copy-start(bf16[512,1024]{0,1:T(8,128)(2,1)} %copy-done.10) | copy-start | bytes 3145732
  476.2 314.1 %copy-start.13 = (bf16[512,1024]{0,1:T(8,128)(2,1)S(1)}, bf16[512,1024]{0,1:T(8,128)(2,1)}, u32[]{:S(2)}) copy-start(bf16[512,1024]{0,1:T(8,128)(2,1)} %copy-done.12) | copy-start | bytes 3145732
  476.2 314.1 %copy-start.81 = (f32[1,2048]{1,0:T(1,128)S(1)}, f32[1,2048]{1,0:T(1,128)}, u32[]{:S(2)}) copy-start(f32[1,2048]{1,0:T(1,128)} %copy-done.80) | copy-start | bytes 24580
  476.2 314.1 %copy-start.87 = (f32[512]{0:T(512)S(1)}, f32[512]{0:T(512)}, u32[]{:S(2)}) copy-start(f32[512]{0:T(512)} %copy-done.86) | copy-start | bytes 6148
  816.1 5.5 collective-permute-start.34
  817.8 13.1 %collective-permute-start.38 = (bf16[512,512]{0,1:T(8,128)(2,1)S(1)}, bf16[512,512]{0,1:T(8,128)(2,1)S(1)}, u32[]{:S(2)}, u32[]{:S(2)}) collective-permute-start(bf16[512,512]{0,1:T(8,128)(2,1)S(1)} %constant_dynamic-slice_fusion.2), channel_id=1, source_target_pairs={{0,16},{16,0},{1,17},{17,1},{2,18},{18,2},{3,19},{19,3},{4,20},{20... | collective-permute-start | bytes 1572872 | tf_op jit(solution)/shard_map/ppermute | solution.py:24
  829.0 48.1 %collective-permute-start.37 = (bf16[512,2048]{0,1:T(8,128)(2,1)}, bf16[512,2048]{0,1:T(8,128)(2,1)S(1)}, u32[]{:S(2)}, u32[]{:S(2)}) collective-permute-start(bf16[512,2048]{0,1:T(8,128)(2,1)} %fusion.1), channel_id=1, source_target_pairs={{0,3},{1,2},{2,1},{3,0},{4,7},{5,6},{6,5},{7,4},{8,11},{9,10},{10,... | collective-permute-start | bytes 6291464 | tf_op jit(solution)/shard_map/ppermute | solution.py:24
  829.0 92.4 %collective-permute-start.36 = (bf16[512,2048]{0,1:T(8,128)(2,1)}, bf16[512,2048]{0,1:T(8,128)(2,1)S(1)}, u32[]{:S(2)}, u32[]{:S(2)}) collective-permute-start(bf16[512,2048]{0,1:T(8,128)(2,1)} %fusion.1), channel_id=1, source_target_pairs={{0,2},{1,3},{2,0},{3,1},{4,6},{5,7},{6,4},{7,5},{8,10},{9,11},{10,... | collective-permute-start | bytes 6291464 | tf_op jit(solution)/shard_map/ppermute | solution.py:24
  830.1 91.3 %collective-permute-start.35 = (bf16[512,2048]{0,1:T(8,128)(2,1)}, bf16[512,2048]{0,1:T(8,128)(2,1)}, u32[]{:S(2)}, u32[]{:S(2)}) collective-permute-start(bf16[512,2048]{0,1:T(8,128)(2,1)} %fusion.1), channel_id=1, source_target_pairs={{0,1},{1,0},{2,3},{3,2},{4,5},{5,4},{6,7},{7,6},{8,9},{9,8},{10,11... | collective-permute-start | bytes 6291464 | tf_op jit(solution)/shard_map/ppermute | solution.py:24
  830.9 13.6 %collective-permute-start.39 = (bf16[512,512]{0,1:T(8,128)(2,1)S(1)}, bf16[512,512]{0,1:T(8,128)(2,1)S(1)}, u32[]{:S(2)}, u32[]{:S(2)}) collective-permute-start(bf16[512,512]{0,1:T(8,128)(2,1)S(1)} %collective-permute-done.38), channel_id=1, source_target_pairs={{0,1},{1,0},{2,3},{3,2},{4,5},{5,4},{6,7},{7,6},{8,9},{9,8},{10,11... | collective-permute-start | bytes 1572872 | tf_op jit(solution)/shard_map/ppermute | solution.py:24
  932.2 165.3 %all-to-all-start.2 = ((bf16[4,128,1024]{2,1,0:T(8,128)(2,1)}), bf16[4,128,1024]{2,1,0:T(8,128)(2,1)S(1)}, u32[]{:S(2)}, u32[]{:S(2)}) async-start(bf16[4,128,1024]{2,1,0:T(8,128)(2,1)} %gather_fusion.4), calls=%async_computation.2 | async-start | bytes 2097152 | tf_op jit(solution)/shard_map/all_to_all | solution.py:443
  935.9 136.8 %collective-permute-start.42 = (f32[5,512]{1,0:T(8,128)S(1)}, f32[5,512]{1,0:T(8,128)S(1)}, u32[]{:S(2)}, u32[]{:S(2)}) collective-permute-start(f32[5,512]{1,0:T(8,128)S(1)} %concatenate.94), channel_id=1, source_target_pairs={{0,16},{16,0},{1,17},{17,1},{2,18},{18,2},{3,19},{19,3},{4,20},{20... | collective-permute-start | bytes 30728 | tf_op jit(solution)/shard_map/ppermute | solution.py:24
  1072.7 5.5 collective-permute-start.43
  1078.3 18.1 %collective-permute-start.44 = (f32[5,512]{1,0:T(8,128)S(1)}, f32[5,512]{1,0:T(8,128)S(1)}, u32[]{:S(2)}, u32[]{:S(2)}) collective-permute-start(f32[5,512]{1,0:T(8,128)S(1)} %add.379), channel_id=1, source_target_pairs={{0,8},{4,12},{8,0},{12,4},{1,9},{5,13},{9,1},{13,5},{2,10},{6,14},... | collective-permute-start | bytes 30728 | tf_op jit(solution)/shard_map/ppermute | solution.py:24
  (102 other events, 1963.7 us)
Sparse Core Ops, SparseCore 0:
  31.1 61.7 all-gather.5
  94.5 33.0 all-gather.7
  129.2 26.5 all-gather.11
  157.3 27.4 all-gather.9
  186.6 28.9 all-gather.13

commit v3 on v2

--- a/solution.py
+++ b/solution.py
@@ -34,6 +34,10 @@
 
 def contract_cols(left, right):
     return lax.dot_general(left, right, (((1,), (1,)), ((), ())), preferred_element_type=WIDE)
+
+
+def added(terms):
+    return sum(term.astype(WIDE) for term in terms)
 
 
 def norm_back(grad_out, normed, scale_row, gain):
@@ -56,7 +60,7 @@
     total = (half.astype(WIDE) + from_middle.astype(WIDE)).astype(LOW)
     handed = lax.ppermute(total, "ctx", [(1, 0), (2, 3)])
     inner = jnp.logical_or(rank == 1, rank == 2)
-    return jnp.where(inner, total, handed).astype(WIDE)
+    return jnp.where(inner, total, handed)
 
 
 PIECE = 256
@@ -65,10 +69,13 @@
 MESH = pl.DeviceIdType.MESH
 
 
-def line_kernel(
-    pieces, left_of, left_ref, right_ref, out_ref, peer, outer_part, middle_part, held,
-    peer_send, peer_recv, in_send, outer_recv, middle_recv, out_send, out_recv, own_done,
-):
+def line_kernel(pieces, left_of, swap, *refs):
+    if swap:
+        (left_ref, right_ref, more_ref, out_ref, more_peer), refs = refs[:5], refs[5:]
+    else:
+        (left_ref, right_ref, out_ref), refs = refs[:3], refs[3:]
+    peer, outer_part, middle_part, held, peer_send, peer_recv, in_send, outer_recv, middle_recv = refs[:9]
+    out_send, out_recv, own_done, more_send, more_recv = refs[9:]
     shard = lax.axis_index("shard")
     ctx = lax.axis_index("ctx")
     tokens = right_ref.shape[0]
@@ -140,6 +147,20 @@
             outer_part.at[index], out_ref.at[:, columns(index)], own_done.at[index]
         )
 
+    strips = min(16, pieces)
+
+    def more_copy(index):
+        size = more_ref.shape[0] // strips
+        lines = pl.ds(pl.multiple_of(index * size, size), size)
+        return pltpu.make_async_remote_copy(
+            src_ref=more_ref.at[lines],
+            dst_ref=more_peer.at[lines],
+            send_sem=more_send.at[index],
+            recv_sem=more_recv.at[index],
+            device_id={"shard": 1 - shard},
+            device_id_type=MESH,
+        )
+
     tile = min(256, rows)
 
     def product(index, start):
@@ -176,6 +197,12 @@
         def _():
             peer_copy(index + AHEAD).start()
 
+        if swap:
+
+            @pl.when(index < strips)
+            def _():
+                more_copy(index).start()
+
         @pl.when(index >= SLOTS)
         def _():
             end_copy(index - SLOTS).wait_send()
@@ -211,6 +238,12 @@
     def _():
         finish(pieces - 1)
 
+    if swap:
+
+        @pl.loop(0, strips)
+        def _(index):
+            more_copy(index).wait()
+
     @pl.loop(0, pieces)
     def _(index):
         peer_copy(index).wait_send()
@@ -229,7 +262,7 @@
             out_copy(index).wait_recv()
 
 
-def line_grads(lefts, rights, identity):
+def line_grads(lefts, rights, identity, more=None):
     left = jnp.stack([value.T for value in lefts])
     right = jnp.concatenate(rights, axis=1)
     tokens, width = right.shape
@@ -242,23 +275,517 @@
 
     flops = 4 * tokens * rows * width
     dma = pltpu.SemaphoreType.DMA
+    swap = more is not None
+    extra = [more] if swap else []
+    out_shape = [jax.ShapeDtypeStruct((rows, width), LOW)]
+    out_shape += [jax.ShapeDtypeStruct(value.shape, LOW) for value in extra]
     return pl.pallas_call(
-        functools.partial(line_kernel, pieces, left_of),
-        out_shape=jax.ShapeDtypeStruct((rows, width), LOW),
-        in_specs=[pl.BlockSpec(memory_space=pltpu.VMEM)] * 2,
-        out_specs=pl.BlockSpec(memory_space=pl.ANY),
+        functools.partial(line_kernel, pieces, left_of, swap),
+        out_shape=out_shape,
+        in_specs=[pl.BlockSpec(memory_space=pltpu.VMEM)] * 2
+        + [pl.BlockSpec(memory_space=pl.ANY) for _ in extra],
+        out_specs=[pl.BlockSpec(memory_space=pl.ANY) for _ in out_shape],
         scratch_shapes=[
             pltpu.VMEM((pieces, tokens, PIECE), LOW),
             pltpu.VMEM((pieces, rows, PIECE), LOW),
             pltpu.VMEM((pieces, rows, PIECE), LOW),
             pltpu.VMEM((SLOTS, rows, PIECE), LOW),
         ]
-        + [dma((pieces,)) for _ in range(8)],
+        + [dma((pieces,)) for _ in range(10)],
         compiler_params=pltpu.CompilerParams(
             collective_id=identity, has_side_effects=True, vmem_limit_bytes=56 * 1024 * 1024
         ),
         cost_estimate=pl.CostEstimate(flops=flops * 8, bytes_accessed=rows * width * 64, transcendentals=0),
-    )(left, right)
+    )(left, right, *extra)
+
+
+def front_kernel(
+    x_blocks, cot_blocks, place, gains, first_mask, second_mask, taps,
+    in_w, out_w, gate_w, up_w, down_w,
+    in_peer, out_peer, gate_peer, up_peer,
+    x_full, h_one, proj, mixed, conv_out, gated, mixer, h_two, cot_full, cot_peer, h_two_peer, h_one_peer, acts, dh_two,
+    x_got, cot_got, out_v, rim, extended, away, pair, pair_got, both_got,
+    da_own, da_send, da_got, gu_v, down_v, dh_sum, ffn_v,
+    send, recv, local,
+):
+    shard = lax.axis_index("shard")
+    ctx = lax.axis_index("ctx")
+    tp = lax.axis_index("tp")
+    core, outer = tp % 2, tp // 2
+    core_mate = tp + 1 - 2 * core
+    outer_mate = lax.rem(tp + 2, 4)
+    ctx_mate = ctx + 1 - 2 * (ctx % 2)
+    tokens, width = x_full.shape
+    part = width // 4
+    half = width // 2
+    blocks, block_rows = x_blocks.shape[0], x_blocks.shape[1]
+    rows = out_w.shape[0]
+    own_rows = pl.ds(pl.multiple_of((ctx % 2) * (rows // 2), rows // 2), rows // 2)
+    other_rows = pl.ds(pl.multiple_of((1 - ctx % 2) * (rows // 2), rows // 2), rows // 2)
+    hidden = gate_w.shape[1]
+    chunk = hidden // CHUNKS
+
+    barrier = pltpu.get_barrier_semaphore()
+    mates = [{"shard": 1 - shard}, {"tp": core_mate}, {"tp": outer_mate}]
+    mates += [{"ctx": lax.rem(ctx + step, blocks)} for step in range(1, blocks)]
+    for mate in mates:
+        pl.semaphore_signal(barrier, inc=1, device_id=mate, device_id_type=MESH)
+    pl.semaphore_wait(barrier, len(mates))
+
+    names = {}
+
+    def remote(name, src, dst, mate):
+        place_of = names.setdefault(name, len(names))
+        return pltpu.make_async_remote_copy(
+            src_ref=src, dst_ref=dst, send_sem=send.at[place_of], recv_sem=recv.at[place_of],
+            device_id=mate, device_id_type=MESH,
+        )
+
+    def columns(start, size):
+        return pl.ds(pl.multiple_of(start * size, size), size)
+
+    own_part = columns(tp, part)
+    own_half, peer_half = columns(shard, half), columns(1 - shard, half)
+
+    def deal(name, source, target, step):
+        to, origin = lax.rem(ctx + step, blocks), lax.rem(ctx + blocks - step, blocks)
+        out = remote(name + str(step), source.at[to], target.at[ctx], {"ctx": to})
+        into = remote(name + str(step), source.at[to], target.at[origin], {"ctx": to})
+        return out, into
+
+    def gather(name, full):
+        mate = columns(outer_mate, part)
+        return (
+            remote(name + "outer", full.at[:, own_part], full.at[:, own_part], {"tp": outer_mate}),
+            remote(name + "core", full.at[:, own_part], full.at[:, own_part], {"tp": core_mate}),
+            remote(name + "more", full.at[:, mate], full.at[:, mate], {"tp": core_mate}),
+        )
+
+    pieces = {}
+    for index, name in enumerate("bvc"):
+        column = (0, 2, 1)[index]
+        pieces[name] = (in_w.at[column], in_peer.at[column])
+    pieces["o"] = (out_w, out_peer)
+    for index in range(CHUNKS):
+        strip = pl.ds(index * chunk, chunk)
+        pieces["g%d" % index] = (gate_w.at[:, strip], gate_peer.at[:, strip])
+        pieces["u%d" % index] = (up_w.at[:, strip], up_peer.at[:, strip])
+
+    def over_shard(name):
+        source, target = pieces[name]
+        return remote(name + "x", source.at[own_rows], target.at[own_rows], {"shard": 1 - shard})
+
+    def over_ctx(name):
+        target = pieces[name][1]
+        return remote(name + "z", target.at[own_rows], target.at[own_rows], {"ctx": ctx_mate})
+
+    def pump(name):
+        over_shard(name).wait_recv()
+        over_ctx(name).start()
+
+    def load(index, source, target):
+        return pltpu.make_async_copy(source, target, local.at[index])
+
+    x_deals = [deal("x", x_blocks, x_got, step) for step in range(1, blocks)]
+    cot_deals = [deal("cot", cot_blocks, cot_got, step) for step in range(1, blocks)]
+    for out, _ in x_deals:
+        out.start()
+    for name in ("b", "v"):
+        over_shard(name).start()
+    own_loads = [load(index, in_w.at[index], gu_v.at[1, 0, index]) for index in range(3)]
+    own_loads.append(load(3, out_w, out_v.at[0]))
+    own_loads.append(load(4, down_w, down_v))
+    for copy in own_loads:
+        copy.start()
+
+    def packed(source, got, deals, full):
+        got[ctx] = source[ctx]
+        for _, into in deals:
+            into.wait_recv()
+        for index in range(blocks):
+            total = place[index, 0] * got[0].astype(WIDE)
+            for other in range(1, blocks):
+                total = total + place[index, other] * got[other].astype(WIDE)
+            full[index * block_rows : (index + 1) * block_rows, own_part] = total.astype(LOW)
+
+    pump("b")
+    over_shard("c").start()
+    packed(x_blocks, x_got, x_deals, x_full)
+    x_outer, x_core, x_more = gather("xg", x_full)
+    x_outer.start()
+    x_core.start()
+    for out, _ in cot_deals:
+        out.start()
+    pump("v")
+    over_shard("o").start()
+    x_outer.wait_recv()
+    x_more.start()
+    packed(cot_blocks, cot_got, cot_deals, cot_full)
+    cot_outer, cot_core, cot_more = gather("cg", cot_full)
+    cot_outer.start()
+    cot_core.start()
+    x_core.wait_recv()
+    x_more.wait_recv()
+
+    step = min(64, tokens)
+
+    @pl.loop(0, tokens // step)
+    def _(index):
+        lines = pl.ds(pl.multiple_of(index * step, step), step)
+        value = x_full[lines].astype(WIDE)
+        scale = lax.rsqrt(jnp.mean(value * value, axis=1, keepdims=True) + EPS)
+        h_one[lines] = (value * scale * gains[0:1]).astype(LOW)
+
+    pump("c")
+    over_shard("g0").start()
+
+    def columns_out(name, full, got):
+        strip = pl.ds(pl.multiple_of((1 - shard) * half + core * part, part), part)
+        target = columns(core, part)
+        first = remote(name + "x", full.at[:, strip], got.at[:, target], {"shard": 1 - shard})
+        second = remote(name + "core", got.at[:, target], got.at[:, target], {"tp": core_mate})
+        return first, second
+
+    cot_first, cot_second = columns_out("cc", cot_full, cot_peer)
+
+    tile = min(256, tokens)
+
+    def over_tiles(body):
+        @pl.loop(0, tokens // tile)
+        def _(index):
+            body(pl.ds(pl.multiple_of(index * tile, tile), tile))
+
+    def project(column, name):
+        target = load(column, in_peer.at[column], gu_v.at[1, 1, column])
+        own_loads[column].wait()
+        over_ctx(name).wait_recv()
+        target.start()
+        target.wait()
+
+        def body(lines):
+            proj[column, lines] = jnp.dot(
+                h_one[lines, own_half], gu_v[1, 0, column], preferred_element_type=WIDE
+            ) + jnp.dot(h_one[lines, peer_half], gu_v[1, 1, column], preferred_element_type=WIDE)
+
+        over_tiles(body)
+
+    project(0, "b")
+    project(2, "v")
+    edge = 16
+    rim_copy = remote(
+        "rim", mixed.at[pl.ds(tokens - edge, edge)], rim, {"ctx": lax.rem(ctx + 1, blocks)}
+    )
+
+    def mix(lines):
+        value = (proj[0, lines] * proj[2, lines]).astype(LOW)
+        mixed[lines] = value
+        extended[pl.ds(lines.start + 8, tile)] = value.astype(WIDE)
+
+    over_tiles(mix)
+
+    @pl.when(ctx < blocks - 1)
+    def _():
+        rim_copy.start()
+
+    pump("o")
+    over_shard("u0").start()
+    cot_outer.wait_recv()
+    cot_more.start()
+    project(1, "c")
+
+    @pl.when(ctx > 0)
+    def _():
+        rim_copy.wait_recv()
+        extended[0:8] = rim[8:16].astype(WIDE)
+
+    @pl.when(ctx == 0)
+    def _():
+        extended[0:8] = jnp.zeros((8, part), WIDE)
+
+    for start in range(0, tokens, tile):
+        lines = pl.ds(start, tile)
+        value = taps[0:1] * extended[pl.ds(start + 8, tile)]
+        value = value + taps[1:2] * (extended[pl.ds(start + 7, tile)] * first_mask[lines])
+        value = value + taps[2:3] * (extended[pl.ds(start + 6, tile)] * second_mask[lines])
+        conv_out[lines] = value
+        gated[lines] = (proj[1, lines] * value).astype(LOW)
+
+    pump("g0")
+    cot_core.wait_recv()
+    cot_more.wait_recv()
+    cot_first.start()
+    out_load = load(3, out_peer, out_v.at[1])
+    own_loads[3].wait()
+    over_ctx("o").wait_recv()
+    out_load.start()
+    out_load.wait()
+
+    def to_half(lines, which):
+        return lax.dot_general(
+            gated[lines], out_v[which], (((1,), (1,)), ((), ())), preferred_element_type=WIDE
+        )
+
+    stages = [pl.ds(start, tile) for start in range(0, tokens, tile)]
+    hops = []
+    for index, lines in enumerate(stages):
+        first = remote("ma%d" % index, away.at[lines], pair_got.at[lines], {"tp": core_mate})
+        second = remote("mb%d" % index, pair.at[lines], both_got.at[lines], {"tp": outer_mate})
+        third = remote("mc%d" % index, mixer.at[core, lines], mixer.at[core, lines], {"tp": core_mate})
+        hops.append((first, second, third))
+        away[lines] = to_half(lines, 1 - core).astype(LOW)
+        first.start()
+    for index, lines in enumerate(stages):
+        value = to_half(lines, core)
+        hops[index][0].wait_recv()
+        pair[lines] = (value + pair_got[lines].astype(WIDE)).astype(LOW)
+        hops[index][1].start()
+
+    pump("u0")
+    over_shard("g1").start()
+    cot_first.wait_recv()
+    over_shard("u1").start()
+    cot_second.start()
+    cot_second.wait_recv()
+    own_loads[4].wait()
+
+    def da_copy(index):
+        strip = pl.ds(index * chunk, chunk)
+        return remote("da%d" % index, da_send.at[:, strip], da_got.at[:, strip], {"shard": 1 - shard})
+
+    for index in range(CHUNKS):
+        strip = pl.ds(index * chunk, chunk)
+
+        def send_part(lines):
+            da_send[lines, strip] = jnp.dot(
+                cot_peer[lines], down_v[:, strip], preferred_element_type=WIDE
+            ).astype(LOW)
+
+        over_tiles(send_part)
+    pump("g1")
+    da_copy(0).start()
+
+    def own_part_of(lines):
+        for index in range(CHUNKS):
+            strip = pl.ds(index * chunk, chunk)
+            da_own[lines, strip] = jnp.dot(
+                cot_full[lines, own_half], down_v[:, strip], preferred_element_type=WIDE
+            ).astype(LOW)
+
+    over_tiles(own_part_of)
+
+    for index, lines in enumerate(stages):
+        hops[index][1].wait_recv()
+        mixer[core, lines] = (pair[lines].astype(WIDE) + both_got[lines].astype(WIDE)).astype(LOW)
+        hops[index][2].start()
+    for index, lines in enumerate(stages):
+        hops[index][2].wait_recv()
+
+    @pl.loop(0, tokens // step)
+    def _(index):
+        lines = pl.ds(pl.multiple_of(index * step, step), step)
+        own = x_full[lines, own_half].astype(WIDE) + mixer[0, lines].astype(WIDE)
+        other = x_full[lines, peer_half].astype(WIDE) + mixer[1, lines].astype(WIDE)
+        total = jnp.sum(own * own, axis=1, keepdims=True) + jnp.sum(other * other, axis=1, keepdims=True)
+        scale = lax.rsqrt(total / width + EPS)
+        h_two[lines, own_half] = (own * scale * gains[1:2, own_half]).astype(LOW)
+        h_two[lines, peer_half] = (other * scale * gains[1:2, peer_half]).astype(LOW)
+
+    h_two_first, h_two_second = columns_out("hc", h_two, h_two_peer)
+    h_one_first, h_one_second = columns_out("ic", h_one, h_one_peer)
+    pump("u1")
+    da_copy(1).start()
+    later = {0: [over_shard("g2")], 1: [over_shard("u2")], 2: [over_shard("u3")], 3: [h_one_first]}
+
+    def own_weights(index):
+        strip = pl.ds(index * chunk, chunk)
+        slot = index % 2
+        return [
+            load(5 + 4 * slot, gate_w.at[:, strip], gu_v.at[slot, 0, 0]),
+            load(6 + 4 * slot, up_w.at[:, strip], gu_v.at[slot, 0, 1]),
+        ]
+
+    def peer_weights(index):
+        strip = pl.ds(index * chunk, chunk)
+        slot = index % 2
+        return [
+            load(7 + 4 * slot, gate_peer.at[:, strip], gu_v.at[slot, 1, 0]),
+            load(8 + 4 * slot, up_peer.at[:, strip], gu_v.at[slot, 1, 1]),
+        ]
+
+    def results(index):
+        slot = index % 2
+        return [
+            load(13 + 3 * slot + kind, ffn_v.at[slot, kind], acts.at[:, pl.ds(kind * hidden + index * chunk, chunk)])
+            for kind in range(3)
+        ]
+
+    for copy in own_weights(0):
+        copy.start()
+    for index in range(CHUNKS):
+        slot = index % 2
+        over_ctx("g%d" % index).wait_recv()
+        over_ctx("u%d" % index).wait_recv()
+        for copy in peer_weights(index):
+            copy.start()
+        if index + 1 < CHUNKS:
+            for copy in own_weights(index + 1):
+                copy.start()
+        da_copy(index).wait_recv()
+        for copy in later[index]:
+            copy.start()
+        for copy in own_weights(index) + peer_weights(index):
+            copy.wait()
+        if index > 1:
+            for copy in results(index - 2):
+                copy.wait()
+        strip = pl.ds(index * chunk, chunk)
+
+        def feed(lines):
+            def pre(kind):
+                return jnp.dot(
+                    h_two[lines, own_half], gu_v[slot, 0, kind], preferred_element_type=WIDE
+                ) + jnp.dot(h_two[lines, peer_half], gu_v[slot, 1, kind], preferred_element_type=WIDE)
+
+            gate_pre, up_pre = pre(0), pre(1)
+            d_act = da_own[lines, strip].astype(WIDE) + da_got[lines, strip].astype(WIDE)
+            sigmoid = jax.nn.sigmoid(gate_pre)
+            silu = gate_pre * sigmoid
+            ffn_v[slot, 0, lines] = (silu * up_pre).astype(LOW)
+            ffn_v[slot, 1, lines] = (
+                d_act * up_pre * sigmoid * (1.0 + gate_pre * (1.0 - sigmoid))
+            ).astype(LOW)
+            ffn_v[slot, 2, lines] = (d_act * silu).astype(LOW)
+
+        over_tiles(feed)
+        for copy in results(index):
+            copy.start()
+        if index == 1:
+            pump("g2")
+            da_copy(2).start()
+            pump("u2")
+            over_shard("g3").start()
+        if index == 2:
+            pump("g3")
+            da_copy(3).start()
+            pump("u3")
+            h_two_first.start()
+
+        def back(lines):
+            for place_of in range(2):
+                term = lax.dot_general(
+                    ffn_v[slot, 1, lines], gu_v[slot, place_of, 0],
+                    (((1,), (1,)), ((), ())), preferred_element_type=WIDE,
+                ) + lax.dot_general(
+                    ffn_v[slot, 2, lines], gu_v[slot, place_of, 1],
+                    (((1,), (1,)), ((), ())), preferred_element_type=WIDE,
+                )
+                if index > 0:
+                    term = term + dh_sum[place_of, lines]
+                if index + 1 < CHUNKS:
+                    dh_sum[place_of, lines] = term
+                else:
+                    dh_two[place_of, lines] = term.astype(LOW)
+
+        over_tiles(back)
+
+    h_two_first.wait_recv()
+    h_two_second.start()
+    h_one_first.wait_recv()
+    h_one_second.start()
+    for index in (CHUNKS - 2, CHUNKS - 1):
+        for copy in results(index):
+            copy.wait()
+    h_two_second.wait_recv()
+    h_one_second.wait_recv()
+
+    for out, _ in x_deals + cot_deals:
+        out.wait_send()
+    for copy in (x_outer, x_core, x_more, cot_outer, cot_core, cot_more, cot_first, cot_second,
+                 h_two_first, h_two_second, h_one_first, h_one_second):
+        copy.wait_send()
+    for name in pieces:
+        over_shard(name).wait_send()
+        over_ctx(name).wait_send()
+    for index in range(CHUNKS):
+        da_copy(index).wait_send()
+    for trio in hops:
+        for copy in trio:
+            copy.wait_send()
+
+    @pl.when(ctx < blocks - 1)
+    def _():
+        rim_copy.wait_send()
+
+
+FRONT_COPIES = 64
+
+
+def front(x_blocks, cot_blocks, place, gains, first_mask, second_mask, taps, in_w, out_w, gate_w, up_w, down_w):
+    tokens = x_blocks.shape[0] * x_blocks.shape[1]
+    part = x_blocks.shape[2]
+    width = gains.shape[1]
+    half = width // 2
+    rows, hidden = gate_w.shape
+    chunk = hidden // CHUNKS
+    vmem = pl.BlockSpec(memory_space=pltpu.VMEM)
+    hbm = pl.BlockSpec(memory_space=pl.ANY)
+    shape = jax.ShapeDtypeStruct
+    outs = [
+        (shape(in_w.shape, LOW), hbm),
+        (shape(out_w.shape, LOW), hbm),
+        (shape(gate_w.shape, LOW), hbm),
+        (shape(up_w.shape, LOW), hbm),
+        (shape((tokens, width), LOW), vmem),
+        (shape((tokens, width), LOW), vmem),
+        (shape((3, tokens, part), WIDE), vmem),
+        (shape((tokens, part), LOW), vmem),
+        (shape((tokens, part), WIDE), vmem),
+        (shape((tokens, part), LOW), vmem),
+        (shape((2, tokens, half), LOW), vmem),
+        (shape((tokens, width), LOW), vmem),
+        (shape((tokens, width), LOW), vmem),
+        (shape((tokens, half), LOW), vmem),
+        (shape((tokens, half), LOW), vmem),
+        (shape((tokens, half), LOW), vmem),
+        (shape((tokens, 3 * hidden), LOW), hbm),
+        (shape((2, tokens, half), LOW), vmem),
+    ]
+    low, wide = (lambda *dims: pltpu.VMEM(dims, LOW)), (lambda *dims: pltpu.VMEM(dims, WIDE))
+    scratch = [
+        low(*x_blocks.shape),
+        low(*x_blocks.shape),
+        low(2, rows, part),
+        low(16, part),
+        wide(tokens + 8, part),
+        low(tokens, half),
+        low(tokens, half),
+        low(tokens, half),
+        low(tokens, half),
+        low(tokens, hidden),
+        low(tokens, hidden),
+        low(tokens, hidden),
+        low(2, 2, 3, rows, chunk),
+        low(rows, hidden),
+        wide(2, tokens, half),
+        low(2, 3, tokens, chunk),
+        pltpu.SemaphoreType.DMA((FRONT_COPIES,)),
+        pltpu.SemaphoreType.DMA((FRONT_COPIES,)),
+        pltpu.SemaphoreType.DMA((24,)),
+    ]
+    return pl.pallas_call(
+        front_kernel,
+        out_shape=[value for value, _ in outs],
+        in_specs=[vmem, vmem, pl.BlockSpec(memory_space=pltpu.SMEM), vmem, vmem, vmem, vmem]
+        + [hbm] * 5,
+        out_specs=[spec for _, spec in outs],
+        scratch_shapes=scratch,
+        compiler_params=pltpu.CompilerParams(
+            collective_id=2, has_side_effects=True, vmem_limit_bytes=63 * 1024 * 1024
+        ),
+        cost_estimate=pl.CostEstimate(
+            flops=2 * tokens * width * hidden * 64, bytes_accessed=1 << 29, transcendentals=0
+        ),
+    )(x_blocks, cot_blocks, place, gains, first_mask, second_mask, taps, in_w, out_w, gate_w, up_w, down_w)
 
 
 class Features:
@@ -298,20 +825,17 @@
         away = jnp.where(first, pair[:, 1], pair[:, 0]).astype(LOW)
         return mine + swapped(away, "tp", 2).astype(WIDE)
 
-    def total_direct(self, full):
+    def all_terms(self, full):
         low = full.astype(LOW)
-        total = full
-        for step in (1, 2, 3):
-            total = total + swapped(low, "tp", step).astype(WIDE)
-        return total
-
-    def scatter_direct(self, full):
+        return [low] + [swapped(low, "tp", step) for step in (1, 2, 3)]
+
+    def own_terms(self, full):
         width = full.shape[1] // 4
-        total = lax.dynamic_slice_in_dim(full, self.rank * width, width, 1)
-        for step in (1, 2, 3):
-            block = lax.dynamic_slice_in_dim(full, (self.rank ^ step) * width, width, 1).astype(LOW)
-            total = total + swapped(block, "tp", step).astype(WIDE)
-        return total
+        blocks = [
+            lax.dynamic_slice_in_dim(full, (self.rank ^ step) * width, width, 1).astype(LOW)
+            for step in range(4)
+        ]
+        return blocks[:1] + [swapped(blocks[step], "tp", step) for step in (1, 2, 3)]
 
     def own(self, full, axis):
         width = full.shape[axis] // lax.axis_size("tp")
@@ -326,18 +850,10 @@
         self.tp = tp
         self.paired = self.count == 2
 
-    def weight(self, rows, direct):
+    def weight(self, rows):
         if not self.paired:
             return (lax.all_gather(rows, "shard", axis=0, tiled=True),)
-        parts = []
-        if direct < rows.shape[0]:
-            share = (rows.shape[0] - direct) // lax.axis_size("ctx")
-            part = lax.dynamic_slice_in_dim(rows, direct + self.ctx_rank * share, share, 0)
-            parts.append(lax.all_gather(swapped(part, "shard", 1), "ctx", axis=0, tiled=True))
-        if direct > 0:
-            parts.insert(0, swapped(rows[:direct], "shard", 1))
-        other = parts[0] if len(parts) == 1 else jnp.concatenate(parts, axis=0)
-        return (rows, other)
+        return (rows, swapped(rows, "shard", 1))
 
     def split(self, full):
         if not self.paired:
@@ -355,16 +871,6 @@
         return jnp.concatenate(
             [jnp.where(first, parts[0], parts[1]), jnp.where(first, parts[1], parts[0])], axis=1
         )
-
-    def halves(self, parts):
-        if self.paired:
-            return parts
-        return jnp.split(parts[0], 2, axis=1)
-
-    def joined(self, halves):
-        if self.paired:
-            return self.join(halves)
-        return jnp.concatenate(halves, axis=1)
 
     def columns(self, full):
         if not self.paired:
@@ -445,39 +951,20 @@
         )
         return reorder(got, returning)
 
-    def weight_grads(lefts, rights, identity):
+    def weight_grads(lefts, rights, identity, more=None):
         flat = [value for group in rights for value in group]
         if shards.paired:
-            summed = line_grads([group[0] for group in lefts], flat, identity)
+            got = line_grads([group[0] for group in lefts], flat, identity, more)
             ends = [0]
             for value in flat:
                 ends.append(ends[-1] + value.shape[1])
-            return [summed[:, a:b].astype(WIDE) for a, b in zip(ends, ends[1:])]
+            return [got[0][:, a:b] for a, b in zip(ends, ends[1:])], (more,) + tuple(got[1:])
         flat_lefts = [value for group in lefts for value in group]
-        return [
+        sums = [
             sum_line(contract_rows(left, shards.tokens(right)).astype(LOW), ctx_rank)
             for left, right in zip(flat_lefts, flat)
         ]
-
-    in_flat = in_weight.reshape(weight_rows, -1)
-    in_w = shards.weight(in_flat, weight_rows // 4)
-    x_packed = to_packed(hidden_in)
-    gains = tp.gather(jnp.stack([norm1_gain, norm2_gain])).astype(WIDE)
-    gain_one, gain_two = gains[0], gains[1]
-    x_full = tp.gather(x_packed)
-    out_w = shards.weight(out_weight, weight_rows)
-    cot_full = tp.gather(to_packed(out_grad))
-
-    width = hidden_count // CHUNKS
-
-    def chunk(weight, index):
-        return weight[:, index * width : (index + 1) * width]
-
-    directs = [0, 0, weight_rows, weight_rows]
-    gate_w, up_w = [], []
-    for index in range(CHUNKS):
-        gate_w.append(shards.weight(chunk(gate_weight, index), directs[index]))
-        up_w.append(shards.weight(chunk(up_weight, index), directs[index]))
+        return sums, shards.weight(more) if more is not None else ()
 
     lengths = seq_lengths[0]
     starts = jnp.cumsum(lengths) - lengths
@@ -488,63 +975,89 @@
     second_own = (position[2 : row_count + 2] >= 2).astype(WIDE)[:, None]
     first_next = (position[3 : row_count + 3] >= 1).astype(WIDE)[:, None]
     second_next = (position[4 : row_count + 4] >= 2).astype(WIDE)[:, None]
-
-    x_float = x_full.astype(WIDE)
-    scale_one = lax.rsqrt(jnp.mean(x_float * x_float, axis=1, keepdims=True) + EPS)
-    normed_one = x_float * scale_one
-    h_one = (normed_one * gain_one).astype(LOW)
-    projected = sum(matmul(part, w) for part, w in zip(shards.split(h_one), in_w))
-    b_part = projected[:, :col_count]
-    c_part = projected[:, col_count : 2 * col_count]
-    v_part = projected[:, 2 * col_count :]
-    mixed = (b_part * v_part).astype(LOW)
+    conv_taps = conv_weight.astype(WIDE)
+    gains = tp.gather(jnp.stack([norm1_gain, norm2_gain])).astype(WIDE)
+    gain_one, gain_two = gains[0], gains[1]
+    in_parts = jnp.moveaxis(in_weight, 1, 0)
+
+    if shards.paired:
+        def blocks_of(values):
+            return reorder(values, send_order).reshape(per_dev, block_rows, col_count)
+
+        place = (targets[None, :] == jnp.arange(per_dev)[:, None]).astype(WIDE)
+        (
+            in_peer, out_peer, _, _, x_full, h_one, proj, mixed, conv_out, gated, mixer, h_two, cot_full,
+            cot_peer, h_two_peer, h_one_peer, acts, dh_two_halves,
+        ) = front(
+            blocks_of(hidden_in), blocks_of(out_grad), place, gains, first_own, second_own, conv_taps,
+            in_parts, out_weight, gate_weight, up_weight, down_weight,
+        )
+        b_part, c_part, v_part = proj[0], proj[1], proj[2]
+        in_w = [jnp.concatenate([w[0], w[1], w[2]], axis=1) for w in (in_parts, in_peer)]
+        out_w = (out_weight, out_peer)
+        mixer_out = shards.join([mixer[0], mixer[1]])
+        cot_cols = jnp.concatenate([shards.split(cot_full)[0], cot_peer], axis=0)
+        h_two_cols = jnp.concatenate([shards.split(h_two)[0], h_two_peer], axis=0)
+        h_one_cols = jnp.concatenate([shards.split(h_one)[0], h_one_peer], axis=0)
+        ffn_rights = [acts[:, kind * hidden_count : (kind + 1) * hidden_count] for kind in range(3)]
+        dh_parts = [dh_two_halves[0], dh_two_halves[1]]
+        x_float = x_full.astype(WIDE)
+        scale_one = lax.rsqrt(jnp.mean(x_float * x_float, axis=1, keepdims=True) + EPS)
+        normed_one = x_float * scale_one
+        resid = x_float + mixer_out.astype(WIDE)
+        scale_two = lax.rsqrt(jnp.mean(resid * resid, axis=1, keepdims=True) + EPS)
+        normed_two = resid * scale_two
+    else:
+        in_w = shards.weight(in_weight.reshape(weight_rows, -1))
+        x_full = tp.gather(to_packed(hidden_in))
+        out_w = shards.weight(out_weight)
+        cot_full = tp.gather(to_packed(out_grad))
+        gate_w, up_w = shards.weight(gate_weight), shards.weight(up_weight)
+        x_float = x_full.astype(WIDE)
+        scale_one = lax.rsqrt(jnp.mean(x_float * x_float, axis=1, keepdims=True) + EPS)
+        normed_one = x_float * scale_one
+        h_one = (normed_one * gain_one).astype(LOW)
+        projected = matmul(h_one, in_w[0])
+        b_part = projected[:, :col_count]
+        c_part = projected[:, col_count : 2 * col_count]
+        v_part = projected[:, 2 * col_count :]
+        mixed = (b_part * v_part).astype(LOW)
+        rim = shifted(mixed[-2:], "ctx", 1)
+        extended = jnp.concatenate([rim, mixed], axis=0).astype(WIDE)
+        prev_one = extended[1 : row_count + 1] * first_own
+        prev_two = extended[0:row_count] * second_own
+        conv_out = (
+            conv_taps[0] * extended[2:] + conv_taps[1] * prev_one + conv_taps[2] * prev_two
+        )
+        gated = (c_part * conv_out).astype(LOW)
+        mixer_halves = jnp.split(contract_cols(gated, out_w[0]), 2, axis=1)
+        mixer_out = jnp.concatenate(tp.total(*mixer_halves), axis=1)
+        resid = x_float + mixer_out.astype(WIDE)
+        scale_two = lax.rsqrt(jnp.mean(resid * resid, axis=1, keepdims=True) + EPS)
+        normed_two = resid * scale_two
+        h_two = (normed_two * gain_two).astype(LOW)
+        cot_cols, h_two_cols, h_one_cols = [shards.columns(v) for v in (cot_full, h_two, h_one)]
+        gate_pre, up_pre = matmul(h_two, gate_w[0]), matmul(h_two, up_w[0])
+        d_act = shards.own_total(matmul(cot_cols, down_weight))
+        sigmoid_gate = jax.nn.sigmoid(gate_pre)
+        silu_gate = gate_pre * sigmoid_gate
+        d_gate = d_act * up_pre * sigmoid_gate * (1.0 + gate_pre * (1.0 - sigmoid_gate))
+        ffn_rights = [v.astype(LOW) for v in (silu_gate * up_pre, d_gate, d_act * silu_gate)]
+        dh_parts = [contract_cols(ffn_rights[1], gate_w[0]) + contract_cols(ffn_rights[2], up_w[0])]
+
+    dh_terms = tp.all_terms(shards.join(dh_parts))
+    ffn_grads, down_w = weight_grads(
+        [[cot_cols], [h_two_cols, h_two_cols]], [ffn_rights[:1], ffn_rights[1:]], 0, down_weight
+    )
+    dh_terms, down_w, ffn_grads = lax.optimization_barrier((dh_terms, down_w, ffn_grads))
+    dh_two = added(dh_terms)
+    ffn_terms = tp.own_terms(shards.join([contract_cols(ffn_rights[0], w) for w in down_w]))
+
     rim = shifted(mixed[-2:], "ctx", 1)
     extended = jnp.concatenate([rim, mixed], axis=0).astype(WIDE)
-    conv_taps = conv_weight.astype(WIDE)
     prev_one = extended[1 : row_count + 1] * first_own
     prev_two = extended[0:row_count] * second_own
     mixed_float = extended[2:]
-    conv_out = conv_taps[0] * mixed_float + conv_taps[1] * prev_one + conv_taps[2] * prev_two
-    gated = (c_part * conv_out).astype(LOW)
-    mixer_parts = [contract_cols(gated, w) for w in out_w]
-    mixer_out = shards.joined(tp.total(*shards.halves(mixer_parts)))
-    resid = x_float + mixer_out.astype(WIDE)
-    scale_two = lax.rsqrt(jnp.mean(resid * resid, axis=1, keepdims=True) + EPS)
-    normed_two = resid * scale_two
-    h_two = (normed_two * gain_two).astype(LOW)
-    h_two_parts = shards.split(h_two)
-
-    cot_cols = shards.columns(cot_full)
-    h_two_cols = shards.columns(h_two)
-    h_one_cols = shards.columns(h_one)
-
-    acts, d_gates, d_ups = [], [], []
-    dh_parts = [None] * len(h_two_parts)
-    for index in range(CHUNKS):
-        down_rows = chunk(down_weight, index)
-        gate_pre = sum(matmul(part, w) for part, w in zip(h_two_parts, gate_w[index]))
-        up_pre = sum(matmul(part, w) for part, w in zip(h_two_parts, up_w[index]))
-        d_act = shards.own_total(matmul(cot_cols, down_rows))
-        sigmoid_gate = jax.nn.sigmoid(gate_pre)
-        silu_gate = gate_pre * sigmoid_gate
-        acts.append((silu_gate * up_pre).astype(LOW))
-        d_gates.append(
-            (d_act * up_pre * sigmoid_gate * (1.0 + gate_pre * (1.0 - sigmoid_gate))).astype(LOW)
-        )
-        d_ups.append((d_act * silu_gate).astype(LOW))
-        for place in range(len(dh_parts)):
-            term = contract_cols(d_gates[-1], gate_w[index][place])
-            term = term + contract_cols(d_ups[-1], up_w[index][place])
-            dh_parts[place] = term if dh_parts[place] is None else dh_parts[place] + term
-    dh_two = tp.total_direct(shards.join(dh_parts))
-    down_w = shards.weight(down_weight, weight_rows)
-    ffn_rights = [jnp.concatenate(parts, axis=1) for parts in (acts, d_gates, d_ups)]
-    down_total, gate_total, up_total = weight_grads(
-        [[cot_cols], [h_two_cols, h_two_cols]], [ffn_rights[:1], ffn_rights[1:]], 0
-    )
-    activated = ffn_rights[0]
-    ffn_own = tp.scatter_direct(shards.join([contract_cols(activated, w) for w in down_w]))
-    block_out = (tp.own(resid, 1) + ffn_own).astype(LOW)
 
     gain_two_grad = tp.own(jnp.sum(dh_two * normed_two, axis=0), 0)
     d_resid = cot_full.astype(WIDE) + norm_back(dh_two, normed_two, scale_two, gain_two)
@@ -573,10 +1086,17 @@
         (d_mixed * b_part).astype(LOW),
     ]
     d_proj_flat = jnp.concatenate(d_proj, axis=1)
-    dh_one = tp.total_direct(shards.join([contract_cols(d_proj_flat, w) for w in in_w]))
-    out_total, in_flat_total = weight_grads(
+    dh_one_terms = tp.all_terms(shards.join([contract_cols(d_proj_flat, w) for w in in_w]))
+    mixer_grads, _ = weight_grads(
         [[shards.columns(d_resid_low)], [h_one_cols]], [[gated], [d_proj_flat]], 1
     )
+    dh_one_terms, ffn_terms, mixer_grads = lax.optimization_barrier(
+        (dh_one_terms, ffn_terms, mixer_grads)
+    )
+    dh_one = added(dh_one_terms)
+    block_out = (tp.own(resid, 1) + added(ffn_terms)).astype(LOW)
+    down_total, gate_total, up_total = [value.astype(WIDE) for value in ffn_grads]
+    out_total, in_flat_total = [value.astype(WIDE) for value in mixer_grads]
     in_total = in_flat_total.reshape(in_weight.shape)
     gain_one_grad = tp.own(jnp.sum(dh_one * normed_one, axis=0), 0)
     d_input = d_resid + norm_back(dh_one, normed_one, scale_one, gain_one)

time: 1120 us -> 880 us (0.79)
  waiting for transfers between devices: 312 us -> 9.92 us
  Pallas kernels: 450 us -> 675 us
  matrix products: 91.6 us -> 10.3 us
  other arithmetic: 118 us -> 66.9 us
  starting transfers between devices: 51 us -> 28.3 us
  between operations: 16 us -> 1.93 us
  local copies, waits for them, and re-layouts: 68.3 us -> 79.5 us
    ppermute x45 -> x16, waiting for transfers between devices: 288 us -> 9.92 us  [swapped(): lax.ppermute(value, axis, [(source, source ^ step) for source in range(co...]
    pallas_call x2 -> x3, Pallas kernels: 450 us -> 675 us  [the longest x2 443 us: line_grads(): pl.pallas_call(functools.partial(line_kernel, pieces, left_of, swap), out...]
    dot_general x24 -> x2, matrix products: 52.2 us -> 1.93 us  [matmul(): return jnp.dot(left, right, preferred_element_type=WIDE)]
    dot_general x22 -> x4, matrix products: 39.4 us -> 8.37 us  [contract_cols(): lax.dot_general(left, right, (((1,), (1,)), ((), ())), preferred_element_...]
    pallas_call x0 -> x9, local copies, waits for them, and re-layouts: none -> 26.9 us  [front(): pl.pallas_call(front_kernel, out_shape=[value for value, _ in outs], in_s...]
    all_to_all x2 -> x0, waiting for transfers between devices: 20.3 us -> none  [to_packed(): lax.all_to_all(reorder(values, send_order), 'ctx', split_axis=0, concat_a...]
    unnamed x226 -> x83, local copies, waits for them, and re-layouts: 28.5 us -> 10.3 us
    add x1 -> x0, other arithmetic: 17.7 us -> none  [on_device(): resid = x_float + mixer_out.astype(WIDE)]
  transfers between devices with their start and end apart: 55 -> 19, of which waited for: 18 -> 3; matrix products, arithmetic and copies ran while one was open for 19% -> 14% of each run, Pallas kernels for 41% -> 51%
where the time goes in v3:
time: 880 us; the launch traced here: 871 us
  Pallas kernels  675 us (77%)
  local copies, waits for them, and re-layouts  79.5 us (9%)
  other arithmetic  66.9 us (8%)
  starting transfers between devices  28.3 us (3%)
  matrix products  10.3 us (1%)
  waiting for transfers between devices  9.92 us (1%)
    pallas_call x2, Pallas kernels, line_grads(): pl.pallas_call(functools.partial(line_kernel, pieces, left_of, swap), out...  443 us
    pallas_call x1, Pallas kernels, front(): pl.pallas_call(front_kernel, out_shape=[value for value, _ in outs], in_s...  231 us
    pallas_call x9, local copies, waits for them, and re-layouts, front(): pl.pallas_call(front_kernel, out_shape=[value for value, _ in outs], in_s...  26.9 us
    ppermute x16, starting transfers between devices, swapped(): lax.ppermute(value, axis, [(source, source ^ step) for source in range(co...  20.6 us
  transfers between devices with their start and end apart: 19, of which 3 were waited for; matrix products, arithmetic and copies ran while one was open for 14% of the time, Pallas kernels for 51%

profile of v3, /device:TPU:0, one launch (start us, length us, event | category | flops | bytes accessed | tf_op | source)
XLA Modules:
  0.0 871.4 jit_solution(3353585468131482871)
XLA Ops:
  2.1 3.0 collective-permute-start
  5.6 1.3 reduce.3
  12.1 1.4 fusion.61
  13.5 3.7 slice_bitcast_fusion.2
  18.5 1.4 gather_fusion
  19.9 1.4 gather_fusion.1
  21.3 0.9 copy.77.first_mask
  23.6 231.4 %shard_map.195 = (bf16[3,1024,512]{2,1,0:T(8,128)(2,1)}, bf16[1024,512]{1,0:T(8,128)(2,1)}, bf16[1024,2048]{1,0:T(8,128)(2,1)}, bf16[1024,2048]{1,0:T(8,128)(2,1...) custom-call(bf16[4,128,512]{2,1,0:T(8,128)(2,1)} %gather_fusion, ...), custom_call_target="tpu_custom_call" | custom-call | flops 274877906944 | bytes 536870912 | tf_op jit(solution)/shard_map/pallas_call | solution.py:775
  255.0 2.9 copy.83
  258.0 1.5 pad_maximum_fusion.2
  260.4 1.0 collective-permute-start.4
  261.3 2.9 copy.82
  264.2 3.0 copy.86
  267.2 4.1 copy.87
  271.3 1.0 constant_dynamic-slice_fusion.4
  272.3 2.3 constant_dynamic-slice_fusion.3
  274.6 2.3 copy.88
  276.9 2.9 copy.80
  279.7 1.5 select_bitcast_fusion.3
  281.2 2.9 copy.79
  284.1 2.4 multiply_reduce_fusion.4
  286.6 2.6 collective-permute-start.14
  289.7 2.4 pad_maximum_fusion.refs_0_
  292.1 312.0 %shard_map.196 = (bf16[1024,6144]{1,0:T(8,128)(2,1)}, bf16[1024,2048]{1,0:T(8,128)(2,1)}) custom-call(bf16[2,1024,1024]{2,1,0:T(8,128)(2,1)} %pad_maximum_fusion.refs_0_, bf16[512,6144]{1,0:T(8,128)(2,1)} %get-tuple-element.59.refs_1_, bf16[1024,2048]{1,0:T(8,128)(2,1)} %refs_2_.1), custom_call_target="tpu_custom_call" | custom-call | flops 103079215104 | bytes 402653184 | tf_op jit(solution)/shard_map/pallas_call | solution.py:282
  604.1 3.9 copy.97
  608.0 2.3 copy.98
  610.3 1.3 constant_dynamic-slice_fusion
  611.6 2.1 slice_bitcast_fusion.5
  613.7 9.0 %fusion.57 = (bf16[1024,2048]{1,0:T(8,128)(2,1)}, bf16[1024,2048]{1,0:T(8,128)(2,1)}, bf16[1024,2048]{1,0:T(8,128)(2,1)}) fusion(bf16[1024,6144]{1,0:T(8,128)(2,1)} %get-tuple-element.61), kind=kLoop, calls=%fused_computation.178 | loop fusion | bytes 25165824 | tf_op jit(solution)/shard_map/slice | solution.py:961
  624.2 5.8 multiply_reduce_fusion
  630.1 9.0 %fusion.56 = (bf16[512,2048]{0,1:T(8,128)(2,1)S(1)}, f32[512,2048]{0,1:T(8,128)}, f32[512,2048]{0,1:T(8,128)}) fusion(f32[512]{0:T(512)S(1)} %broadcast_multiply_fusion.2, bf16[512,1024]{0,1:T(8,128)(2,1)S(1)} %copy-done.3, bf16[512,1024]{0,1:T(8,128)(2,1)S(1)} %copy-done.2, bf16[512,2048]{0,1:T(8,128)(2,1)S(1)} %copy.79, f32[2048]{0:T(1024)S(1)} %bitcast.114, ...), kind=kLoop, calls=%fused_computation.177 | loop fusion | flops 22020096 | bytes 25178112 | tf_op jit(solution)/shard_map/convert_element_type | solution.py:1064
  640.0 1.0 copy-done.13
  641.6 1.2 fusion.21
  642.8 1.6 collective-permute-start.5
  645.2 2.4 fusion.15
  647.6 2.4 broadcast_select_fusion
  650.1 4.8 fusion.23
  654.9 1.0 collective-permute-start.10
  655.8 1.2 collective-permute-start.9
  657.8 1.8 fusion.7
  659.7 1.8 select_convert_fusion.1
  662.5 1.6 pad_maximum_fusion.4.refs_1_
  664.2 1.0 collective-permute-start.7
  665.5 2.6 pad_maximum_fusion.1.refs_0_
  668.1 1.6 collective-permute-done.10
  669.7 131.2 %shard_map.197 = bf16[1024,2048]{1,0:T(8,128)(2,1)} custom-call(bf16[2,1024,1024]{2,1,0:T(8,128)(2,1)} %pad_maximum_fusion.1.refs_0_, bf16[512,2048]{1,0:T(8,128)(2,1)} %pad_maximum_fusion.4.refs_1_), custom_call_target="tpu_custom_call" | custom-call | flops 34359738368 | bytes 134217728 | tf_op jit(solution)/shard_map/pallas_call | solution.py:282
  800.9 3.9 slice.169
  804.8 3.9 multiply_reduce_fusion.1
  808.7 1.6 fusion.30
  810.4 1.9 add_convert_fusion
  812.9 1.7 gather_fusion.2
  814.6 3.5 all-to-all-start
  818.3 4.4 collective-permute-start.15
  823.4 1.0 collective-permute-done.15
  824.4 2.0 collective-permute-start.16
  826.4 7.3 collective-permute-done.16
  833.8 4.8 collective-permute-start.17
  838.6 6.8 convert_element_type.159
  845.4 4.4 convert_element_type.160
  849.9 4.4 convert_element_type.161
  854.3 5.4 copy.100
  859.8 6.7 copy.101
  866.4 1.6 convert_element_type.158
  869.9 1.0 fusion.58
  (176 shorter events, 20.8 us)
Async XLA Ops:
  0.6 17.9 %copy-start = (bf16[512,512]{1,0:T(8,128)(2,1)S(1)}, bf16[512,512]{1,0:T(8,128)(2,1)}, u32[]{:S(2)}) copy-start(bf16[512,512]{1,0:T(8,128)(2,1)} %param.12) | copy-start | bytes 1572868
  2.1 15.1 %collective-permute-start = (bf16[2,512]{1,0:T(2,128)(2,1)S(1)}, bf16[2,512]{1,0:T(2,128)(2,1)S(1)}, u32[]{:S(2)}, u32[]{:S(2)}) collective-permute-start(bf16[2,512]{1,0:T(2,128)(2,1)S(1)} %pad_maximum_fusion.10), channel_id=1, source_target_pairs={{0,2},{1,3},{2,0},{3,1},{4,6},{5,7},{6,4},{7,5},{8,10},{9,11},{10,... | collective-permute-start | bytes 6152 | tf_op jit(solution)/shard_map/ppermute | solution.py:24
  7.9 0.7 copy-start.33
  12.1 9.2 %copy-start.26 = (f32[512]{0:T(512)}, f32[512]{0:T(512)S(1)}, u32[]{:S(2)}) copy-start(f32[512]{0:T(512)S(1)} %get-tuple-element.176) | copy-start | bytes 6148
  12.1 10.0 %copy-start.24 = (f32[512]{0:T(512)}, f32[512]{0:T(512)S(1)}, u32[]{:S(2)}) copy-start(f32[512]{0:T(512)S(1)} %get-tuple-element.174) | copy-start | bytes 6148
  13.5 4.4 copy-start.21
  13.5 6.4 copy-start.18
  17.2 5.8 collective-permute-start.1
  259.5 363.7 %collective-permute-start.2 = (bf16[512,2048]{0,1:T(8,128)(2,1)}, bf16[512,2048]{0,1:T(8,128)(2,1)}, u32[]{:S(2)}, u32[]{:S(2)}) collective-permute-start(bf16[512,2048]{0,1:T(8,128)(2,1)} %pad_maximum_fusion.2), channel_id=1, source_target_pairs={{0,1},{1,0},{2,3},{3,2},{4,5},{5,4},{6,7},{7,6},{8,9},{9,8},{10,11... | collective-permute-start | bytes 6291464 | tf_op jit(solution)/shard_map/ppermute | solution.py:24
  259.9 363.3 %collective-permute-start.3 = (bf16[512,2048]{0,1:T(8,128)(2,1)}, bf16[512,2048]{0,1:T(8,128)(2,1)}, u32[]{:S(2)}, u32[]{:S(2)}) collective-permute-start(bf16[512,2048]{0,1:T(8,128)(2,1)} %pad_maximum_fusion.2), channel_id=1, source_target_pairs={{0,2},{1,3},{2,0},{3,1},{4,6},{5,7},{6,4},{7,5},{8,10},{9,11},{10,... | collective-permute-start | bytes 6291464 | tf_op jit(solution)/shard_map/ppermute | solution.py:24
  260.4 362.8 %collective-permute-start.4 = (bf16[512,2048]{0,1:T(8,128)(2,1)}, bf16[512,2048]{0,1:T(8,128)(2,1)}, u32[]{:S(2)}, u32[]{:S(2)}) collective-permute-start(bf16[512,2048]{0,1:T(8,128)(2,1)} %pad_maximum_fusion.2), channel_id=1, source_target_pairs={{0,3},{1,2},{2,1},{3,0},{4,7},{5,6},{6,5},{7,4},{8,11},{9,10},{10,... | collective-permute-start | bytes 6291464 | tf_op jit(solution)/shard_map/ppermute | solution.py:24
  264.2 7.1 copy-start.6
  284.1 2.5 copy-start.17
  284.1 5.1 copy-start.9
  284.1 5.1 copy-start.10
  286.5 2.9 copy-start.8
  286.5 3.0 copy-start.11
  286.6 336.4 %collective-permute-start.14 = (bf16[2,512]{1,0:T(2,128)(2,1)S(1)}, bf16[2,512]{1,0:T(2,128)(2,1)S(1)}, u32[]{:S(2)}, u32[]{:S(2)}) collective-permute-start(bf16[2,512]{1,0:T(2,128)(2,1)S(1)} %slice.173), channel_id=1, source_target_pairs={{0,4},{4,8},{8,12},{1,5},{5,9},{9,13},{2,6},{6,10},{10,14},{3,7},{... | collective-permute-start | bytes 6152 | tf_op jit(solution)/shard_map/ppermute | solution.py:19
  611.6 2.1 copy-start.20
  613.7 9.0 %copy-start.12 = (bf16[512,1024]{0,1:T(8,128)(2,1)S(1)}, bf16[512,1024]{0,1:T(8,128)(2,1)}, u32[]{:S(2)}) copy-start(bf16[512,1024]{0,1:T(8,128)(2,1)} %copy.98) | copy-start | bytes 3145732
  622.7 1.2 copy-start.2
  622.7 1.5 copy-start.3
  624.2 5.8 copy-start.7
  624.2 21.0 %slice-start.1 = ((s8[6291456]{0:T(1024)(128)(4,1)}), s8[4194304]{0:T(1024)(128)(4,1)S(1)}, s32[]{:S(2)}) async-start(s8[6291456]{0:T(1024)(128)(4,1)} %bitcast.129), calls=%async_computation.2 | async-start | bytes 8388608
  630.0 9.2 %copy-start.32 = (bf16[1024,512]{1,0:T(8,128)(2,1)S(1)}, bf16[1024,512]{1,0:T(8,128)(2,1)}, u32[]{:S(2)}) copy-start(bf16[1024,512]{1,0:T(8,128)(2,1)} %out_w.1) | copy-start | bytes 3145732
  630.0 15.2 %slice-start.2 = ((s8[6291456]{0:T(1024)(128)(4,1)}), s8[2097152]{0:T(1024)(128)(4,1)S(1)}, s32[]{:S(2)}) async-start(s8[6291456]{0:T(1024)(128)(4,1)} %bitcast.129), calls=%async_computation.3 | async-start | bytes 4194304
  639.1 1.9 copy-start.13
  639.1 1.9 copy-start.25
  639.1 1.9 copy-start.27
  639.1 2.2 copy-start.35
  639.1 2.5 copy-start.36
  641.6 3.7 copy-start.31
  642.8 14.2 %collective-permute-start.5 = (bf16[2,512]{1,0:T(2,128)(2,1)S(1)}, bf16[2,512]{1,0:T(2,128)(2,1)S(1)}, u32[]{:S(2)}, u32[]{:S(2)}) collective-permute-start(bf16[2,512]{1,0:T(2,128)(2,1)S(1)} %slice.201), channel_id=1, source_target_pairs={{4,0},{8,4},{12,8},{5,1},{9,5},{13,9},{6,2},{10,6},{14,10},{7,3},{... | collective-permute-start | bytes 6152 | tf_op jit(solution)/shard_map/ppermute | solution.py:19
  644.6 3.0 copy-start.37
  644.6 16.9 %collective-permute-start.12 = (bf16[512,512]{0,1:T(8,128)(2,1)S(1)}, bf16[512,512]{0,1:T(8,128)(2,1)S(1)}, u32[]{:S(2)}, u32[]{:S(2)}) collective-permute-start(bf16[512,512]{0,1:T(8,128)(2,1)S(1)} %constant_dynamic-slice_fusion.1), channel_id=1, source_target_pairs={{0,16},{16,0},{1,17},{17,1},{2,18},{18,2},{3,19},{19,3},{4,20},{20... | collective-permute-start | bytes 1572872 | tf_op jit(solution)/shard_map/ppermute | solution.py:24
  650.0 7.1 copy-start.22
  650.0 7.1 copy-start.23
  650.0 7.1 copy-start.28
  650.0 7.1 copy-start.29
  650.0 7.1 copy-start.30
  654.9 14.9 %collective-permute-start.10 = (bf16[512,512]{0,1:T(8,128)(2,1)S(1)}, bf16[512,512]{0,1:T(8,128)(2,1)S(1)}, u32[]{:S(2)}, u32[]{:S(2)}) collective-permute-start(bf16[512,512]{0,1:T(8,128)(2,1)S(1)} %get-tuple-element.150), channel_id=1, source_target_pairs={{0,2},{1,3},{2,0},{3,1},{4,6},{5,7},{6,4},{7,5},{8,10},{9,11},{10,... | collective-permute-start | bytes 1572872 | tf_op jit(solution)/shard_map/ppermute | solution.py:24
  655.8 149.0 %collective-permute-start.11 = (bf16[512,512]{0,1:T(8,128)(2,1)}, bf16[512,512]{0,1:T(8,128)(2,1)}, u32[]{:S(2)}, u32[]{:S(2)}) collective-permute-start(bf16[512,512]{0,1:T(8,128)(2,1)} %get-tuple-element.147), channel_id=1, source_target_pairs={{0,3},{1,2},{2,1},{3,0},{4,7},{5,6},{6,5},{7,4},{8,11},{9,10},{10,... | collective-permute-start | bytes 1572872 | tf_op jit(solution)/shard_map/ppermute | solution.py:24
  655.8 149.0 %collective-permute-start.9 = (bf16[512,512]{0,1:T(8,128)(2,1)}, bf16[512,512]{0,1:T(8,128)(2,1)}, u32[]{:S(2)}, u32[]{:S(2)}) collective-permute-start(bf16[512,512]{0,1:T(8,128)(2,1)} %get-tuple-element.149), channel_id=1, source_target_pairs={{0,1},{1,0},{2,3},{3,2},{4,5},{5,4},{6,7},{7,6},{8,9},{9,8},{10,11... | collective-permute-start | bytes 1572872 | tf_op jit(solution)/shard_map/ppermute | solution.py:24
  657.8 1.9 copy-start.14
  657.8 1.9 copy-start.15
  657.8 1.9 copy-start.16
  661.5 1.0 copy-start.19
  661.5 2.7 collective-permute-start.13
  661.7 143.1 %collective-permute-start.6 = (bf16[512,2048]{0,1:T(8,128)(2,1)S(1)}, bf16[512,2048]{0,1:T(8,128)(2,1)}, u32[]{:S(2)}, u32[]{:S(2)}) collective-permute-start(bf16[512,2048]{0,1:T(8,128)(2,1)S(1)} %pad_maximum_fusion.3), channel_id=1, source_target_pairs={{0,1},{1,0},{2,3},{3,2},{4,5},{5,4},{6,7},{7,6},{8,9},{9,8},{10,11... | collective-permute-start | bytes 6291464 | tf_op jit(solution)/shard_map/ppermute | solution.py:24
  664.2 140.7 %collective-permute-start.7 = (bf16[512,2048]{0,1:T(8,128)(2,1)S(1)}, bf16[512,2048]{0,1:T(8,128)(2,1)}, u32[]{:S(2)}, u32[]{:S(2)}) collective-permute-start(bf16[512,2048]{0,1:T(8,128)(2,1)S(1)} %pad_maximum_fusion.3), channel_id=1, source_target_pairs={{0,2},{1,3},{2,0},{3,1},{4,6},{5,7},{6,4},{7,5},{8,10},{9,11},{10,... | collective-permute-start | bytes 6291464 | tf_op jit(solution)/shard_map/ppermute | solution.py:24
  669.7 135.1 %collective-permute-start.8 = (bf16[512,2048]{0,1:T(8,128)(2,1)S(1)}, bf16[512,2048]{0,1:T(8,128)(2,1)S(1)}, u32[]{:S(2)}, u32[]{:S(2)}) collective-permute-start(bf16[512,2048]{0,1:T(8,128)(2,1)S(1)} %pad_maximum_fusion.3), channel_id=1, source_target_pairs={{0,3},{1,2},{2,1},{3,0},{4,7},{5,6},{6,5},{7,4},{8,11},{9,10},{10,... | collective-permute-start | bytes 6291464 | tf_op jit(solution)/shard_map/ppermute | solution.py:24
  812.3 10.3 %copy-start.34 = (s32[4]{0:T(128)S(1)}, s32[4]{0:T(128)}, u32[]{:S(2)}) copy-start(s32[4]{0:T(128)} %copy-done.33) | copy-start | bytes 52
  814.6 54.7 %all-to-all-start = ((bf16[4,128,1024]{2,1,0:T(8,128)(2,1)}), bf16[4,128,1024]{2,1,0:T(8,128)(2,1)S(1)}, u32[]{:S(2)}, u32[]{:S(2)}) async-start(bf16[4,128,1024]{2,1,0:T(8,128)(2,1)} %gather_fusion.2), calls=%async_computation | async-start | bytes 2097152 | tf_op jit(solution)/shard_map/all_to_all | solution.py:949
  818.3 6.1 collective-permute-start.15
  824.4 9.4 %collective-permute-start.16 = (f32[5,512]{1,0:T(8,128)S(1)}, f32[5,512]{1,0:T(8,128)S(1)}, u32[]{:S(2)}, u32[]{:S(2)}) collective-permute-start(f32[5,512]{1,0:T(8,128)S(1)} %add.184), channel_id=1, source_target_pairs={{0,4},{4,0},{8,12},{12,8},{1,5},{5,1},{9,13},{13,9},{2,6},{6,2},{1... | collective-permute-start | bytes 30728 | tf_op jit(solution)/shard_map/ppermute | solution.py:24
  833.8 34.3 %collective-permute-start.17 = (f32[5,512]{1,0:T(8,128)S(1)}, f32[5,512]{1,0:T(8,128)S(1)}, u32[]{:S(2)}, u32[]{:S(2)}) collective-permute-start(f32[5,512]{1,0:T(8,128)S(1)} %add.185), channel_id=1, source_target_pairs={{0,8},{4,12},{8,0},{12,4},{1,9},{5,13},{9,1},{13,5},{2,10},{6,14},... | collective-permute-start | bytes 30728 | tf_op jit(solution)/shard_map/ppermute | solution.py:24
  838.6 6.8 copy-start.5
  845.4 4.5 copy-start.4
  859.7 6.7 slice-start
  859.8 11.2 %copy-start.1 = (bf16[512,512]{1,0:T(8,128)(2,1)S(1)}, bf16[512,512]{1,0:T(8,128)(2,1)}, u32[]{:S(2)}) copy-start(bf16[512,512]{1,0:T(8,128)(2,1)} %param.12) | copy-start | bytes 1572868

commit v4 on v3

--- a/solution.py
+++ b/solution.py
@@ -69,13 +69,10 @@
 MESH = pl.DeviceIdType.MESH
 
 
-def line_kernel(pieces, left_of, swap, *refs):
-    if swap:
-        (left_ref, right_ref, more_ref, out_ref, more_peer), refs = refs[:5], refs[5:]
-    else:
-        (left_ref, right_ref, out_ref), refs = refs[:3], refs[3:]
-    peer, outer_part, middle_part, held, peer_send, peer_recv, in_send, outer_recv, middle_recv = refs[:9]
-    out_send, out_recv, own_done, more_send, more_recv = refs[9:]
+def line_kernel(
+    pieces, left_of, left_ref, right_ref, out_ref, peer, outer_part, middle_part, held,
+    peer_send, peer_recv, in_send, outer_recv, middle_recv, out_send, out_recv, own_done,
+):
     shard = lax.axis_index("shard")
     ctx = lax.axis_index("ctx")
     tokens = right_ref.shape[0]
@@ -147,20 +144,6 @@
             outer_part.at[index], out_ref.at[:, columns(index)], own_done.at[index]
         )
 
-    strips = min(16, pieces)
-
-    def more_copy(index):
-        size = more_ref.shape[0] // strips
-        lines = pl.ds(pl.multiple_of(index * size, size), size)
-        return pltpu.make_async_remote_copy(
-            src_ref=more_ref.at[lines],
-            dst_ref=more_peer.at[lines],
-            send_sem=more_send.at[index],
-            recv_sem=more_recv.at[index],
-            device_id={"shard": 1 - shard},
-            device_id_type=MESH,
-        )
-
     tile = min(256, rows)
 
     def product(index, start):
@@ -197,12 +180,6 @@
         def _():
             peer_copy(index + AHEAD).start()
 
-        if swap:
-
-            @pl.when(index < strips)
-            def _():
-                more_copy(index).start()
-
         @pl.when(index >= SLOTS)
         def _():
             end_copy(index - SLOTS).wait_send()
@@ -238,12 +215,6 @@
     def _():
         finish(pieces - 1)
 
-    if swap:
-
-        @pl.loop(0, strips)
-        def _(index):
-            more_copy(index).wait()
-
     @pl.loop(0, pieces)
     def _(index):
         peer_copy(index).wait_send()
@@ -262,7 +233,7 @@
             out_copy(index).wait_recv()
 
 
-def line_grads(lefts, rights, identity, more=None):
+def line_grads(lefts, rights, identity):
     left = jnp.stack([value.T for value in lefts])
     right = jnp.concatenate(rights, axis=1)
     tokens, width = right.shape
@@ -275,38 +246,34 @@
 
     flops = 4 * tokens * rows * width
     dma = pltpu.SemaphoreType.DMA
-    swap = more is not None
-    extra = [more] if swap else []
-    out_shape = [jax.ShapeDtypeStruct((rows, width), LOW)]
-    out_shape += [jax.ShapeDtypeStruct(value.shape, LOW) for value in extra]
     return pl.pallas_call(
-        functools.partial(line_kernel, pieces, left_of, swap),
-        out_shape=out_shape,
-        in_specs=[pl.BlockSpec(memory_space=pltpu.VMEM)] * 2
-        + [pl.BlockSpec(memory_space=pl.ANY) for _ in extra],
-        out_specs=[pl.BlockSpec(memory_space=pl.ANY) for _ in out_shape],
+        functools.partial(line_kernel, pieces, left_of),
+        out_shape=jax.ShapeDtypeStruct((rows, width), LOW),
+        in_specs=[pl.BlockSpec(memory_space=pltpu.VMEM)] * 2,
+        out_specs=pl.BlockSpec(memory_space=pl.ANY),
         scratch_shapes=[
             pltpu.VMEM((pieces, tokens, PIECE), LOW),
             pltpu.VMEM((pieces, rows, PIECE), LOW),
             pltpu.VMEM((pieces, rows, PIECE), LOW),
             pltpu.VMEM((SLOTS, rows, PIECE), LOW),
         ]
-        + [dma((pieces,)) for _ in range(10)],
+        + [dma((pieces,)) for _ in range(8)],
         compiler_params=pltpu.CompilerParams(
             collective_id=identity, has_side_effects=True, vmem_limit_bytes=56 * 1024 * 1024
         ),
         cost_estimate=pl.CostEstimate(flops=flops * 8, bytes_accessed=rows * width * 64, transcendentals=0),
-    )(left, right, *extra)
+    )(left, right)
 
 
 def front_kernel(
     x_blocks, cot_blocks, place, gains, first_mask, second_mask, taps,
     in_w, out_w, gate_w, up_w, down_w,
-    in_peer, out_peer, gate_peer, up_peer,
-    x_full, h_one, proj, mixed, conv_out, gated, mixer, h_two, cot_full, cot_peer, h_two_peer, h_one_peer, acts, dh_two,
-    x_got, cot_got, out_v, rim, extended, away, pair, pair_got, both_got,
-    da_own, da_send, da_got, gu_v, down_v, dh_sum, ffn_v,
-    send, recv, local,
+    in_peer, out_peer, gate_peer, up_peer, outer_land, middle_land, rights_peer,
+    x_out, h_one_out, proj_out, mixed_out, conv_out, gated_out, mixer_out, cot_out, act_out, dh_out, grads,
+    x_got, cot_got, x_full, h_one, cot_full, cot_peer, h_two, h_two_peer, proj, mixed, gated, mixer, conv_v,
+    out_v, rim, extended, away, pair, pair_got, both_got, dh_got,
+    da_got, in_v, gu_v, down_v, dh_sum, ffn_v, right_v, outer_v, middle_v, held, totals,
+    send, recv, local, in_send, outer_recv, middle_recv, out_send, out_recv, own_done,
 ):
     shard = lax.axis_index("shard")
     ctx = lax.axis_index("ctx")
@@ -371,8 +338,12 @@
         pieces["g%d" % index] = (gate_w.at[:, strip], gate_peer.at[:, strip])
         pieces["u%d" % index] = (up_w.at[:, strip], up_peer.at[:, strip])
 
+    direct = ["%s%d" % (kind, index) for kind in "gu" for index in range(2, CHUNKS)]
+
     def over_shard(name):
         source, target = pieces[name]
+        if name in direct:
+            return remote(name + "x", source, target, {"shard": 1 - shard})
         return remote(name + "x", source.at[own_rows], target.at[own_rows], {"shard": 1 - shard})
 
     def over_ctx(name):
@@ -390,9 +361,9 @@
     cot_deals = [deal("cot", cot_blocks, cot_got, step) for step in range(1, blocks)]
     for out, _ in x_deals:
         out.start()
-    for name in ("b", "v"):
+    for name in ("b", "v", "c", "o", "g0", "u0"):
         over_shard(name).start()
-    own_loads = [load(index, in_w.at[index], gu_v.at[1, 0, index]) for index in range(3)]
+    own_loads = [load(index, in_w.at[index], in_v.at[0, index]) for index in range(3)]
     own_loads.append(load(3, out_w, out_v.at[0]))
     own_loads.append(load(4, down_w, down_v))
     for copy in own_loads:
@@ -409,7 +380,6 @@
             full[index * block_rows : (index + 1) * block_rows, own_part] = total.astype(LOW)
 
     pump("b")
-    over_shard("c").start()
     packed(x_blocks, x_got, x_deals, x_full)
     x_outer, x_core, x_more = gather("xg", x_full)
     x_outer.start()
@@ -417,7 +387,6 @@
     for out, _ in cot_deals:
         out.start()
     pump("v")
-    over_shard("o").start()
     x_outer.wait_recv()
     x_more.start()
     packed(cot_blocks, cot_got, cot_deals, cot_full)
@@ -427,6 +396,8 @@
     x_core.wait_recv()
     x_more.wait_recv()
 
+    x_store = load(5, x_full, x_out)
+    x_store.start()
     step = min(64, tokens)
 
     @pl.loop(0, tokens // step)
@@ -436,8 +407,9 @@
         scale = lax.rsqrt(jnp.mean(value * value, axis=1, keepdims=True) + EPS)
         h_one[lines] = (value * scale * gains[0:1]).astype(LOW)
 
+    h_one_store = load(6, h_one, h_one_out)
+    h_one_store.start()
     pump("c")
-    over_shard("g0").start()
 
     def columns_out(name, full, got):
         strip = pl.ds(pl.multiple_of((1 - shard) * half + core * part, part), part)
@@ -456,7 +428,7 @@
             body(pl.ds(pl.multiple_of(index * tile, tile), tile))
 
     def project(column, name):
-        target = load(column, in_peer.at[column], gu_v.at[1, 1, column])
+        target = load(column, in_peer.at[column], in_v.at[1, column])
         own_loads[column].wait()
         over_ctx(name).wait_recv()
         target.start()
@@ -464,8 +436,8 @@
 
         def body(lines):
             proj[column, lines] = jnp.dot(
-                h_one[lines, own_half], gu_v[1, 0, column], preferred_element_type=WIDE
-            ) + jnp.dot(h_one[lines, peer_half], gu_v[1, 1, column], preferred_element_type=WIDE)
+                h_one[lines, own_half], in_v[0, column], preferred_element_type=WIDE
+            ) + jnp.dot(h_one[lines, peer_half], in_v[1, column], preferred_element_type=WIDE)
 
         over_tiles(body)
 
@@ -488,7 +460,6 @@
         rim_copy.start()
 
     pump("o")
-    over_shard("u0").start()
     cot_outer.wait_recv()
     cot_more.start()
     project(1, "c")
@@ -507,13 +478,22 @@
         value = taps[0:1] * extended[pl.ds(start + 8, tile)]
         value = value + taps[1:2] * (extended[pl.ds(start + 7, tile)] * first_mask[lines])
         value = value + taps[2:3] * (extended[pl.ds(start + 6, tile)] * second_mask[lines])
-        conv_out[lines] = value
+        conv_v[lines] = value
         gated[lines] = (proj[1, lines] * value).astype(LOW)
+
+    stores = [
+        load(7, proj, proj_out), load(8, mixed, mixed_out), load(9, conv_v, conv_out), load(10, gated, gated_out)
+    ]
+    for copy in stores:
+        copy.start()
 
     pump("g0")
     cot_core.wait_recv()
     cot_more.wait_recv()
     cot_first.start()
+    over_shard("g1").start()
+    cot_store = load(11, cot_full, cot_out)
+    cot_store.start()
     out_load = load(3, out_peer, out_v.at[1])
     own_loads[3].wait()
     over_ctx("o").wait_recv()
@@ -540,13 +520,13 @@
         pair[lines] = (value + pair_got[lines].astype(WIDE)).astype(LOW)
         hops[index][1].start()
 
+    da_send, da_own = h_one, x_full
     pump("u0")
-    over_shard("g1").start()
     cot_first.wait_recv()
-    over_shard("u1").start()
     cot_second.start()
     cot_second.wait_recv()
     own_loads[4].wait()
+    h_one_store.wait()
 
     def da_copy(index):
         strip = pl.ds(index * chunk, chunk)
@@ -561,24 +541,19 @@
             ).astype(LOW)
 
         over_tiles(send_part)
-    pump("g1")
-    da_copy(0).start()
-
-    def own_part_of(lines):
-        for index in range(CHUNKS):
-            strip = pl.ds(index * chunk, chunk)
-            da_own[lines, strip] = jnp.dot(
-                cot_full[lines, own_half], down_v[:, strip], preferred_element_type=WIDE
-            ).astype(LOW)
-
-    over_tiles(own_part_of)
+        if index == 0:
+            da_copy(0).start()
+            over_shard("u1").start()
 
     for index, lines in enumerate(stages):
         hops[index][1].wait_recv()
         mixer[core, lines] = (pair[lines].astype(WIDE) + both_got[lines].astype(WIDE)).astype(LOW)
         hops[index][2].start()
+    pump("g1")
     for index, lines in enumerate(stages):
         hops[index][2].wait_recv()
+    mixer_store = load(12, mixer, mixer_out)
+    mixer_store.start()
 
     @pl.loop(0, tokens // step)
     def _(index):
@@ -591,133 +566,391 @@
         h_two[lines, peer_half] = (other * scale * gains[1:2, peer_half]).astype(LOW)
 
     h_two_first, h_two_second = columns_out("hc", h_two, h_two_peer)
-    h_one_first, h_one_second = columns_out("ic", h_one, h_one_peer)
-    pump("u1")
-    da_copy(1).start()
-    later = {0: [over_shard("g2")], 1: [over_shard("u2")], 2: [over_shard("u3")], 3: [h_one_first]}
+    x_store.wait()
+    for copy in (x_outer, x_core, x_more):
+        copy.wait_send()
+
+    def own_part_of(lines):
+        for index in range(CHUNKS):
+            strip = pl.ds(index * chunk, chunk)
+            da_own[lines, strip] = jnp.dot(
+                cot_full[lines, own_half], down_v[:, strip], preferred_element_type=WIDE
+            ).astype(LOW)
+
+    over_tiles(own_part_of)
+
+    def turned(place_of, source, start, first):
+        for row in range(0, half, 256):
+            for line in range(0, tokens, 256):
+                block = source[pl.ds(line, 256), pl.ds(pl.multiple_of(start + row, 256), 256)]
+                down_v[pl.ds(row, 256), pl.ds(place_of * half + first + line, 256)] = block.T
+
+    turned(0, cot_full, shard * half, 0)
+    turned(0, cot_peer, 0, tokens)
+    turned(1, h_two, shard * half, 0)
 
     def own_weights(index):
         strip = pl.ds(index * chunk, chunk)
-        slot = index % 2
+        room = gu_v if index % 2 == 0 else in_v
+        base = 13 + 4 * (index % 2)
         return [
-            load(5 + 4 * slot, gate_w.at[:, strip], gu_v.at[slot, 0, 0]),
-            load(6 + 4 * slot, up_w.at[:, strip], gu_v.at[slot, 0, 1]),
+            load(base, gate_w.at[:, strip], room.at[0, 0]),
+            load(base + 1, up_w.at[:, strip], room.at[0, 1]),
         ]
 
     def peer_weights(index):
         strip = pl.ds(index * chunk, chunk)
-        slot = index % 2
+        room = gu_v if index % 2 == 0 else in_v
+        base = 15 + 4 * (index % 2)
         return [
-            load(7 + 4 * slot, gate_peer.at[:, strip], gu_v.at[slot, 1, 0]),
-            load(8 + 4 * slot, up_peer.at[:, strip], gu_v.at[slot, 1, 1]),
+            load(base, gate_peer.at[:, strip], room.at[1, 0]),
+            load(base + 1, up_peer.at[:, strip], room.at[1, 1]),
         ]
 
-    def results(index):
-        slot = index % 2
-        return [
-            load(13 + 3 * slot + kind, ffn_v.at[slot, kind], acts.at[:, pl.ds(kind * hidden + index * chunk, chunk)])
-            for kind in range(3)
-        ]
-
-    for copy in own_weights(0):
-        copy.start()
-    for index in range(CHUNKS):
-        slot = index % 2
-        over_ctx("g%d" % index).wait_recv()
-        over_ctx("u%d" % index).wait_recv()
+    def act_store(index):
+        return load(21 + index % 2, ffn_v.at[index % 2, 0], act_out.at[:, pl.ds(index * chunk, chunk)])
+
+    def right_copy(index, kind):
+        strip = pl.ds(kind * hidden + index * chunk, chunk)
+        return remote(
+            "r%d%d" % (index, kind), ffn_v.at[index % 2, kind], rights_peer.at[:, strip], {"shard": 1 - shard}
+        )
+
+    def right_load(index, kind):
+        strip = pl.ds(kind * hidden + index * chunk, chunk)
+        return load(23 + kind, rights_peer.at[:, strip], right_v.at[kind])
+
+    def ready(index):
+        for kind in "gu":
+            if "%s%d" % (kind, index) not in direct:
+                over_ctx("%s%d" % (kind, index)).wait_recv()
         for copy in peer_weights(index):
             copy.start()
+
+    def feed(index, lines):
+        room = gu_v if index % 2 == 0 else in_v
+        slot = index % 2
+        strip = pl.ds(index * chunk, chunk)
+
+        def pre(kind):
+            return jnp.dot(
+                h_two[lines, own_half], room[0, kind], preferred_element_type=WIDE
+            ) + jnp.dot(h_two[lines, peer_half], room[1, kind], preferred_element_type=WIDE)
+
+        gate_pre, up_pre = pre(0), pre(1)
+        d_act = da_own[lines, strip].astype(WIDE) + da_got[lines, strip].astype(WIDE)
+        sigmoid = jax.nn.sigmoid(gate_pre)
+        silu = gate_pre * sigmoid
+        ffn_v[slot, 0, lines] = (silu * up_pre).astype(LOW)
+        ffn_v[slot, 1, lines] = (
+            d_act * up_pre * sigmoid * (1.0 + gate_pre * (1.0 - sigmoid))
+        ).astype(LOW)
+        ffn_v[slot, 2, lines] = (d_act * silu).astype(LOW)
+
+    def back(index, lines):
+        room = gu_v if index % 2 == 0 else in_v
+        slot = index % 2
+        for place_of in range(2):
+            term = lax.dot_general(
+                ffn_v[slot, 1, lines], room[place_of, 0],
+                (((1,), (1,)), ((), ())), preferred_element_type=WIDE,
+            ) + lax.dot_general(
+                ffn_v[slot, 2, lines], room[place_of, 1],
+                (((1,), (1,)), ((), ())), preferred_element_type=WIDE,
+            )
+            if index > 0:
+                term = term + dh_sum[place_of, lines]
+            dh_sum[place_of, lines] = term
+
+    def feed_start(index):
+        da_copy(index).wait_recv()
+        for copy in own_weights(index) + peer_weights(index):
+            copy.wait()
+        if index > 1:
+            act_store(index - 2).wait()
+            for kind in range(3):
+                right_copy(index - 2, kind).wait_send()
+
+    middle = jnp.logical_or(ctx == 1, ctx == 2)
+    end = jnp.logical_not(middle)
+    inward = jnp.where(ctx < 2, ctx + 1, ctx - 1)
+    outward = jnp.where(ctx == 1, 0, 3)
+    per_kind = chunk // PIECE
+    per_chunk = 3 * per_kind
+    line_rows = min(256, rows)
+
+    def grad_columns(piece):
+        index, turn = piece // per_chunk, piece % per_chunk
+        kind, sub = turn // per_kind, turn % per_kind
+        return pl.ds(pl.multiple_of(kind * hidden + index * chunk + sub * PIECE, PIECE), PIECE)
+
+    def inward_copy(piece, land, sems):
+        return pltpu.make_async_remote_copy(
+            src_ref=held.at[piece % SLOTS], dst_ref=land.at[piece], send_sem=in_send.at[piece],
+            recv_sem=sems.at[piece], device_id={"ctx": inward}, device_id_type=MESH,
+        )
+
+    def outward_copy(piece):
+        return pltpu.make_async_remote_copy(
+            src_ref=totals.at[piece % SLOTS], dst_ref=grads.at[:, grad_columns(piece)], send_sem=out_send.at[piece],
+            recv_sem=out_recv.at[piece], device_id={"ctx": outward}, device_id_type=MESH,
+        )
+
+    def total_store(piece):
+        return pltpu.make_async_copy(totals.at[piece % SLOTS], grads.at[:, grad_columns(piece)], own_done.at[piece])
+
+    def stage_in(piece, land, room):
+        copy = pltpu.make_async_copy(land.at[piece], room, local.at[26])
+        copy.start()
+        copy.wait()
+
+    def finish(piece):
+        inward_copy(piece, middle_land, middle_recv).wait_recv()
+        stage_in(piece, middle_land, middle_v)
+
+        @pl.when(piece >= SLOTS)
+        def _():
+            outward_copy(piece - SLOTS).wait_send()
+            total_store(piece - SLOTS).wait()
+
+        @pl.loop(0, rows // line_rows)
+        def _(start):
+            lines = pl.ds(pl.multiple_of(start * line_rows, line_rows), line_rows)
+            total = held[piece % SLOTS, lines].astype(WIDE) + middle_v[lines].astype(WIDE)
+            totals[piece % SLOTS, lines] = total.astype(LOW)
+
+        outward_copy(piece).start()
+        total_store(piece).start()
+
+    def grad_piece(piece):
+        index, turn = piece // per_chunk, piece % per_chunk
+        kind, sub = turn // per_kind, turn % per_kind
+        strip = pl.ds(pl.multiple_of(sub * PIECE, PIECE), PIECE)
+        left = jnp.where(kind == 0, 0, half)
+
+        @pl.when(piece >= SLOTS)
+        def _():
+            inward_copy(piece - SLOTS, outer_land, outer_recv).wait_send()
+
+        def product(start):
+            lines = pl.ds(pl.multiple_of(start * line_rows, line_rows), line_rows)
+            own = jnp.dot(
+                down_v[lines, pl.ds(pl.multiple_of(left, tokens), tokens)],
+                ffn_v[index % 2, kind, :, strip],
+                preferred_element_type=WIDE,
+            )
+            other = jnp.dot(
+                down_v[lines, pl.ds(pl.multiple_of(left + tokens, tokens), tokens)],
+                right_v[kind, :, strip],
+                preferred_element_type=WIDE,
+            )
+            return lines, own + other
+
+        @pl.when(end)
+        def _():
+            @pl.loop(0, rows // line_rows)
+            def _(start):
+                lines, value = product(start)
+                held[piece % SLOTS, lines] = value.astype(LOW)
+
+            inward_copy(piece, outer_land, outer_recv).start()
+
+        @pl.when(middle)
+        def _():
+            inward_copy(piece, outer_land, outer_recv).wait_recv()
+            stage_in(piece, outer_land, outer_v)
+
+            @pl.loop(0, rows // line_rows)
+            def _(start):
+                lines, value = product(start)
+                held[piece % SLOTS, lines] = (value + outer_v[lines].astype(WIDE)).astype(LOW)
+
+            inward_copy(piece, middle_land, middle_recv).start()
+
+            @pl.when(piece >= 1)
+            def _():
+                finish(piece - 1)
+
+    def got_right(index, kind):
+        right_copy(index, kind).wait_recv()
+        copy = right_load(index, kind)
+        copy.start()
+        copy.wait()
+
+    dh_away = remote("dh1", away, pair_got, {"tp": core_mate})
+    dh_pair = remote("dh2", pair, dh_got, {"tp": outer_mate})
+    dh_last = remote("dh3", mixer.at[core], mixer.at[core], {"tp": core_mate})
+    tiles = [pl.ds(start, tile) for start in range(0, tokens, tile)]
+
+    def whole_feed(index):
+        feed_start(index)
+        for lines in tiles:
+            feed(index, lines)
+        act_store(index).start()
+
+    def whole_back(index):
+        for lines in tiles:
+            back(index, lines)
         if index + 1 < CHUNKS:
             for copy in own_weights(index + 1):
                 copy.start()
-        da_copy(index).wait_recv()
-        for copy in later[index]:
-            copy.start()
-        for copy in own_weights(index) + peer_weights(index):
-            copy.wait()
-        if index > 1:
-            for copy in results(index - 2):
-                copy.wait()
-        strip = pl.ds(index * chunk, chunk)
-
-        def feed(lines):
-            def pre(kind):
-                return jnp.dot(
-                    h_two[lines, own_half], gu_v[slot, 0, kind], preferred_element_type=WIDE
-                ) + jnp.dot(h_two[lines, peer_half], gu_v[slot, 1, kind], preferred_element_type=WIDE)
-
-            gate_pre, up_pre = pre(0), pre(1)
-            d_act = da_own[lines, strip].astype(WIDE) + da_got[lines, strip].astype(WIDE)
-            sigmoid = jax.nn.sigmoid(gate_pre)
-            silu = gate_pre * sigmoid
-            ffn_v[slot, 0, lines] = (silu * up_pre).astype(LOW)
-            ffn_v[slot, 1, lines] = (
-                d_act * up_pre * sigmoid * (1.0 + gate_pre * (1.0 - sigmoid))
-            ).astype(LOW)
-            ffn_v[slot, 2, lines] = (d_act * silu).astype(LOW)
-
-        over_tiles(feed)
-        for copy in results(index):
-            copy.start()
-        if index == 1:
-            pump("g2")
-            da_copy(2).start()
-            pump("u2")
-            over_shard("g3").start()
-        if index == 2:
-            pump("g3")
-            da_copy(3).start()
-            pump("u3")
-            h_two_first.start()
-
-        def back(lines):
-            for place_of in range(2):
-                term = lax.dot_general(
-                    ffn_v[slot, 1, lines], gu_v[slot, place_of, 0],
-                    (((1,), (1,)), ((), ())), preferred_element_type=WIDE,
-                ) + lax.dot_general(
-                    ffn_v[slot, 2, lines], gu_v[slot, place_of, 1],
-                    (((1,), (1,)), ((), ())), preferred_element_type=WIDE,
-                )
-                if index > 0:
-                    term = term + dh_sum[place_of, lines]
-                if index + 1 < CHUNKS:
-                    dh_sum[place_of, lines] = term
-                else:
-                    dh_two[place_of, lines] = term.astype(LOW)
-
-        over_tiles(back)
-
-    h_two_first.wait_recv()
-    h_two_second.start()
-    h_one_first.wait_recv()
-    h_one_second.start()
-    for index in (CHUNKS - 2, CHUNKS - 1):
-        for copy in results(index):
-            copy.wait()
-    h_two_second.wait_recv()
-    h_one_second.wait_recv()
+
+    for copy in own_weights(0):
+        copy.start()
+    ready(0)
+    whole_feed(0)
+    right_copy(0, 0).start()
+    da_copy(1).start()
+    h_two_first.start()
+    right_copy(0, 1).start()
+    right_copy(0, 2).start()
+    whole_back(0)
+    pump("u1")
+
+    def event_start():
+        got_right(0, 0)
+
+    def event_first():
+        ready(1)
+        whole_feed(1)
+        for kind in range(3):
+            right_copy(1, kind).start()
+        for name in ("g2", "u2"):
+            over_shard(name).start()
+        da_copy(2).start()
+        over_shard("g3").start()
+        h_two_first.wait_recv()
+        h_two_second.start()
+        h_two_second.wait_recv()
+        turned(1, h_two_peer, 0, tokens)
+        got_right(0, 1)
+
+    def event_second():
+        over_shard("g2").wait_recv()
+        over_shard("u2").wait_recv()
+        ready(2)
+        whole_feed(2)
+        right_copy(2, 0).start()
+        right_copy(2, 1).start()
+        over_shard("u3").start()
+        da_copy(3).start()
+        right_copy(2, 2).start()
+        got_right(1, 2)
+
+    def event_third():
+        over_shard("g3").wait_recv()
+        over_shard("u3").wait_recv()
+        ready(3)
+        whole_feed(3)
+        for kind in range(3):
+            right_copy(3, kind).start()
+        got_right(2, 2)
+
+    def dh_one_hop():
+        whole_back(3)
+        mixer_store.wait()
+        for trio in hops:
+            for copy in trio:
+                copy.wait_send()
+
+        def body(lines):
+            away[lines] = dh_sum[1 - core, lines].astype(LOW)
+
+        over_tiles(body)
+        dh_away.start()
+
+    def dh_two_hops():
+        dh_away.wait_recv()
+
+        def body(lines):
+            pair[lines] = (dh_sum[core, lines] + pair_got[lines].astype(WIDE)).astype(LOW)
+
+        over_tiles(body)
+        dh_pair.start()
+        got_right(3, 0)
+
+    def dh_three_hops():
+        dh_pair.wait_recv()
+
+        def body(lines):
+            mixer[core, lines] = (pair[lines].astype(WIDE) + dh_got[lines].astype(WIDE)).astype(LOW)
+
+        over_tiles(body)
+        dh_last.start()
+        got_right(3, 1)
+
+    events = {
+        0: event_start,
+        2: event_first,
+        3: lambda: whole_back(1),
+        4: lambda: got_right(0, 2),
+        6: lambda: got_right(1, 0),
+        8: lambda: got_right(1, 1),
+        10: event_second,
+        11: lambda: whole_back(2),
+        12: lambda: got_right(2, 0),
+        14: lambda: got_right(2, 1),
+        16: event_third,
+        17: dh_one_hop,
+        18: dh_two_hops,
+        20: dh_three_hops,
+        22: lambda: got_right(3, 2),
+    }
+    pieces_in_all = CHUNKS * per_chunk
+
+    @pl.loop(0, pieces_in_all)
+    def _(piece):
+        for turn, event in events.items():
+            pl.when(piece == turn)(event)
+        grad_piece(piece)
+
+    @pl.when(middle)
+    def _():
+        finish(pieces_in_all - 1)
+
+    dh_last.wait_recv()
+    dh_store = load(27, mixer, dh_out)
+    dh_store.start()
 
     for out, _ in x_deals + cot_deals:
         out.wait_send()
-    for copy in (x_outer, x_core, x_more, cot_outer, cot_core, cot_more, cot_first, cot_second,
-                 h_two_first, h_two_second, h_one_first, h_one_second):
+    for copy in (cot_outer, cot_core, cot_more, cot_first, cot_second, h_two_first, h_two_second,
+                 dh_away, dh_pair, dh_last):
         copy.wait_send()
     for name in pieces:
         over_shard(name).wait_send()
-        over_ctx(name).wait_send()
+        if name not in direct:
+            over_ctx(name).wait_send()
     for index in range(CHUNKS):
         da_copy(index).wait_send()
-    for trio in hops:
-        for copy in trio:
-            copy.wait_send()
+    for index in (CHUNKS - 2, CHUNKS - 1):
+        act_store(index).wait()
+        for kind in range(3):
+            right_copy(index, kind).wait_send()
+    for copy in stores + [cot_store, dh_store]:
+        copy.wait()
 
     @pl.when(ctx < blocks - 1)
     def _():
         rim_copy.wait_send()
 
-
-FRONT_COPIES = 64
+    @pl.loop(0, pieces_in_all)
+    def _(piece):
+        @pl.when(piece >= pieces_in_all - SLOTS)
+        def _():
+            inward_copy(piece, outer_land, outer_recv).wait_send()
+
+            @pl.when(middle)
+            def _():
+                outward_copy(piece).wait_send()
+                total_store(piece).wait()
+
+        @pl.when(end)
+        def _():
+            outward_copy(piece).wait_recv()
+
+
+FRONT_COPIES = 72
 
 
 def front(x_blocks, cot_blocks, place, gains, first_mask, second_mask, taps, in_w, out_w, gate_w, up_w, down_w):
@@ -727,33 +960,46 @@
     half = width // 2
     rows, hidden = gate_w.shape
     chunk = hidden // CHUNKS
+    pieces = 3 * hidden // PIECE
     vmem = pl.BlockSpec(memory_space=pltpu.VMEM)
     hbm = pl.BlockSpec(memory_space=pl.ANY)
     shape = jax.ShapeDtypeStruct
     outs = [
-        (shape(in_w.shape, LOW), hbm),
-        (shape(out_w.shape, LOW), hbm),
-        (shape(gate_w.shape, LOW), hbm),
-        (shape(up_w.shape, LOW), hbm),
-        (shape((tokens, width), LOW), vmem),
-        (shape((tokens, width), LOW), vmem),
-        (shape((3, tokens, part), WIDE), vmem),
-        (shape((tokens, part), LOW), vmem),
-        (shape((tokens, part), WIDE), vmem),
-        (shape((tokens, part), LOW), vmem),
-        (shape((2, tokens, half), LOW), vmem),
-        (shape((tokens, width), LOW), vmem),
-        (shape((tokens, width), LOW), vmem),
-        (shape((tokens, half), LOW), vmem),
-        (shape((tokens, half), LOW), vmem),
-        (shape((tokens, half), LOW), vmem),
-        (shape((tokens, 3 * hidden), LOW), hbm),
-        (shape((2, tokens, half), LOW), vmem),
+        shape(in_w.shape, LOW),
+        shape(out_w.shape, LOW),
+        shape(gate_w.shape, LOW),
+        shape(up_w.shape, LOW),
+        shape((pieces, rows, PIECE), LOW),
+        shape((pieces, rows, PIECE), LOW),
+        shape((tokens, 3 * hidden), LOW),
+        shape((tokens, width), LOW),
+        shape((tokens, width), LOW),
+        shape((3, tokens, part), WIDE),
+        shape((tokens, part), LOW),
+        shape((tokens, part), WIDE),
+        shape((tokens, part), LOW),
+        shape((2, tokens, half), LOW),
+        shape((tokens, width), LOW),
+        shape((tokens, hidden), LOW),
+        shape((2, tokens, half), LOW),
+        shape((rows, 3 * hidden), LOW),
     ]
     low, wide = (lambda *dims: pltpu.VMEM(dims, LOW)), (lambda *dims: pltpu.VMEM(dims, WIDE))
+    dma = pltpu.SemaphoreType.DMA
     scratch = [
         low(*x_blocks.shape),
         low(*x_blocks.shape),
+        low(tokens, width),
+        low(tokens, width),
+        low(tokens, width),
+        low(tokens, half),
+        low(tokens, width),
+        low(tokens, half),
+        wide(3, tokens, part),
+        low(tokens, part),
+        low(tokens, part),
+        low(2, tokens, half),
+        wide(tokens, part),
         low(2, rows, part),
         low(16, part),
         wide(tokens + 8, part),
@@ -761,23 +1007,28 @@
         low(tokens, half),
         low(tokens, half),
         low(tokens, half),
+        low(tokens, half),
         low(tokens, hidden),
-        low(tokens, hidden),
-        low(tokens, hidden),
-        low(2, 2, 3, rows, chunk),
+        low(2, 3, rows, part),
+        low(2, 2, rows, chunk),
         low(rows, hidden),
         wide(2, tokens, half),
         low(2, 3, tokens, chunk),
-        pltpu.SemaphoreType.DMA((FRONT_COPIES,)),
-        pltpu.SemaphoreType.DMA((FRONT_COPIES,)),
-        pltpu.SemaphoreType.DMA((24,)),
-    ]
+        low(3, tokens, chunk),
+        low(rows, PIECE),
+        low(rows, PIECE),
+        low(SLOTS, rows, PIECE),
+        low(SLOTS, rows, PIECE),
+        dma((FRONT_COPIES,)),
+        dma((FRONT_COPIES,)),
+        dma((28,)),
+    ] + [dma((pieces,)) for _ in range(6)]
     return pl.pallas_call(
         front_kernel,
-        out_shape=[value for value, _ in outs],
+        out_shape=outs,
         in_specs=[vmem, vmem, pl.BlockSpec(memory_space=pltpu.SMEM), vmem, vmem, vmem, vmem]
         + [hbm] * 5,
-        out_specs=[spec for _, spec in outs],
+        out_specs=[hbm for _ in outs],
         scratch_shapes=scratch,
         compiler_params=pltpu.CompilerParams(
             collective_id=2, has_side_effects=True, vmem_limit_bytes=63 * 1024 * 1024
@@ -951,20 +1202,19 @@
         )
         return reorder(got, returning)
 
-    def weight_grads(lefts, rights, identity, more=None):
+    def weight_grads(lefts, rights, identity):
         flat = [value for group in rights for value in group]
         if shards.paired:
-            got = line_grads([group[0] for group in lefts], flat, identity, more)
+            summed = line_grads([group[0] for group in lefts], flat, identity)
             ends = [0]
             for value in flat:
                 ends.append(ends[-1] + value.shape[1])
-            return [got[0][:, a:b] for a, b in zip(ends, ends[1:])], (more,) + tuple(got[1:])
+            return [summed[:, a:b] for a, b in zip(ends, ends[1:])]
         flat_lefts = [value for group in lefts for value in group]
-        sums = [
+        return [
             sum_line(contract_rows(left, shards.tokens(right)).astype(LOW), ctx_rank)
             for left, right in zip(flat_lefts, flat)
         ]
-        return sums, shards.weight(more) if more is not None else ()
 
     lengths = seq_lengths[0]
     starts = jnp.cumsum(lengths) - lengths
@@ -986,8 +1236,8 @@
 
         place = (targets[None, :] == jnp.arange(per_dev)[:, None]).astype(WIDE)
         (
-            in_peer, out_peer, _, _, x_full, h_one, proj, mixed, conv_out, gated, mixer, h_two, cot_full,
-            cot_peer, h_two_peer, h_one_peer, acts, dh_two_halves,
+            in_peer, out_peer, _, _, _, _, rights_peer, x_full, h_one, proj, mixed, conv_out, gated, mixer,
+            cot_full, act, dh_halves, ffn_sums,
         ) = front(
             blocks_of(hidden_in), blocks_of(out_grad), place, gains, first_own, second_own, conv_taps,
             in_parts, out_weight, gate_weight, up_weight, down_weight,
@@ -996,11 +1246,10 @@
         in_w = [jnp.concatenate([w[0], w[1], w[2]], axis=1) for w in (in_parts, in_peer)]
         out_w = (out_weight, out_peer)
         mixer_out = shards.join([mixer[0], mixer[1]])
-        cot_cols = jnp.concatenate([shards.split(cot_full)[0], cot_peer], axis=0)
-        h_two_cols = jnp.concatenate([shards.split(h_two)[0], h_two_peer], axis=0)
-        h_one_cols = jnp.concatenate([shards.split(h_one)[0], h_one_peer], axis=0)
-        ffn_rights = [acts[:, kind * hidden_count : (kind + 1) * hidden_count] for kind in range(3)]
-        dh_parts = [dh_two_halves[0], dh_two_halves[1]]
+        h_one_cols = shards.columns(h_one)
+        dh_two = shards.join([dh_halves[0], dh_halves[1]]).astype(WIDE)
+        act_all = jnp.concatenate([act, rights_peer[:, :hidden_count]], axis=0)
+        ffn_grads = [ffn_sums[:, kind * hidden_count : (kind + 1) * hidden_count] for kind in range(3)]
         x_float = x_full.astype(WIDE)
         scale_one = lax.rsqrt(jnp.mean(x_float * x_float, axis=1, keepdims=True) + EPS)
         normed_one = x_float * scale_one
@@ -1043,15 +1292,16 @@
         silu_gate = gate_pre * sigmoid_gate
         d_gate = d_act * up_pre * sigmoid_gate * (1.0 + gate_pre * (1.0 - sigmoid_gate))
         ffn_rights = [v.astype(LOW) for v in (silu_gate * up_pre, d_gate, d_act * silu_gate)]
-        dh_parts = [contract_cols(ffn_rights[1], gate_w[0]) + contract_cols(ffn_rights[2], up_w[0])]
-
-    dh_terms = tp.all_terms(shards.join(dh_parts))
-    ffn_grads, down_w = weight_grads(
-        [[cot_cols], [h_two_cols, h_two_cols]], [ffn_rights[:1], ffn_rights[1:]], 0, down_weight
-    )
-    dh_terms, down_w, ffn_grads = lax.optimization_barrier((dh_terms, down_w, ffn_grads))
-    dh_two = added(dh_terms)
-    ffn_terms = tp.own_terms(shards.join([contract_cols(ffn_rights[0], w) for w in down_w]))
+        act_all = shards.tokens(ffn_rights[0])
+        dh_terms = tp.all_terms(
+            contract_cols(ffn_rights[1], gate_w[0]) + contract_cols(ffn_rights[2], up_w[0])
+        )
+        dh_two = added(dh_terms)
+        ffn_grads = weight_grads(
+            [[cot_cols], [h_two_cols, h_two_cols]], [ffn_rights[:1], ffn_rights[1:]], 0
+        )
+
+    ffn_terms = tp.own_terms(shards.own_tokens(contract_cols(act_all, down_weight)))
 
     rim = shifted(mixed[-2:], "ctx", 1)
     extended = jnp.concatenate([rim, mixed], axis=0).astype(WIDE)
@@ -1087,7 +1337,7 @@
     ]
     d_proj_flat = jnp.concatenate(d_proj, axis=1)
     dh_one_terms = tp.all_terms(shards.join([contract_cols(d_proj_flat, w) for w in in_w]))
-    mixer_grads, _ = weight_grads(
+    mixer_grads = weight_grads(
         [[shards.columns(d_resid_low)], [h_one_cols]], [[gated], [d_proj_flat]], 1
     )
     dh_one_terms, ffn_terms, mixer_grads = lax.optimization_barrier(

time: 880 us -> 797 us (0.906)
  Pallas kernels: 675 us -> 608 us
  local copies, waits for them, and re-layouts: 79.5 us -> 59.5 us
  waiting for transfers between devices: 9.92 us -> 27.8 us
  other arithmetic: 66.9 us -> 54.8 us
    pallas_call x3 -> x2, Pallas kernels: 675 us -> 608 us  [the longest x1 480 us: front(): pl.pallas_call(front_kernel, out_shape=outs, in_specs=[vmem, vmem, pl.Blo...]
    ppermute x16, waiting for transfers between devices: 9.92 us -> 24.2 us  [swapped(): lax.ppermute(value, axis, [(source, source ^ step) for source in range(co...]
    pallas_call x9 -> x5, local copies, waits for them, and re-layouts: 26.9 us -> 17.2 us  [front(): pl.pallas_call(front_kernel, out_shape=outs, in_specs=[vmem, vmem, pl.Blo...]
  transfers between devices with their start and end apart: 19 -> 19, of which waited for: 3 -> 4; matrix products, arithmetic and copies ran while one was open for 14% -> 14% of each run, Pallas kernels for 51% -> 16%
where the time goes in v4:
time: 797 us; the launch traced here: 790 us
  Pallas kernels  608 us (76%)
  local copies, waits for them, and re-layouts  59.5 us (7%)
  other arithmetic  54.8 us (7%)
  waiting for transfers between devices  27.8 us (3%)
  starting transfers between devices  24.6 us (3%)
  matrix products  13.3 us (2%)
    pallas_call x1, Pallas kernels, front(): pl.pallas_call(front_kernel, out_shape=outs, in_specs=[vmem, vmem, pl.Blo...  480 us
    pallas_call x1, Pallas kernels, line_grads(): pl.pallas_call(functools.partial(line_kernel, pieces, left_of), out_shape...  129 us
    ppermute x16, waiting for transfers between devices, swapped(): lax.ppermute(value, axis, [(source, source ^ step) for source in range(co...  24.2 us
    ppermute x16, starting transfers between devices, swapped(): lax.ppermute(value, axis, [(source, source ^ step) for source in range(co...  18 us
    pallas_call x5, local copies, waits for them, and re-layouts, front(): pl.pallas_call(front_kernel, out_shape=outs, in_specs=[vmem, vmem, pl.Blo...  17.2 us
  transfers between devices with their start and end apart: 19, of which 4 were waited for; matrix products, arithmetic and copies ran while one was open for 14% of the time, Pallas kernels for 16%

profile of v4, /device:TPU:0, one launch (start us, length us, event | category | flops | bytes accessed | tf_op | source)
XLA Modules:
  0.0 790.0 jit_solution(191520534967061635)
XLA Ops:
  0.7 0.7 stack.36
  1.4 0.7 stack.37
  2.1 3.0 collective-permute-start
  5.6 1.3 reduce.3
  7.2 0.7 sort.51
  8.6 0.6 gather_fusion.4
  9.8 0.8 reduce-window_clone.1
  10.7 0.7 subtract_bitcast_fusion
  11.4 0.7 fusion.50
  12.1 1.4 fusion.67
  13.5 3.6 slice_bitcast_fusion.2
  18.4 1.4 gather_fusion
  19.8 1.4 gather_fusion.1
  21.2 0.9 copy.61.first_mask
  22.0 0.9 copy.62.second_mask
  22.9 0.8 sort.53
  24.4 479.5 %shard_map.195 = (bf16[3,1024,512]{2,1,0:T(8,128)(2,1)}, bf16[1024,512]{1,0:T(8,128)(2,1)}, bf16[1024,2048]{1,0:T(8,128)(2,1)}, bf16[1024,2048]{1,0:T(8,128)(2,1...) custom-call(bf16[4,128,512]{2,1,0:T(8,128)(2,1)} %gather_fusion, ...), custom_call_target="tpu_custom_call" | custom-call | flops 274877906944 | bytes 536870912 | tf_op jit(solution)/shard_map/pallas_call | solution.py:1026
  504.0 0.9 slice.177
  504.8 1.3 collective-permute-start.14
  506.2 3.9 copy.64
  510.1 2.5 copy.67
  512.7 2.9 copy.63
  515.5 2.5 select_bitcast_fusion.1
  518.0 0.8 multiply_reduce_fusion.2
  518.8 3.2 fusion.5
  522.1 3.9 copy.66
  526.0 6.1 fusion.62
  532.2 1.9 fusion.68
  534.1 0.9 constant_dynamic-slice_fusion.2
  535.6 3.9 copy.73
  539.5 1.3 constant_dynamic-slice_fusion
  540.8 1.6 collective-permute-start.12
  542.4 1.7 slice.169
  544.1 6.5 fusion.23
  551.7 0.8 copy-done.17
  553.2 0.9 copy-done.13
  554.7 1.2 fusion.30
  556.0 1.7 collective-permute-start.2
  557.9 3.6 collective-permute-done.2
  562.3 1.8 fusion.17
  564.1 1.8 select_convert_fusion.1
  567.3 1.6 pad_maximum_fusion.3.right_ref
  568.9 1.6 collective-permute-start.5
  570.6 1.1 collective-permute-done.13
  571.8 9.7 %collective-permute-done.6 = bf16[512,1024]{0,1:T(8,128)(2,1)S(1)} collective-permute-done((bf16[512,1024]{0,1:T(8,128)(2,1)S(1)}, bf16[512,1024]{0,1:T(8,128)(2,1)S(1)}, u32[]{:S(2)}, u32[]{:S(2)}) %collective-permute-start.6) | collective-permute-done | bytes 1048608 | tf_op jit(solution)/shard_map/ppermute | solution.py:24
  581.7 4.7 fusion.39
  587.0 2.4 pad_maximum_fusion.left_ref
  589.4 1.9 collective-permute-start.9
  591.2 128.8 %shard_map.196 = bf16[1024,2048]{1,0:T(8,128)(2,1)} custom-call(bf16[2,1024,1024]{2,1,0:T(8,128)(2,1)} %pad_maximum_fusion.left_ref, bf16[512,2048]{1,0:T(8,128)(2,1)} %pad_maximum_fusion.3.right_ref), custom_call_target="tpu_custom_call" | custom-call | flops 34359738368 | bytes 134217728 | tf_op jit(solution)/shard_map/pallas_call | solution.py:249
  720.0 3.7 slice.173
  723.8 6.5 multiply_reduce_fusion
  730.5 0.7 collective-permute-start.15
  731.2 2.2 fusion.31
  733.5 1.7 add_convert_fusion
  735.8 1.7 gather_fusion.2
  737.5 3.5 all-to-all-start
  741.1 2.1 collective-permute-start.16
  743.2 13.4 %collective-permute-done.16 = f32[5,512]{1,0:T(8,128)S(1)} collective-permute-done((f32[5,512]{1,0:T(8,128)S(1)}, f32[5,512]{1,0:T(8,128)S(1)}, u32[]{:S(2)}, u32[]{:S(2)}) %collective-permute-start.16) | collective-permute-done | bytes 10272 | tf_op jit(solution)/shard_map/ppermute | solution.py:24
  756.6 4.8 collective-permute-start.17
  761.4 11.8 %slice_convert_fusion = (f32[1024,2048]{1,0:T(8,128)}, f32[1024,2048]{1,0:T(8,128)}, f32[1024,2048]{1,0:T(8,128)}) fusion(bf16[1024,6144]{1,0:T(8,128)(2,1)} %get-tuple-element.63), kind=kLoop, calls=%fused_computation.22 | loop fusion | flops 6291456 | bytes 37748736 | tf_op jit(solution)/shard_map/convert_element_type | solution.py:1348
  773.3 5.4 copy.76
  778.7 6.7 copy.77
  785.4 1.6 convert_element_type.132
  788.8 1.0 fusion.64
  (171 shorter events, 12.6 us)
Async XLA Ops:
  0.6 17.8 %copy-start = (bf16[512,512]{1,0:T(8,128)(2,1)S(1)}, bf16[512,512]{1,0:T(8,128)(2,1)}, u32[]{:S(2)}) copy-start(bf16[512,512]{1,0:T(8,128)(2,1)} %param.12) | copy-start | bytes 1572868
  2.1 15.0 %collective-permute-start = (bf16[2,512]{1,0:T(2,128)(2,1)S(1)}, bf16[2,512]{1,0:T(2,128)(2,1)S(1)}, u32[]{:S(2)}, u32[]{:S(2)}) collective-permute-start(bf16[2,512]{1,0:T(2,128)(2,1)S(1)} %pad_maximum_fusion.9), channel_id=1, source_target_pairs={{0,2},{1,3},{2,0},{3,1},{4,6},{5,7},{6,4},{7,5},{8,10},{9,11},{10,... | collective-permute-start | bytes 6152 | tf_op jit(solution)/shard_map/ppermute | solution.py:24
  12.1 9.1 %copy-start.32 = (f32[512]{0:T(512)}, f32[512]{0:T(512)S(1)}, u32[]{:S(2)}) copy-start(f32[512]{0:T(512)S(1)} %get-tuple-element.152) | copy-start | bytes 6148
  12.1 10.0 %copy-start.30 = (f32[512]{0:T(512)}, f32[512]{0:T(512)S(1)}, u32[]{:S(2)}) copy-start(f32[512]{0:T(512)S(1)} %get-tuple-element.150) | copy-start | bytes 6148
  13.5 4.3 copy-start.27
  13.5 6.3 copy-start.18
  17.2 6.6 collective-permute-start.1
  23.8 0.6 copy-start.25
  504.0 6.2 copy-start.12
  504.8 46.8 %collective-permute-start.14 = (bf16[2,512]{1,0:T(2,128)(2,1)S(1)}, bf16[2,512]{1,0:T(2,128)(2,1)S(1)}, u32[]{:S(2)}, u32[]{:S(2)}) collective-permute-start(bf16[2,512]{1,0:T(2,128)(2,1)S(1)} %slice.177), channel_id=1, source_target_pairs={{0,4},{4,8},{8,12},{1,5},{5,9},{9,13},{2,6},{6,10},{10,14},{3,7},{... | collective-permute-start | bytes 6152 | tf_op jit(solution)/shard_map/ppermute | solution.py:19
  518.0 4.1 copy-start.2
  518.0 4.1 copy-start.3
  518.0 4.1 copy-start.4
  518.0 4.1 copy-start.5
  518.0 0.8 copy-start.24
  526.0 6.2 copy-start.38
  532.1 2.0 copy-start.6
  532.2 2.8 copy-start.9
  535.1 30.9 %collective-permute-start.10 = (bf16[512,512]{0,1:T(8,128)(2,1)}, bf16[512,512]{0,1:T(8,128)(2,1)S(1)}, u32[]{:S(2)}, u32[]{:S(2)}) collective-permute-start(bf16[512,512]{0,1:T(8,128)(2,1)} %constant_dynamic-slice_fusion.2), channel_id=1, source_target_pairs={{0,16},{16,0},{1,17},{17,1},{2,18},{18,2},{3,19},{19,3},{4,20},{20... | collective-permute-start | bytes 1572872 | tf_op jit(solution)/shard_map/ppermute | solution.py:24
  539.5 4.6 copy-start.37
  540.8 26.4 %collective-permute-start.12 = (bf16[512,512]{0,1:T(8,128)(2,1)S(1)}, bf16[512,512]{0,1:T(8,128)(2,1)S(1)}, u32[]{:S(2)}, u32[]{:S(2)}) collective-permute-start(bf16[512,512]{0,1:T(8,128)(2,1)S(1)} %constant_dynamic-slice_fusion), channel_id=1, source_target_pairs={{0,16},{16,0},{1,17},{17,1},{2,18},{18,2},{3,19},{19,3},{4,20},{20... | collective-permute-start | bytes 1572872 | tf_op jit(solution)/shard_map/ppermute | solution.py:24
  544.1 7.3 copy-start.11
  550.7 1.9 copy-start.42
  550.8 30.7 %collective-permute-start.6 = (bf16[512,1024]{0,1:T(8,128)(2,1)S(1)}, bf16[512,1024]{0,1:T(8,128)(2,1)S(1)}, u32[]{:S(2)}, u32[]{:S(2)}) collective-permute-start(bf16[512,1024]{0,1:T(8,128)(2,1)S(1)} %slice.216), channel_id=1, source_target_pairs={{0,16},{16,0},{1,17},{17,1},{2,18},{18,2},{3,19},{19,3},{4,20},{20... | collective-permute-start | bytes 3145736 | tf_op jit(solution)/shard_map/ppermute | solution.py:24
  551.4 1.0 copy-start.17
  551.4 1.8 copy-start.7
  551.4 2.8 copy-start.13
  551.4 2.8 copy-start.31
  551.4 2.7 copy-start.33
  551.4 3.0 copy-start.40
  551.4 3.3 copy-start.41
  554.7 3.0 copy-start.8
  555.9 5.7 copy-start.28
  556.0 5.7 copy-start.29
  556.0 5.7 copy-start.34
  556.0 5.7 copy-start.35
  556.0 5.7 copy-start.36
  556.0 5.5 collective-permute-start.2
  562.2 1.9 copy-start.14
  562.2 1.9 copy-start.15
  562.3 1.9 copy-start.16
  565.9 1.3 copy-start.23
  566.0 2.9 collective-permute-start.11
  566.2 157.6 %collective-permute-start.3 = (bf16[512,2048]{0,1:T(8,128)(2,1)S(1)}, bf16[512,2048]{0,1:T(8,128)(2,1)}, u32[]{:S(2)}, u32[]{:S(2)}) collective-permute-start(bf16[512,2048]{0,1:T(8,128)(2,1)S(1)} %pad_maximum_fusion.2), channel_id=1, source_target_pairs={{0,1},{1,0},{2,3},{3,2},{4,5},{5,4},{6,7},{7,6},{8,9},{9,8},{10,11... | collective-permute-start | bytes 6291464 | tf_op jit(solution)/shard_map/ppermute | solution.py:24
  566.7 157.1 %collective-permute-start.4 = (bf16[512,2048]{0,1:T(8,128)(2,1)S(1)}, bf16[512,2048]{0,1:T(8,128)(2,1)}, u32[]{:S(2)}, u32[]{:S(2)}) collective-permute-start(bf16[512,2048]{0,1:T(8,128)(2,1)S(1)} %pad_maximum_fusion.2), channel_id=1, source_target_pairs={{0,2},{1,3},{2,0},{3,1},{4,6},{5,7},{6,4},{7,5},{8,10},{9,11},{10,... | collective-permute-start | bytes 6291464 | tf_op jit(solution)/shard_map/ppermute | solution.py:24
  567.2 4.4 collective-permute-start.13
  568.9 154.9 %collective-permute-start.5 = (bf16[512,2048]{0,1:T(8,128)(2,1)S(1)}, bf16[512,2048]{0,1:T(8,128)(2,1)}, u32[]{:S(2)}, u32[]{:S(2)}) collective-permute-start(bf16[512,2048]{0,1:T(8,128)(2,1)S(1)} %pad_maximum_fusion.2), channel_id=1, source_target_pairs={{0,3},{1,2},{2,1},{3,0},{4,7},{5,6},{6,5},{7,4},{8,11},{9,10},{10,... | collective-permute-start | bytes 6291464 | tf_op jit(solution)/shard_map/ppermute | solution.py:24
  581.7 4.7 copy-start.10
  586.3 3.0 collective-permute-start.7
  589.4 134.4 %collective-permute-start.8 = (bf16[512,512]{0,1:T(8,128)(2,1)}, bf16[512,512]{0,1:T(8,128)(2,1)S(1)}, u32[]{:S(2)}, u32[]{:S(2)}) collective-permute-start(bf16[512,512]{0,1:T(8,128)(2,1)} %get-tuple-element.126), channel_id=1, source_target_pairs={{0,2},{1,3},{2,0},{3,1},{4,6},{5,7},{6,4},{7,5},{8,10},{9,11},{10,... | collective-permute-start | bytes 1572872 | tf_op jit(solution)/shard_map/ppermute | solution.py:24
  589.4 134.4 %collective-permute-start.9 = (bf16[512,512]{0,1:T(8,128)(2,1)}, bf16[512,512]{0,1:T(8,128)(2,1)S(1)}, u32[]{:S(2)}, u32[]{:S(2)}) collective-permute-start(bf16[512,512]{0,1:T(8,128)(2,1)} %get-tuple-element.123), channel_id=1, source_target_pairs={{0,3},{1,2},{2,1},{3,0},{4,7},{5,6},{6,5},{7,4},{8,11},{9,10},{10,... | collective-permute-start | bytes 1572872 | tf_op jit(solution)/shard_map/ppermute | solution.py:24
  720.0 3.8 copy-start.26
  723.8 6.6 copy-start.19
  723.8 6.6 copy-start.21
  730.3 3.1 copy-start.20
  730.3 3.1 copy-start.22
  730.5 10.6 %collective-permute-start.15 = (f32[5,512]{1,0:T(8,128)S(1)}, f32[5,512]{1,0:T(8,128)S(1)}, u32[]{:S(2)}, u32[]{:S(2)}) collective-permute-start(f32[5,512]{1,0:T(8,128)S(1)} %concatenate.73), channel_id=1, source_target_pairs={{0,16},{16,0},{1,17},{17,1},{2,18},{18,2},{3,19},{19,3},{4,20},{20... | collective-permute-start | bytes 30728 | tf_op jit(solution)/shard_map/ppermute | solution.py:24
  735.3 5.8 copy-start.39
  737.5 50.6 %all-to-all-start = ((bf16[4,128,1024]{2,1,0:T(8,128)(2,1)}), bf16[4,128,1024]{2,1,0:T(8,128)(2,1)S(1)}, u32[]{:S(2)}, u32[]{:S(2)}) async-start(bf16[4,128,1024]{2,1,0:T(8,128)(2,1)} %gather_fusion.2), calls=%async_computation | async-start | bytes 2097152 | tf_op jit(solution)/shard_map/all_to_all | solution.py:1200
  741.1 15.5 %collective-permute-start.16 = (f32[5,512]{1,0:T(8,128)S(1)}, f32[5,512]{1,0:T(8,128)S(1)}, u32[]{:S(2)}, u32[]{:S(2)}) collective-permute-start(f32[5,512]{1,0:T(8,128)S(1)} %add.174), channel_id=1, source_target_pairs={{0,4},{4,0},{8,12},{12,8},{1,5},{5,1},{9,13},{13,9},{2,6},{6,2},{1... | collective-permute-start | bytes 30728 | tf_op jit(solution)/shard_map/ppermute | solution.py:24
  756.6 30.4 %collective-permute-start.17 = (f32[5,512]{1,0:T(8,128)S(1)}, f32[5,512]{1,0:T(8,128)S(1)}, u32[]{:S(2)}, u32[]{:S(2)}) collective-permute-start(f32[5,512]{1,0:T(8,128)S(1)} %add.175), channel_id=1, source_target_pairs={{0,8},{4,12},{8,0},{12,4},{1,9},{5,13},{9,1},{13,5},{2,10},{6,14},... | collective-permute-start | bytes 30728 | tf_op jit(solution)/shard_map/ppermute | solution.py:24
  778.7 6.7 slice-start
  778.7 11.2 %copy-start.1 = (bf16[512,512]{1,0:T(8,128)(2,1)S(1)}, bf16[512,512]{1,0:T(8,128)(2,1)}, u32[]{:S(2)}) copy-start(bf16[512,512]{1,0:T(8,128)(2,1)} %param.12) | copy-start | bytes 1572868

commit v5 on v4

--- a/solution.py
+++ b/solution.py
@@ -1,5 +1,3 @@
-import functools
-
 import jax
 import jax.numpy as jnp
 from jax import lax
@@ -66,213 +64,18 @@
 PIECE = 256
 AHEAD = 4
 SLOTS = 4
+TOTALS = 2
 MESH = pl.DeviceIdType.MESH
 
 
-def line_kernel(
-    pieces, left_of, left_ref, right_ref, out_ref, peer, outer_part, middle_part, held,
-    peer_send, peer_recv, in_send, outer_recv, middle_recv, out_send, out_recv, own_done,
-):
-    shard = lax.axis_index("shard")
-    ctx = lax.axis_index("ctx")
-    tokens = right_ref.shape[0]
-    rows = left_ref.shape[1]
-    middle = jnp.logical_or(ctx == 1, ctx == 2)
-    end = jnp.logical_not(middle)
-    low_side = ctx < 2
-    inward = jnp.where(low_side, ctx + 1, ctx - 1)
-    outward = jnp.where(ctx == 1, 0, 3)
-
-    barrier = pltpu.get_barrier_semaphore()
-    pl.semaphore_signal(barrier, inc=1, device_id={"shard": 1 - shard}, device_id_type=MESH)
-    pl.semaphore_signal(barrier, inc=1, device_id={"ctx": inward}, device_id_type=MESH)
-
-    @pl.when(middle)
-    def _():
-        pl.semaphore_signal(barrier, inc=1, device_id={"ctx": outward}, device_id_type=MESH)
-        pl.semaphore_wait(barrier, 3)
-
-    @pl.when(end)
-    def _():
-        pl.semaphore_wait(barrier, 2)
-
-    def columns(index):
-        return pl.ds(pl.multiple_of(index * PIECE, PIECE), PIECE)
-
-    def peer_copy(index):
-        return pltpu.make_async_remote_copy(
-            src_ref=right_ref.at[:, columns(index)],
-            dst_ref=peer.at[index],
-            send_sem=peer_send.at[index],
-            recv_sem=peer_recv.at[index],
-            device_id={"shard": 1 - shard},
-            device_id_type=MESH,
-        )
-
-    def end_copy(index):
-        return pltpu.make_async_remote_copy(
-            src_ref=held.at[index % SLOTS],
-            dst_ref=outer_part.at[index],
-            send_sem=in_send.at[index],
-            recv_sem=outer_recv.at[index],
-            device_id={"ctx": inward},
-            device_id_type=MESH,
-        )
-
-    def middle_copy(index):
-        return pltpu.make_async_remote_copy(
-            src_ref=held.at[index % SLOTS],
-            dst_ref=middle_part.at[index],
-            send_sem=in_send.at[index],
-            recv_sem=middle_recv.at[index],
-            device_id={"ctx": inward},
-            device_id_type=MESH,
-        )
-
-    def out_copy(index):
-        return pltpu.make_async_remote_copy(
-            src_ref=outer_part.at[index],
-            dst_ref=out_ref.at[:, columns(index)],
-            send_sem=out_send.at[index],
-            recv_sem=out_recv.at[index],
-            device_id={"ctx": outward},
-            device_id_type=MESH,
-        )
-
-    def own_copy(index):
-        return pltpu.make_async_copy(
-            outer_part.at[index], out_ref.at[:, columns(index)], own_done.at[index]
-        )
-
-    tile = min(256, rows)
-
-    def product(index, start):
-        lines = pl.ds(pl.multiple_of(start * tile, tile), tile)
-        left = left_of(index)
-        own = jnp.dot(
-            left_ref[left, lines, :tokens],
-            right_ref[:, columns(index)],
-            preferred_element_type=WIDE,
-        )
-        other = jnp.dot(
-            left_ref[left, lines, tokens:], peer[index], preferred_element_type=WIDE
-        )
-        return lines, own + other
-
-    def finish(index):
-        middle_copy(index).wait_recv()
-
-        @pl.loop(0, rows // tile)
-        def _(start):
-            lines = pl.ds(pl.multiple_of(start * tile, tile), tile)
-            total = held[index % SLOTS, lines].astype(WIDE) + middle_part[index, lines].astype(WIDE)
-            outer_part[index, lines] = total.astype(LOW)
-
-        out_copy(index).start()
-        own_copy(index).start()
-
-    for index in range(min(AHEAD, pieces)):
-        peer_copy(index).start()
-
-    @pl.loop(0, pieces)
-    def _(index):
-        @pl.when(index + AHEAD < pieces)
-        def _():
-            peer_copy(index + AHEAD).start()
-
-        @pl.when(index >= SLOTS)
-        def _():
-            end_copy(index - SLOTS).wait_send()
-
-        peer_copy(index).wait_recv()
-
-        @pl.when(end)
-        def _():
-            @pl.loop(0, rows // tile)
-            def _(start):
-                lines, value = product(index, start)
-                held[index % SLOTS, lines] = value.astype(LOW)
-
-            end_copy(index).start()
-
-        @pl.when(middle)
-        def _():
-            end_copy(index).wait_recv()
-
-            @pl.loop(0, rows // tile)
-            def _(start):
-                lines, value = product(index, start)
-                value = value + outer_part[index, lines].astype(WIDE)
-                held[index % SLOTS, lines] = value.astype(LOW)
-
-            middle_copy(index).start()
-
-            @pl.when(index >= 1)
-            def _():
-                finish(index - 1)
-
-    @pl.when(middle)
-    def _():
-        finish(pieces - 1)
-
-    @pl.loop(0, pieces)
-    def _(index):
-        peer_copy(index).wait_send()
-
-        @pl.when(index >= pieces - SLOTS)
-        def _():
-            end_copy(index).wait_send()
-
-        @pl.when(middle)
-        def _():
-            out_copy(index).wait_send()
-            own_copy(index).wait()
-
-        @pl.when(end)
-        def _():
-            out_copy(index).wait_recv()
-
-
-def line_grads(lefts, rights, identity):
-    left = jnp.stack([value.T for value in lefts])
-    right = jnp.concatenate(rights, axis=1)
-    tokens, width = right.shape
-    rows = left.shape[1]
-    pieces = width // PIECE
-    first = rights[0].shape[1] // PIECE
-
-    def left_of(index):
-        return jnp.where(index < first, 0, 1)
-
-    flops = 4 * tokens * rows * width
-    dma = pltpu.SemaphoreType.DMA
-    return pl.pallas_call(
-        functools.partial(line_kernel, pieces, left_of),
-        out_shape=jax.ShapeDtypeStruct((rows, width), LOW),
-        in_specs=[pl.BlockSpec(memory_space=pltpu.VMEM)] * 2,
-        out_specs=pl.BlockSpec(memory_space=pl.ANY),
-        scratch_shapes=[
-            pltpu.VMEM((pieces, tokens, PIECE), LOW),
-            pltpu.VMEM((pieces, rows, PIECE), LOW),
-            pltpu.VMEM((pieces, rows, PIECE), LOW),
-            pltpu.VMEM((SLOTS, rows, PIECE), LOW),
-        ]
-        + [dma((pieces,)) for _ in range(8)],
-        compiler_params=pltpu.CompilerParams(
-            collective_id=identity, has_side_effects=True, vmem_limit_bytes=56 * 1024 * 1024
-        ),
-        cost_estimate=pl.CostEstimate(flops=flops * 8, bytes_accessed=rows * width * 64, transcendentals=0),
-    )(left, right)
-
-
 def front_kernel(
-    x_blocks, cot_blocks, place, gains, first_mask, second_mask, taps,
+    x_blocks, cot_blocks, place, gains, masks, taps,
     in_w, out_w, gate_w, up_w, down_w,
     in_peer, out_peer, gate_peer, up_peer, outer_land, middle_land, rights_peer,
-    x_out, h_one_out, proj_out, mixed_out, conv_out, gated_out, mixer_out, cot_out, act_out, dh_out, grads,
+    x_out, h_one_out, mixer_out, act_out, grads, dealt, tap_sums, gain_sums,
     x_got, cot_got, x_full, h_one, cot_full, cot_peer, h_two, h_two_peer, proj, mixed, gated, mixer, conv_v,
     out_v, rim, extended, away, pair, pair_got, both_got, dh_got,
-    da_got, in_v, gu_v, down_v, dh_sum, ffn_v, right_v, outer_v, middle_v, held, totals,
+    da_got, in_v, gu_v, down_v, dh_sum, ffn_v, right_v, outer_v, middle_v, held, totals, d_ext, edge_v, rim_back,
     send, recv, local, in_send, outer_recv, middle_recv, out_send, out_recv, own_done,
 ):
     shard = lax.axis_index("shard")
@@ -476,24 +279,16 @@
     for start in range(0, tokens, tile):
         lines = pl.ds(start, tile)
         value = taps[0:1] * extended[pl.ds(start + 8, tile)]
-        value = value + taps[1:2] * (extended[pl.ds(start + 7, tile)] * first_mask[lines])
-        value = value + taps[2:3] * (extended[pl.ds(start + 6, tile)] * second_mask[lines])
+        value = value + taps[1:2] * (extended[pl.ds(start + 7, tile)] * masks[lines, 0:1])
+        value = value + taps[2:3] * (extended[pl.ds(start + 6, tile)] * masks[lines, 1:2])
         conv_v[lines] = value
         gated[lines] = (proj[1, lines] * value).astype(LOW)
-
-    stores = [
-        load(7, proj, proj_out), load(8, mixed, mixed_out), load(9, conv_v, conv_out), load(10, gated, gated_out)
-    ]
-    for copy in stores:
-        copy.start()
 
     pump("g0")
     cot_core.wait_recv()
     cot_more.wait_recv()
     cot_first.start()
     over_shard("g1").start()
-    cot_store = load(11, cot_full, cot_out)
-    cot_store.start()
     out_load = load(3, out_peer, out_v.at[1])
     own_loads[3].wait()
     over_ctx("o").wait_recv()
@@ -524,7 +319,7 @@
     pump("u0")
     cot_first.wait_recv()
     cot_second.start()
-    cot_second.wait_recv()
+    cot_second.wait()
     own_loads[4].wait()
     h_one_store.wait()
 
@@ -677,12 +472,17 @@
     outward = jnp.where(ctx == 1, 0, 3)
     per_kind = chunk // PIECE
     per_chunk = 3 * per_kind
+    ffn_pieces = CHUNKS * per_chunk
+    pieces_in_all = ffn_pieces + 4 * part // PIECE
     line_rows = min(256, rows)
 
     def grad_columns(piece):
         index, turn = piece // per_chunk, piece % per_chunk
         kind, sub = turn // per_kind, turn % per_kind
-        return pl.ds(pl.multiple_of(kind * hidden + index * chunk + sub * PIECE, PIECE), PIECE)
+        start = jnp.where(
+            piece < ffn_pieces, kind * hidden + index * chunk + sub * PIECE, piece * PIECE
+        )
+        return pl.ds(pl.multiple_of(start, PIECE), PIECE)
 
     def inward_copy(piece, land, sems):
         return pltpu.make_async_remote_copy(
@@ -692,12 +492,12 @@
 
     def outward_copy(piece):
         return pltpu.make_async_remote_copy(
-            src_ref=totals.at[piece % SLOTS], dst_ref=grads.at[:, grad_columns(piece)], send_sem=out_send.at[piece],
+            src_ref=totals.at[piece % TOTALS], dst_ref=grads.at[:, grad_columns(piece)], send_sem=out_send.at[piece],
             recv_sem=out_recv.at[piece], device_id={"ctx": outward}, device_id_type=MESH,
         )
 
     def total_store(piece):
-        return pltpu.make_async_copy(totals.at[piece % SLOTS], grads.at[:, grad_columns(piece)], own_done.at[piece])
+        return pltpu.make_async_copy(totals.at[piece % TOTALS], grads.at[:, grad_columns(piece)], own_done.at[piece])
 
     def stage_in(piece, land, room):
         copy = pltpu.make_async_copy(land.at[piece], room, local.at[26])
@@ -708,25 +508,28 @@
         inward_copy(piece, middle_land, middle_recv).wait_recv()
         stage_in(piece, middle_land, middle_v)
 
-        @pl.when(piece >= SLOTS)
+        @pl.when(piece >= TOTALS)
         def _():
-            outward_copy(piece - SLOTS).wait_send()
-            total_store(piece - SLOTS).wait()
+            outward_copy(piece - TOTALS).wait_send()
+            total_store(piece - TOTALS).wait()
 
         @pl.loop(0, rows // line_rows)
         def _(start):
             lines = pl.ds(pl.multiple_of(start * line_rows, line_rows), line_rows)
             total = held[piece % SLOTS, lines].astype(WIDE) + middle_v[lines].astype(WIDE)
-            totals[piece % SLOTS, lines] = total.astype(LOW)
+            totals[piece % TOTALS, lines] = total.astype(LOW)
 
         outward_copy(piece).start()
         total_store(piece).start()
 
     def grad_piece(piece):
-        index, turn = piece // per_chunk, piece % per_chunk
-        kind, sub = turn // per_kind, turn % per_kind
+        after = piece >= ffn_pieces
+        turn = jnp.where(after, jnp.maximum(piece - ffn_pieces - per_kind, 0), piece % per_chunk)
+        kind, sub = turn // per_kind, piece % per_kind
+        slot = jnp.where(after, jnp.where(piece < ffn_pieces + per_kind, 1, 0), piece // per_chunk % 2)
         strip = pl.ds(pl.multiple_of(sub * PIECE, PIECE), PIECE)
-        left = jnp.where(kind == 0, 0, half)
+        left_first = jnp.where(after, piece < ffn_pieces + per_kind, kind == 0)
+        left = jnp.where(left_first, 0, half)
 
         @pl.when(piece >= SLOTS)
         def _():
@@ -736,7 +539,7 @@
             lines = pl.ds(pl.multiple_of(start * line_rows, line_rows), line_rows)
             own = jnp.dot(
                 down_v[lines, pl.ds(pl.multiple_of(left, tokens), tokens)],
-                ffn_v[index % 2, kind, :, strip],
+                ffn_v[slot, kind, :, strip],
                 preferred_element_type=WIDE,
             )
             other = jnp.dot(
@@ -821,7 +624,7 @@
         over_shard("g3").start()
         h_two_first.wait_recv()
         h_two_second.start()
-        h_two_second.wait_recv()
+        h_two_second.wait()
         turned(1, h_two_peer, 0, tokens)
         got_right(0, 1)
 
@@ -837,6 +640,253 @@
         right_copy(2, 2).start()
         got_right(1, 2)
 
+    back_blocks, d_resid = cot_got, dh_sum.at[1, :, pl.ds(0, part)]
+    hone_first, hone_second = columns_out("ic", h_one_out, cot_peer)
+    dr_first, dr_second = columns_out("dc", h_two, h_two_peer)
+    mixer_rights = 3 * hidden
+
+    def mixer_right(kind):
+        source = gated if kind == 0 else ffn_v.at[0, kind - 1]
+        strip = pl.ds(mixer_rights + kind * part, part)
+        return remote("m%d" % kind, source, rights_peer.at[:, strip], {"shard": 1 - shard})
+
+    def got_mixer_right(kind):
+        mixer_right(kind).wait_recv()
+        room = right_v.at[max(kind - 1, 0)]
+        copy = load(23, rights_peer.at[:, pl.ds(mixer_rights + kind * part, part)], room)
+        copy.start()
+        copy.wait()
+
+    x_reload = load(5, x_out, x_full)
+    mixer_reloads = [
+        load(6, mixer_out.at[0], h_one.at[:, own_half]), load(7, mixer_out.at[1], h_one.at[:, peer_half])
+    ]
+    h_one_reload = load(8, h_one_out.at[:, own_half], dh_got)
+    in_reloads = [load(13 + column, in_w.at[column], in_v.at[0, column]) for column in range(3)]
+    in_reloads += [load(16 + column, in_peer.at[column], in_v.at[1, column]) for column in range(3)]
+    fine = min(32, tokens)
+
+    def reload():
+        for index in range(CHUNKS):
+            da_copy(index).wait_send()
+        for copy in [x_reload] + mixer_reloads + in_reloads:
+            copy.start()
+
+    def resid_back():
+        dh_last.wait_recv()
+        h_one_reload.start()
+        for copy in [x_reload] + mixer_reloads:
+            copy.wait()
+        h_two_first.wait_send()
+        gain_sums[...] = jnp.zeros((2, width), WIDE)
+
+        @pl.loop(0, tokens // fine)
+        def _(index):
+            lines = pl.ds(pl.multiple_of(index * fine, fine), fine)
+
+            def halves(columns_of, which):
+                resid = x_full[lines, columns_of].astype(WIDE) + h_one[lines, columns_of].astype(WIDE)
+                return resid, mixer[which, lines].astype(WIDE)
+
+            own, own_grad = halves(own_half, 0)
+            other, other_grad = halves(peer_half, 1)
+            total = jnp.sum(own * own, axis=1, keepdims=True) + jnp.sum(other * other, axis=1, keepdims=True)
+            scale = lax.rsqrt(total / width + EPS)
+            own, other = own * scale, other * scale
+            own_scaled, other_scaled = own_grad * gains[1:2, own_half], other_grad * gains[1:2, peer_half]
+            mean = (
+                jnp.sum(own_scaled * own, axis=1, keepdims=True)
+                + jnp.sum(other_scaled * other, axis=1, keepdims=True)
+            ) / width
+            h_two[lines, own_half] = (
+                cot_full[lines, own_half].astype(WIDE) + scale * (own_scaled - own * mean)
+            ).astype(LOW)
+            h_two[lines, peer_half] = (
+                cot_full[lines, peer_half].astype(WIDE) + scale * (other_scaled - other * mean)
+            ).astype(LOW)
+            gain_sums[1:2, own_half] += jnp.sum(own_grad * own, axis=0, keepdims=True)
+            gain_sums[1:2, peer_half] += jnp.sum(other_grad * other, axis=0, keepdims=True)
+            resid = x_full[lines, own_part].astype(WIDE) + h_one[lines, own_part].astype(WIDE)
+            which = jnp.where(outer == shard, 0, 1)
+            scaled = mixer[which, lines, columns(core, part)].astype(WIDE) * gains[1:2, own_part]
+            d_resid[lines] = cot_full[lines, own_part].astype(WIDE) + scale * (
+                scaled - resid * scale * mean
+            )
+
+        dr_first.start()
+
+    rim_out = remote(
+        "rim_back", edge_v, rim_back, {"ctx": lax.rem(ctx + blocks - 1, blocks)}
+    )
+
+    def conv_back():
+        act_store(CHUNKS - 2).wait()
+        for kind in range(3):
+            right_copy(CHUNKS - 2, kind).wait_send()
+
+        def body(lines):
+            d_gated = jnp.dot(
+                h_two[lines, own_half], out_v[0], preferred_element_type=WIDE
+            ) + jnp.dot(h_two[lines, peer_half], out_v[1], preferred_element_type=WIDE)
+            d_ext[lines] = (d_gated * proj[1, lines]).astype(LOW).astype(WIDE)
+            ffn_v[0, 1, lines] = (d_gated * conv_v[lines]).astype(LOW)
+
+        for lines in tiles:
+            body(lines)
+        edge_v[...] = d_ext[0:16].astype(LOW)
+
+        @pl.when(ctx > 0)
+        def _():
+            rim_out.start()
+
+        turned(0, h_two, shard * half, 0)
+
+    def out_ready():
+        dr_first.wait_recv()
+        dr_second.start()
+        act_store(CHUNKS - 1).wait()
+        right_copy(CHUNKS - 1, 0).wait_send()
+
+        def body(lines):
+            ffn_v[1, 0, lines] = gated[lines]
+
+        over_tiles(body)
+        dr_second.wait_recv()
+        turned(0, h_two_peer, 0, tokens)
+        got_mixer_right(0)
+
+    def proj_back():
+        @pl.when(ctx < blocks - 1)
+        def _():
+            rim_out.wait_recv()
+            d_ext[tokens : tokens + 8] = rim_back[0:8].astype(WIDE)
+
+        @pl.when(ctx == blocks - 1)
+        def _():
+            d_ext[tokens : tokens + 8] = jnp.zeros((8, part), WIDE)
+
+        sums = [jnp.zeros((1, part), WIDE) for _ in range(3)]
+        size = 128
+        for start in range(0, tokens, size):
+            lines = pl.ds(start, size)
+            own = d_ext[lines]
+            d_mixed = taps[0:1] * own
+            d_mixed = d_mixed + taps[1:2] * (d_ext[pl.ds(start + 1, size)] * masks[lines, 2:3])
+            d_mixed = d_mixed + taps[2:3] * (d_ext[pl.ds(start + 2, size)] * masks[lines, 3:4])
+            ffn_v[0, 0, lines] = (d_mixed * proj[2, lines]).astype(LOW)
+            ffn_v[0, 2, lines] = (d_mixed * proj[0, lines]).astype(LOW)
+            for tap in range(3):
+                value = own * extended[pl.ds(start + 8 - tap, size)]
+                if tap > 0:
+                    value = value * masks[lines, tap - 1 : tap]
+                sums[tap] = sums[tap] + jnp.sum(value, axis=0, keepdims=True)
+        for tap in range(3):
+            tap_sums[tap : tap + 1] = sums[tap]
+        for kind in range(1, 4):
+            mixer_right(kind).start()
+
+    def in_ready():
+        hone_first.wait_recv()
+        hone_second.start()
+        h_one_reload.wait()
+        turned(1, dh_got, 0, 0)
+        hone_second.wait_recv()
+        turned(1, cot_peer, 0, tokens)
+        got_mixer_right(1)
+
+    back_away = remote("bh1", away, pair_got, {"tp": core_mate})
+    back_pair = remote("bh2", pair, both_got, {"tp": outer_mate})
+    back_last = remote("bh3", mixer.at[core], mixer.at[core], {"tp": core_mate})
+
+    def to_inputs(lines, which):
+        total = None
+        for column in range(3):
+            term = lax.dot_general(
+                ffn_v[0, column, lines], in_v[which, column],
+                (((1,), (1,)), ((), ())), preferred_element_type=WIDE,
+            )
+            total = term if total is None else total + term
+        return total
+
+    def back_one_hop():
+        for copy in (dh_away, dh_pair, dh_last):
+            copy.wait_send()
+        for copy in in_reloads:
+            copy.wait()
+
+        def body(lines):
+            away[lines] = to_inputs(lines, 1 - core).astype(LOW)
+
+        over_tiles(body)
+        back_away.start()
+
+        def rest(lines):
+            dh_sum[0, lines] = to_inputs(lines, core)
+
+        over_tiles(rest)
+
+    def back_two_hops():
+        back_away.wait_recv()
+
+        def body(lines):
+            pair[lines] = (dh_sum[0, lines] + pair_got[lines].astype(WIDE)).astype(LOW)
+
+        over_tiles(body)
+        back_pair.start()
+        got_mixer_right(2)
+
+    def back_three_hops():
+        back_pair.wait_recv()
+
+        def body(lines):
+            mixer[core, lines] = (pair[lines].astype(WIDE) + both_got[lines].astype(WIDE)).astype(LOW)
+
+        over_tiles(body)
+        back_last.start()
+        got_mixer_right(3)
+
+    def give_back(step):
+        to, origin = lax.rem(ctx + step, blocks), lax.rem(ctx + blocks - step, blocks)
+        name = "give" + str(step)
+        return (
+            remote(name, back_blocks.at[to], dealt.at[ctx], {"ctx": to}),
+            remote(name, back_blocks.at[to], dealt.at[origin], {"ctx": to}),
+        )
+
+    given = [give_back(step) for step in range(1, blocks)]
+    kept = load(9, back_blocks.at[ctx], dealt.at[ctx])
+
+    def input_back():
+        back_last.wait_recv()
+
+        @pl.loop(0, tokens // fine)
+        def _(index):
+            lines = pl.ds(pl.multiple_of(index * fine, fine), fine)
+            own, other = x_full[lines, own_half].astype(WIDE), x_full[lines, peer_half].astype(WIDE)
+            own_grad, other_grad = mixer[0, lines].astype(WIDE), mixer[1, lines].astype(WIDE)
+            total = jnp.sum(own * own, axis=1, keepdims=True) + jnp.sum(other * other, axis=1, keepdims=True)
+            scale = lax.rsqrt(total / width + EPS)
+            own, other = own * scale, other * scale
+            mean = (
+                jnp.sum(own_grad * gains[0:1, own_half] * own, axis=1, keepdims=True)
+                + jnp.sum(other_grad * gains[0:1, peer_half] * other, axis=1, keepdims=True)
+            ) / width
+            gain_sums[0:1, own_half] += jnp.sum(own_grad * own, axis=0, keepdims=True)
+            gain_sums[0:1, peer_half] += jnp.sum(other_grad * other, axis=0, keepdims=True)
+            which = jnp.where(outer == shard, 0, 1)
+            scaled = mixer[which, lines, columns(core, part)].astype(WIDE) * gains[0:1, own_part]
+            normed = x_full[lines, own_part].astype(WIDE) * scale
+            d_resid[lines] = d_resid[lines] + scale * (scaled - normed * mean)
+
+        for to in range(blocks):
+            total = place[0, to] * d_resid[0:block_rows]
+            for index in range(1, blocks):
+                total = total + place[index, to] * d_resid[index * block_rows : (index + 1) * block_rows]
+            back_blocks[to] = total.astype(LOW)
+        for out, _ in given:
+            out.start()
+        kept.start()
+
     def event_third():
         over_shard("g3").wait_recv()
         over_shard("u3").wait_recv()
@@ -844,6 +894,8 @@
         whole_feed(3)
         for kind in range(3):
             right_copy(3, kind).start()
+        hone_first.start()
+        mixer_right(0).start()
         got_right(2, 2)
 
     def dh_one_hop():
@@ -867,6 +919,7 @@
 
         over_tiles(body)
         dh_pair.start()
+        reload()
         got_right(3, 0)
 
     def dh_three_hops():
@@ -894,9 +947,17 @@
         17: dh_one_hop,
         18: dh_two_hops,
         20: dh_three_hops,
+        21: resid_back,
         22: lambda: got_right(3, 2),
+        23: conv_back,
+        24: out_ready,
+        25: proj_back,
+        26: in_ready,
+        27: back_one_hop,
+        28: back_two_hops,
+        30: back_three_hops,
+        31: input_back,
     }
-    pieces_in_all = CHUNKS * per_chunk
 
     @pl.loop(0, pieces_in_all)
     def _(piece):
@@ -908,31 +969,31 @@
     def _():
         finish(pieces_in_all - 1)
 
-    dh_last.wait_recv()
-    dh_store = load(27, mixer, dh_out)
-    dh_store.start()
-
     for out, _ in x_deals + cot_deals:
         out.wait_send()
-    for copy in (cot_outer, cot_core, cot_more, cot_first, cot_second, h_two_first, h_two_second,
-                 dh_away, dh_pair, dh_last):
+    for copy in (cot_outer, cot_core, cot_more, cot_first,
+                 hone_first, hone_second, dr_first, dr_second, back_away, back_pair, back_last):
         copy.wait_send()
     for name in pieces:
         over_shard(name).wait_send()
         if name not in direct:
             over_ctx(name).wait_send()
-    for index in range(CHUNKS):
-        da_copy(index).wait_send()
-    for index in (CHUNKS - 2, CHUNKS - 1):
-        act_store(index).wait()
-        for kind in range(3):
-            right_copy(index, kind).wait_send()
-    for copy in stores + [cot_store, dh_store]:
-        copy.wait()
+    for kind in (1, 2):
+        right_copy(CHUNKS - 1, kind).wait_send()
+    for kind in range(4):
+        mixer_right(kind).wait_send()
+    kept.wait()
+    for out, into in given:
+        out.wait_send()
+        into.wait_recv()
 
     @pl.when(ctx < blocks - 1)
     def _():
         rim_copy.wait_send()
+
+    @pl.when(ctx > 0)
+    def _():
+        rim_out.wait_send()
 
     @pl.loop(0, pieces_in_all)
     def _(piece):
@@ -940,27 +1001,27 @@
         def _():
             inward_copy(piece, outer_land, outer_recv).wait_send()
 
-            @pl.when(middle)
-            def _():
-                outward_copy(piece).wait_send()
-                total_store(piece).wait()
+        @pl.when(jnp.logical_and(middle, piece >= pieces_in_all - TOTALS))
+        def _():
+            outward_copy(piece).wait_send()
+            total_store(piece).wait()
 
         @pl.when(end)
         def _():
             outward_copy(piece).wait_recv()
 
 
-FRONT_COPIES = 72
-
-
-def front(x_blocks, cot_blocks, place, gains, first_mask, second_mask, taps, in_w, out_w, gate_w, up_w, down_w):
+FRONT_COPIES = 88
+
+
+def front(x_blocks, cot_blocks, place, gains, masks, taps, in_w, out_w, gate_w, up_w, down_w):
     tokens = x_blocks.shape[0] * x_blocks.shape[1]
     part = x_blocks.shape[2]
     width = gains.shape[1]
     half = width // 2
     rows, hidden = gate_w.shape
     chunk = hidden // CHUNKS
-    pieces = 3 * hidden // PIECE
+    pieces = (3 * hidden + width) // PIECE
     vmem = pl.BlockSpec(memory_space=pltpu.VMEM)
     hbm = pl.BlockSpec(memory_space=pl.ANY)
     shape = jax.ShapeDtypeStruct
@@ -971,18 +1032,15 @@
         shape(up_w.shape, LOW),
         shape((pieces, rows, PIECE), LOW),
         shape((pieces, rows, PIECE), LOW),
-        shape((tokens, 3 * hidden), LOW),
+        shape((tokens, 3 * hidden + width), LOW),
         shape((tokens, width), LOW),
         shape((tokens, width), LOW),
-        shape((3, tokens, part), WIDE),
-        shape((tokens, part), LOW),
-        shape((tokens, part), WIDE),
-        shape((tokens, part), LOW),
         shape((2, tokens, half), LOW),
-        shape((tokens, width), LOW),
         shape((tokens, hidden), LOW),
-        shape((2, tokens, half), LOW),
-        shape((rows, 3 * hidden), LOW),
+        shape((rows, 3 * hidden + width), LOW),
+        shape(x_blocks.shape, LOW),
+        shape((3, part), WIDE),
+        shape((2, width), WIDE),
     ]
     low, wide = (lambda *dims: pltpu.VMEM(dims, LOW)), (lambda *dims: pltpu.VMEM(dims, WIDE))
     dma = pltpu.SemaphoreType.DMA
@@ -1018,7 +1076,10 @@
         low(rows, PIECE),
         low(rows, PIECE),
         low(SLOTS, rows, PIECE),
-        low(SLOTS, rows, PIECE),
+        low(TOTALS, rows, PIECE),
+        wide(tokens + 8, part),
+        low(16, part),
+        low(16, part),
         dma((FRONT_COPIES,)),
         dma((FRONT_COPIES,)),
         dma((28,)),
@@ -1026,9 +1087,9 @@
     return pl.pallas_call(
         front_kernel,
         out_shape=outs,
-        in_specs=[vmem, vmem, pl.BlockSpec(memory_space=pltpu.SMEM), vmem, vmem, vmem, vmem]
+        in_specs=[vmem, vmem, pl.BlockSpec(memory_space=pltpu.SMEM)] + [vmem] * 3
         + [hbm] * 5,
-        out_specs=[hbm for _ in outs],
+        out_specs=[hbm] * (len(outs) - 2) + [vmem] * 2,
         scratch_shapes=scratch,
         compiler_params=pltpu.CompilerParams(
             collective_id=2, has_side_effects=True, vmem_limit_bytes=63 * 1024 * 1024
@@ -1036,7 +1097,7 @@
         cost_estimate=pl.CostEstimate(
             flops=2 * tokens * width * hidden * 64, bytes_accessed=1 << 29, transcendentals=0
         ),
-    )(x_blocks, cot_blocks, place, gains, first_mask, second_mask, taps, in_w, out_w, gate_w, up_w, down_w)
+    )(x_blocks, cot_blocks, place, gains, masks, taps, in_w, out_w, gate_w, up_w, down_w)
 
 
 class Features:
@@ -1235,27 +1296,22 @@
             return reorder(values, send_order).reshape(per_dev, block_rows, col_count)
 
         place = (targets[None, :] == jnp.arange(per_dev)[:, None]).astype(WIDE)
-        (
-            in_peer, out_peer, _, _, _, _, rights_peer, x_full, h_one, proj, mixed, conv_out, gated, mixer,
-            cot_full, act, dh_halves, ffn_sums,
-        ) = front(
-            blocks_of(hidden_in), blocks_of(out_grad), place, gains, first_own, second_own, conv_taps,
+        _, _, _, _, _, _, rights_peer, x_full, _, mixer, act, sums, dealt, taps_grad, gain_sums = front(
+            blocks_of(hidden_in), blocks_of(out_grad), place, gains,
+            jnp.concatenate([first_own, second_own, first_next, second_next], axis=1), conv_taps,
             in_parts, out_weight, gate_weight, up_weight, down_weight,
         )
-        b_part, c_part, v_part = proj[0], proj[1], proj[2]
-        in_w = [jnp.concatenate([w[0], w[1], w[2]], axis=1) for w in (in_parts, in_peer)]
-        out_w = (out_weight, out_peer)
-        mixer_out = shards.join([mixer[0], mixer[1]])
-        h_one_cols = shards.columns(h_one)
-        dh_two = shards.join([dh_halves[0], dh_halves[1]]).astype(WIDE)
         act_all = jnp.concatenate([act, rights_peer[:, :hidden_count]], axis=0)
-        ffn_grads = [ffn_sums[:, kind * hidden_count : (kind + 1) * hidden_count] for kind in range(3)]
-        x_float = x_full.astype(WIDE)
-        scale_one = lax.rsqrt(jnp.mean(x_float * x_float, axis=1, keepdims=True) + EPS)
-        normed_one = x_float * scale_one
-        resid = x_float + mixer_out.astype(WIDE)
-        scale_two = lax.rsqrt(jnp.mean(resid * resid, axis=1, keepdims=True) + EPS)
-        normed_two = resid * scale_two
+        ffn_terms = tp.own_terms(shards.own_tokens(contract_cols(act_all, down_weight)))
+        resid_own = tp.own(x_full, 1).astype(WIDE) + tp.own(shards.join([mixer[0], mixer[1]]), 1).astype(WIDE)
+        block_out = (resid_own + added(ffn_terms)).astype(LOW)
+        block_dealt = to_dealt(block_out)
+        input_dealt = reorder(dealt.reshape(row_count, col_count), returning)
+        ends = [hidden_count, 2 * hidden_count, 3 * hidden_count, 3 * hidden_count + col_count]
+        parts = [value.astype(WIDE) for value in jnp.split(sums, ends, axis=1)]
+        down_total, gate_total, up_total, out_total, in_flat_total = parts
+        in_total = in_flat_total.reshape(in_weight.shape)
+        gain_one_grad, gain_two_grad = tp.own(gain_sums, 1)
     else:
         in_w = shards.weight(in_weight.reshape(weight_rows, -1))
         x_full = tp.gather(to_packed(hidden_in))
@@ -1301,57 +1357,57 @@
             [[cot_cols], [h_two_cols, h_two_cols]], [ffn_rights[:1], ffn_rights[1:]], 0
         )
 
-    ffn_terms = tp.own_terms(shards.own_tokens(contract_cols(act_all, down_weight)))
-
-    rim = shifted(mixed[-2:], "ctx", 1)
-    extended = jnp.concatenate([rim, mixed], axis=0).astype(WIDE)
-    prev_one = extended[1 : row_count + 1] * first_own
-    prev_two = extended[0:row_count] * second_own
-    mixed_float = extended[2:]
-
-    gain_two_grad = tp.own(jnp.sum(dh_two * normed_two, axis=0), 0)
-    d_resid = cot_full.astype(WIDE) + norm_back(dh_two, normed_two, scale_two, gain_two)
-    d_resid_low = d_resid.astype(LOW)
-    d_gated = sum(matmul(part, w) for part, w in zip(shards.split(d_resid_low), out_w))
-    d_conv = (d_gated * c_part).astype(LOW)
-    d_c_part = d_gated * conv_out
-    rim_back = shifted(d_conv[:2], "ctx", -1)
-    d_conv_float = d_conv.astype(WIDE)
-    back_ext = jnp.concatenate([d_conv, rim_back], axis=0).astype(WIDE)
-    d_mixed = (
-        conv_taps[0] * d_conv_float
-        + conv_taps[1] * back_ext[1 : row_count + 1] * first_next
-        + conv_taps[2] * back_ext[2:] * second_next
-    )
-    taps_grad = jnp.stack(
-        [
-            jnp.sum(d_conv_float * mixed_float, axis=0),
-            jnp.sum(d_conv_float * prev_one, axis=0),
-            jnp.sum(d_conv_float * prev_two, axis=0),
+        ffn_terms = tp.own_terms(shards.own_tokens(contract_cols(act_all, down_weight)))
+
+        rim = shifted(mixed[-2:], "ctx", 1)
+        extended = jnp.concatenate([rim, mixed], axis=0).astype(WIDE)
+        prev_one = extended[1 : row_count + 1] * first_own
+        prev_two = extended[0:row_count] * second_own
+        mixed_float = extended[2:]
+
+        gain_two_grad = tp.own(jnp.sum(dh_two * normed_two, axis=0), 0)
+        d_resid = cot_full.astype(WIDE) + norm_back(dh_two, normed_two, scale_two, gain_two)
+        d_resid_low = d_resid.astype(LOW)
+        d_gated = sum(matmul(part, w) for part, w in zip(shards.split(d_resid_low), out_w))
+        d_conv = (d_gated * c_part).astype(LOW)
+        d_c_part = d_gated * conv_out
+        rim_back = shifted(d_conv[:2], "ctx", -1)
+        d_conv_float = d_conv.astype(WIDE)
+        back_ext = jnp.concatenate([d_conv, rim_back], axis=0).astype(WIDE)
+        d_mixed = (
+            conv_taps[0] * d_conv_float
+            + conv_taps[1] * back_ext[1 : row_count + 1] * first_next
+            + conv_taps[2] * back_ext[2:] * second_next
+        )
+        taps_grad = jnp.stack(
+            [
+                jnp.sum(d_conv_float * mixed_float, axis=0),
+                jnp.sum(d_conv_float * prev_one, axis=0),
+                jnp.sum(d_conv_float * prev_two, axis=0),
+            ]
+        )
+        d_proj = [
+            (d_mixed * v_part).astype(LOW),
+            d_c_part.astype(LOW),
+            (d_mixed * b_part).astype(LOW),
         ]
-    )
-    d_proj = [
-        (d_mixed * v_part).astype(LOW),
-        d_c_part.astype(LOW),
-        (d_mixed * b_part).astype(LOW),
-    ]
-    d_proj_flat = jnp.concatenate(d_proj, axis=1)
-    dh_one_terms = tp.all_terms(shards.join([contract_cols(d_proj_flat, w) for w in in_w]))
-    mixer_grads = weight_grads(
-        [[shards.columns(d_resid_low)], [h_one_cols]], [[gated], [d_proj_flat]], 1
-    )
-    dh_one_terms, ffn_terms, mixer_grads = lax.optimization_barrier(
-        (dh_one_terms, ffn_terms, mixer_grads)
-    )
-    dh_one = added(dh_one_terms)
-    block_out = (tp.own(resid, 1) + added(ffn_terms)).astype(LOW)
-    down_total, gate_total, up_total = [value.astype(WIDE) for value in ffn_grads]
-    out_total, in_flat_total = [value.astype(WIDE) for value in mixer_grads]
-    in_total = in_flat_total.reshape(in_weight.shape)
-    gain_one_grad = tp.own(jnp.sum(dh_one * normed_one, axis=0), 0)
-    d_input = d_resid + norm_back(dh_one, normed_one, scale_one, gain_one)
-    dealt = to_dealt(jnp.concatenate([block_out, tp.own(d_input, 1).astype(LOW)], axis=1))
-    block_dealt, input_dealt = dealt[:, :col_count], dealt[:, col_count:]
+        d_proj_flat = jnp.concatenate(d_proj, axis=1)
+        dh_one_terms = tp.all_terms(shards.join([contract_cols(d_proj_flat, w) for w in in_w]))
+        mixer_grads = weight_grads(
+            [[shards.columns(d_resid_low)], [h_one_cols]], [[gated], [d_proj_flat]], 1
+        )
+        dh_one_terms, ffn_terms, mixer_grads = lax.optimization_barrier(
+            (dh_one_terms, ffn_terms, mixer_grads)
+        )
+        dh_one = added(dh_one_terms)
+        block_out = (tp.own(resid, 1) + added(ffn_terms)).astype(LOW)
+        down_total, gate_total, up_total = [value.astype(WIDE) for value in ffn_grads]
+        out_total, in_flat_total = [value.astype(WIDE) for value in mixer_grads]
+        in_total = in_flat_total.reshape(in_weight.shape)
+        gain_one_grad = tp.own(jnp.sum(dh_one * normed_one, axis=0), 0)
+        d_input = d_resid + norm_back(dh_one, normed_one, scale_one, gain_one)
+        dealt = to_dealt(jnp.concatenate([block_out, tp.own(d_input, 1).astype(LOW)], axis=1))
+        block_dealt, input_dealt = dealt[:, :col_count], dealt[:, col_count:]
 
     small = jnp.concatenate([taps_grad, gain_one_grad[None], gain_two_grad[None]], axis=0)
     small_sum = butterfly_sum(butterfly_sum(small, "shard"), "ctx")

time: 797 us -> 709 us (0.89)
  local copies, waits for them, and re-layouts: 59.5 us -> 30.1 us
  Pallas kernels: 608 us -> 580 us
  other arithmetic: 54.8 us -> 32.2 us
  starting transfers between devices: 24.6 us -> 16 us
    pallas_call x1 -> x0, Pallas kernels: 129 us -> none  [line_grads(): pl.pallas_call(functools.partial(line_kernel, pieces, left_of), out_shape...]
    pallas_call x1, Pallas kernels: 480 us -> 580 us  [front(): pl.pallas_call(front_kernel, out_shape=outs, in_specs=[vmem, vmem, pl.Blo...]
    pallas_call x5 -> x0, local copies, waits for them, and re-layouts: 17.2 us -> none  [front(): pl.pallas_call(front_kernel, out_shape=outs, in_specs=[vmem, vmem, pl.Blo...]
    convert_element_type x9 -> x3, other arithmetic: 25 us -> 13.7 us  [the longest x2 11.8 us: on_device(): parts = [value.astype(WIDE) for value in jnp.split(sums, ends, axis=1)]]
    ppermute x16 -> x9, waiting for transfers between devices: 24.2 us -> 35 us  [swapped(): lax.ppermute(value, axis, [(source, source ^ step) for source in range(co...]
    reduce_sum x3 -> x0, other arithmetic: 10.5 us -> none  [the longest x1 6.5 us: on_device(): gain_one_grad = tp.own(jnp.sum(dh_one * normed_one, axis=0), 0)]
    ppermute x16 -> x9, starting transfers between devices: 18 us -> 10 us  [swapped(): lax.ppermute(value, axis, [(source, source ^ step) for source in range(co...]
  transfers between devices with their start and end apart: 19 -> 10, of which waited for: 4 -> 3; matrix products, arithmetic and copies ran while one was open for 14% -> 9% of each run, Pallas kernels for 16% -> 0%
where the time goes in v5:
time: 709 us; the launch traced here: 702 us
  Pallas kernels  580 us (82%)
  waiting for transfers between devices  35.1 us (5%)
  other arithmetic  32.2 us (5%)
  local copies, waits for them, and re-layouts  30.1 us (4%)
  starting transfers between devices  16 us (2%)
    pallas_call x1, Pallas kernels, front(): pl.pallas_call(front_kernel, out_shape=outs, in_specs=[vmem, vmem, pl.Blo...  580 us
    ppermute x9, waiting for transfers between devices, swapped(): lax.ppermute(value, axis, [(source, source ^ step) for source in range(co...  35 us
  transfers between devices with their start and end apart: 10, of which 3 were waited for; matrix products, arithmetic and copies ran while one was open for 9% of the time, Pallas kernels for 0%

profile of v5, /device:TPU:0, one launch (start us, length us, event | category | flops | bytes accessed | tf_op | source)
XLA Modules:
  0.0 701.7 jit_solution(7161924034149948259)
XLA Ops:
  0.6 0.0 copy-start
  0.7 0.7 stack.18
  1.4 0.7 stack.19
  2.1 3.0 collective-permute-start
  5.1 0.8 reduce-window_clone.1
  6.0 0.7 subtract_bitcast_fusion
  6.6 0.1 select_reduce_fusion
  6.7 0.1 slice_compare_fusion.3
  6.8 0.5 broadcast.126
  7.4 1.3 reduce.3
  8.7 0.1 reshape_squeeze.3
  8.8 0.1 copy.51
  8.9 0.7 sort.51
  9.7 0.6 sort.52
  10.3 0.6 gather_fusion.5
  11.0 0.6 fusion.17.place
  11.6 0.7 sort.53
  12.3 0.6 pad_clamp_fusion.1
  12.9 0.0 collective-permute-done
  13.0 0.1 collective-permute-start.1
  13.0 0.6 pad_clamp_fusion
  13.6 0.9 copy.55.masks
  14.5 1.4 gather_fusion
  15.9 2.4 gather_fusion.1
  18.3 1.3 convert_element_type.51.taps
  19.6 0.6 maximum_convert_fusion.gains
  20.2 580.5 %shard_map.195 = (bf16[3,1024,512]{2,1,0:T(8,128)(2,1)}, bf16[1024,512]{1,0:T(8,128)(2,1)}, bf16[1024,2048]{1,0:T(8,128)(2,1)}, bf16[1024,2048]{1,0:T(8,128)(2,1...) custom-call(bf16[4,128,512]{2,1,0:T(8,128)(2,1)} %gather_fusion, ...), custom_call_target="tpu_custom_call" | custom-call | flops 274877906944 | bytes 536870912 | tf_op jit(solution)/shard_map/pallas_call | solution.py:1087
  600.7 0.0 copy-start.5
  600.7 0.8 constant_dynamic-slice_fusion
  601.6 0.9 pad_maximum_fusion
  602.5 1.5 collective-permute-start.6
  604.0 1.8 slice.62
  605.8 0.0 slice-start
  605.8 0.0 slice-start.2
  605.9 0.0 slice-start.3
  605.9 6.5 fusion.4
  612.4 1.0 slice.85
  613.4 0.5 collective-permute-start.2
  614.0 9.0 %slice_convert_fusion = (f32[1024,2048]{1,0:T(8,128)}, f32[1024,2048]{1,0:T(8,128)}, f32[1024,2048]{1,0:T(8,128)}) fusion(bf16[1024,8192]{1,0:T(8,128)(2,1)S(1)} %bitcast.49), kind=kLoop, calls=%fused_computation.10 | loop fusion | flops 6291456 | bytes 37748736 | tf_op jit(solution)/shard_map/convert_element_type | solution.py:1311
  623.0 12.7 %collective-permute-done.2 = bf16[512,1024]{1,0:T(8,128)(2,1)} collective-permute-done((bf16[512,1024]{1,0:T(8,128)(2,1)}, bf16[512,1024]{1,0:T(8,128)(2,1)}, u32[]{:S(2)}, u32[]{:S(2)}) %collective-permute-start.2) | collective-permute-done | bytes 1048608 | tf_op jit(solution)/shard_map/ppermute | solution.py:22
  635.7 1.4 broadcast_select_fusion
  637.0 1.0 fusion.10
  638.0 0.1 collective-permute-start.3
  638.1 0.6 collective-permute-start.4
  638.7 1.3 collective-permute-start.5
  639.9 0.1 select_bitcast_fusion
  640.1 0.7 fusion.25
  640.8 0.0 collective-permute-start.7
  640.8 12.0 %collective-permute-done.4 = bf16[512,512]{1,0:T(8,128)(2,1)S(1)} collective-permute-done((bf16[512,512]{1,0:T(8,128)(2,1)S(1)}, bf16[512,512]{1,0:T(8,128)(2,1)S(1)}, u32[]{:S(2)}, u32[]{:S(2)}) %collective-permute-start.4) | collective-permute-done | bytes 524320 | tf_op jit(solution)/shard_map/ppermute | solution.py:22
  652.9 10.3 %collective-permute-done.5 = bf16[512,512]{1,0:T(8,128)(2,1)S(1)} collective-permute-done((bf16[512,512]{1,0:T(8,128)(2,1)S(1)}, bf16[512,512]{1,0:T(8,128)(2,1)S(1)}, u32[]{:S(2)}, u32[]{:S(2)}) %collective-permute-start.5) | collective-permute-done | bytes 524320 | tf_op jit(solution)/shard_map/ppermute | solution.py:22
  663.2 1.9 add_convert_fusion
  665.1 1.5 gather_fusion.2
  666.5 6.0 all-to-all-start
  672.5 5.5 slice_convert_fusion.3
  678.0 0.0 collective-permute-done.7
  678.0 3.0 collective-permute-start.8
  681.0 2.8 slice_convert_fusion.4
  683.8 6.6 copy.57
  690.4 6.6 copy.58
  697.0 1.5 gather_fusion.4
  698.5 0.0 collective-permute-done.8
  698.5 0.6 slice.86
  699.1 0.6 fusion.26
  699.7 1.5 gather_fusion.3
  (47 shorter events, 0.3 us)
Async XLA Ops:
  0.6 13.9 %copy-start = (bf16[512,512]{1,0:T(8,128)(2,1)S(1)}, bf16[512,512]{1,0:T(8,128)(2,1)}, u32[]{:S(2)}) copy-start(bf16[512,512]{1,0:T(8,128)(2,1)} %param.12) | copy-start | bytes 1572868
  2.1 10.8 %collective-permute-start = (bf16[2,512]{1,0:T(2,128)(2,1)S(1)}, bf16[2,512]{1,0:T(2,128)(2,1)S(1)}, u32[]{:S(2)}, u32[]{:S(2)}) collective-permute-start(bf16[2,512]{1,0:T(2,128)(2,1)S(1)} %pad_maximum_fusion.2), channel_id=1, source_target_pairs={{0,2},{1,3},{2,0},{3,1},{4,6},{5,7},{6,4},{7,5},{8,10},{9,11},{10,... | collective-permute-start | bytes 6152 | tf_op jit(solution)/shard_map/ppermute | solution.py:22
  13.0 6.6 collective-permute-start.1
  600.7 5.1 copy-start.5
  602.5 37.6 %collective-permute-start.6 = (f32[5,512]{1,0:T(8,128)S(1)}, f32[5,512]{1,0:T(8,128)}, u32[]{:S(2)}, u32[]{:S(2)}) collective-permute-start(f32[5,512]{1,0:T(8,128)S(1)} %pad_maximum_fusion), channel_id=1, source_target_pairs={{0,16},{16,0},{1,17},{17,1},{2,18},{18,2},{3,19},{19,3},{4,20},{20... | collective-permute-start | bytes 30728 | tf_op jit(solution)/shard_map/ppermute | solution.py:22
  605.8 8.1 %slice-start = ((s8[16777216]{0:T(1024)(128)(4,1)}), s8[4194304]{0:T(1024)(128)(4,1)S(1)}, s32[]{:S(2)}) async-start(s8[16777216]{0:T(1024)(128)(4,1)} %bitcast.48), calls=%async_computation.1 | async-start | bytes 8388608
  605.8 8.1 %slice-start.1 = ((s8[16777216]{0:T(1024)(128)(4,1)}), s8[4194304]{0:T(1024)(128)(4,1)S(1)}, s32[]{:S(2)}) async-start(s8[16777216]{0:T(1024)(128)(4,1)} %bitcast.48), calls=%async_computation.2 | async-start | bytes 8388608
  605.8 8.1 %slice-start.2 = ((s8[16777216]{0:T(1024)(128)(4,1)}), s8[4194304]{0:T(1024)(128)(4,1)S(1)}, s32[]{:S(2)}) async-start(s8[16777216]{0:T(1024)(128)(4,1)} %bitcast.48), calls=%async_computation.3 | async-start | bytes 8388608
  605.9 8.1 %slice-start.3 = ((s8[16777216]{0:T(1024)(128)(4,1)}), s8[4194304]{0:T(1024)(128)(4,1)S(1)}, s32[]{:S(2)}) async-start(s8[16777216]{0:T(1024)(128)(4,1)} %bitcast.48), calls=%async_computation.4 | async-start | bytes 8388608
  613.4 22.2 %collective-permute-start.2 = (bf16[512,1024]{1,0:T(8,128)(2,1)}, bf16[512,1024]{1,0:T(8,128)(2,1)}, u32[]{:S(2)}, u32[]{:S(2)}) collective-permute-start(bf16[512,1024]{1,0:T(8,128)(2,1)} %slice.85), channel_id=1, source_target_pairs={{0,16},{16,0},{1,17},{17,1},{2,18},{18,2},{3,19},{19,3},{4,20},{20... | collective-permute-start | bytes 3145736 | tf_op jit(solution)/shard_map/ppermute | solution.py:22
  623.0 17.0 %copy-start.2 = (bf16[2,512,1024]{2,1,0:T(8,128)(2,1)S(1)}, bf16[2,512,1024]{2,1,0:T(8,128)(2,1)}, u32[]{:S(2)}) copy-start(bf16[2,512,1024]{2,1,0:T(8,128)(2,1)} %get-tuple-element.24) | copy-start | bytes 6291460
  637.0 3.1 copy-start.4
  638.0 2.8 collective-permute-start.3
  638.1 14.8 %collective-permute-start.4 = (bf16[512,512]{1,0:T(8,128)(2,1)S(1)}, bf16[512,512]{1,0:T(8,128)(2,1)S(1)}, u32[]{:S(2)}, u32[]{:S(2)}) collective-permute-start(bf16[512,512]{1,0:T(8,128)(2,1)S(1)} %get-tuple-element.92), channel_id=1, source_target_pairs={{0,2},{1,3},{2,0},{3,1},{4,6},{5,7},{6,4},{7,5},{8,10},{9,11},{10,... | collective-permute-start | bytes 1572872 | tf_op jit(solution)/shard_map/ppermute | solution.py:22
  638.7 24.5 %collective-permute-start.5 = (bf16[512,512]{1,0:T(8,128)(2,1)S(1)}, bf16[512,512]{1,0:T(8,128)(2,1)S(1)}, u32[]{:S(2)}, u32[]{:S(2)}) collective-permute-start(bf16[512,512]{1,0:T(8,128)(2,1)S(1)} %get-tuple-element.93), channel_id=1, source_target_pairs={{0,3},{1,2},{2,1},{3,0},{4,7},{5,6},{6,5},{7,4},{8,11},{9,10},{10,... | collective-permute-start | bytes 1572872 | tf_op jit(solution)/shard_map/ppermute | solution.py:22
  640.8 37.2 %collective-permute-start.7 = (f32[5,512]{1,0:T(8,128)S(1)}, f32[5,512]{1,0:T(8,128)S(1)}, u32[]{:S(2)}, u32[]{:S(2)}) collective-permute-start(f32[5,512]{1,0:T(8,128)S(1)} %fusion.25), channel_id=1, source_target_pairs={{0,4},{4,0},{8,12},{12,8},{1,5},{5,1},{9,13},{13,9},{2,6},{6,2},{1... | collective-permute-start | bytes 30728 | tf_op jit(solution)/shard_map/ppermute | solution.py:22
  666.5 33.2 %all-to-all-start = ((bf16[4,128,512]{2,1,0:T(8,128)(2,1)}), bf16[4,128,512]{2,1,0:T(8,128)(2,1)S(1)}, u32[]{:S(2)}, u32[]{:S(2)}) async-start(bf16[4,128,512]{2,1,0:T(8,128)(2,1)} %gather_fusion.2), calls=%async_computation | async-start | bytes 1048576 | tf_op jit(solution)/shard_map/all_to_all | solution.py:1261
  678.0 20.5 %collective-permute-start.8 = (f32[5,512]{1,0:T(8,128)S(1)}, f32[5,512]{1,0:T(8,128)S(1)}, u32[]{:S(2)}, u32[]{:S(2)}) collective-permute-start(f32[5,512]{1,0:T(8,128)S(1)} %add.104), channel_id=1, source_target_pairs={{0,8},{4,12},{8,0},{12,4},{1,9},{5,13},{9,1},{13,5},{2,10},{6,14},... | collective-permute-start | bytes 30728 | tf_op jit(solution)/shard_map/ppermute | solution.py:22
  690.4 6.7 copy-start.3
  690.4 10.8 %copy-start.1 = (bf16[512,512]{1,0:T(8,128)(2,1)S(1)}, bf16[512,512]{1,0:T(8,128)(2,1)}, u32[]{:S(2)}) copy-start(bf16[512,512]{1,0:T(8,128)(2,1)} %param.12) | copy-start | bytes 1572868

commit v6 on v5

--- a/solution.py
+++ b/solution.py
@@ -72,7 +72,7 @@
     x_blocks, cot_blocks, place, gains, masks, taps,
     in_w, out_w, gate_w, up_w, down_w,
     in_peer, out_peer, gate_peer, up_peer, outer_land, middle_land, rights_peer,
-    x_out, h_one_out, mixer_out, act_out, grads, dealt, tap_sums, gain_sums,
+    x_out, h_one_out, mixer_out, act_out, grads, dealt, dealt_out, tap_sums, gain_sums,
     x_got, cot_got, x_full, h_one, cot_full, cot_peer, h_two, h_two_peer, proj, mixed, gated, mixer, conv_v,
     out_v, rim, extended, away, pair, pair_got, both_got, dh_got,
     da_got, in_v, gu_v, down_v, dh_sum, ffn_v, right_v, outer_v, middle_v, held, totals, d_ext, edge_v, rim_back,
@@ -640,7 +640,7 @@
         right_copy(2, 2).start()
         got_right(1, 2)
 
-    back_blocks, d_resid = cot_got, dh_sum.at[1, :, pl.ds(0, part)]
+    back_blocks, d_resid, resid_own = cot_got, dh_sum.at[1, :, pl.ds(0, part)], dh_sum.at[1, :, pl.ds(part, part)]
     hone_first, hone_second = columns_out("ic", h_one_out, cot_peer)
     dr_first, dr_second = columns_out("dc", h_two, h_two_peer)
     mixer_rights = 3 * hidden
@@ -669,7 +669,9 @@
     def reload():
         for index in range(CHUNKS):
             da_copy(index).wait_send()
-        for copy in [x_reload] + mixer_reloads + in_reloads:
+        act_store(CHUNKS - 1).wait()
+        act_store(CHUNKS - 2).wait()
+        for copy in [x_reload] + mixer_reloads + in_reloads + down_loads + [act_own_load]:
             copy.start()
 
     def resid_back():
@@ -707,6 +709,7 @@
             gain_sums[1:2, own_half] += jnp.sum(own_grad * own, axis=0, keepdims=True)
             gain_sums[1:2, peer_half] += jnp.sum(other_grad * other, axis=0, keepdims=True)
             resid = x_full[lines, own_part].astype(WIDE) + h_one[lines, own_part].astype(WIDE)
+            resid_own[lines] = resid
             which = jnp.where(outer == shard, 0, 1)
             scaled = mixer[which, lines, columns(core, part)].astype(WIDE) * gains[1:2, own_part]
             d_resid[lines] = cot_full[lines, own_part].astype(WIDE) + scale * (
@@ -720,7 +723,6 @@
     )
 
     def conv_back():
-        act_store(CHUNKS - 2).wait()
         for kind in range(3):
             right_copy(CHUNKS - 2, kind).wait_send()
 
@@ -744,7 +746,6 @@
     def out_ready():
         dr_first.wait_recv()
         dr_second.start()
-        act_store(CHUNKS - 1).wait()
         right_copy(CHUNKS - 1, 0).wait_send()
 
         def body(lines):
@@ -845,16 +846,115 @@
         back_last.start()
         got_mixer_right(3)
 
-    def give_back(step):
+    def give_back(name, block, target, step):
         to, origin = lax.rem(ctx + step, blocks), lax.rem(ctx + blocks - step, blocks)
-        name = "give" + str(step)
+        name = name + str(step)
         return (
-            remote(name, back_blocks.at[to], dealt.at[ctx], {"ctx": to}),
-            remote(name, back_blocks.at[to], dealt.at[origin], {"ctx": to}),
-        )
-
-    given = [give_back(step) for step in range(1, blocks)]
+            remote(name, block(to), target.at[ctx], {"ctx": to}),
+            remote(name, block(to), target.at[origin], {"ctx": to}),
+        )
+
+    def out_block(to):
+        return gated.at[pl.ds(pl.multiple_of(to * block_rows, block_rows), block_rows)]
+
+    given = [give_back("give", lambda to: back_blocks.at[to], dealt, step) for step in range(1, blocks)]
+    given_out = [give_back("out", out_block, dealt_out, step) for step in range(1, blocks)]
     kept = load(9, back_blocks.at[ctx], dealt.at[ctx])
+    kept_out = load(10, out_block(ctx), dealt_out.at[ctx])
+
+    down_loads = [
+        load(index, down_w.at[:, pl.ds(index * chunk, chunk)], gu_v.at[index // 2, index % 2])
+        for index in range(CHUNKS)
+    ]
+    act_own_load = load(21, act_out, da_got)
+    act_peer_load = load(22, rights_peer.at[:, pl.ds(0, hidden)], da_got)
+    ffn_first = remote(
+        "fx", cot_full.at[:, pl.ds(half, half)], h_one.at[:, pl.ds(0, half)], {"shard": 1 - shard}
+    )
+    ffn_core = [
+        remote("fc0", cot_full.at[:, columns(1 - core, part)], out_v.at[0, pl.ds(0, tokens)], {"tp": core_mate}),
+        remote("fc1", h_one.at[:, columns(1 - core, part)], out_v.at[1, pl.ds(0, tokens)], {"tp": core_mate}),
+    ]
+    kept_which = jnp.where(outer == shard, 0, 1)
+
+    def ffn_pair(which):
+        return pl.ds(pl.multiple_of(half + which * part, part), part)
+
+    ffn_outer = [
+        remote(
+            "fy%d" % index,
+            h_one.at[pl.ds(index * block_rows, block_rows), ffn_pair(1 - kept_which)],
+            x_got.at[index],
+            {"tp": outer_mate},
+        )
+        for index in range(blocks)
+    ]
+
+    def ffn_part(start):
+        def body(lines):
+            total = None
+            for index in range(CHUNKS):
+                term = lax.dot_general(
+                    da_got[lines, pl.ds(index * chunk, chunk)], gu_v[index // 2, index % 2],
+                    (((1,), (1,)), ((), ())), preferred_element_type=WIDE,
+                )
+                total = term if total is None else total + term
+            cot_full[lines, pl.ds(start, half)] = total.astype(LOW)
+
+        over_tiles(body)
+
+    def ffn_own():
+        for copy in (cot_outer, cot_core, cot_more, cot_first):
+            copy.wait_send()
+        for copy in down_loads:
+            copy.wait()
+        act_own_load.wait()
+        ffn_part(0)
+        act_peer_load.start()
+
+    def ffn_peer():
+        act_peer_load.wait()
+        ffn_part(half)
+        ffn_first.start()
+
+    def ffn_to_core():
+        ffn_first.wait_recv()
+        for copy in ffn_core:
+            copy.start()
+
+    def ffn_to_outer():
+        for copy in ffn_core:
+            copy.wait_recv()
+
+        def body(lines):
+            own = columns(core, part)
+            h_one[lines, ffn_pair(0)] = (
+                cot_full[lines, own].astype(WIDE) + out_v[0, lines].astype(WIDE)
+            ).astype(LOW)
+            h_one[lines, ffn_pair(1)] = (
+                h_one[lines, own].astype(WIDE) + out_v[1, lines].astype(WIDE)
+            ).astype(LOW)
+
+        over_tiles(body)
+        for copy in ffn_outer:
+            copy.start()
+
+    def block_back():
+        mixer_right(0).wait_send()
+        for index, copy in enumerate(ffn_outer):
+            copy.wait_recv()
+            lines = pl.ds(index * block_rows, block_rows)
+            resid_own[lines] = (
+                resid_own[lines] + h_one[lines, ffn_pair(kept_which)].astype(WIDE) + x_got[index].astype(WIDE)
+            )
+        for to in range(blocks):
+            total = place[0, to] * resid_own[0:block_rows]
+            for index in range(1, blocks):
+                total = total + place[index, to] * resid_own[index * block_rows : (index + 1) * block_rows]
+            gated[to * block_rows : (to + 1) * block_rows] = total.astype(LOW)
+        for out, _ in given_out:
+            out.start()
+        kept_out.start()
 
     def input_back():
         back_last.wait_recv()
@@ -932,6 +1032,22 @@
         dh_last.start()
         got_right(3, 1)
 
+    def last_rights():
+        ffn_own()
+        got_right(3, 2)
+
+    def proj_and_ffn():
+        proj_back()
+        ffn_peer()
+
+    def back_and_ffn():
+        ffn_to_outer()
+        back_three_hops()
+
+    def ends_back():
+        input_back()
+        block_back()
+
     events = {
         0: event_start,
         2: event_first,
@@ -948,15 +1064,16 @@
         18: dh_two_hops,
         20: dh_three_hops,
         21: resid_back,
-        22: lambda: got_right(3, 2),
+        22: last_rights,
         23: conv_back,
         24: out_ready,
-        25: proj_back,
+        25: proj_and_ffn,
         26: in_ready,
         27: back_one_hop,
         28: back_two_hops,
-        30: back_three_hops,
-        31: input_back,
+        29: ffn_to_core,
+        30: back_and_ffn,
+        31: ends_back,
     }
 
     @pl.loop(0, pieces_in_all)
@@ -971,8 +1088,8 @@
 
     for out, _ in x_deals + cot_deals:
         out.wait_send()
-    for copy in (cot_outer, cot_core, cot_more, cot_first,
-                 hone_first, hone_second, dr_first, dr_second, back_away, back_pair, back_last):
+    for copy in (hone_first, hone_second, dr_first, dr_second, back_away, back_pair, back_last,
+                 ffn_first, *ffn_core, *ffn_outer):
         copy.wait_send()
     for name in pieces:
         over_shard(name).wait_send()
@@ -980,10 +1097,11 @@
             over_ctx(name).wait_send()
     for kind in (1, 2):
         right_copy(CHUNKS - 1, kind).wait_send()
-    for kind in range(4):
+    for kind in range(1, 4):
         mixer_right(kind).wait_send()
     kept.wait()
-    for out, into in given:
+    kept_out.wait()
+    for out, into in given + given_out:
         out.wait_send()
         into.wait_recv()
 
@@ -1011,7 +1129,7 @@
             outward_copy(piece).wait_recv()
 
 
-FRONT_COPIES = 88
+FRONT_COPIES = 104
 
 
 def front(x_blocks, cot_blocks, place, gains, masks, taps, in_w, out_w, gate_w, up_w, down_w):
@@ -1038,6 +1156,7 @@
         shape((2, tokens, half), LOW),
         shape((tokens, hidden), LOW),
         shape((rows, 3 * hidden + width), LOW),
+        shape(x_blocks.shape, LOW),
         shape(x_blocks.shape, LOW),
         shape((3, part), WIDE),
         shape((2, width), WIDE),
@@ -1296,16 +1415,12 @@
             return reorder(values, send_order).reshape(per_dev, block_rows, col_count)
 
         place = (targets[None, :] == jnp.arange(per_dev)[:, None]).astype(WIDE)
-        _, _, _, _, _, _, rights_peer, x_full, _, mixer, act, sums, dealt, taps_grad, gain_sums = front(
+        *_, sums, dealt, dealt_out, taps_grad, gain_sums = front(
             blocks_of(hidden_in), blocks_of(out_grad), place, gains,
             jnp.concatenate([first_own, second_own, first_next, second_next], axis=1), conv_taps,
             in_parts, out_weight, gate_weight, up_weight, down_weight,
         )
-        act_all = jnp.concatenate([act, rights_peer[:, :hidden_count]], axis=0)
-        ffn_terms = tp.own_terms(shards.own_tokens(contract_cols(act_all, down_weight)))
-        resid_own = tp.own(x_full, 1).astype(WIDE) + tp.own(shards.join([mixer[0], mixer[1]]), 1).astype(WIDE)
-        block_out = (resid_own + added(ffn_terms)).astype(LOW)
-        block_dealt = to_dealt(block_out)
+        block_dealt = reorder(dealt_out.reshape(row_count, col_count), returning)
         input_dealt = reorder(dealt.reshape(row_count, col_count), returning)
         ends = [hidden_count, 2 * hidden_count, 3 * hidden_count, 3 * hidden_count + col_count]
         parts = [value.astype(WIDE) for value in jnp.split(sums, ends, axis=1)]

time: 709 us -> 667 us (0.941)
  waiting for transfers between devices: 35.1 us -> 0.01 us
  Pallas kernels: 580 us -> 594 us
    ppermute x9 -> x5, waiting for transfers between devices: 35 us -> 0.01 us  [swapped(): lax.ppermute(value, axis, [(source, source ^ step) for source in range(co...]
    pallas_call x1, Pallas kernels: 580 us -> 594 us  [front(): pl.pallas_call(front_kernel, out_shape=outs, in_specs=[vmem, vmem, pl.Blo...]
  transfers between devices with their start and end apart: 10 -> 5, of which waited for: 3 -> 0; matrix products, arithmetic and copies ran while one was open for 9% -> 8% of each run, Pallas kernels for 0% -> 0%
where the time goes in v6:
time: 667 us; the launch traced here: 660 us
  Pallas kernels  594 us (89%)
  other arithmetic  29.2 us (4%)
  local copies, waits for them, and re-layouts  25.6 us (4%)
  starting transfers between devices  9.17 us (1%)
    pallas_call x1, Pallas kernels, front(): pl.pallas_call(front_kernel, out_shape=outs, in_specs=[vmem, vmem, pl.Blo...  594 us
    convert_element_type x2, other arithmetic, on_device(): parts = [value.astype(WIDE) for value in jnp.split(sums, ends, axis=1)]  14.7 us
  transfers between devices with their start and end apart: 5, of which 0 were waited for; matrix products, arithmetic and copies ran while one was open for 8% of the time, Pallas kernels for 0%

profile of v6, /device:TPU:0, one launch (start us, length us, event | category | flops | bytes accessed | tf_op | source)
XLA Modules:
  0.0 659.6 jit_solution(1684479684193855043)
XLA Ops:
  0.6 0.0 copy-start
  0.7 0.7 stack.18
  1.4 0.7 stack.19
  2.1 3.0 collective-permute-start
  5.1 0.8 reduce-window_clone.1
  6.0 0.7 subtract_bitcast_fusion
  6.6 0.1 select_reduce_fusion
  6.7 0.1 slice_compare_fusion.3
  6.8 0.5 broadcast.117
  7.4 1.3 reduce.3
  8.7 0.1 reshape_squeeze.3
  8.8 0.1 copy.47
  8.9 0.7 sort.51
  9.6 0.7 sort.53
  10.4 0.6 sort.52
  11.1 0.6 gather_fusion.4
  11.7 0.6 fusion.5.place
  12.3 0.0 collective-permute-done
  12.4 0.1 collective-permute-start.1
  12.5 0.6 pad_clamp_fusion
  13.1 0.9 copy.51.masks
  13.9 0.0 copy-done
  13.9 1.4 gather_fusion
  15.3 2.4 gather_fusion.1
  17.7 1.3 convert_element_type.28.taps
  19.0 0.0 collective-permute-done.1
  19.0 0.6 maximum_convert_fusion.gains
  19.7 594.3 %shard_map.195 = (bf16[3,1024,512]{2,1,0:T(8,128)(2,1)}, bf16[1024,512]{1,0:T(8,128)(2,1)}, bf16[1024,2048]{1,0:T(8,128)(2,1)}, bf16[1024,2048]{1,0:T(8,128)(2,1...) custom-call(bf16[4,128,512]{2,1,0:T(8,128)(2,1)} %gather_fusion, ...), custom_call_target="tpu_custom_call" | custom-call | flops 274877906944 | bytes 536870912 | tf_op jit(solution)/shard_map/pallas_call | solution.py:1206
  614.0 0.7 constant_dynamic-slice_fusion
  614.7 0.7 pad_maximum_fusion
  615.4 0.2 collective-permute-start.2
  615.5 0.0 copy-start.4
  615.6 11.8 %slice_convert_fusion = (f32[1024,2048]{1,0:T(8,128)}, f32[1024,2048]{1,0:T(8,128)}, f32[1024,2048]{1,0:T(8,128)}) fusion(bf16[1024,8192]{1,0:T(8,128)(2,1)} %get-tuple-element.23), kind=kLoop, calls=%fused_computation.5 | loop fusion | flops 6291456 | bytes 37748736 | tf_op jit(solution)/shard_map/convert_element_type | solution.py:1426
  627.4 0.0 collective-permute-done.2
  627.4 0.0 copy-done.4
  627.4 0.1 collective-permute-start.3
  627.5 5.5 slice_convert_fusion.3
  633.0 0.0 collective-permute-done.3
  633.0 5.8 collective-permute-start.4
  638.8 2.8 slice_convert_fusion.4
  641.7 6.6 %copy.52 = f32[1024,1536]{0,1:T(8,128)} copy(f32[1024,1536]{1,0:T(8,128)} %slice_convert_fusion.3) | data formatting | bytes 12582912 | tf_op jit(solution)/shard_map/reshape | solution.py:1428
  648.3 0.0 copy-start.1
  648.3 0.0 copy-start.3
  648.3 0.0 copy-start.2
  648.3 6.7 %copy.53 = f32[1024,3,512]{2,0,1:T(8,128)} copy(f32[1024,3,512]{0,2,1:T(8,128)} %bitcast.43) | data formatting | bytes 12582912
  654.9 0.0 copy-done.3
  654.9 1.5 gather_fusion.3
  656.4 0.0 copy-done.2
  656.4 1.5 gather_fusion.2
  657.9 0.0 collective-permute-done.4
  657.9 0.6 slice.60
  658.5 0.6 fusion.12
  659.1 0.0 copy-done.1
  (27 shorter events, 0.2 us)
Async XLA Ops:
  0.6 13.3 %copy-start = (bf16[512,512]{1,0:T(8,128)(2,1)S(1)}, bf16[512,512]{1,0:T(8,128)(2,1)}, u32[]{:S(2)}) copy-start(bf16[512,512]{1,0:T(8,128)(2,1)} %param.12) | copy-start | bytes 1572868
  2.1 10.3 %collective-permute-start = (bf16[2,512]{1,0:T(2,128)(2,1)S(1)}, bf16[2,512]{1,0:T(2,128)(2,1)S(1)}, u32[]{:S(2)}, u32[]{:S(2)}) collective-permute-start(bf16[2,512]{1,0:T(2,128)(2,1)S(1)} %pad_maximum_fusion.2), channel_id=1, source_target_pairs={{0,2},{1,3},{2,0},{3,1},{4,6},{5,7},{6,4},{7,5},{8,10},{9,11},{10,... | collective-permute-start | bytes 6152 | tf_op jit(solution)/shard_map/ppermute | solution.py:22
  12.4 6.6 %collective-permute-start.1 = (bf16[2,2,512]{2,1,0:T(2,128)(2,1)S(1)}, bf16[2,2,512]{2,1,0:T(2,128)(2,1)S(1)}, u32[]{:S(2)}, u32[]{:S(2)}) collective-permute-start(bf16[2,2,512]{2,1,0:T(2,128)(2,1)S(1)} %pad_maximum_fusion.1), channel_id=1, source_target_pairs={{0,1},{1,0},{2,3},{3,2},{4,5},{5,4},{6,7},{7,6},{8,9},{9,8},{10,11... | collective-permute-start | bytes 12296 | tf_op jit(solution)/shard_map/ppermute | solution.py:22
  615.4 12.0 %collective-permute-start.2 = (f32[5,512]{1,0:T(8,128)S(1)}, f32[5,512]{1,0:T(8,128)S(1)}, u32[]{:S(2)}, u32[]{:S(2)}) collective-permute-start(f32[5,512]{1,0:T(8,128)S(1)} %pad_maximum_fusion), channel_id=1, source_target_pairs={{0,16},{16,0},{1,17},{17,1},{2,18},{18,2},{3,19},{19,3},{4,20},{20... | collective-permute-start | bytes 30728 | tf_op jit(solution)/shard_map/ppermute | solution.py:22
  615.5 11.8 %copy-start.4 = (f32[3,512]{1,0:T(4,128)S(1)}, f32[3,512]{1,0:T(4,128)}, u32[]{:S(2)}) copy-start(f32[3,512]{1,0:T(4,128)} %get-tuple-element.24) | copy-start | bytes 18436
  627.4 5.5 collective-permute-start.3
  633.0 25.0 %collective-permute-start.4 = (f32[5,512]{1,0:T(8,128)S(1)}, f32[5,512]{1,0:T(8,128)S(1)}, u32[]{:S(2)}, u32[]{:S(2)}) collective-permute-start(f32[5,512]{1,0:T(8,128)S(1)} %add.64), channel_id=1, source_target_pairs={{0,8},{4,12},{8,0},{12,4},{1,9},{5,13},{9,1},{13,5},{2,10},{6,14},... | collective-permute-start | bytes 30728 | tf_op jit(solution)/shard_map/ppermute | solution.py:22
  648.3 10.9 %copy-start.1 = (bf16[512,512]{1,0:T(8,128)(2,1)S(1)}, bf16[512,512]{1,0:T(8,128)(2,1)}, u32[]{:S(2)}) copy-start(bf16[512,512]{1,0:T(8,128)(2,1)} %param.12) | copy-start | bytes 1572868
  648.3 6.7 %copy-start.3 = (bf16[4,128,512]{2,1,0:T(8,128)(2,1)S(1)}, bf16[4,128,512]{2,1,0:T(8,128)(2,1)}, u32[]{:S(2)}) copy-start(bf16[4,128,512]{2,1,0:T(8,128)(2,1)} %get-tuple-element.22) | copy-start | bytes 1572868
  648.3 8.2 %copy-start.2 = (bf16[4,128,512]{2,1,0:T(8,128)(2,1)S(1)}, bf16[4,128,512]{2,1,0:T(8,128)(2,1)}, u32[]{:S(2)}) copy-start(bf16[4,128,512]{2,1,0:T(8,128)(2,1)} %get-tuple-element.20) | copy-start | bytes 1572868

commit v7 on v6

--- a/solution.py
+++ b/solution.py
@@ -69,11 +69,11 @@
 
 
 def front_kernel(
-    x_blocks, cot_blocks, place, gains, masks, taps,
+    x_in, cot_in, sending, place, own_gains, masks, taps,
     in_w, out_w, gate_w, up_w, down_w,
     in_peer, out_peer, gate_peer, up_peer, outer_land, middle_land, rights_peer,
-    x_out, h_one_out, mixer_out, act_out, grads, dealt, dealt_out, tap_sums, gain_sums,
-    x_got, cot_got, x_full, h_one, cot_full, cot_peer, h_two, h_two_peer, proj, mixed, gated, mixer, conv_v,
+    x_out, h_one_out, mixer_out, act_out, grads, dealt, dealt_out, small_sums,
+    x_blocks, cot_blocks, gains, gain_sums, small, small_got, x_got, cot_got, x_full, h_one, cot_full, cot_peer, h_two, h_two_peer, proj, mixed, gated, mixer, conv_v,
     out_v, rim, extended, away, pair, pair_got, both_got, dh_got,
     da_got, in_v, gu_v, down_v, dh_sum, ffn_v, right_v, outer_v, middle_v, held, totals, d_ext, edge_v, rim_back,
     send, recv, local, in_send, outer_recv, middle_recv, out_send, out_recv, own_done,
@@ -160,17 +160,49 @@
     def load(index, source, target):
         return pltpu.make_async_copy(source, target, local.at[index])
 
+    def own_weights(index):
+        strip = pl.ds(index * chunk, chunk)
+        room = gu_v if index % 2 == 0 else in_v
+        base = 13 + 4 * (index % 2)
+        return [
+            load(base, gate_w.at[:, strip], room.at[0, 0]),
+            load(base + 1, up_w.at[:, strip], room.at[0, 1]),
+        ]
+
+    def peer_weights(index):
+        strip = pl.ds(index * chunk, chunk)
+        room = gu_v if index % 2 == 0 else in_v
+        base = 15 + 4 * (index % 2)
+        return [
+            load(base, gate_peer.at[:, strip], room.at[1, 0]),
+            load(base + 1, up_peer.at[:, strip], room.at[1, 1]),
+        ]
+
+    def to_blocks(source, target):
+        for to in range(blocks):
+            total = sending[to, 0] * source[0:block_rows].astype(WIDE)
+            for slot in range(1, blocks):
+                lines = pl.ds(slot * block_rows, block_rows)
+                total = total + sending[to, slot] * source[lines].astype(WIDE)
+            target[to] = total.astype(LOW)
+
+    for name in ("b", "v", "c", "o", "g0", "u0"):
+        over_shard(name).start()
+    gains[:, own_part] = own_gains[...]
+    gain_outer, gain_core, gain_more = gather("gg", gains)
+    gain_outer.start()
+    gain_core.start()
+    to_blocks(x_in, x_blocks)
     x_deals = [deal("x", x_blocks, x_got, step) for step in range(1, blocks)]
     cot_deals = [deal("cot", cot_blocks, cot_got, step) for step in range(1, blocks)]
     for out, _ in x_deals:
         out.start()
-    for name in ("b", "v", "c", "o", "g0", "u0"):
-        over_shard(name).start()
     own_loads = [load(index, in_w.at[index], in_v.at[0, index]) for index in range(3)]
     own_loads.append(load(3, out_w, out_v.at[0]))
     own_loads.append(load(4, down_w, down_v))
-    for copy in own_loads:
+    for copy in own_loads + own_weights(0):
         copy.start()
+    to_blocks(cot_in, cot_blocks)
 
     def packed(source, got, deals, full):
         got[ctx] = source[ctx]
@@ -196,8 +228,12 @@
     cot_outer, cot_core, cot_more = gather("cg", cot_full)
     cot_outer.start()
     cot_core.start()
+    gain_outer.wait_recv()
+    gain_more.start()
     x_core.wait_recv()
     x_more.wait_recv()
+    gain_core.wait_recv()
+    gain_more.wait_recv()
 
     x_store = load(5, x_full, x_out)
     x_store.start()
@@ -340,27 +376,79 @@
             da_copy(0).start()
             over_shard("u1").start()
 
+    def act_store(index):
+        return load(21 + index % 2, ffn_v.at[index % 2, 0], act_out.at[:, pl.ds(index * chunk, chunk)])
+
+    def right_copy(index, kind):
+        strip = pl.ds(kind * hidden + index * chunk, chunk)
+        return remote(
+            "r%d%d" % (index, kind), ffn_v.at[index % 2, kind], rights_peer.at[:, strip], {"shard": 1 - shard}
+        )
+
+    def right_load(index, kind):
+        strip = pl.ds(kind * hidden + index * chunk, chunk)
+        return load(23 + kind, rights_peer.at[:, strip], right_v.at[kind])
+
+    def ready(index):
+        for kind in "gu":
+            if "%s%d" % (kind, index) not in direct:
+                over_ctx("%s%d" % (kind, index)).wait_recv()
+        for copy in peer_weights(index):
+            copy.start()
+
+    def feed(index, lines, kinds=(0, 1, 2)):
+        room = gu_v if index % 2 == 0 else in_v
+        slot = index % 2
+        strip = pl.ds(index * chunk, chunk)
+
+        def pre(kind):
+            return jnp.dot(
+                h_two[lines, own_half], room[0, kind], preferred_element_type=WIDE
+            ) + jnp.dot(h_two[lines, peer_half], room[1, kind], preferred_element_type=WIDE)
+
+        gate_pre, up_pre = pre(0), pre(1)
+        sigmoid = jax.nn.sigmoid(gate_pre)
+        silu = gate_pre * sigmoid
+        if 0 in kinds:
+            ffn_v[slot, 0, lines] = (silu * up_pre).astype(LOW)
+        if 1 not in kinds:
+            return
+        d_act = da_own[lines, strip].astype(WIDE) + da_got[lines, strip].astype(WIDE)
+        ffn_v[slot, 1, lines] = (
+            d_act * up_pre * sigmoid * (1.0 + gate_pre * (1.0 - sigmoid))
+        ).astype(LOW)
+        ffn_v[slot, 2, lines] = (d_act * silu).astype(LOW)
+
+    pump("g1")
+    ready(0)
+    tiles = [pl.ds(start, tile) for start in range(0, tokens, tile)]
     for index, lines in enumerate(stages):
         hops[index][1].wait_recv()
         mixer[core, lines] = (pair[lines].astype(WIDE) + both_got[lines].astype(WIDE)).astype(LOW)
         hops[index][2].start()
-    pump("g1")
-    for index, lines in enumerate(stages):
         hops[index][2].wait_recv()
+
+        @pl.loop(0, tile // step)
+        def _(turn, start=index * tile):
+            lines = pl.ds(pl.multiple_of(start + turn * step, step), step)
+            own = x_full[lines, own_half].astype(WIDE) + mixer[0, lines].astype(WIDE)
+            other = x_full[lines, peer_half].astype(WIDE) + mixer[1, lines].astype(WIDE)
+            total = jnp.sum(own * own, axis=1, keepdims=True) + jnp.sum(other * other, axis=1, keepdims=True)
+            scale = lax.rsqrt(total / width + EPS)
+            h_two[lines, own_half] = (own * scale * gains[1:2, own_half]).astype(LOW)
+            h_two[lines, peer_half] = (other * scale * gains[1:2, peer_half]).astype(LOW)
+
+        if index == 0:
+            for copy in own_weights(0) + peer_weights(0):
+                copy.wait()
+        feed(0, lines, (0,))
+    right_copy(0, 0).start()
+    act_store(0).start()
     mixer_store = load(12, mixer, mixer_out)
     mixer_store.start()
 
-    @pl.loop(0, tokens // step)
-    def _(index):
-        lines = pl.ds(pl.multiple_of(index * step, step), step)
-        own = x_full[lines, own_half].astype(WIDE) + mixer[0, lines].astype(WIDE)
-        other = x_full[lines, peer_half].astype(WIDE) + mixer[1, lines].astype(WIDE)
-        total = jnp.sum(own * own, axis=1, keepdims=True) + jnp.sum(other * other, axis=1, keepdims=True)
-        scale = lax.rsqrt(total / width + EPS)
-        h_two[lines, own_half] = (own * scale * gains[1:2, own_half]).astype(LOW)
-        h_two[lines, peer_half] = (other * scale * gains[1:2, peer_half]).astype(LOW)
-
     h_two_first, h_two_second = columns_out("hc", h_two, h_two_peer)
+    h_two_first.start()
     x_store.wait()
     for copy in (x_outer, x_core, x_more):
         copy.wait_send()
@@ -383,64 +471,6 @@
     turned(0, cot_full, shard * half, 0)
     turned(0, cot_peer, 0, tokens)
     turned(1, h_two, shard * half, 0)
-
-    def own_weights(index):
-        strip = pl.ds(index * chunk, chunk)
-        room = gu_v if index % 2 == 0 else in_v
-        base = 13 + 4 * (index % 2)
-        return [
-            load(base, gate_w.at[:, strip], room.at[0, 0]),
-            load(base + 1, up_w.at[:, strip], room.at[0, 1]),
-        ]
-
-    def peer_weights(index):
-        strip = pl.ds(index * chunk, chunk)
-        room = gu_v if index % 2 == 0 else in_v
-        base = 15 + 4 * (index % 2)
-        return [
-            load(base, gate_peer.at[:, strip], room.at[1, 0]),
-            load(base + 1, up_peer.at[:, strip], room.at[1, 1]),
-        ]
-
-    def act_store(index):
-        return load(21 + index % 2, ffn_v.at[index % 2, 0], act_out.at[:, pl.ds(index * chunk, chunk)])
-
-    def right_copy(index, kind):
-        strip = pl.ds(kind * hidden + index * chunk, chunk)
-        return remote(
-            "r%d%d" % (index, kind), ffn_v.at[index % 2, kind], rights_peer.at[:, strip], {"shard": 1 - shard}
-        )
-
-    def right_load(index, kind):
-        strip = pl.ds(kind * hidden + index * chunk, chunk)
-        return load(23 + kind, rights_peer.at[:, strip], right_v.at[kind])
-
-    def ready(index):
-        for kind in "gu":
-            if "%s%d" % (kind, index) not in direct:
-                over_ctx("%s%d" % (kind, index)).wait_recv()
-        for copy in peer_weights(index):
-            copy.start()
-
-    def feed(index, lines):
-        room = gu_v if index % 2 == 0 else in_v
-        slot = index % 2
-        strip = pl.ds(index * chunk, chunk)
-
-        def pre(kind):
-            return jnp.dot(
-                h_two[lines, own_half], room[0, kind], preferred_element_type=WIDE
-            ) + jnp.dot(h_two[lines, peer_half], room[1, kind], preferred_element_type=WIDE)
-
-        gate_pre, up_pre = pre(0), pre(1)
-        d_act = da_own[lines, strip].astype(WIDE) + da_got[lines, strip].astype(WIDE)
-        sigmoid = jax.nn.sigmoid(gate_pre)
-        silu = gate_pre * sigmoid
-        ffn_v[slot, 0, lines] = (silu * up_pre).astype(LOW)
-        ffn_v[slot, 1, lines] = (
-            d_act * up_pre * sigmoid * (1.0 + gate_pre * (1.0 - sigmoid))
-        ).astype(LOW)
-        ffn_v[slot, 2, lines] = (d_act * silu).astype(LOW)
 
     def back(index, lines):
         room = gu_v if index % 2 == 0 else in_v
@@ -583,8 +613,6 @@
     dh_away = remote("dh1", away, pair_got, {"tp": core_mate})
     dh_pair = remote("dh2", pair, dh_got, {"tp": outer_mate})
     dh_last = remote("dh3", mixer.at[core], mixer.at[core], {"tp": core_mate})
-    tiles = [pl.ds(start, tile) for start in range(0, tokens, tile)]
-
     def whole_feed(index):
         feed_start(index)
         for lines in tiles:
@@ -598,22 +626,27 @@
             for copy in own_weights(index + 1):
                 copy.start()
 
-    for copy in own_weights(0):
-        copy.start()
-    ready(0)
-    whole_feed(0)
-    right_copy(0, 0).start()
-    da_copy(1).start()
-    h_two_first.start()
+    da_copy(0).wait_recv()
+    for lines in tiles:
+        feed(0, lines, (1, 2))
     right_copy(0, 1).start()
     right_copy(0, 2).start()
+    da_copy(1).start()
     whole_back(0)
     pump("u1")
 
     def event_start():
         got_right(0, 0)
 
+    def event_columns():
+        h_two_first.wait_recv()
+        h_two_second.start()
+        h_two_second.wait()
+        turned(1, h_two_peer, 0, tokens)
+        got_right(0, 1)
+
     def event_first():
+        got_right(0, 2)
         ready(1)
         whole_feed(1)
         for kind in range(3):
@@ -622,11 +655,6 @@
             over_shard(name).start()
         da_copy(2).start()
         over_shard("g3").start()
-        h_two_first.wait_recv()
-        h_two_second.start()
-        h_two_second.wait()
-        turned(1, h_two_peer, 0, tokens)
-        got_right(0, 1)
 
     def event_second():
         over_shard("g2").wait_recv()
@@ -781,8 +809,9 @@
                 if tap > 0:
                     value = value * masks[lines, tap - 1 : tap]
                 sums[tap] = sums[tap] + jnp.sum(value, axis=0, keepdims=True)
+        small[...] = jnp.zeros(small.shape, WIDE)
         for tap in range(3):
-            tap_sums[tap : tap + 1] = sums[tap]
+            small[tap : tap + 1] = sums[tap]
         for kind in range(1, 4):
             mixer_right(kind).start()
 
@@ -1044,15 +1073,28 @@
         ffn_to_outer()
         back_three_hops()
 
+    small_shard = remote("ss", small, small_got.at[blocks], {"shard": 1 - shard})
+
+    def small_ctx(step):
+        to, origin = lax.rem(ctx + step, blocks), lax.rem(ctx + blocks - step, blocks)
+        return (
+            remote("sc%d" % step, small_got.at[ctx], small_got.at[ctx], {"ctx": to}),
+            remote("sc%d" % step, small_got.at[ctx], small_got.at[origin], {"ctx": to}),
+        )
+
+    small_steps = [small_ctx(step) for step in range(1, blocks)]
+
     def ends_back():
         input_back()
         block_back()
+        small[3:5] = gain_sums[:, own_part]
+        small_shard.start()
 
     events = {
         0: event_start,
-        2: event_first,
-        3: lambda: whole_back(1),
-        4: lambda: got_right(0, 2),
+        2: event_columns,
+        4: event_first,
+        5: lambda: whole_back(1),
         6: lambda: got_right(1, 0),
         8: lambda: got_right(1, 1),
         10: event_second,
@@ -1082,13 +1124,27 @@
             pl.when(piece == turn)(event)
         grad_piece(piece)
 
+    small_shard.wait_recv()
+    small_got[ctx] = small[...] + small_got[blocks]
+    for out, _ in small_steps:
+        out.start()
+
     @pl.when(middle)
     def _():
         finish(pieces_in_all - 1)
 
+    for _, into in small_steps:
+        into.wait_recv()
+    total = small_got[0]
+    for index in range(1, blocks):
+        total = total + small_got[index]
+    small_sums[...] = total
+
     for out, _ in x_deals + cot_deals:
         out.wait_send()
-    for copy in (hone_first, hone_second, dr_first, dr_second, back_away, back_pair, back_last,
+    for out, _ in small_steps:
+        out.wait_send()
+    for copy in (small_shard, gain_outer, gain_core, gain_more, hone_first, hone_second, dr_first, dr_second, back_away, back_pair, back_last,
                  ffn_first, *ffn_core, *ffn_outer):
         copy.wait_send()
     for name in pieces:
@@ -1129,15 +1185,16 @@
             outward_copy(piece).wait_recv()
 
 
-FRONT_COPIES = 104
-
-
-def front(x_blocks, cot_blocks, place, gains, masks, taps, in_w, out_w, gate_w, up_w, down_w):
-    tokens = x_blocks.shape[0] * x_blocks.shape[1]
-    part = x_blocks.shape[2]
-    width = gains.shape[1]
+FRONT_COPIES = 112
+
+
+def front(x_in, cot_in, sending, place, own_gains, masks, taps, in_w, out_w, gate_w, up_w, down_w):
+    tokens, part = x_in.shape
+    blocks = place.shape[0]
+    block_shape = (blocks, tokens // blocks, part)
+    rows, hidden = gate_w.shape
+    width = 4 * part
     half = width // 2
-    rows, hidden = gate_w.shape
     chunk = hidden // CHUNKS
     pieces = (3 * hidden + width) // PIECE
     vmem = pl.BlockSpec(memory_space=pltpu.VMEM)
@@ -1156,16 +1213,21 @@
         shape((2, tokens, half), LOW),
         shape((tokens, hidden), LOW),
         shape((rows, 3 * hidden + width), LOW),
-        shape(x_blocks.shape, LOW),
-        shape(x_blocks.shape, LOW),
-        shape((3, part), WIDE),
-        shape((2, width), WIDE),
+        shape(block_shape, LOW),
+        shape(block_shape, LOW),
+        shape((8, part), WIDE),
     ]
     low, wide = (lambda *dims: pltpu.VMEM(dims, LOW)), (lambda *dims: pltpu.VMEM(dims, WIDE))
     dma = pltpu.SemaphoreType.DMA
     scratch = [
-        low(*x_blocks.shape),
-        low(*x_blocks.shape),
+        low(*block_shape),
+        low(*block_shape),
+        wide(8, width),
+        wide(2, width),
+        wide(8, part),
+        wide(blocks + 1, 8, part),
+        low(*block_shape),
+        low(*block_shape),
         low(tokens, width),
         low(tokens, width),
         low(tokens, width),
@@ -1206,9 +1268,9 @@
     return pl.pallas_call(
         front_kernel,
         out_shape=outs,
-        in_specs=[vmem, vmem, pl.BlockSpec(memory_space=pltpu.SMEM)] + [vmem] * 3
+        in_specs=[vmem, vmem] + [pl.BlockSpec(memory_space=pltpu.SMEM)] * 2 + [vmem] * 3
         + [hbm] * 5,
-        out_specs=[hbm] * (len(outs) - 2) + [vmem] * 2,
+        out_specs=[hbm] * (len(outs) - 1) + [vmem],
         scratch_shapes=scratch,
         compiler_params=pltpu.CompilerParams(
             collective_id=2, has_side_effects=True, vmem_limit_bytes=63 * 1024 * 1024
@@ -1216,7 +1278,7 @@
         cost_estimate=pl.CostEstimate(
             flops=2 * tokens * width * hidden * 64, bytes_accessed=1 << 29, transcendentals=0
         ),
-    )(x_blocks, cot_blocks, place, gains, masks, taps, in_w, out_w, gate_w, up_w, down_w)
+    )(x_in, cot_in, sending, place, own_gains, masks, taps, in_w, out_w, gate_w, up_w, down_w)
 
 
 class Features:
@@ -1331,6 +1393,14 @@
             return lax.all_to_all(product.astype(LOW), "shard", split_axis=0, concat_axis=1, tiled=True)
         rows = product.shape[0] // 2
         return self.join([product[:rows].astype(LOW), swapped(product[rows:].astype(LOW), "shard", 1)])
+
+
+def deal_routes(dealing, own_blocks, ctx_rank, per_dev, per_peer):
+    send_order = jnp.argsort(own_blocks // per_dev, stable=True)
+    wanted = jnp.where(dealing // per_dev == ctx_rank, 0, 1)
+    chosen = jnp.argsort(wanted, axis=1, stable=True)[:, :per_peer]
+    targets = (jnp.take_along_axis(dealing, chosen, 1) % per_dev).reshape(-1)
+    return send_order, targets, jnp.argsort(targets), jnp.argsort(send_order)
 
 
 def on_device(
@@ -1359,12 +1429,6 @@
     block_rows = row_count // per_dev
     dealing = deal_order[0].reshape(ctx_size, per_dev)
     own_blocks = lax.dynamic_index_in_dim(dealing, ctx_rank, 0, keepdims=False)
-    send_order = jnp.argsort(own_blocks // per_dev, stable=True)
-    wanted = jnp.where(dealing // per_dev == ctx_rank, 0, 1)
-    chosen = jnp.argsort(wanted, axis=1, stable=True)[:, :per_peer]
-    targets = (jnp.take_along_axis(dealing, chosen, 1) % per_dev).reshape(-1)
-    placing = jnp.argsort(targets)
-    returning = jnp.argsort(send_order)
 
     def reorder(values, index):
         blocks = values.reshape(per_dev, block_rows, values.shape[1])
@@ -1406,29 +1470,33 @@
     first_next = (position[3 : row_count + 3] >= 1).astype(WIDE)[:, None]
     second_next = (position[4 : row_count + 4] >= 2).astype(WIDE)[:, None]
     conv_taps = conv_weight.astype(WIDE)
-    gains = tp.gather(jnp.stack([norm1_gain, norm2_gain])).astype(WIDE)
-    gain_one, gain_two = gains[0], gains[1]
-    in_parts = jnp.moveaxis(in_weight, 1, 0)
+    gains = jnp.stack([norm1_gain, norm2_gain])
 
     if shards.paired:
-        def blocks_of(values):
-            return reorder(values, send_order).reshape(per_dev, block_rows, col_count)
-
-        place = (targets[None, :] == jnp.arange(per_dev)[:, None]).astype(WIDE)
-        *_, sums, dealt, dealt_out, taps_grad, gain_sums = front(
-            blocks_of(hidden_in), blocks_of(out_grad), place, gains,
+        goes_to = own_blocks // per_dev
+        slots = jnp.arange(per_dev, dtype=jnp.int32)
+        sending = (goes_to[None, :] == slots[:, None]).astype(WIDE)
+        wants = ctx_rank * per_dev + slots
+        place = jnp.sum((dealing[None] == wants[:, None, None]).astype(WIDE), axis=2)
+        *_, sums, dealt, dealt_out, small_sum = front(
+            hidden_in, out_grad, sending, place, jnp.pad(gains.astype(WIDE), ((0, 6), (0, 0))),
             jnp.concatenate([first_own, second_own, first_next, second_next], axis=1), conv_taps,
-            in_parts, out_weight, gate_weight, up_weight, down_weight,
-        )
-        block_dealt = reorder(dealt_out.reshape(row_count, col_count), returning)
-        input_dealt = reorder(dealt.reshape(row_count, col_count), returning)
+            jnp.moveaxis(in_weight, 1, 0), out_weight, gate_weight, up_weight, down_weight,
+        )
+        block_dealt = reorder(dealt_out.reshape(row_count, col_count), goes_to)
+        input_dealt = reorder(dealt.reshape(row_count, col_count), goes_to)
         ends = [hidden_count, 2 * hidden_count, 3 * hidden_count, 3 * hidden_count + col_count]
-        parts = [value.astype(WIDE) for value in jnp.split(sums, ends, axis=1)]
-        down_total, gate_total, up_total, out_total, in_flat_total = parts
-        in_total = in_flat_total.reshape(in_weight.shape)
-        gain_one_grad, gain_two_grad = tp.own(gain_sums, 1)
+        ends += [ends[-1] + col_count, ends[-1] + 2 * col_count]
+        down_total, gate_total, up_total, out_total, *in_parts = jnp.split(sums, ends, axis=1)
+        in_total = jnp.moveaxis(jnp.stack(in_parts).astype(WIDE), 0, 1)
+        down_total, gate_total, up_total, out_total = [
+            value.astype(WIDE) for value in (down_total, gate_total, up_total, out_total)
+        ]
     else:
         in_w = shards.weight(in_weight.reshape(weight_rows, -1))
+        send_order, targets, placing, returning = deal_routes(dealing, own_blocks, ctx_rank, per_dev, per_peer)
+        full_gains = tp.gather(gains).astype(WIDE)
+        gain_one, gain_two = full_gains[0], full_gains[1]
         x_full = tp.gather(to_packed(hidden_in))
         out_w = shards.weight(out_weight)
         cot_full = tp.gather(to_packed(out_grad))
@@ -1523,9 +1591,9 @@
         d_input = d_resid + norm_back(dh_one, normed_one, scale_one, gain_one)
         dealt = to_dealt(jnp.concatenate([block_out, tp.own(d_input, 1).astype(LOW)], axis=1))
         block_dealt, input_dealt = dealt[:, :col_count], dealt[:, col_count:]
-
-    small = jnp.concatenate([taps_grad, gain_one_grad[None], gain_two_grad[None]], axis=0)
-    small_sum = butterfly_sum(butterfly_sum(small, "shard"), "ctx")
+        small = jnp.concatenate([taps_grad, gain_one_grad[None], gain_two_grad[None]], axis=0)
+        small_sum = butterfly_sum(butterfly_sum(small, "shard"), "ctx")
+
     return (
         block_dealt,
         input_dealt,

time: 667 us -> 641 us (0.961)
  local copies, waits for them, and re-layouts: 25.6 us -> 6.79 us
  starting transfers between devices: 9.17 us -> 0 us
    ppermute x5 -> x0, starting transfers between devices: 9.17 us -> none  [swapped(): lax.ppermute(value, axis, [(source, source ^ step) for source in range(co...]
    unnamed x13 -> x9, local copies, waits for them, and re-layouts: 7.22 us -> 0.53 us
    convert_element_type x4 -> x3, other arithmetic: 15.9 us -> 16.5 us  [the longest x2 15.9 us: on_device(): value.astype(WIDE)]
  transfers between devices with their start and end apart: 5 -> 0, of which waited for: 0 -> 0; matrix products, arithmetic and copies ran while one was open for 8% -> 0% of each run, Pallas kernels for 0% -> 0%
where the time goes in v7:
time: 641 us; the launch traced here: 634 us
  Pallas kernels  600 us (94%)
  other arithmetic  26 us (4%)
  local copies, waits for them, and re-layouts  6.79 us (1%)
    pallas_call x1, Pallas kernels, front(): pl.pallas_call(front_kernel, out_shape=outs, in_specs=[vmem, vmem] + [pl....  600 us
    convert_element_type x2, other arithmetic, on_device(): value.astype(WIDE)  15.9 us

profile of v7, /device:TPU:0, one launch (start us, length us, event | category | flops | bytes accessed | tf_op | source)
XLA Modules:
  0.0 633.8 jit_solution(15102549749148895657)
XLA Ops:
  0.7 0.8 reduce-window_clone.1
  1.5 0.7 subtract_bitcast_fusion
  2.1 0.1 select_reduce_fusion
  2.2 0.1 slice_compare_fusion.3
  2.4 0.9 copy.28.masks
  3.3 0.5 broadcast.128
  3.8 1.3 reduce.3
  5.1 0.1 reshape_squeeze.3
  5.2 0.0 copy-start.3
  5.2 0.6 fusion.4.sending
  5.8 0.7 convert_reduce_fusion.place
  6.5 0.7 stack.21
  7.2 0.7 stack.22
  7.9 0.6 fusion.3.own_gains
  8.5 0.0 copy-done.3
  8.5 1.3 convert_element_type.31.taps
  9.8 599.8 %shard_map.195 = (bf16[3,1024,512]{2,1,0:T(8,128)(2,1)}, bf16[1024,512]{1,0:T(8,128)(2,1)}, bf16[1024,2048]{1,0:T(8,128)(2,1)}, bf16[1024,2048]{1,0:T(8,128)(2,1...) custom-call(bf16[512,512]{1,0:T(8,128)(2,1)} %x_in.1, ...), custom_call_target="tpu_custom_call" | custom-call | flops 274877906944 | bytes 536870912 | tf_op jit(solution)/shard_map/pallas_call | solution.py:1268
  609.6 4.1 slice_convert_fusion.3
  613.7 0.0 copy-start.1
  613.7 0.0 copy-start
  613.7 3.2 convert_bitcast_fusion
  616.9 0.7 fusion.6
  617.6 0.0 copy-done.1
  617.6 1.4 gather_fusion.1
  619.0 0.0 copy-done
  619.0 1.4 gather_fusion
  620.4 0.0 copy-start.2
  620.4 11.8 %slice_convert_fusion = (f32[1024,2048]{1,0:T(8,128)}, f32[1024,2048]{1,0:T(8,128)}, f32[1024,2048]{1,0:T(8,128)}) fusion(bf16[1024,8192]{1,0:T(8,128)(2,1)} %get-tuple-element.16), kind=kLoop, calls=%fused_computation.3 | loop fusion | flops 6291456 | bytes 37748736 | tf_op jit(solution)/shard_map/convert_element_type | solution.py:1493
  632.2 0.0 copy-done.2
  632.2 0.6 fusion.8
  632.8 0.6 slice.22
  (10 shorter events, 0.1 us)
Async XLA Ops:
  5.2 3.3 copy-start.3
  613.7 3.9 copy-start.1
  613.7 5.3 copy-start
  620.4 11.8 %copy-start.2 = (f32[8,512]{1,0:T(8,128)S(1)}, f32[8,512]{1,0:T(8,128)}, u32[]{:S(2)}) copy-start(f32[8,512]{1,0:T(8,128)} %get-tuple-element.17) | copy-start | bytes 49156

commit v8 on v7

--- a/solution.py
+++ b/solution.py
@@ -141,7 +141,7 @@
         pieces["g%d" % index] = (gate_w.at[:, strip], gate_peer.at[:, strip])
         pieces["u%d" % index] = (up_w.at[:, strip], up_peer.at[:, strip])
 
-    direct = ["%s%d" % (kind, index) for kind in "gu" for index in range(2, CHUNKS)]
+    direct = ["g2", "u2", "u3"]
 
     def over_shard(name):
         source, target = pieces[name]
@@ -250,15 +250,37 @@
     h_one_store.start()
     pump("c")
 
-    def columns_out(name, full, got):
-        strip = pl.ds(pl.multiple_of((1 - shard) * half + core * part, part), part)
-        target = columns(core, part)
-        first = remote(name + "x", full.at[:, strip], got.at[:, target], {"shard": 1 - shard})
-        second = remote(name + "core", got.at[:, target], got.at[:, target], {"tp": core_mate})
-        return first, second
-
-    cot_first, cot_second = columns_out("cc", cot_full, cot_peer)
-
+    class Columns:
+        def __init__(self, name, full, got):
+            size = half // 4
+            source = pl.ds(pl.multiple_of((1 - shard) * half + tp * size, size), size)
+            own, mate = columns(tp, size), columns(outer_mate, size)
+            self.shard = remote(name + "x", full.at[:, source], got.at[:, own], {"shard": 1 - shard})
+            self.outer = remote(name + "y", got.at[:, own], got.at[:, own], {"tp": outer_mate})
+            self.core = remote(name + "c", got.at[:, own], got.at[:, own], {"tp": core_mate})
+            self.more = remote(name + "m", got.at[:, mate], got.at[:, mate], {"tp": core_mate})
+
+        def start(self):
+            self.shard.start()
+
+        def spread(self):
+            self.shard.wait_recv()
+            self.outer.start()
+            self.core.start()
+
+        def done(self):
+            self.outer.wait_recv()
+            self.more.start()
+            self.core.wait()
+            self.more.wait()
+            self.outer.wait_send()
+
+        def wait_send(self):
+            self.shard.wait_send()
+
+    cot_strip, cot_target = columns(2 * (1 - shard) + core, part), columns(core, part)
+    cot_first = remote("ccx", cot_full.at[:, cot_strip], cot_peer.at[:, cot_target], {"shard": 1 - shard})
+    cot_second = remote("ccc", cot_peer.at[:, cot_target], cot_peer.at[:, cot_target], {"tp": core_mate})
     tile = min(256, tokens)
 
     def over_tiles(body):
@@ -447,8 +469,8 @@
     mixer_store = load(12, mixer, mixer_out)
     mixer_store.start()
 
-    h_two_first, h_two_second = columns_out("hc", h_two, h_two_peer)
-    h_two_first.start()
+    h_two_columns = Columns("hc", h_two, h_two_peer)
+    h_two_columns.start()
     x_store.wait()
     for copy in (x_outer, x_core, x_more):
         copy.wait_send()
@@ -639,9 +661,7 @@
         got_right(0, 0)
 
     def event_columns():
-        h_two_first.wait_recv()
-        h_two_second.start()
-        h_two_second.wait()
+        h_two_columns.done()
         turned(1, h_two_peer, 0, tokens)
         got_right(0, 1)
 
@@ -664,13 +684,14 @@
         right_copy(2, 0).start()
         right_copy(2, 1).start()
         over_shard("u3").start()
+        right_copy(2, 2).start()
         da_copy(3).start()
-        right_copy(2, 2).start()
         got_right(1, 2)
+        pump("g3")
 
     back_blocks, d_resid, resid_own = cot_got, dh_sum.at[1, :, pl.ds(0, part)], dh_sum.at[1, :, pl.ds(part, part)]
-    hone_first, hone_second = columns_out("ic", h_one_out, cot_peer)
-    dr_first, dr_second = columns_out("dc", h_two, h_two_peer)
+    h_one_columns = Columns("ic", h_one_out, cot_peer)
+    dr_columns = Columns("dc", h_two, h_two_peer)
     mixer_rights = 3 * hidden
 
     def mixer_right(kind):
@@ -707,7 +728,7 @@
         h_one_reload.start()
         for copy in [x_reload] + mixer_reloads:
             copy.wait()
-        h_two_first.wait_send()
+        h_two_columns.wait_send()
         gain_sums[...] = jnp.zeros((2, width), WIDE)
 
         @pl.loop(0, tokens // fine)
@@ -744,7 +765,7 @@
                 scaled - resid * scale * mean
             )
 
-        dr_first.start()
+        dr_columns.start()
 
     rim_out = remote(
         "rim_back", edge_v, rim_back, {"ctx": lax.rem(ctx + blocks - 1, blocks)}
@@ -772,15 +793,13 @@
         turned(0, h_two, shard * half, 0)
 
     def out_ready():
-        dr_first.wait_recv()
-        dr_second.start()
         right_copy(CHUNKS - 1, 0).wait_send()
 
         def body(lines):
             ffn_v[1, 0, lines] = gated[lines]
 
         over_tiles(body)
-        dr_second.wait_recv()
+        dr_columns.done()
         turned(0, h_two_peer, 0, tokens)
         got_mixer_right(0)
 
@@ -812,15 +831,17 @@
         small[...] = jnp.zeros(small.shape, WIDE)
         for tap in range(3):
             small[tap : tap + 1] = sums[tap]
-        for kind in range(1, 4):
-            mixer_right(kind).start()
+        ffn_peer()
+        mixer_right(1).start()
+        ffn_first[0].start()
+        mixer_right(2).start()
+        ffn_first[1].start()
+        mixer_right(3).start()
 
     def in_ready():
-        hone_first.wait_recv()
-        hone_second.start()
         h_one_reload.wait()
         turned(1, dh_got, 0, 0)
-        hone_second.wait_recv()
+        h_one_columns.done()
         turned(1, cot_peer, 0, tokens)
         got_mixer_right(1)
 
@@ -863,7 +884,6 @@
 
         over_tiles(body)
         back_pair.start()
-        got_mixer_right(2)
 
     def back_three_hops():
         back_pair.wait_recv()
@@ -873,7 +893,6 @@
 
         over_tiles(body)
         back_last.start()
-        got_mixer_right(3)
 
     def give_back(name, block, target, step):
         to, origin = lax.rem(ctx + step, blocks), lax.rem(ctx + blocks - step, blocks)
@@ -897,9 +916,13 @@
     ]
     act_own_load = load(21, act_out, da_got)
     act_peer_load = load(22, rights_peer.at[:, pl.ds(0, hidden)], da_got)
-    ffn_first = remote(
-        "fx", cot_full.at[:, pl.ds(half, half)], h_one.at[:, pl.ds(0, half)], {"shard": 1 - shard}
-    )
+    ffn_first = [
+        remote(
+            "fx%d" % index, cot_full.at[:, pl.ds(half + index * part, part)],
+            h_one.at[:, pl.ds(index * part, part)], {"shard": 1 - shard},
+        )
+        for index in range(2)
+    ]
     ffn_core = [
         remote("fc0", cot_full.at[:, columns(1 - core, part)], out_v.at[0, pl.ds(0, tokens)], {"tp": core_mate}),
         remote("fc1", h_one.at[:, columns(1 - core, part)], out_v.at[1, pl.ds(0, tokens)], {"tp": core_mate}),
@@ -944,10 +967,10 @@
     def ffn_peer():
         act_peer_load.wait()
         ffn_part(half)
-        ffn_first.start()
 
     def ffn_to_core():
-        ffn_first.wait_recv()
+        for copy in ffn_first:
+            copy.wait_recv()
         for copy in ffn_core:
             copy.start()
 
@@ -1017,13 +1040,12 @@
         kept.start()
 
     def event_third():
-        over_shard("g3").wait_recv()
         over_shard("u3").wait_recv()
         ready(3)
         whole_feed(3)
         for kind in range(3):
             right_copy(3, kind).start()
-        hone_first.start()
+        h_one_columns.start()
         mixer_right(0).start()
         got_right(2, 2)
 
@@ -1061,17 +1083,29 @@
         dh_last.start()
         got_right(3, 1)
 
-    def last_rights():
+    def rights_and_conv():
+        got_right(3, 2)
+        conv_back()
+
+    def spread_columns():
+        h_one_columns.spread()
+        dr_columns.spread()
         ffn_own()
-        got_right(3, 2)
-
-    def proj_and_ffn():
-        proj_back()
-        ffn_peer()
-
-    def back_and_ffn():
+
+    def back_and_right():
+        got_mixer_right(2)
+        back_two_hops()
+
+    def outer_and_back():
+        got_mixer_right(3)
         ffn_to_outer()
         back_three_hops()
+
+    def ends_back():
+        block_back()
+        input_back()
+        small[3:5] = gain_sums[:, own_part]
+        small_shard.start()
 
     small_shard = remote("ss", small, small_got.at[blocks], {"shard": 1 - shard})
 
@@ -1084,14 +1118,9 @@
 
     small_steps = [small_ctx(step) for step in range(1, blocks)]
 
-    def ends_back():
-        input_back()
-        block_back()
-        small[3:5] = gain_sums[:, own_part]
-        small_shard.start()
-
     events = {
         0: event_start,
+        1: h_two_columns.spread,
         2: event_columns,
         4: event_first,
         5: lambda: whole_back(1),
@@ -1106,15 +1135,15 @@
         18: dh_two_hops,
         20: dh_three_hops,
         21: resid_back,
-        22: last_rights,
-        23: conv_back,
+        22: rights_and_conv,
+        23: spread_columns,
         24: out_ready,
-        25: proj_and_ffn,
+        25: proj_back,
         26: in_ready,
         27: back_one_hop,
-        28: back_two_hops,
+        28: back_and_right,
         29: ffn_to_core,
-        30: back_and_ffn,
+        30: outer_and_back,
         31: ends_back,
     }
 
@@ -1144,8 +1173,8 @@
         out.wait_send()
     for out, _ in small_steps:
         out.wait_send()
-    for copy in (small_shard, gain_outer, gain_core, gain_more, hone_first, hone_second, dr_first, dr_second, back_away, back_pair, back_last,
-                 ffn_first, *ffn_core, *ffn_outer):
+    for copy in (small_shard, gain_outer, gain_core, gain_more, h_one_columns, dr_columns, back_away, back_pair, back_last,
+                 *ffn_first, *ffn_core, *ffn_outer):
         copy.wait_send()
     for name in pieces:
         over_shard(name).wait_send()
@@ -1207,7 +1236,7 @@
         shape(up_w.shape, LOW),
         shape((pieces, rows, PIECE), LOW),
         shape((pieces, rows, PIECE), LOW),
-        shape((tokens, 3 * hidden + width), LOW),
+        shape((tokens, 3 * hidden + width + half), LOW),
         shape((tokens, width), LOW),
         shape((tokens, width), LOW),
         shape((2, tokens, half), LOW),

time: 641 us -> 630 us (0.983)
  Pallas kernels: 600 us -> 589 us
    pallas_call x1, Pallas kernels: 600 us -> 589 us  [front(): pl.pallas_call(front_kernel, out_shape=outs, in_specs=[vmem, vmem] + [pl....]
where the time goes in v8:
time: 630 us; the launch traced here: 623 us
  Pallas kernels  589 us (93%)
  other arithmetic  26 us (4%)
  local copies, waits for them, and re-layouts  6.79 us (1%)
    pallas_call x1, Pallas kernels, front(): pl.pallas_call(front_kernel, out_shape=outs, in_specs=[vmem, vmem] + [pl....  589 us
    convert_element_type x2, other arithmetic, on_device(): value.astype(WIDE)  15.9 us

profile of v8, /device:TPU:0, one launch (start us, length us, event | category | flops | bytes accessed | tf_op | source)
XLA Modules:
  0.0 622.8 jit_solution(16031779316241972548)
XLA Ops:
  0.7 0.8 reduce-window_clone.1
  1.5 0.7 subtract_bitcast_fusion
  2.1 0.1 select_reduce_fusion
  2.2 0.1 slice_compare_fusion.3
  2.4 0.9 copy.28.masks
  3.3 0.5 broadcast.128
  3.8 1.3 reduce.3
  5.1 0.1 reshape_squeeze.3
  5.2 0.0 copy-start.3
  5.2 0.6 fusion.4.sending
  5.8 0.7 convert_reduce_fusion.place
  6.5 0.7 stack.21
  7.2 0.7 stack.22
  7.9 0.6 fusion.3.own_gains
  8.5 0.0 copy-done.3
  8.5 1.3 convert_element_type.31.taps
  9.8 588.8 %shard_map.195 = (bf16[3,1024,512]{2,1,0:T(8,128)(2,1)}, bf16[1024,512]{1,0:T(8,128)(2,1)}, bf16[1024,2048]{1,0:T(8,128)(2,1)}, bf16[1024,2048]{1,0:T(8,128)(2,1...) custom-call(bf16[512,512]{1,0:T(8,128)(2,1)} %x_in.1, ...), custom_call_target="tpu_custom_call" | custom-call | flops 274877906944 | bytes 536870912 | tf_op jit(solution)/shard_map/pallas_call | solution.py:1297
  598.6 4.1 slice_convert_fusion.3
  602.7 0.0 copy-start.1
  602.7 0.0 copy-start
  602.7 3.2 convert_bitcast_fusion
  605.9 0.7 fusion.6
  606.6 0.0 copy-done.1
  606.6 1.4 gather_fusion.1
  608.0 0.0 copy-done
  608.0 1.4 gather_fusion
  609.4 0.0 copy-start.2
  609.4 11.8 %slice_convert_fusion = (f32[1024,2048]{1,0:T(8,128)}, f32[1024,2048]{1,0:T(8,128)}, f32[1024,2048]{1,0:T(8,128)}) fusion(bf16[1024,8192]{1,0:T(8,128)(2,1)} %get-tuple-element.16), kind=kLoop, calls=%fused_computation.3 | loop fusion | flops 6291456 | bytes 37748736 | tf_op jit(solution)/shard_map/convert_element_type | solution.py:1522
  621.2 0.0 copy-done.2
  621.2 0.6 fusion.8
  621.8 0.6 slice.22
  (10 shorter events, 0.1 us)
Async XLA Ops:
  5.2 3.3 copy-start.3
  602.7 3.9 copy-start.1
  602.7 5.3 copy-start
  609.4 11.8 %copy-start.2 = (f32[8,512]{1,0:T(8,128)S(1)}, f32[8,512]{1,0:T(8,128)}, u32[]{:S(2)}) copy-start(f32[8,512]{1,0:T(8,128)} %get-tuple-element.17) | copy-start | bytes 49156

commit v9 on v8

--- a/solution.py
+++ b/solution.py
@@ -686,7 +686,10 @@
         over_shard("u3").start()
         right_copy(2, 2).start()
         da_copy(3).start()
-        got_right(1, 2)
+        got_right(2, 0)
+
+    def back_second():
+        whole_back(2)
         pump("g3")
 
     back_blocks, d_resid, resid_own = cot_got, dh_sum.at[1, :, pl.ds(0, part)], dh_sum.at[1, :, pl.ds(part, part)]
@@ -1126,9 +1129,9 @@
         5: lambda: whole_back(1),
         6: lambda: got_right(1, 0),
         8: lambda: got_right(1, 1),
-        10: event_second,
-        11: lambda: whole_back(2),
-        12: lambda: got_right(2, 0),
+        10: lambda: got_right(1, 2),
+        12: event_second,
+        13: back_second,
         14: lambda: got_right(2, 1),
         16: event_third,
         17: dh_one_hop,

time: 630 us -> 625 us (level)
  Pallas kernels: 589 us -> 582 us
    pallas_call x1, Pallas kernels: 589 us -> 582 us  [front(): pl.pallas_call(front_kernel, out_shape=outs, in_specs=[vmem, vmem] + [pl....]
where the time goes in v9:
time: 625 us; the launch traced here: 616 us
  Pallas kernels  582 us (93%)
  other arithmetic  26 us (4%)
  local copies, waits for them, and re-layouts  6.79 us (1%)
    pallas_call x1, Pallas kernels, front(): pl.pallas_call(front_kernel, out_shape=outs, in_specs=[vmem, vmem] + [pl....  582 us
    convert_element_type x2, other arithmetic, on_device(): value.astype(WIDE)  15.9 us

profile of v9, /device:TPU:0, one launch (start us, length us, event | category | flops | bytes accessed | tf_op | source)
XLA Modules:
  0.0 615.8 jit_solution(4931809803856970337)
XLA Ops:
  0.7 0.8 reduce-window_clone.1
  1.5 0.7 subtract_bitcast_fusion
  2.1 0.1 select_reduce_fusion
  2.2 0.1 slice_compare_fusion.3
  2.4 0.9 copy.28.masks
  3.3 0.5 broadcast.128
  3.8 1.3 reduce.3
  5.1 0.1 reshape_squeeze.3
  5.2 0.0 copy-start.3
  5.2 0.6 fusion.4.sending
  5.8 0.7 convert_reduce_fusion.place
  6.5 0.7 stack.21
  7.2 0.7 stack.22
  7.9 0.6 fusion.3.own_gains
  8.5 0.0 copy-done.3
  8.5 1.3 convert_element_type.31.taps
  9.8 581.9 %shard_map.195 = (bf16[3,1024,512]{2,1,0:T(8,128)(2,1)}, bf16[1024,512]{1,0:T(8,128)(2,1)}, bf16[1024,2048]{1,0:T(8,128)(2,1)}, bf16[1024,2048]{1,0:T(8,128)(2,1...) custom-call(bf16[512,512]{1,0:T(8,128)(2,1)} %x_in.1, ...), custom_call_target="tpu_custom_call" | custom-call | flops 274877906944 | bytes 536870912 | tf_op jit(solution)/shard_map/pallas_call | solution.py:1300
  591.6 4.1 slice_convert_fusion.3
  595.7 0.0 copy-start.1
  595.7 0.0 copy-start
  595.7 3.2 convert_bitcast_fusion
  598.9 0.7 fusion.6
  599.6 0.0 copy-done.1
  599.6 1.4 gather_fusion.1
  601.0 0.0 copy-done
  601.0 1.4 gather_fusion
  602.4 0.0 copy-start.2
  602.4 11.8 %slice_convert_fusion = (f32[1024,2048]{1,0:T(8,128)}, f32[1024,2048]{1,0:T(8,128)}, f32[1024,2048]{1,0:T(8,128)}) fusion(bf16[1024,8192]{1,0:T(8,128)(2,1)} %get-tuple-element.16), kind=kLoop, calls=%fused_computation.3 | loop fusion | flops 6291456 | bytes 37748736 | tf_op jit(solution)/shard_map/convert_element_type | solution.py:1525
  614.2 0.0 copy-done.2
  614.2 0.6 fusion.8
  614.8 0.6 slice.22
  (10 shorter events, 0.1 us)
Async XLA Ops:
  5.2 3.3 copy-start.3
  595.7 3.9 copy-start.1
  595.7 5.3 copy-start
  602.4 11.8 %copy-start.2 = (f32[8,512]{1,0:T(8,128)S(1)}, f32[8,512]{1,0:T(8,128)}, u32[]{:S(2)}) copy-start(f32[8,512]{1,0:T(8,128)} %get-tuple-element.17) | copy-start | bytes 49156
